TPU v7x, 32 devices: a whole 2x2x4 slice. The times are simulated.
32 devices in a mesh: narrow: 4 (over x, core), wide: 8 (over z, y).
Axes of the slice: x: 2, y: 2, z: 4, core: 2. Of those that a mesh axis runs over, the one named last changes fastest.
Arguments:
- panel: float32 [131072, 128], P(('narrow', 'wide')), may hold values from -6 to 6
- flips: int32 [131072], P(('narrow', 'wide')), may hold values from 0 to 1
- picks: int32 [8192], replicated, may hold values from 0 to 131071, as said below
Outputs:
- mixed: float32 [131072, 128], P(('narrow', 'wide'))
- sketch: float32 [8192, 128], P(('narrow', 'wide'))
- gram: float32 [128, 128], replicated
Inputs may be any that keep to these rules, and one draw needn't show every extreme that they name: Split picks into aligned blocks of 256 entries, one block for each device in the order of narrow+wide. In every block, at most 8 entries name rows of any one device's block of 4096 rows, and some device's block is named exactly 8 times. Within a device's block the row is uniform; repeats may occur.
All inputs are finite; a program needn't handle non-finite values.
Results may differ from a plain program's by a relative error of at most 0.00011.
Values sent between devices are 32-bit elements; how exact they have to be, the bound alone decides.
No kernel may reach another device: no remote copies, remote signals or barrier semaphores. Data moves between devices by JAX's collectives and lax.ppermute only.
A program may use at most 64 MiB of HBM per device.

v0:
```python
import jax
import jax.numpy as jnp
from jax import lax
from jax.sharding import PartitionSpec as P


def from_partner(value, axis, apart):
    mask = 2**apart
    pairs = [(source, source ^ mask) for source in range(lax.axis_size(axis))]
    return lax.ppermute(value, axis, pairs)


def hadamard(order):
    index = jnp.arange(order, dtype=jnp.int32)
    both = index[:, None] & index[None, :]
    parity = jnp.zeros((order, order), jnp.int32)
    level = 0
    while 1 << level < order:
        parity = parity ^ both >> level & 1
        level += 1
    return (1 - 2 * parity).astype(jnp.float32)


def on_device(panel, flips, picks):
    rows_here, width = panel.shape
    inner = rows_here // 64
    devices = lax.axis_size("narrow") * lax.axis_size("wide")
    signed = panel * (1 - 2 * flips).astype(jnp.float32)[:, None]
    shaped = signed.reshape(64, inner, width)
    shaped = jnp.einsum("ap,pqc->aqc", hadamard(64), shaped, precision=lax.Precision.HIGHEST)
    shaped = jnp.einsum("bq,aqc->abc", hadamard(inner), shaped, precision=lax.Precision.HIGHEST)
    local = shaped.reshape(rows_here, width)
    for level in range(lax.axis_size("narrow").bit_length() - 1):
        partner = from_partner(local, "narrow", level)
        upper = lax.axis_index("narrow") >> level & 1 == 1
        local = jnp.where(upper, partner - local, local + partner)
    for level in range(lax.axis_size("wide").bit_length() - 1):
        partner = from_partner(local, "wide", level)
        upper = lax.axis_index("wide") >> level & 1 == 1
        local = jnp.where(upper, partner - local, local + partner)
    mixed = local * (1.0 / float(rows_here * devices) ** 0.5)
    me = lax.axis_index(("narrow", "wide"))
    base = me * rows_here
    wanted = picks - base
    owned = (wanted >= 0) & (wanted < rows_here)
    chosen = jnp.take(mixed, jnp.clip(wanted, 0, rows_here - 1), axis=0)
    sketch = lax.psum_scatter(
        jnp.where(owned[:, None], chosen, jnp.zeros_like(chosen)),
        ("narrow", "wide"),
        scatter_dimension=0,
        tiled=True,
    )
    total = float(picks.shape[0])
    part = jnp.dot(
        sketch.T, sketch, precision=lax.Precision.HIGHEST, preferred_element_type=jnp.float32
    )
    gram = lax.psum(part, ("narrow", "wide")) / total
    return (mixed, sketch, gram)


def solution(mesh):
    in_specs = (P(("narrow", "wide"), None), P(("narrow", "wide")), P())
    out_specs = (P(("narrow", "wide"), None), P(("narrow", "wide"), None), P())
    return jax.shard_map(
        on_device, mesh=mesh, in_specs=in_specs, out_specs=out_specs, check_vma=False
    )
```

profile of v0, /device:TPU:0, one launch (start us, length us, event | category | flops | bytes accessed | tf_op | source)
XLA Modules:
  0.0 577.5 jit_solution(13922971044433143078)
XLA Ops:
  7.2 0.0 reduce-scatter.2.cloned.1.call-start
  7.2 0.7 subtract_convert_fusion
  7.9 2.2 broadcast_multiply_fusion
  10.1 3.0 fusion.2
  13.2 3.3 fusion
  16.5 0.0 copy-start.3
  16.5 0.5 collective-permute-start
  17.0 0.8 copy-done.3
  17.8 3.1 collective-permute-done
  20.9 2.4 add_select_fusion.3
  23.4 0.0 copy-start.2
  23.4 2.9 collective-permute-start.1
  26.3 46.0 %collective-permute-done.1 = f32[4096,128]{1,0:T(8,128)} collective-permute-done((f32[4096,128]{1,0:T(8,128)S(1)}, f32[4096,128]{1,0:T(8,128)}, u32[]{:S(2)}, u32[]{:S(2)}) %collective-permute-start.1) | collective-permute-done | bytes 2097184 | tf_op jit(solution)/shard_map/ppermute | solution.py:10
  72.3 2.4 add_select_fusion.2
  74.8 1.8 collective-permute-start.2
  76.6 45.5 %collective-permute-done.2 = f32[4096,128]{1,0:T(8,128)} collective-permute-done((f32[4096,128]{1,0:T(8,128)S(1)}, f32[4096,128]{1,0:T(8,128)}, u32[]{:S(2)}, u32[]{:S(2)}) %collective-permute-start.2) | collective-permute-done | bytes 2097184 | tf_op jit(solution)/shard_map/ppermute | solution.py:10
  122.1 3.1 add_select_fusion.1
  125.2 1.5 collective-permute-start.3
  126.7 45.1 %collective-permute-done.3 = f32[4096,128]{1,0:T(8,128)} collective-permute-done((f32[4096,128]{1,0:T(8,128)}, f32[4096,128]{1,0:T(8,128)}, u32[]{:S(2)}, u32[]{:S(2)}) %collective-permute-start.3) | collective-permute-done | bytes 2097184 | tf_op jit(solution)/shard_map/ppermute | solution.py:10
  171.8 2.4 add_select_fusion
  174.3 2.2 collective-permute-start.4
  176.6 89.0 %collective-permute-done.4 = f32[4096,128]{1,0:T(8,128)} collective-permute-done((f32[4096,128]{1,0:T(8,128)S(1)}, f32[4096,128]{1,0:T(8,128)}, u32[]{:S(2)}, u32[]{:S(2)}) %collective-permute-start.4) | collective-permute-done | bytes 2097184 | tf_op jit(solution)/shard_map/ppermute | solution.py:10
  265.6 2.5 select_multiply_fusion
  268.1 27.7 %gather_fusion = f32[8192,128]{1,0:T(8,128)} fusion(f32[4096,128]{1,0:T(8,128)S(1)} %select_multiply_fusion, s32[8192]{0:T(1024)S(1)} %fusion.8), kind=kCustom, calls=%fused_computation | custom fusion | bytes 8421376 | tf_op jit(solution)/shard_map/jit(_take)/gather | solution.py:46
  295.9 7.6 %select_select_fusion = f32[8192,128]{1,0:T(8,128)} fusion(f32[8192,128]{1,0:T(8,128)} %gather_fusion, pred[8192]{0:T(1024)(128)(4,1)S(1)} %get-tuple-element.4, pred[8192]{0:T(1024)(128)(4,1)S(1)} %get-tuple-element.3), kind=kLoop, calls=%fused_computation.1 | loop fusion | flops 2097152 | bytes 8404992 | tf_op jit(solution)/shard_map/jit(_where)/select_n | solution.py:48
  303.5 0.0 reduce-scatter.2.cloned.1.call-update
  303.5 0.0 all-reduce.2.cloned.1.call-start
  303.5 144.3 %reduce-scatter.2.cloned.1.call-done = f32[256,128]{1,0:T(8,128)} async-done(((f32[8192,128]{1,0:T(8,128)}), f32[256,128]{1,0:T(8,128)}) %reduce-scatter.2.cloned.1.call-update) | async-done | bytes 131088 | tf_op jit(solution)/shard_map/reduce_scatter | solution.py:47
  447.8 2.0 fusion.21
  449.8 0.0 all-reduce.2.cloned.1.call-update
  449.9 119.3 %all-reduce.2.cloned.1.call-done = f32[128,128]{1,0:T(8,128)} async-done(((f32[128,128]{1,0:T(8,128)}), f32[128,128]{1,0:T(8,128)}) %all-reduce.2.cloned.1.call-update) | async-done | bytes 65552 | tf_op jit(solution)/shard_map/psum | solution.py:57
  569.2 1.5 broadcast_multiply_fusion.1
  (9 shorter events, 0.1 us)
Async XLA Ops:
  7.2 440.7 %reduce-scatter.2.cloned.1.call-start = ((), (), s32[]{:S(2)}) async-start(), calls=%async_computation.1 | async-start | bytes 4325376 | tf_op jit(solution)/shard_map/reduce_scatter | solution.py:47
  16.5 1.3 copy-start.3
  16.5 4.4 collective-permute-start
  23.4 2.9 copy-start.2
  23.4 49.0 %collective-permute-start.1 = (f32[4096,128]{1,0:T(8,128)S(1)}, f32[4096,128]{1,0:T(8,128)}, u32[]{:S(2)}, u32[]{:S(2)}) collective-permute-start(f32[4096,128]{1,0:T(8,128)S(1)} %add_select_fusion.3), channel_id=1, source_target_pairs={{0,16},{8,24},{16,0},{24,8},{1,17},{9,25},{17,1},{25,9},{2,18},{10... | collective-permute-start | bytes 6291464 | tf_op jit(solution)/shard_map/ppermute | solution.py:10
  74.8 47.3 %collective-permute-start.2 = (f32[4096,128]{1,0:T(8,128)S(1)}, f32[4096,128]{1,0:T(8,128)}, u32[]{:S(2)}, u32[]{:S(2)}) collective-permute-start(f32[4096,128]{1,0:T(8,128)S(1)} %add_select_fusion.2), channel_id=1, source_target_pairs={{0,1},{1,0},{2,3},{3,2},{4,5},{5,4},{6,7},{7,6},{8,9},{9,8},{10,11... | collective-permute-start | bytes 6291464 | tf_op jit(solution)/shard_map/ppermute | solution.py:10
  125.2 46.6 %collective-permute-start.3 = (f32[4096,128]{1,0:T(8,128)}, f32[4096,128]{1,0:T(8,128)}, u32[]{:S(2)}, u32[]{:S(2)}) collective-permute-start(f32[4096,128]{1,0:T(8,128)} %add_select_fusion.1), channel_id=1, source_target_pairs={{0,2},{1,3},{2,0},{3,1},{4,6},{5,7},{6,4},{7,5},{8,10},{9,11},{10,... | collective-permute-start | bytes 6291464 | tf_op jit(solution)/shard_map/ppermute | solution.py:10
  126.7 49.8 %copy-start.4 = (s32[8192]{0:T(1024)S(1)}, s32[8192]{0:T(1024)}, u32[]{:S(2)}) copy-start(s32[8192]{0:T(1024)} %param.5) | copy-start | bytes 98308
  174.3 2.3 copy-start.1
  174.3 91.4 %collective-permute-start.4 = (f32[4096,128]{1,0:T(8,128)S(1)}, f32[4096,128]{1,0:T(8,128)}, u32[]{:S(2)}, u32[]{:S(2)}) collective-permute-start(f32[4096,128]{1,0:T(8,128)S(1)} %add_select_fusion), channel_id=1, source_target_pairs={{0,4},{1,5},{2,6},{3,7},{4,0},{5,1},{6,2},{7,3},{8,12},{9,13},{10,... | collective-permute-start | bytes 6291464 | tf_op jit(solution)/shard_map/ppermute | solution.py:10
  268.1 27.7 %copy-start = (f32[4096,128]{1,0:T(8,128)}, f32[4096,128]{1,0:T(8,128)S(1)}, u32[]{:S(2)}) copy-start(f32[4096,128]{1,0:T(8,128)S(1)} %select_multiply_fusion) | copy-start | bytes 6291460
  303.5 265.7 %all-reduce.2.cloned.1.call-start = ((), (), s32[]{:S(2)}) async-start(), calls=%async_computation.2 | async-start | bytes 131072 | tf_op jit(solution)/shard_map/psum | solution.py:57
Sparse Core Ops, SparseCore 0:
  303.6 144.1 reduce-scatter.1
  454.0 115.1 all-reduce.1
where the time goes:
time: 579 us; the launch traced here: 578 us
  waiting for transfers between devices  492 us (85%)
  local copies, waits for them, and re-layouts  28.5 us (5%)
  other arithmetic  25 us (4%)
  between operations  14.1 us (2%)
  starting transfers between devices  9.09 us (2%)
  matrix products  8.3 us (1%)
    ppermute x5, waiting for transfers between devices, from_partner(): return lax.ppermute(value, axis, pairs)  229 us
    reduce_scatter x1, waiting for transfers between devices, on_device(): lax.psum_scatter(jnp.where(owned[:, None], chosen, jnp.zeros_like(chosen)...  144 us
    psum x1, waiting for transfers between devices, on_device(): gram = lax.psum(part, ('narrow', 'wide')) / total  119 us
    gather x1, local copies, waits for them, and re-layouts, on_device(): chosen = jnp.take(mixed, jnp.clip(wanted, 0, rows_here - 1), axis=0)  27.7 us
  transfers between devices with their start and end apart: 7, of which 7 were waited for; matrix products, arithmetic and copies ran while one was open for 0% of the time, Pallas kernels for 0%

commit v1 on v0

v1 whole, which is shorter than its diff:
```python
import functools

import jax
import jax.numpy as jnp
from jax import lax
from jax.experimental import pallas as pl
from jax.experimental.pallas import tpu as pltpu
from jax.sharding import PartitionSpec as P

BLOCK = 256
AXES = ("narrow", "wide")


def signs(order):
    rows = lax.broadcasted_iota(jnp.int32, (order, order), 0)
    both = rows & lax.broadcasted_iota(jnp.int32, (order, order), 1)
    parity = jnp.zeros((order, order), jnp.int32)
    for level in range(order.bit_length() - 1):
        parity = parity ^ (both >> level & 1)
    return (1 - 2 * parity).astype(jnp.float32)


def local_kernel(scale, flips_ref, panel_ref, *refs):
    *outs, held = refs
    blocks = panel_ref.shape[0] // BLOCK
    width = panel_ref.shape[1]
    lanes = flips_ref.shape[1]
    per = BLOCK // lanes
    base = signs(BLOCK)
    for b in range(blocks):
        row = jnp.concatenate([flips_ref[b * per + i : b * per + i + 1, :] for i in range(per)], axis=1)
        mixer = (base * (1 - 2 * row).astype(jnp.float32)).astype(jnp.bfloat16)
        values = panel_ref[b * BLOCK : (b + 1) * BLOCK, :]
        high = values.astype(jnp.bfloat16)
        rest = values - high.astype(jnp.float32)
        middle = rest.astype(jnp.bfloat16)
        low = (rest - middle.astype(jnp.float32)).astype(jnp.bfloat16)
        parts = jnp.concatenate([high, middle, low], axis=1)
        out = jnp.dot(mixer, parts, preferred_element_type=jnp.float32)
        held[b] = out[:, :width] + out[:, width : 2 * width] + out[:, 2 * width :]
    strip = 16
    share = blocks // len(outs)

    def body(step, carry):
        at = pl.multiple_of(step * strip, strip)
        items = [held[b, pl.ds(at, strip), :] for b in range(blocks)]
        apart = 1
        while apart < blocks:
            items = [
                items[b] + items[b ^ apart] if b & apart == 0 else items[b ^ apart] - items[b]
                for b in range(blocks)
            ]
            apart *= 2
        for b in range(blocks):
            spot = pl.multiple_of((b % share) * BLOCK + at, strip)
            outs[b // share][pl.ds(spot, strip), :] = items[b] * scale
        return carry

    lax.fori_loop(0, BLOCK // strip, body, 0)


def local_transform(panel, flips, scale, pieces):
    rows, width = panel.shape
    return pl.pallas_call(
        functools.partial(local_kernel, scale),
        out_shape=[jax.ShapeDtypeStruct((rows // pieces, width), jnp.float32)] * pieces,
        in_specs=[pl.BlockSpec(memory_space=pltpu.VMEM)] * 2,
        out_specs=[pl.BlockSpec(memory_space=pltpu.VMEM)] * pieces,
        scratch_shapes=[pltpu.VMEM((rows // BLOCK, BLOCK, width), jnp.float32)],
        compiler_params=pltpu.CompilerParams(vmem_limit_bytes=32 * 2**20),
    )(flips.reshape(rows // 128, 128), panel)


def exchange(value, axis, level):
    mask = 2**level
    pairs = [(source, source ^ mask) for source in range(lax.axis_size(axis))]
    partner = lax.ppermute(value, axis, pairs)
    sign = (1 - 2 * (lax.axis_index(axis) >> level & 1)).astype(jnp.float32)
    return partner + sign * value


def send_rows(picks, base, rows_here, devices, most):
    offsets = picks.reshape(devices, -1) - base
    owned = (offsets >= 0) & (offsets < rows_here)
    rank = jnp.cumsum(owned.astype(jnp.int32), axis=1) - 1
    slot = jnp.arange(most, dtype=jnp.int32)
    hit = owned[:, None, :] & (rank[:, None, :] == slot[None, :, None])
    rows = jnp.sum(jnp.where(hit, offsets[:, None, :], 0), axis=2)
    return rows, jnp.any(hit, axis=2)


def landing(block, rows_here, most):
    owners = block // rows_here
    order = jnp.arange(block.shape[0], dtype=jnp.int32)
    earlier = (owners[:, None] == owners[None, :]) & (order[None, :] < order[:, None])
    return owners * most + jnp.sum(earlier.astype(jnp.int32), axis=1)


def on_device(panel, flips, picks):
    rows_here, width = panel.shape
    narrow, wide = lax.axis_size("narrow"), lax.axis_size("wide")
    devices = narrow * wide
    scale = 1.0 / float(rows_here * devices) ** 0.5
    stages = [("narrow", l) for l in range(narrow.bit_length() - 1)]
    stages += [("wide", l) for l in range(wide.bit_length() - 1)]
    head, rest = stages[0], stages[1:]
    orders = [
        [rest[-1]] + rest[:-1],
        [rest[-1]] + rest[:-1],
        rest,
        [rest[-2]] + rest[:-2] + [rest[-1]],
    ]
    chunks = local_transform(panel, flips, scale, len(orders))
    done = []
    for value, order in zip(chunks, orders):
        for axis, level in [head] + order:
            value = exchange(value, axis, level)
        done.append(value)
    mixed = jnp.concatenate(done, axis=0)

    me = lax.axis_index(AXES)
    per = picks.shape[0] // devices
    most = -(-per // devices)
    rows, filled = send_rows(picks, me * rows_here, rows_here, devices, most)
    chosen = jnp.take(mixed, rows.reshape(-1), axis=0, mode="clip")
    kept = jnp.where(filled.reshape(-1)[:, None], chosen, 0.0)
    part = lax.dot_general(
        kept, kept, (((0,), (0,)), ((), ())),
        precision=lax.Precision.HIGHEST, preferred_element_type=jnp.float32,
    )
    both = jnp.concatenate(
        [chosen.reshape(devices, most, width), part.reshape(devices, -1, width)], axis=1
    )
    landed = lax.all_to_all(both, AXES, 0, 0, tiled=True)
    spots = landing(lax.dynamic_slice(picks, (me * per,), (per,)), rows_here, most)
    sketch = jnp.take(landed[:, :most].reshape(devices * most, width), spots, axis=0, mode="clip")
    mine = jnp.sum(landed[:, most:], axis=0) / float(picks.shape[0])
    gram = lax.all_to_all(
        jnp.broadcast_to(mine[None], (devices,) + mine.shape), AXES, 0, 0, tiled=True
    ).reshape(width, width)
    return (mixed, sketch, gram)


def solution(mesh):
    in_specs = (P(AXES, None), P(AXES), P())
    out_specs = (P(AXES, None), P(AXES, None), P())
    return jax.shard_map(
        on_device, mesh=mesh, in_specs=in_specs, out_specs=out_specs, check_vma=False
    )
```

time: 579 us -> 174 us (0.30)
  waiting for transfers between devices: 492 us -> 128 us
  local copies, waits for them, and re-layouts: 28.5 us -> 6.06 us
  starting transfers between devices: 9.09 us -> 29.8 us
  other arithmetic: 25 us -> 6.4 us
  between operations: 14.1 us -> 0.9 us
  matrix products: 8.3 us -> 0.49 us
    reduce_scatter x1 -> x0, waiting for transfers between devices: 144 us -> none  [on_device(): lax.psum_scatter(jnp.where(owned[:, None], chosen, jnp.zeros_like(chosen)...]
    psum x1 -> x0, waiting for transfers between devices: 119 us -> none  [on_device(): gram = lax.psum(part, ('narrow', 'wide')) / total]
    ppermute x5 -> x20, waiting for transfers between devices: 229 us -> 112 us  [exchange(): partner = lax.ppermute(value, axis, pairs)]
    gather x1 -> x2, local copies, waits for them, and re-layouts: 27.7 us -> 2.07 us  [the longest x1 1.34 us: on_device(): jnp.take(landed[:, :most].reshape(devices * most, width), spots, axis=0,...]
    select_n x5 -> x1, other arithmetic: 18.1 us -> 0.08 us  [landing(): owners = block // rows_here]
    all_to_all x0 -> x2, waiting for transfers between devices: none -> 16.3 us  [the longest x1 10.4 us: on_device(): landed = lax.all_to_all(both, AXES, 0, 0, tiled=True)]
    ppermute x5 -> x20, starting transfers between devices: 9.01 us -> 23.6 us  [exchange(): partner = lax.ppermute(value, axis, pairs)]
    dot_general x3 -> x1, matrix products: 8.3 us -> 0.49 us  [on_device(): lax.dot_general(kept, kept, (((0,), (0,)), ((), ())), precision=lax.Preci...]
  transfers between devices with their start and end apart: 7 -> 22, of which waited for: 7 -> 12; matrix products, arithmetic and copies ran while one was open for 0% -> 4% of each run, Pallas kernels for 0% -> 0%
where the time goes in v1:
time: 174 us
  waiting for transfers between devices  128 us (74%)
  starting transfers between devices  29.8 us (17%)
  other arithmetic  6.4 us (4%)
  local copies, waits for them, and re-layouts  6.06 us (3%)
  Pallas kernels  1.95 us (1%)
    ppermute x20, waiting for transfers between devices, exchange(): partner = lax.ppermute(value, axis, pairs)  112 us
    ppermute x20, starting transfers between devices, exchange(): partner = lax.ppermute(value, axis, pairs)  23.6 us
    all_to_all x1, waiting for transfers between devices, on_device(): landed = lax.all_to_all(both, AXES, 0, 0, tiled=True)  10.4 us
    all_to_all x1, waiting for transfers between devices, on_device(): lax.all_to_all(jnp.broadcast_to(mine[None], (devices,) + mine.shape), AXE...  5.91 us
    all_to_all x1, starting transfers between devices, on_device(): landed = lax.all_to_all(both, AXES, 0, 0, tiled=True)  3.7 us
  transfers between devices with their start and end apart: 22, of which 12 were waited for; matrix products, arithmetic and copies ran while one was open for 4% of the time, Pallas kernels for 0%

profile of v1, /device:TPU:0, one launch (start us, length us, event | category | flops | bytes accessed | tf_op | source)
XLA Modules:
  0.0 173.9 jit_solution(10680018330360046487)
XLA Ops:
  0.6 1.6 copy-done
  2.2 0.7 copy-done.1
  2.9 1.9 %shard_map.58 = (f32[1024,128]{1,0:T(8,128)S(1)}, f32[1024,128]{1,0:T(8,128)S(1)}, f32[1024,128]{1,0:T(8,128)S(1)}, f32[1024,128]{1,0:T(8,128)S(1)}) custom-call(s32[32,128]{1,0:T(8,128)S(1)} %bitcast.12, f32[4096,128]{1,0:T(8,128)S(1)} %copy-done), custom_call_target="tpu_custom_call" | custom-call | tf_op jit(solution)/shard_map/pallas_call | solution.py:64
  8.6 1.1 multiply_add_fusion.19
  9.7 4.1 %collective-permute-start.1 = (f32[1024,128]{1,0:T(8,128)S(1)}, f32[1024,128]{1,0:T(8,128)S(1)}, u32[]{:S(2)}, u32[]{:S(2)}) collective-permute-start(f32[1024,128]{1,0:T(8,128)S(1)} %multiply_add_fusion.19), channel_id=1, source_target_pairs={{0,4},{1,5},{2,6},{3,7},{4,0},{5,1},{6,2},{7,3},{8,12},{9,13},{10,... | collective-permute-start | bytes 1572872 | tf_op jit(solution)/shard_map/ppermute | solution.py:77
  13.7 1.1 multiply_add_fusion.14
  15.0 1.9 %collective-permute-start.11 = (f32[1024,128]{1,0:T(8,128)S(1)}, f32[1024,128]{1,0:T(8,128)S(1)}, u32[]{:S(2)}, u32[]{:S(2)}) collective-permute-start(f32[1024,128]{1,0:T(8,128)S(1)} %multiply_add_fusion.9), channel_id=1, source_target_pairs={{0,16},{8,24},{16,0},{24,8},{1,17},{9,25},{17,1},{25,9},{2,18},{10... | collective-permute-start | bytes 1572872 | tf_op jit(solution)/shard_map/ppermute | solution.py:77
  16.9 1.6 collective-permute-start.16
  18.6 30.4 %collective-permute-done.1 = f32[1024,128]{1,0:T(8,128)S(1)} collective-permute-done((f32[1024,128]{1,0:T(8,128)S(1)}, f32[1024,128]{1,0:T(8,128)S(1)}, u32[]{:S(2)}, u32[]{:S(2)}) %collective-permute-start.1) | collective-permute-done | bytes 524320 | tf_op jit(solution)/shard_map/ppermute | solution.py:77
  49.0 1.9 %collective-permute-start.2 = (f32[1024,128]{1,0:T(8,128)S(1)}, f32[1024,128]{1,0:T(8,128)S(1)}, u32[]{:S(2)}, u32[]{:S(2)}) collective-permute-start(f32[1024,128]{1,0:T(8,128)S(1)} %multiply_add_fusion.18), channel_id=1, source_target_pairs={{0,16},{8,24},{16,0},{24,8},{1,17},{9,25},{17,1},{25,9},{2,18},{10... | collective-permute-start | bytes 1572872 | tf_op jit(solution)/shard_map/ppermute | solution.py:77
  50.9 8.7 %collective-permute-done.6 = f32[1024,128]{1,0:T(8,128)S(1)} collective-permute-done((f32[1024,128]{1,0:T(8,128)S(1)}, f32[1024,128]{1,0:T(8,128)S(1)}, u32[]{:S(2)}, u32[]{:S(2)}) %collective-permute-start.6) | collective-permute-done | bytes 524320 | tf_op jit(solution)/shard_map/ppermute | solution.py:77
  59.7 1.6 collective-permute-start.7
  61.3 1.6 collective-permute-start.12
  64.2 10.4 %collective-permute-done.7 = f32[1024,128]{1,0:T(8,128)S(1)} collective-permute-done((f32[1024,128]{1,0:T(8,128)S(1)}, f32[1024,128]{1,0:T(8,128)S(1)}, u32[]{:S(2)}, u32[]{:S(2)}) %collective-permute-start.7) | collective-permute-done | bytes 524320 | tf_op jit(solution)/shard_map/ppermute | solution.py:77
  74.6 1.6 collective-permute-start.8
  77.0 7.3 %collective-permute-done.17 = f32[1024,128]{1,0:T(8,128)S(1)} collective-permute-done((f32[1024,128]{1,0:T(8,128)S(1)}, f32[1024,128]{1,0:T(8,128)S(1)}, u32[]{:S(2)}, u32[]{:S(2)}) %collective-permute-start.17) | collective-permute-done | bytes 524320 | tf_op jit(solution)/shard_map/ppermute | solution.py:77
  84.4 1.3 collective-permute-start.18
  85.7 1.8 %collective-permute-done.3 = f32[1024,128]{1,0:T(8,128)S(1)} collective-permute-done((f32[1024,128]{1,0:T(8,128)S(1)}, f32[1024,128]{1,0:T(8,128)S(1)}, u32[]{:S(2)}, u32[]{:S(2)}) %collective-permute-start.3) | collective-permute-done | bytes 524320 | tf_op jit(solution)/shard_map/ppermute | solution.py:77
  87.6 0.7 collective-permute-start.4
  88.3 10.5 %collective-permute-done.8 = f32[1024,128]{1,0:T(8,128)S(1)} collective-permute-done((f32[1024,128]{1,0:T(8,128)S(1)}, f32[1024,128]{1,0:T(8,128)S(1)}, u32[]{:S(2)}, u32[]{:S(2)}) %collective-permute-start.8) | collective-permute-done | bytes 524320 | tf_op jit(solution)/shard_map/ppermute | solution.py:77
  99.5 3.4 %collective-permute-start.14 = (f32[1024,128]{1,0:T(8,128)S(1)}, f32[1024,128]{1,0:T(8,128)S(1)}, u32[]{:S(2)}, u32[]{:S(2)}) collective-permute-start(f32[1024,128]{1,0:T(8,128)S(1)} %multiply_add_fusion.6), channel_id=1, source_target_pairs={{0,4},{1,5},{2,6},{3,7},{4,0},{5,1},{6,2},{7,3},{8,12},{9,13},{10,... | collective-permute-start | bytes 1572872 | tf_op jit(solution)/shard_map/ppermute | solution.py:77
  103.0 4.9 %collective-permute-done.18 = f32[1024,128]{1,0:T(8,128)S(1)} collective-permute-done((f32[1024,128]{1,0:T(8,128)S(1)}, f32[1024,128]{1,0:T(8,128)S(1)}, u32[]{:S(2)}, u32[]{:S(2)}) %collective-permute-start.18) | collective-permute-done | bytes 524320 | tf_op jit(solution)/shard_map/ppermute | solution.py:77
  108.1 12.7 %collective-permute-done.9 = f32[1024,128]{1,0:T(8,128)S(1)} collective-permute-done((f32[1024,128]{1,0:T(8,128)S(1)}, f32[1024,128]{1,0:T(8,128)S(1)}, u32[]{:S(2)}, u32[]{:S(2)}) %collective-permute-start.9) | collective-permute-done | bytes 524320 | tf_op jit(solution)/shard_map/ppermute | solution.py:77
  120.8 17.0 %collective-permute-done.14 = f32[1024,128]{1,0:T(8,128)S(1)} collective-permute-done((f32[1024,128]{1,0:T(8,128)S(1)}, f32[1024,128]{1,0:T(8,128)S(1)}, u32[]{:S(2)}, u32[]{:S(2)}) %collective-permute-start.14) | collective-permute-done | bytes 524320 | tf_op jit(solution)/shard_map/ppermute | solution.py:77
  137.8 8.3 %collective-permute-done.19 = f32[1024,128]{1,0:T(8,128)S(1)} collective-permute-done((f32[1024,128]{1,0:T(8,128)S(1)}, f32[1024,128]{1,0:T(8,128)S(1)}, u32[]{:S(2)}, u32[]{:S(2)}) %collective-permute-start.19) | collective-permute-done | bytes 524320 | tf_op jit(solution)/shard_map/ppermute | solution.py:77
  146.4 0.7 gather_fusion
  147.6 0.7 pad_maximum_fusion.1
  148.3 3.7 %all-to-all-start = ((f32[32,12,128]{2,1,0:T(8,128)}), f32[32,12,128]{2,1,0:T(8,128)S(1)}, u32[]{:S(2)}, u32[]{:S(2)}) async-start(f32[32,12,128]{2,1,0:T(8,128)} %pad_maximum_fusion.1), calls=%async_computation | async-start | bytes 524288 | tf_op jit(solution)/shard_map/all_to_all | solution.py:134
  152.3 10.4 %all-to-all-done = f32[32,12,128]{2,1,0:T(8,128)S(1)} async-done(((f32[32,12,128]{2,1,0:T(8,128)}), f32[32,12,128]{2,1,0:T(8,128)S(1)}, u32[]{:S(2)}, u32[]{:S(2)}) %all-to-all-start) | async-done | bytes 196640 | tf_op jit(solution)/shard_map/all_to_all | solution.py:134
  163.4 2.6 %all-to-all-start.1 = ((f32[32,4,128]{2,1,0:T(4,128)}), f32[32,4,128]{2,1,0:T(4,128)S(1)}, u32[]{:S(2)}, u32[]{:S(2)}) async-start(f32[32,4,128]{2,1,0:T(4,128)} %broadcast_in_dim.55), calls=%async_computation.1 | async-start | bytes 131072 | tf_op jit(solution)/shard_map/all_to_all | solution.py:138
  166.0 1.3 gather_fusion.1
  167.3 5.9 %all-to-all-done.1 = f32[32,4,128]{2,1,0:T(4,128)S(1)} async-done(((f32[32,4,128]{2,1,0:T(4,128)}), f32[32,4,128]{2,1,0:T(4,128)S(1)}, u32[]{:S(2)}, u32[]{:S(2)}) %all-to-all-start.1) | async-done | bytes 65568 | tf_op jit(solution)/shard_map/all_to_all | solution.py:138
  (69 shorter events, 9.5 us)
Async XLA Ops:
  0.6 1.6 copy-start
  2.2 0.7 copy-start.1
  2.9 3.1 %copy-start.3 = (s32[8192]{0:T(1024)S(1)}, s32[8192]{0:T(1024)}, u32[]{:S(2)}) copy-start(s32[8192]{0:T(1024)} %param.5) | copy-start | bytes 98308
  4.9 3.7 %collective-permute-start = (f32[1024,128]{1,0:T(8,128)S(1)}, f32[1024,128]{1,0:T(8,128)}, u32[]{:S(2)}, u32[]{:S(2)}) collective-permute-start(f32[1024,128]{1,0:T(8,128)S(1)} %get-tuple-element.7), channel_id=1, source_target_pairs={{0,8},{8,0},{16,24},{24,16},{1,9},{9,1},{17,25},{25,17},{2,10},{10... | collective-permute-start | bytes 1572872 | tf_op jit(solution)/shard_map/ppermute | solution.py:77
  5.4 8.3 %collective-permute-start.5 = (f32[1024,128]{1,0:T(8,128)S(1)}, f32[1024,128]{1,0:T(8,128)}, u32[]{:S(2)}, u32[]{:S(2)}) collective-permute-start(f32[1024,128]{1,0:T(8,128)S(1)} %get-tuple-element.8), channel_id=1, source_target_pairs={{0,8},{8,0},{16,24},{24,16},{1,9},{9,1},{17,25},{25,17},{2,10},{10... | collective-permute-start | bytes 1572872 | tf_op jit(solution)/shard_map/ppermute | solution.py:77
  5.5 9.4 %collective-permute-start.10 = (f32[1024,128]{1,0:T(8,128)S(1)}, f32[1024,128]{1,0:T(8,128)S(1)}, u32[]{:S(2)}, u32[]{:S(2)}) collective-permute-start(f32[1024,128]{1,0:T(8,128)S(1)} %get-tuple-element.9), channel_id=1, source_target_pairs={{0,8},{8,0},{16,24},{24,16},{1,9},{9,1},{17,25},{25,17},{2,10},{10... | collective-permute-start | bytes 1572872 | tf_op jit(solution)/shard_map/ppermute | solution.py:77
  5.9 10.9 %collective-permute-start.15 = (f32[1024,128]{1,0:T(8,128)S(1)}, f32[1024,128]{1,0:T(8,128)S(1)}, u32[]{:S(2)}, u32[]{:S(2)}) collective-permute-start(f32[1024,128]{1,0:T(8,128)S(1)} %get-tuple-element.10), channel_id=1, source_target_pairs={{0,8},{8,0},{16,24},{24,16},{1,9},{9,1},{17,25},{25,17},{2,10},{10... | collective-permute-start | bytes 1572872 | tf_op jit(solution)/shard_map/ppermute | solution.py:77
  9.7 39.3 %collective-permute-start.1 = (f32[1024,128]{1,0:T(8,128)S(1)}, f32[1024,128]{1,0:T(8,128)S(1)}, u32[]{:S(2)}, u32[]{:S(2)}) collective-permute-start(f32[1024,128]{1,0:T(8,128)S(1)} %multiply_add_fusion.19), channel_id=1, source_target_pairs={{0,4},{1,5},{2,6},{3,7},{4,0},{5,1},{6,2},{7,3},{8,12},{9,13},{10,... | collective-permute-start | bytes 1572872 | tf_op jit(solution)/shard_map/ppermute | solution.py:77
  14.8 44.8 %collective-permute-start.6 = (f32[1024,128]{1,0:T(8,128)S(1)}, f32[1024,128]{1,0:T(8,128)S(1)}, u32[]{:S(2)}, u32[]{:S(2)}) collective-permute-start(f32[1024,128]{1,0:T(8,128)S(1)} %multiply_add_fusion.14), channel_id=1, source_target_pairs={{0,4},{1,5},{2,6},{3,7},{4,0},{5,1},{6,2},{7,3},{8,12},{9,13},{10,... | collective-permute-start | bytes 1572872 | tf_op jit(solution)/shard_map/ppermute | solution.py:77
  15.0 46.3 %collective-permute-start.11 = (f32[1024,128]{1,0:T(8,128)S(1)}, f32[1024,128]{1,0:T(8,128)S(1)}, u32[]{:S(2)}, u32[]{:S(2)}) collective-permute-start(f32[1024,128]{1,0:T(8,128)S(1)} %multiply_add_fusion.9), channel_id=1, source_target_pairs={{0,16},{8,24},{16,0},{24,8},{1,17},{9,25},{17,1},{25,9},{2,18},{10... | collective-permute-start | bytes 1572872 | tf_op jit(solution)/shard_map/ppermute | solution.py:77
  16.9 46.0 %collective-permute-start.16 = (f32[1024,128]{1,0:T(8,128)S(1)}, f32[1024,128]{1,0:T(8,128)S(1)}, u32[]{:S(2)}, u32[]{:S(2)}) collective-permute-start(f32[1024,128]{1,0:T(8,128)S(1)} %multiply_add_fusion.4), channel_id=1, source_target_pairs={{0,2},{1,3},{2,0},{3,1},{4,6},{5,7},{6,4},{7,5},{8,10},{9,11},{10,... | collective-permute-start | bytes 1572872 | tf_op jit(solution)/shard_map/ppermute | solution.py:77
  49.0 14.6 %collective-permute-start.2 = (f32[1024,128]{1,0:T(8,128)S(1)}, f32[1024,128]{1,0:T(8,128)S(1)}, u32[]{:S(2)}, u32[]{:S(2)}) collective-permute-start(f32[1024,128]{1,0:T(8,128)S(1)} %multiply_add_fusion.18), channel_id=1, source_target_pairs={{0,16},{8,24},{16,0},{24,8},{1,17},{9,25},{17,1},{25,9},{2,18},{10... | collective-permute-start | bytes 1572872 | tf_op jit(solution)/shard_map/ppermute | solution.py:77
  59.7 14.9 %collective-permute-start.7 = (f32[1024,128]{1,0:T(8,128)S(1)}, f32[1024,128]{1,0:T(8,128)S(1)}, u32[]{:S(2)}, u32[]{:S(2)}) collective-permute-start(f32[1024,128]{1,0:T(8,128)S(1)} %multiply_add_fusion.13), channel_id=1, source_target_pairs={{0,16},{8,24},{16,0},{24,8},{1,17},{9,25},{17,1},{25,9},{2,18},{10... | collective-permute-start | bytes 1572872 | tf_op jit(solution)/shard_map/ppermute | solution.py:77
  61.3 15.0 %collective-permute-start.12 = (f32[1024,128]{1,0:T(8,128)S(1)}, f32[1024,128]{1,0:T(8,128)S(1)}, u32[]{:S(2)}, u32[]{:S(2)}) collective-permute-start(f32[1024,128]{1,0:T(8,128)S(1)} %multiply_add_fusion.8), channel_id=1, source_target_pairs={{0,1},{1,0},{2,3},{3,2},{4,5},{5,4},{6,7},{7,6},{8,9},{9,8},{10,11... | collective-permute-start | bytes 1572872 | tf_op jit(solution)/shard_map/ppermute | solution.py:77
  63.0 21.4 %collective-permute-start.17 = (f32[1024,128]{1,0:T(8,128)S(1)}, f32[1024,128]{1,0:T(8,128)S(1)}, u32[]{:S(2)}, u32[]{:S(2)}) collective-permute-start(f32[1024,128]{1,0:T(8,128)S(1)} %multiply_add_fusion.3), channel_id=1, source_target_pairs={{0,16},{8,24},{16,0},{24,8},{1,17},{9,25},{17,1},{25,9},{2,18},{10... | collective-permute-start | bytes 1572872 | tf_op jit(solution)/shard_map/ppermute | solution.py:77
  63.6 23.9 %collective-permute-start.3 = (f32[1024,128]{1,0:T(8,128)S(1)}, f32[1024,128]{1,0:T(8,128)S(1)}, u32[]{:S(2)}, u32[]{:S(2)}) collective-permute-start(f32[1024,128]{1,0:T(8,128)S(1)} %multiply_add_fusion.17), channel_id=1, source_target_pairs={{0,1},{1,0},{2,3},{3,2},{4,5},{5,4},{6,7},{7,6},{8,9},{9,8},{10,11... | collective-permute-start | bytes 1572872 | tf_op jit(solution)/shard_map/ppermute | solution.py:77
  74.6 24.1 %collective-permute-start.8 = (f32[1024,128]{1,0:T(8,128)S(1)}, f32[1024,128]{1,0:T(8,128)S(1)}, u32[]{:S(2)}, u32[]{:S(2)}) collective-permute-start(f32[1024,128]{1,0:T(8,128)S(1)} %multiply_add_fusion.12), channel_id=1, source_target_pairs={{0,1},{1,0},{2,3},{3,2},{4,5},{5,4},{6,7},{7,6},{8,9},{9,8},{10,11... | collective-permute-start | bytes 1572872 | tf_op jit(solution)/shard_map/ppermute | solution.py:77
  76.3 23.1 %collective-permute-start.13 = (f32[1024,128]{1,0:T(8,128)S(1)}, f32[1024,128]{1,0:T(8,128)S(1)}, u32[]{:S(2)}, u32[]{:S(2)}) collective-permute-start(f32[1024,128]{1,0:T(8,128)S(1)} %multiply_add_fusion.7), channel_id=1, source_target_pairs={{0,2},{1,3},{2,0},{3,1},{4,6},{5,7},{6,4},{7,5},{8,10},{9,11},{10,... | collective-permute-start | bytes 1572872 | tf_op jit(solution)/shard_map/ppermute | solution.py:77
  84.4 23.5 %collective-permute-start.18 = (f32[1024,128]{1,0:T(8,128)S(1)}, f32[1024,128]{1,0:T(8,128)S(1)}, u32[]{:S(2)}, u32[]{:S(2)}) collective-permute-start(f32[1024,128]{1,0:T(8,128)S(1)} %multiply_add_fusion.2), channel_id=1, source_target_pairs={{0,1},{1,0},{2,3},{3,2},{4,5},{5,4},{6,7},{7,6},{8,9},{9,8},{10,11... | collective-permute-start | bytes 1572872 | tf_op jit(solution)/shard_map/ppermute | solution.py:77
  87.6 20.5 %collective-permute-start.4 = (f32[1024,128]{1,0:T(8,128)S(1)}, f32[1024,128]{1,0:T(8,128)S(1)}, u32[]{:S(2)}, u32[]{:S(2)}) collective-permute-start(f32[1024,128]{1,0:T(8,128)S(1)} %multiply_add_fusion.16), channel_id=1, source_target_pairs={{0,2},{1,3},{2,0},{3,1},{4,6},{5,7},{6,4},{7,5},{8,10},{9,11},{10,... | collective-permute-start | bytes 1572872 | tf_op jit(solution)/shard_map/ppermute | solution.py:77
  98.8 22.0 %collective-permute-start.9 = (f32[1024,128]{1,0:T(8,128)S(1)}, f32[1024,128]{1,0:T(8,128)S(1)}, u32[]{:S(2)}, u32[]{:S(2)}) collective-permute-start(f32[1024,128]{1,0:T(8,128)S(1)} %multiply_add_fusion.11), channel_id=1, source_target_pairs={{0,2},{1,3},{2,0},{3,1},{4,6},{5,7},{6,4},{7,5},{8,10},{9,11},{10,... | collective-permute-start | bytes 1572872 | tf_op jit(solution)/shard_map/ppermute | solution.py:77
  99.5 38.2 %collective-permute-start.14 = (f32[1024,128]{1,0:T(8,128)S(1)}, f32[1024,128]{1,0:T(8,128)S(1)}, u32[]{:S(2)}, u32[]{:S(2)}) collective-permute-start(f32[1024,128]{1,0:T(8,128)S(1)} %multiply_add_fusion.6), channel_id=1, source_target_pairs={{0,4},{1,5},{2,6},{3,7},{4,0},{5,1},{6,2},{7,3},{8,12},{9,13},{10,... | collective-permute-start | bytes 1572872 | tf_op jit(solution)/shard_map/ppermute | solution.py:77
  108.0 38.2 %collective-permute-start.19 = (f32[1024,128]{1,0:T(8,128)S(1)}, f32[1024,128]{1,0:T(8,128)S(1)}, u32[]{:S(2)}, u32[]{:S(2)}) collective-permute-start(f32[1024,128]{1,0:T(8,128)S(1)} %multiply_add_fusion.1), channel_id=1, source_target_pairs={{0,4},{1,5},{2,6},{3,7},{4,0},{5,1},{6,2},{7,3},{8,12},{9,13},{10,... | collective-permute-start | bytes 1572872 | tf_op jit(solution)/shard_map/ppermute | solution.py:77
  146.4 27.5 %copy-start.2 = (f32[4096,128]{1,0:T(8,128)}, f32[4096,128]{1,0:T(8,128)S(1)}, u32[]{:S(2)}) copy-start(f32[4096,128]{1,0:T(8,128)S(1)} %pad_maximum_fusion) | copy-start | bytes 6291460
  148.3 14.4 %all-to-all-start = ((f32[32,12,128]{2,1,0:T(8,128)}), f32[32,12,128]{2,1,0:T(8,128)S(1)}, u32[]{:S(2)}, u32[]{:S(2)}) async-start(f32[32,12,128]{2,1,0:T(8,128)} %pad_maximum_fusion.1), calls=%async_computation | async-start | bytes 524288 | tf_op jit(solution)/shard_map/all_to_all | solution.py:134
  163.4 9.9 %all-to-all-start.1 = ((f32[32,4,128]{2,1,0:T(4,128)}), f32[32,4,128]{2,1,0:T(4,128)S(1)}, u32[]{:S(2)}, u32[]{:S(2)}) async-start(f32[32,4,128]{2,1,0:T(4,128)} %broadcast_in_dim.55), calls=%async_computation.1 | async-start | bytes 131072 | tf_op jit(solution)/shard_map/all_to_all | solution.py:138

commit v2 on v1

--- a/solution.py
+++ b/solution.py
@@ -71,12 +71,26 @@
     )(flips.reshape(rows // 128, 128), panel)
 
 
-def exchange(value, axis, level):
-    mask = 2**level
-    pairs = [(source, source ^ mask) for source in range(lax.axis_size(axis))]
-    partner = lax.ppermute(value, axis, pairs)
-    sign = (1 - 2 * (lax.axis_index(axis) >> level & 1)).astype(jnp.float32)
-    return partner + sign * value
+def launch(value, stage):
+    axis, level = stage
+    pairs = [(source, source ^ 2**level) for source in range(lax.axis_size(axis))]
+    return lax.ppermute(value, axis, pairs), value, stage
+
+
+def sign_of(stage):
+    axis, level = stage
+    return (1 - 2 * (lax.axis_index(axis) >> level & 1)).astype(jnp.float32)
+
+
+def bit_of(stage):
+    axis, level = stage
+    return 2**level * (lax.axis_size("wide") if axis == "narrow" else 1)
+
+
+def land(sent, other):
+    partner, value, stage = sent
+    partner = after(partner, other)
+    return partner + sign_of(stage) * value
 
 
 def send_rows(picks, base, rows_here, devices, most):
@@ -89,6 +103,11 @@
     return rows, jnp.any(hit, axis=2)
 
 
+def pick_rows(held, picks, owner, rows_here, devices, most):
+    rows, _ = send_rows(picks, owner * rows_here, rows_here, devices, most)
+    return jnp.take(held, rows.reshape(-1), axis=0, mode="clip")
+
+
 def landing(block, rows_here, most):
     owners = block // rows_here
     order = jnp.arange(block.shape[0], dtype=jnp.int32)
@@ -96,34 +115,70 @@
     return owners * most + jnp.sum(earlier.astype(jnp.int32), axis=1)
 
 
+def after(value, *others):
+    return lax.optimization_barrier((value, others))[0]
+
+
 def on_device(panel, flips, picks):
     rows_here, width = panel.shape
     narrow, wide = lax.axis_size("narrow"), lax.axis_size("wide")
     devices = narrow * wide
     scale = 1.0 / float(rows_here * devices) ** 0.5
-    stages = [("narrow", l) for l in range(narrow.bit_length() - 1)]
-    stages += [("wide", l) for l in range(wide.bit_length() - 1)]
-    head, rest = stages[0], stages[1:]
-    orders = [
-        [rest[-1]] + rest[:-1],
-        [rest[-1]] + rest[:-1],
-        rest,
-        [rest[-2]] + rest[:-2] + [rest[-1]],
-    ]
-    chunks = local_transform(panel, flips, scale, len(orders))
-    done = []
-    for value, order in zip(chunks, orders):
-        for axis, level in [head] + order:
-            value = exchange(value, axis, level)
-        done.append(value)
-    mixed = jnp.concatenate(done, axis=0)
+    near = [("narrow", l) for l in range(narrow.bit_length() - 1)]
+    near += [("wide", l) for l in range(wide.bit_length() - 3)]
+    far, mid = ("wide", wide.bit_length() - 2), ("wide", wide.bit_length() - 3)
+    near = [stage for stage in near if stage not in (far, mid)]
+    head, first, second = near[0], near[1:], near[:0:-1]
 
     me = lax.axis_index(AXES)
     per = picks.shape[0] // devices
     most = -(-per // devices)
+
+    c = local_transform(panel, flips, scale, 4)
+    quarter = rows_here // 4
+    z = {}
+    z[0] = launch(c[0], far)
+    z[2] = launch(c[2], mid)
+    k = {1: launch(c[1], head), 3: launch(c[3], head)}
+    last = c[0]
+
+    def settle(sent, *stage):
+        nonlocal last
+        out = land(sent, last)
+        last = out
+        return out
+
+    v = {1: settle(k[1]), 3: settle(k[3])}
+    for one, two in zip(first, second):
+        k = {1: launch(v[1], one), 3: launch(v[3], two)}
+        v = {1: settle(k[1]), 3: settle(k[3])}
+    z[1] = launch(v[1], far)
+    z[3] = launch(v[3], mid)
+    v[0] = settle(z[0])
+    v[2] = settle(z[2])
+    for one, two in zip([head] + first, [head] + second):
+        k = {0: launch(v[0], one), 2: launch(v[2], two)}
+        v[0], v[2] = settle(k[0]), settle(k[2])
+    z[2] = launch(v[2], far)
+    v[1] = settle(z[1])
+    v[3] = settle(z[3])
+
+    held = jnp.concatenate([v[0], v[1], v[2], v[3]], axis=0)
+    near_mid = pick_rows(held, picks, me ^ bit_of(mid), rows_here, devices, most)
+    near_far = pick_rows(held, picks, me ^ bit_of(far), rows_here, devices, most)
+    give_mid = launch(near_mid, mid)
+    give_far = launch(near_far, far)
+    z[0] = launch(v[0], mid)
+    z[3] = launch(v[3], far)
+    z[1] = launch(v[1], mid)
     rows, filled = send_rows(picks, me * rows_here, rows_here, devices, most)
-    chosen = jnp.take(mixed, rows.reshape(-1), axis=0, mode="clip")
-    kept = jnp.where(filled.reshape(-1)[:, None], chosen, 0.0)
+    rows, filled = rows.reshape(-1), filled.reshape(-1)
+    own = jnp.take(held, rows, axis=0, mode="clip")
+    upper = (rows >= 2 * quarter)[:, None]
+    chosen = jnp.where(
+        upper, give_far[0] + sign_of(far) * own, give_mid[0] + sign_of(mid) * own
+    )
+    kept = jnp.where(filled[:, None], chosen, 0.0)
     part = lax.dot_general(
         kept, kept, (((0,), (0,)), ((), ())),
         precision=lax.Precision.HIGHEST, preferred_element_type=jnp.float32,
@@ -132,12 +187,16 @@
         [chosen.reshape(devices, most, width), part.reshape(devices, -1, width)], axis=1
     )
     landed = lax.all_to_all(both, AXES, 0, 0, tiled=True)
-    spots = landing(lax.dynamic_slice(picks, (me * per,), (per,)), rows_here, most)
-    sketch = jnp.take(landed[:, :most].reshape(devices * most, width), spots, axis=0, mode="clip")
     mine = jnp.sum(landed[:, most:], axis=0) / float(picks.shape[0])
     gram = lax.all_to_all(
         jnp.broadcast_to(mine[None], (devices,) + mine.shape), AXES, 0, 0, tiled=True
     ).reshape(width, width)
+    spots = landing(lax.dynamic_slice(picks, (me * per,), (per,)), rows_here, most)
+    sketch = jnp.take(landed[:, :most].reshape(devices * most, width), spots, axis=0, mode="clip")
+    last = gram
+    mixed = jnp.concatenate(
+        [settle(z[0]), settle(z[1]), settle(z[2]), settle(z[3])], axis=0
+    )
     return (mixed, sketch, gram)
 
 

time: 174 us -> 170 us (0.977)
  waiting for transfers between devices: 128 us -> 101 us
  other arithmetic: 6.4 us -> 20.5 us
  local copies, waits for them, and re-layouts: 6.06 us -> 11.7 us
  starting transfers between devices: 29.8 us -> 31.8 us
    ppermute x20 -> x22, waiting for transfers between devices: 112 us -> 55.1 us  [launch(): return (lax.ppermute(value, axis, pairs), value, stage)]
    all_to_all x1, waiting for transfers between devices: 5.91 us -> 41.4 us  [on_device(): lax.all_to_all(jnp.broadcast_to(mine[None], (devices,) + mine.shape), AXE...]
    add x20, other arithmetic: 3.15 us -> 11.6 us  [land(): return partner + sign_of(stage) * value]
    all_to_all x1, waiting for transfers between devices: 10.4 us -> 4.61 us  [on_device(): landed = lax.all_to_all(both, AXES, 0, 0, tiled=True)]
    gather x1 -> x3, local copies, waits for them, and re-layouts: 0.73 us -> 3.41 us  [the longest x2 2.68 us: pick_rows(): return jnp.take(held, rows.reshape(-1), axis=0, mode='clip')]
    ppermute x20 -> x22, starting transfers between devices: 23.6 us -> 25.9 us  [launch(): return (lax.ppermute(value, axis, pairs), value, stage)]
    unnamed x9 -> x17, local copies, waits for them, and re-layouts: 2.94 us -> 5.27 us
  transfers between devices with their start and end apart: 22 -> 24, of which waited for: 12 -> 11; matrix products, arithmetic and copies ran while one was open for 4% -> 14% of each run, Pallas kernels for 0% -> 0%
where the time goes in v2:
time: 170 us; the launch traced here: 169 us
  waiting for transfers between devices  101 us (59%)
  starting transfers between devices  31.8 us (19%)
  other arithmetic  20.5 us (12%)
  local copies, waits for them, and re-layouts  11.7 us (7%)
  Pallas kernels  1.94 us (1%)
    ppermute x22, waiting for transfers between devices, launch(): return (lax.ppermute(value, axis, pairs), value, stage)  55.1 us
    all_to_all x1, waiting for transfers between devices, on_device(): lax.all_to_all(jnp.broadcast_to(mine[None], (devices,) + mine.shape), AXE...  41.4 us
    ppermute x22, starting transfers between devices, launch(): return (lax.ppermute(value, axis, pairs), value, stage)  25.9 us
    add x20, other arithmetic, land(): return partner + sign_of(stage) * value  11.6 us
    unnamed x17, local copies, waits for them, and re-layouts  5.27 us
    all_to_all x1, waiting for transfers between devices, on_device(): landed = lax.all_to_all(both, AXES, 0, 0, tiled=True)  4.61 us
  transfers between devices with their start and end apart: 24, of which 11 were waited for; matrix products, arithmetic and copies ran while one was open for 14% of the time, Pallas kernels for 0%

profile of v2, /device:TPU:0, one launch (start us, length us, event | category | flops | bytes accessed | tf_op | source)
XLA Modules:
  0.0 168.8 jit_solution(7513246485137214995)
XLA Ops:
  0.6 1.6 copy-done
  2.9 1.9 %shard_map.58 = (f32[1024,128]{1,0:T(8,128)S(1)}, f32[1024,128]{1,0:T(8,128)S(1)}, f32[1024,128]{1,0:T(8,128)S(1)}, f32[1024,128]{1,0:T(8,128)S(1)}) custom-call(s32[32,128]{1,0:T(8,128)S(1)} %bitcast.24, f32[4096,128]{1,0:T(8,128)S(1)} %copy-done), custom_call_target="tpu_custom_call" | custom-call | tf_op jit(solution)/shard_map/pallas_call | solution.py:64
  5.5 4.0 %collective-permute-start = (f32[1024,128]{1,0:T(8,128)S(1)}, f32[1024,128]{1,0:T(8,128)}, u32[]{:S(2)}, u32[]{:S(2)}) collective-permute-start(f32[1024,128]{1,0:T(8,128)S(1)} %get-tuple-element.27), channel_id=1, source_target_pairs={{0,4},{1,5},{2,6},{3,7},{4,0},{5,1},{6,2},{7,3},{8,12},{9,13},{10,... | collective-permute-start | bytes 1572872 | tf_op jit(solution)/shard_map/ppermute | solution.py:77
  9.5 1.6 collective-permute-start.8
  13.4 1.6 collective-permute-start.4
  16.1 1.6 collective-permute-start.3
  18.0 9.0 %collective-permute-done.4 = f32[1024,128]{1,0:T(8,128)} collective-permute-done((f32[1024,128]{1,0:T(8,128)S(1)}, f32[1024,128]{1,0:T(8,128)}, u32[]{:S(2)}, u32[]{:S(2)}) %collective-permute-start.4) | collective-permute-done | bytes 524320 | tf_op jit(solution)/shard_map/ppermute | solution.py:77
  28.0 1.6 collective-permute-start.6
  29.7 1.6 collective-permute-start.5
  32.5 8.1 %collective-permute-done.6 = f32[1024,128]{1,0:T(8,128)} collective-permute-done((f32[1024,128]{1,0:T(8,128)S(1)}, f32[1024,128]{1,0:T(8,128)}, u32[]{:S(2)}, u32[]{:S(2)}) %collective-permute-start.6) | collective-permute-done | bytes 524320 | tf_op jit(solution)/shard_map/ppermute | solution.py:77
  46.3 1.6 collective-permute-start.9
  47.9 1.4 collective-permute-start.12
  50.7 9.7 %collective-permute-done.9 = f32[1024,128]{1,0:T(8,128)} collective-permute-done((f32[1024,128]{1,0:T(8,128)S(1)}, f32[1024,128]{1,0:T(8,128)}, u32[]{:S(2)}, u32[]{:S(2)}) %collective-permute-start.9) | collective-permute-done | bytes 524320 | tf_op jit(solution)/shard_map/ppermute | solution.py:77
  61.5 1.4 collective-permute-start.11
  64.1 1.6 collective-permute-start.15
  66.5 8.2 %collective-permute-done.11 = f32[1024,128]{1,0:T(8,128)S(1)} collective-permute-done((f32[1024,128]{1,0:T(8,128)S(1)}, f32[1024,128]{1,0:T(8,128)S(1)}, u32[]{:S(2)}, u32[]{:S(2)}) %collective-permute-start.11) | collective-permute-done | bytes 524320 | tf_op jit(solution)/shard_map/ppermute | solution.py:77
  74.7 2.3 %collective-permute-done.15 = f32[1024,128]{1,0:T(8,128)} collective-permute-done((f32[1024,128]{1,0:T(8,128)S(1)}, f32[1024,128]{1,0:T(8,128)}, u32[]{:S(2)}, u32[]{:S(2)}) %collective-permute-start.15) | collective-permute-done | bytes 524320 | tf_op jit(solution)/shard_map/ppermute | solution.py:77
  78.1 12.1 %collective-permute-done.14 = f32[1024,128]{1,0:T(8,128)S(1)} collective-permute-done((f32[1024,128]{1,0:T(8,128)S(1)}, f32[1024,128]{1,0:T(8,128)S(1)}, u32[]{:S(2)}, u32[]{:S(2)}) %collective-permute-start.14) | collective-permute-done | bytes 524320 | tf_op jit(solution)/shard_map/ppermute | solution.py:77
  92.0 1.3 gather_fusion
  93.4 1.3 gather_fusion.2
  97.5 3.1 %collective-permute-done.17 = f32[256,128]{1,0:T(8,128)S(1)} collective-permute-done((f32[256,128]{1,0:T(8,128)}, f32[256,128]{1,0:T(8,128)S(1)}, u32[]{:S(2)}, u32[]{:S(2)}) %collective-permute-start.17) | collective-permute-done | bytes 131104 | tf_op jit(solution)/shard_map/ppermute | solution.py:77
  100.6 2.5 %collective-permute-done.18 = f32[256,128]{1,0:T(8,128)S(1)} collective-permute-done((f32[256,128]{1,0:T(8,128)}, f32[256,128]{1,0:T(8,128)S(1)}, u32[]{:S(2)}, u32[]{:S(2)}) %collective-permute-start.18) | collective-permute-done | bytes 131104 | tf_op jit(solution)/shard_map/ppermute | solution.py:77
  104.5 2.6 %all-to-all-start = ((f32[32,12,128]{2,1,0:T(8,128)}), f32[32,12,128]{2,1,0:T(8,128)S(1)}, u32[]{:S(2)}, u32[]{:S(2)}) async-start(f32[32,12,128]{2,1,0:T(8,128)} %pad_maximum_fusion.2), calls=%async_computation | async-start | bytes 524288 | tf_op jit(solution)/shard_map/all_to_all | solution.py:189
  108.0 1.8 %collective-permute-start.13 = (f32[1024,128]{1,0:T(8,128)S(1)}, f32[1024,128]{1,0:T(8,128)}, u32[]{:S(2)}, u32[]{:S(2)}) collective-permute-start(f32[1024,128]{1,0:T(8,128)S(1)} %multiply_add_fusion.7), channel_id=1, source_target_pairs={{0,2},{1,3},{2,0},{3,1},{4,6},{5,7},{6,4},{7,5},{8,10},{9,11},{10,... | collective-permute-start | bytes 1572872 | tf_op jit(solution)/shard_map/ppermute | solution.py:77
  110.1 2.7 %collective-permute-start.20 = (f32[1024,128]{1,0:T(8,128)S(1)}, f32[1024,128]{1,0:T(8,128)S(1)}, u32[]{:S(2)}, u32[]{:S(2)}) collective-permute-start(f32[1024,128]{1,0:T(8,128)S(1)} %multiply_add_fusion.6), channel_id=1, source_target_pairs={{0,4},{1,5},{2,6},{3,7},{4,0},{5,1},{6,2},{7,3},{8,12},{9,13},{10,... | collective-permute-start | bytes 1572872 | tf_op jit(solution)/shard_map/ppermute | solution.py:77
  113.0 4.6 %all-to-all-done = f32[32,12,128]{2,1,0:T(8,128)S(1)} async-done(((f32[32,12,128]{2,1,0:T(8,128)}), f32[32,12,128]{2,1,0:T(8,128)S(1)}, u32[]{:S(2)}, u32[]{:S(2)}) %all-to-all-start) | async-done | bytes 196640 | tf_op jit(solution)/shard_map/all_to_all | solution.py:189
  118.3 3.3 %all-to-all-start.1 = ((f32[32,4,128]{2,1,0:T(4,128)}), f32[32,4,128]{2,1,0:T(4,128)}, u32[]{:S(2)}, u32[]{:S(2)}) async-start(f32[32,4,128]{2,1,0:T(4,128)} %broadcast_in_dim.91), calls=%async_computation.1 | async-start | bytes 131072 | tf_op jit(solution)/shard_map/all_to_all | solution.py:191
  121.7 1.3 gather_fusion.3
  123.0 41.4 %all-to-all-done.1 = f32[32,4,128]{2,1,0:T(4,128)} async-done(((f32[32,4,128]{2,1,0:T(4,128)}), f32[32,4,128]{2,1,0:T(4,128)}, u32[]{:S(2)}, u32[]{:S(2)}) %all-to-all-start.1) | async-done | bytes 65568 | tf_op jit(solution)/shard_map/all_to_all | solution.py:191
  164.4 1.2 multiply_add_fusion.3
  165.8 1.5 pad_maximum_fusion.1
  167.3 1.5 copy.25
  (109 shorter events, 26.9 us)
Async XLA Ops:
  0.6 1.6 copy-start
  2.2 0.7 copy-start.1
  2.9 8.1 %copy-start.7 = (s32[8192]{0:T(1024)S(1)}, s32[8192]{0:T(1024)}, u32[]{:S(2)}) copy-start(s32[8192]{0:T(1024)} %param.5) | copy-start | bytes 98308
  4.9 8.5 %collective-permute-start.2 = (f32[1024,128]{1,0:T(8,128)S(1)}, f32[1024,128]{1,0:T(8,128)S(1)}, u32[]{:S(2)}, u32[]{:S(2)}) collective-permute-start(f32[1024,128]{1,0:T(8,128)S(1)} %get-tuple-element.29), channel_id=1, source_target_pairs={{0,8},{8,0},{16,24},{24,16},{1,9},{9,1},{17,25},{25,17},{2,10},{10... | collective-permute-start | bytes 1572872 | tf_op jit(solution)/shard_map/ppermute | solution.py:77
  5.4 9.6 %collective-permute-start.1 = (f32[1024,128]{1,0:T(8,128)S(1)}, f32[1024,128]{1,0:T(8,128)}, u32[]{:S(2)}, u32[]{:S(2)}) collective-permute-start(f32[1024,128]{1,0:T(8,128)S(1)} %get-tuple-element.28), channel_id=1, source_target_pairs={{0,8},{8,0},{16,24},{24,16},{1,9},{9,1},{17,25},{25,17},{2,10},{10... | collective-permute-start | bytes 1572872 | tf_op jit(solution)/shard_map/ppermute | solution.py:77
  5.5 36.5 %collective-permute-start = (f32[1024,128]{1,0:T(8,128)S(1)}, f32[1024,128]{1,0:T(8,128)}, u32[]{:S(2)}, u32[]{:S(2)}) collective-permute-start(f32[1024,128]{1,0:T(8,128)S(1)} %get-tuple-element.27), channel_id=1, source_target_pairs={{0,4},{1,5},{2,6},{3,7},{4,0},{5,1},{6,2},{7,3},{8,12},{9,13},{10,... | collective-permute-start | bytes 1572872 | tf_op jit(solution)/shard_map/ppermute | solution.py:77
  9.5 33.6 %collective-permute-start.8 = (f32[1024,128]{1,0:T(8,128)S(1)}, f32[1024,128]{1,0:T(8,128)}, u32[]{:S(2)}, u32[]{:S(2)}) collective-permute-start(f32[1024,128]{1,0:T(8,128)S(1)} %get-tuple-element.37), channel_id=1, source_target_pairs={{0,2},{1,3},{2,0},{3,1},{4,6},{5,7},{6,4},{7,5},{8,10},{9,11},{10,... | collective-permute-start | bytes 1572872 | tf_op jit(solution)/shard_map/ppermute | solution.py:77
  13.4 13.5 %collective-permute-start.4 = (f32[1024,128]{1,0:T(8,128)S(1)}, f32[1024,128]{1,0:T(8,128)}, u32[]{:S(2)}, u32[]{:S(2)}) collective-permute-start(f32[1024,128]{1,0:T(8,128)S(1)} %multiply_add_fusion.19), channel_id=1, source_target_pairs={{0,16},{8,24},{16,0},{24,8},{1,17},{9,25},{17,1},{25,9},{2,18},{10... | collective-permute-start | bytes 1572872 | tf_op jit(solution)/shard_map/ppermute | solution.py:77
  16.1 13.6 %collective-permute-start.3 = (f32[1024,128]{1,0:T(8,128)S(1)}, f32[1024,128]{1,0:T(8,128)S(1)}, u32[]{:S(2)}, u32[]{:S(2)}) collective-permute-start(f32[1024,128]{1,0:T(8,128)S(1)} %multiply_add_fusion.18), channel_id=1, source_target_pairs={{0,1},{1,0},{2,3},{3,2},{4,5},{5,4},{6,7},{7,6},{8,9},{9,8},{10,11... | collective-permute-start | bytes 1572872 | tf_op jit(solution)/shard_map/ppermute | solution.py:77
  28.0 12.6 %collective-permute-start.6 = (f32[1024,128]{1,0:T(8,128)S(1)}, f32[1024,128]{1,0:T(8,128)}, u32[]{:S(2)}, u32[]{:S(2)}) collective-permute-start(f32[1024,128]{1,0:T(8,128)S(1)} %multiply_add_fusion.17), channel_id=1, source_target_pairs={{0,1},{1,0},{2,3},{3,2},{4,5},{5,4},{6,7},{7,6},{8,9},{9,8},{10,11... | collective-permute-start | bytes 1572872 | tf_op jit(solution)/shard_map/ppermute | solution.py:77
  29.7 12.2 %collective-permute-start.5 = (f32[1024,128]{1,0:T(8,128)S(1)}, f32[1024,128]{1,0:T(8,128)S(1)}, u32[]{:S(2)}, u32[]{:S(2)}) collective-permute-start(f32[1024,128]{1,0:T(8,128)S(1)} %multiply_add_fusion.16), channel_id=1, source_target_pairs={{0,16},{8,24},{16,0},{24,8},{1,17},{9,25},{17,1},{25,9},{2,18},{10... | collective-permute-start | bytes 1572872 | tf_op jit(solution)/shard_map/ppermute | solution.py:77
  43.1 2.1 %collective-permute-start.7 = (f32[1024,128]{1,0:T(8,128)S(1)}, f32[1024,128]{1,0:T(8,128)}, u32[]{:S(2)}, u32[]{:S(2)}) collective-permute-start(f32[1024,128]{1,0:T(8,128)S(1)} %multiply_add_fusion.13), channel_id=1, source_target_pairs={{0,8},{8,0},{16,24},{24,16},{1,9},{9,1},{17,25},{25,17},{2,10},{10... | collective-permute-start | bytes 1572872 | tf_op jit(solution)/shard_map/ppermute | solution.py:77
  44.3 3.6 %collective-permute-start.10 = (f32[1024,128]{1,0:T(8,128)S(1)}, f32[1024,128]{1,0:T(8,128)S(1)}, u32[]{:S(2)}, u32[]{:S(2)}) collective-permute-start(f32[1024,128]{1,0:T(8,128)S(1)} %multiply_add_fusion.12), channel_id=1, source_target_pairs={{0,8},{8,0},{16,24},{24,16},{1,9},{9,1},{17,25},{25,17},{2,10},{10... | collective-permute-start | bytes 1572872 | tf_op jit(solution)/shard_map/ppermute | solution.py:77
  46.3 14.1 %collective-permute-start.9 = (f32[1024,128]{1,0:T(8,128)S(1)}, f32[1024,128]{1,0:T(8,128)}, u32[]{:S(2)}, u32[]{:S(2)}) collective-permute-start(f32[1024,128]{1,0:T(8,128)S(1)} %multiply_add_fusion.11), channel_id=1, source_target_pairs={{0,16},{8,24},{16,0},{24,8},{1,17},{9,25},{17,1},{25,9},{2,18},{10... | collective-permute-start | bytes 1572872 | tf_op jit(solution)/shard_map/ppermute | solution.py:77
  47.9 15.0 %copy-start.6 = (f32[1024,128]{1,0:T(8,128)}, f32[1024,128]{1,0:T(8,128)S(1)}, u32[]{:S(2)}) copy-start(f32[1024,128]{1,0:T(8,128)S(1)} %multiply_add_fusion.10) | copy-start | bytes 1572868
  47.9 15.0 %collective-permute-start.12 = (f32[1024,128]{1,0:T(8,128)S(1)}, f32[1024,128]{1,0:T(8,128)S(1)}, u32[]{:S(2)}, u32[]{:S(2)}) collective-permute-start(f32[1024,128]{1,0:T(8,128)S(1)} %multiply_add_fusion.10), channel_id=1, source_target_pairs={{0,1},{1,0},{2,3},{3,2},{4,5},{5,4},{6,7},{7,6},{8,9},{9,8},{10,11... | collective-permute-start | bytes 1572872 | tf_op jit(solution)/shard_map/ppermute | solution.py:77
  61.5 13.2 %collective-permute-start.11 = (f32[1024,128]{1,0:T(8,128)S(1)}, f32[1024,128]{1,0:T(8,128)S(1)}, u32[]{:S(2)}, u32[]{:S(2)}) collective-permute-start(f32[1024,128]{1,0:T(8,128)S(1)} %multiply_add_fusion.9), channel_id=1, source_target_pairs={{0,1},{1,0},{2,3},{3,2},{4,5},{5,4},{6,7},{7,6},{8,9},{9,8},{10,11... | collective-permute-start | bytes 1572872 | tf_op jit(solution)/shard_map/ppermute | solution.py:77
  64.1 13.0 %collective-permute-start.15 = (f32[1024,128]{1,0:T(8,128)S(1)}, f32[1024,128]{1,0:T(8,128)}, u32[]{:S(2)}, u32[]{:S(2)}) collective-permute-start(f32[1024,128]{1,0:T(8,128)S(1)} %multiply_add_fusion.8), channel_id=1, source_target_pairs={{0,16},{8,24},{16,0},{24,8},{1,17},{9,25},{17,1},{25,9},{2,18},{10... | collective-permute-start | bytes 1572872 | tf_op jit(solution)/shard_map/ppermute | solution.py:77
  65.6 24.6 %collective-permute-start.14 = (f32[1024,128]{1,0:T(8,128)S(1)}, f32[1024,128]{1,0:T(8,128)S(1)}, u32[]{:S(2)}, u32[]{:S(2)}) collective-permute-start(f32[1024,128]{1,0:T(8,128)S(1)} %multiply_add_fusion.15), channel_id=1, source_target_pairs={{0,4},{1,5},{2,6},{3,7},{4,0},{5,1},{6,2},{7,3},{8,12},{9,13},{10,... | collective-permute-start | bytes 1572872 | tf_op jit(solution)/shard_map/ppermute | solution.py:77
  66.0 24.3 %collective-permute-start.16 = (f32[1024,128]{1,0:T(8,128)S(1)}, f32[1024,128]{1,0:T(8,128)S(1)}, u32[]{:S(2)}, u32[]{:S(2)}) collective-permute-start(f32[1024,128]{1,0:T(8,128)S(1)} %multiply_add_fusion.14), channel_id=1, source_target_pairs={{0,2},{1,3},{2,0},{3,1},{4,6},{5,7},{6,4},{7,5},{8,10},{9,11},{10,... | collective-permute-start | bytes 1572872 | tf_op jit(solution)/shard_map/ppermute | solution.py:77
  90.3 0.8 copy-start.4
  91.1 0.8 copy-start.2
  93.4 7.2 %collective-permute-start.17 = (f32[256,128]{1,0:T(8,128)}, f32[256,128]{1,0:T(8,128)S(1)}, u32[]{:S(2)}, u32[]{:S(2)}) collective-permute-start(f32[256,128]{1,0:T(8,128)} %gather_fusion), channel_id=1, source_target_pairs={{0,4},{1,5},{2,6},{3,7},{4,0},{5,1},{6,2},{7,3},{8,12},{9,13},{10,... | collective-permute-start | bytes 393224 | tf_op jit(solution)/shard_map/ppermute | solution.py:77
  94.7 8.4 %collective-permute-start.18 = (f32[256,128]{1,0:T(8,128)}, f32[256,128]{1,0:T(8,128)S(1)}, u32[]{:S(2)}, u32[]{:S(2)}) collective-permute-start(f32[256,128]{1,0:T(8,128)} %gather_fusion.2), channel_id=1, source_target_pairs={{0,2},{1,3},{2,0},{3,1},{4,6},{5,7},{6,4},{7,5},{8,10},{9,11},{10,... | collective-permute-start | bytes 393224 | tf_op jit(solution)/shard_map/ppermute | solution.py:77
  103.7 61.9 %copy-start.5 = (f32[1024,128]{1,0:T(8,128)S(1)}, f32[1024,128]{1,0:T(8,128)}, u32[]{:S(2)}) copy-start(f32[1024,128]{1,0:T(8,128)} %copy-done.4) | copy-start | bytes 1572868
  104.5 13.2 %all-to-all-start = ((f32[32,12,128]{2,1,0:T(8,128)}), f32[32,12,128]{2,1,0:T(8,128)S(1)}, u32[]{:S(2)}, u32[]{:S(2)}) async-start(f32[32,12,128]{2,1,0:T(8,128)} %pad_maximum_fusion.2), calls=%async_computation | async-start | bytes 524288 | tf_op jit(solution)/shard_map/all_to_all | solution.py:189
  108.0 56.4 %collective-permute-start.13 = (f32[1024,128]{1,0:T(8,128)S(1)}, f32[1024,128]{1,0:T(8,128)}, u32[]{:S(2)}, u32[]{:S(2)}) collective-permute-start(f32[1024,128]{1,0:T(8,128)S(1)} %multiply_add_fusion.7), channel_id=1, source_target_pairs={{0,2},{1,3},{2,0},{3,1},{4,6},{5,7},{6,4},{7,5},{8,10},{9,11},{10,... | collective-permute-start | bytes 1572872 | tf_op jit(solution)/shard_map/ppermute | solution.py:77
  109.8 55.8 %collective-permute-start.19 = (f32[1024,128]{1,0:T(8,128)}, f32[1024,128]{1,0:T(8,128)S(1)}, u32[]{:S(2)}, u32[]{:S(2)}) collective-permute-start(f32[1024,128]{1,0:T(8,128)} %copy-done.4), channel_id=1, source_target_pairs={{0,2},{1,3},{2,0},{3,1},{4,6},{5,7},{6,4},{7,5},{8,10},{9,11},{10,... | collective-permute-start | bytes 1572872 | tf_op jit(solution)/shard_map/ppermute | solution.py:77
  110.1 55.6 %collective-permute-start.20 = (f32[1024,128]{1,0:T(8,128)S(1)}, f32[1024,128]{1,0:T(8,128)S(1)}, u32[]{:S(2)}, u32[]{:S(2)}) collective-permute-start(f32[1024,128]{1,0:T(8,128)S(1)} %multiply_add_fusion.6), channel_id=1, source_target_pairs={{0,4},{1,5},{2,6},{3,7},{4,0},{5,1},{6,2},{7,3},{8,12},{9,13},{10,... | collective-permute-start | bytes 1572872 | tf_op jit(solution)/shard_map/ppermute | solution.py:77
  112.8 53.0 %collective-permute-start.21 = (f32[1024,128]{1,0:T(8,128)}, f32[1024,128]{1,0:T(8,128)S(1)}, u32[]{:S(2)}, u32[]{:S(2)}) collective-permute-start(f32[1024,128]{1,0:T(8,128)} %copy-done.2), channel_id=1, source_target_pairs={{0,4},{1,5},{2,6},{3,7},{4,0},{5,1},{6,2},{7,3},{8,12},{9,13},{10,... | collective-permute-start | bytes 1572872 | tf_op jit(solution)/shard_map/ppermute | solution.py:77
  118.3 46.1 %all-to-all-start.1 = ((f32[32,4,128]{2,1,0:T(4,128)}), f32[32,4,128]{2,1,0:T(4,128)}, u32[]{:S(2)}, u32[]{:S(2)}) async-start(f32[32,4,128]{2,1,0:T(4,128)} %broadcast_in_dim.91), calls=%async_computation.1 | async-start | bytes 131072 | tf_op jit(solution)/shard_map/all_to_all | solution.py:191
  164.4 1.3 copy-start.3

commit v3 on v1

--- a/solution.py
+++ b/solution.py
@@ -39,7 +39,7 @@
         out = jnp.dot(mixer, parts, preferred_element_type=jnp.float32)
         held[b] = out[:, :width] + out[:, width : 2 * width] + out[:, 2 * width :]
     strip = 16
-    share = blocks // len(outs)
+    places = [(i, j) for i in range(len(outs)) for j in range(outs[i].shape[0] // BLOCK)]
 
     def body(step, carry):
         at = pl.multiple_of(step * strip, strip)
@@ -52,31 +52,62 @@
             ]
             apart *= 2
         for b in range(blocks):
-            spot = pl.multiple_of((b % share) * BLOCK + at, strip)
-            outs[b // share][pl.ds(spot, strip), :] = items[b] * scale
+            which, place = places[b]
+            spot = pl.multiple_of(place * BLOCK + at, strip)
+            outs[which][pl.ds(spot, strip), :] = items[b] * scale
         return carry
 
     lax.fori_loop(0, BLOCK // strip, body, 0)
 
 
-def local_transform(panel, flips, scale, pieces):
+def local_transform(panel, flips, scale, shares):
     rows, width = panel.shape
     return pl.pallas_call(
         functools.partial(local_kernel, scale),
-        out_shape=[jax.ShapeDtypeStruct((rows // pieces, width), jnp.float32)] * pieces,
+        out_shape=[jax.ShapeDtypeStruct((share, width), jnp.float32) for share in shares],
         in_specs=[pl.BlockSpec(memory_space=pltpu.VMEM)] * 2,
-        out_specs=[pl.BlockSpec(memory_space=pltpu.VMEM)] * pieces,
+        out_specs=[pl.BlockSpec(memory_space=pltpu.VMEM)] * len(shares),
         scratch_shapes=[pltpu.VMEM((rows // BLOCK, BLOCK, width), jnp.float32)],
         compiler_params=pltpu.CompilerParams(vmem_limit_bytes=32 * 2**20),
     )(flips.reshape(rows // 128, 128), panel)
 
 
-def exchange(value, axis, level):
-    mask = 2**level
-    pairs = [(source, source ^ mask) for source in range(lax.axis_size(axis))]
-    partner = lax.ppermute(value, axis, pairs)
-    sign = (1 - 2 * (lax.axis_index(axis) >> level & 1)).astype(jnp.float32)
-    return partner + sign * value
+def launch(value, stage):
+    axis, level = stage
+    pairs = [(source, source ^ 2**level) for source in range(lax.axis_size(axis))]
+    return lax.ppermute(value, axis, pairs), value, stage
+
+
+def sign_of(stage):
+    axis, level = stage
+    return (1 - 2 * (lax.axis_index(axis) >> level & 1)).astype(jnp.float32)
+
+
+def bit_of(stage):
+    axis, level = stage
+    return 2**level * (lax.axis_size("wide") if axis == "narrow" else 1)
+
+
+class Chain:
+    def __init__(self):
+        self.last = ()
+
+    def end(self, sent):
+        partner, value, stage = sent
+        partner = after(partner, self.last)
+        self.last = partner + sign_of(stage) * value
+        return self.last
+
+    def begin(self, value, stages):
+        for stage in stages[:-1]:
+            value = self.end(launch(value, stage))
+        return launch(value, stages[-1])
+
+
+def split(value, parts):
+    units = value.shape[0] // 16
+    cuts = [16 * (units * i // parts) for i in range(parts + 1)]
+    return [value[low:high] for low, high in zip(cuts, cuts[1:])]
 
 
 def send_rows(picks, base, rows_here, devices, most):
@@ -96,34 +127,88 @@
     return owners * most + jnp.sum(earlier.astype(jnp.int32), axis=1)
 
 
+def after(value, *others):
+    return lax.optimization_barrier((value, others))[0]
+
+
 def on_device(panel, flips, picks):
     rows_here, width = panel.shape
     narrow, wide = lax.axis_size("narrow"), lax.axis_size("wide")
     devices = narrow * wide
     scale = 1.0 / float(rows_here * devices) ** 0.5
-    stages = [("narrow", l) for l in range(narrow.bit_length() - 1)]
-    stages += [("wide", l) for l in range(wide.bit_length() - 1)]
-    head, rest = stages[0], stages[1:]
-    orders = [
-        [rest[-1]] + rest[:-1],
-        [rest[-1]] + rest[:-1],
-        rest,
-        [rest[-2]] + rest[:-2] + [rest[-1]],
-    ]
-    chunks = local_transform(panel, flips, scale, len(orders))
-    done = []
-    for value, order in zip(chunks, orders):
-        for axis, level in [head] + order:
-            value = exchange(value, axis, level)
-        done.append(value)
-    mixed = jnp.concatenate(done, axis=0)
+    levels = wide.bit_length() - 1
+    far, mid = ("wide", levels - 1), ("wide", levels - 2)
+    near = [("narrow", l) for l in range(narrow.bit_length() - 1)]
+    near += [("wide", l) for l in range(levels - 2)]
+    core, first, second = near[:1], near[1:2], near[2:]
 
     me = lax.axis_index(AXES)
     per = picks.shape[0] // devices
     most = -(-per // devices)
+    cuts = [0, 5, 8, 11, 16]
+    cuts = [cut * rows_here // 16 for cut in cuts]
+
+    c = local_transform(panel, flips, scale, [b - a for a, b in zip(cuts, cuts[1:])])
+    chain = Chain()
+
+    def halves(value):
+        return [launch(part, far) for part in split(value, 2)]
+
+    far0 = halves(c[0])
+    mid2 = launch(c[2], mid)
+    core1, core3 = chain.begin(c[1], core), chain.begin(c[3], core)
     rows, filled = send_rows(picks, me * rows_here, rows_here, devices, most)
-    chosen = jnp.take(mixed, rows.reshape(-1), axis=0, mode="clip")
-    kept = jnp.where(filled.reshape(-1)[:, None], chosen, 0.0)
+    rows, filled = rows.reshape(-1), filled.reshape(-1)
+    rows_mid = send_rows(picks, (me ^ bit_of(mid)) * rows_here, rows_here, devices, most)[0].reshape(-1)
+    rows_far = send_rows(picks, (me ^ bit_of(far)) * rows_here, rows_here, devices, most)[0].reshape(-1)
+    spots = landing(lax.dynamic_slice(picks, (me * per,), (per,)), rows_here, most)
+
+    first1 = chain.begin(chain.end(core1), first)
+    second3 = chain.begin(chain.end(core3), second)
+    chain.last = (chain.last, rows, filled, rows_mid, rows_far, spots)
+    second1 = chain.begin(chain.end(first1), second)
+    v0 = [chain.end(far0[0])]
+    mid3 = launch(chain.end(second3), mid)
+    core2 = chain.begin(chain.end(mid2), core)
+    first2 = chain.begin(chain.end(core2), first)
+    far1 = halves(chain.end(second1))
+    second2 = chain.begin(chain.end(first2), second)
+    v0 = jnp.concatenate(v0 + [chain.end(far0[1])], axis=0)
+    core0 = chain.begin(v0, core)
+    first0 = chain.begin(chain.end(core0), first)
+    v1 = [chain.end(far1[0])]
+    far2 = halves(chain.end(second2))
+    v1 = jnp.concatenate(v1 + [chain.end(far1[1])], axis=0)
+    mid1 = launch(v1, mid)
+    second0 = chain.begin(chain.end(first0), second)
+    first3 = chain.begin(chain.end(mid3), first)
+    v2 = [chain.end(far2[0])]
+    v3 = chain.end(first3)
+    v0 = chain.end(second0)
+    v2 = jnp.concatenate(v2 + [chain.end(far2[1])], axis=0)
+    v1 = chain.end(mid1)
+
+    held = jnp.concatenate([v0, v1, v2, v3], axis=0)
+    wanted = jnp.concatenate([rows_far, rows_mid, rows])
+    taken = jnp.take(held, wanted, axis=0, mode="clip")
+    count = devices * most
+    give_far = launch(taken[:count], far)
+    give_mid = launch(taken[count : 2 * count], mid)
+    own = taken[2 * count :]
+    parts0, parts3 = split(v0, 2), split(v3, 2)
+    ends0, ends3 = [], []
+
+    def more(step, gate):
+        ends3.append(launch(after(parts3[step], gate), far))
+        ends0.append(launch(after(parts0[step], gate), mid))
+
+    got_far = chain.end((give_far[0], own, far))
+    got_mid = chain.end((give_mid[0], own, mid))
+    place = rows[:, None]
+    chosen = jnp.where(
+        place >= cuts[3], got_far, jnp.where(place < cuts[1], got_mid, own)
+    )
+    kept = jnp.where(filled[:, None], chosen, 0.0)
     part = lax.dot_general(
         kept, kept, (((0,), (0,)), ((), ())),
         precision=lax.Precision.HIGHEST, preferred_element_type=jnp.float32,
@@ -132,12 +217,19 @@
         [chosen.reshape(devices, most, width), part.reshape(devices, -1, width)], axis=1
     )
     landed = lax.all_to_all(both, AXES, 0, 0, tiled=True)
-    spots = landing(lax.dynamic_slice(picks, (me * per,), (per,)), rows_here, most)
+    more(0, both)
+    mine = jnp.sum(landed[:, most:], axis=0) / float(picks.shape[0])
+    shared = jnp.broadcast_to(mine[None], (devices,) + mine.shape)
+    gram = lax.all_to_all(shared, AXES, 0, 0, tiled=True).reshape(width, width)
+    more(1, shared)
     sketch = jnp.take(landed[:, :most].reshape(devices * most, width), spots, axis=0, mode="clip")
-    mine = jnp.sum(landed[:, most:], axis=0) / float(picks.shape[0])
-    gram = lax.all_to_all(
-        jnp.broadcast_to(mine[None], (devices,) + mine.shape), AXES, 0, 0, tiled=True
-    ).reshape(width, width)
+    chain.last = (chain.last, landed)
+    final0, final3 = [], []
+    for step in range(2):
+        final3.append(chain.end(ends3[step]))
+        final0.append(chain.end(ends0[step]))
+        chain.last = (chain.last, gram, sketch)
+    mixed = jnp.concatenate(final0 + [v1, v2] + final3, axis=0)
     return (mixed, sketch, gram)
 
 

time: 174 us -> 180 us (1.034)
  waiting for transfers between devices: 128 us -> 103 us
  other arithmetic: 6.4 us -> 18.5 us
  starting transfers between devices: 29.8 us -> 39.8 us
  local copies, waits for them, and re-layouts: 6.06 us -> 14.4 us
    ppermute x20 -> x27, waiting for transfers between devices: 112 us -> 90.9 us  [launch(): return (lax.ppermute(value, axis, pairs), value, stage)]
    ppermute x20 -> x27, starting transfers between devices: 23.6 us -> 32.7 us  [launch(): return (lax.ppermute(value, axis, pairs), value, stage)]
    all_to_all x1, waiting for transfers between devices: 5.91 us -> 0.95 us  [on_device(): gram = lax.all_to_all(shared, AXES, 0, 0, tiled=True).reshape(width, width)]
    unnamed x9 -> x27, local copies, waits for them, and re-layouts: 2.94 us -> 5.89 us
    reduce_sum x1 -> x3, other arithmetic: 0.62 us -> 3.24 us  [send_rows(): rows = jnp.sum(jnp.where(hit, offsets[:, None, :], 0), axis=2)]
    unnamed x0 -> x4, other arithmetic: none -> 2.41 us
    all_to_all x1, starting transfers between devices: 2.57 us -> 4.51 us  [on_device(): gram = lax.all_to_all(shared, AXES, 0, 0, tiled=True).reshape(width, width)]
    add x20, other arithmetic: 3.15 us -> 4.97 us  [end(): self.last = partner + sign_of(stage) * value]
  transfers between devices with their start and end apart: 22 -> 29, of which waited for: 12 -> 18; matrix products, arithmetic and copies ran while one was open for 4% -> 10% of each run, Pallas kernels for 0% -> 0%
where the time goes in v3:
time: 180 us; the launch traced here: 179 us
  waiting for transfers between devices  103 us (57%)
  starting transfers between devices  39.8 us (22%)
  other arithmetic  18.5 us (10%)
  local copies, waits for them, and re-layouts  14.4 us (8%)
  Pallas kernels  1.94 us (1%)
    ppermute x27, waiting for transfers between devices, launch(): return (lax.ppermute(value, axis, pairs), value, stage)  90.9 us
    ppermute x27, starting transfers between devices, launch(): return (lax.ppermute(value, axis, pairs), value, stage)  32.7 us
    all_to_all x1, waiting for transfers between devices, on_device(): landed = lax.all_to_all(both, AXES, 0, 0, tiled=True)  11.2 us
    unnamed x27, local copies, waits for them, and re-layouts  5.89 us
    add x20, other arithmetic, end(): self.last = partner + sign_of(stage) * value  4.97 us
    all_to_all x1, starting transfers between devices, on_device(): gram = lax.all_to_all(shared, AXES, 0, 0, tiled=True).reshape(width, width)  4.51 us
  transfers between devices with their start and end apart: 29, of which 18 were waited for; matrix products, arithmetic and copies ran while one was open for 10% of the time, Pallas kernels for 0%

profile of v3, /device:TPU:0, one launch (start us, length us, event | category | flops | bytes accessed | tf_op | source)
XLA Modules:
  0.0 179.2 jit_solution(14664423401475507864)
XLA Ops:
  0.6 1.6 copy-done
  2.9 1.9 %shard_map.58 = (f32[1280,128]{1,0:T(8,128)S(1)}, f32[768,128]{1,0:T(8,128)S(1)}, f32[768,128]{1,0:T(8,128)S(1)}, f32[1280,128]{1,0:T(8,128)S(1)}) custom-call(s32[32,128]{1,0:T(8,128)S(1)} %bitcast.24, f32[4096,128]{1,0:T(8,128)S(1)} %copy-done), custom_call_target="tpu_custom_call" | custom-call | tf_op jit(solution)/shard_map/pallas_call | solution.py:65
  6.2 4.0 %collective-permute-start = (f32[640,128]{1,0:T(8,128)}, f32[640,128]{1,0:T(8,128)}, u32[]{:S(2)}, u32[]{:S(2)}) collective-permute-start(f32[640,128]{1,0:T(8,128)} %slice.63), channel_id=1, source_target_pairs={{0,4},{1,5},{2,6},{3,7},{4,0},{5,1},{6,2},{7,3},{8,12},{9,13},{10,... | collective-permute-start | bytes 983048 | tf_op jit(solution)/shard_map/ppermute | solution.py:78
  10.2 1.6 collective-permute-start.5
  19.1 1.6 collective-permute-start.2
  20.7 1.6 collective-permute-start.6
  25.3 4.5 %collective-permute-done.2 = f32[768,128]{1,0:T(8,128)} collective-permute-done((f32[768,128]{1,0:T(8,128)S(1)}, f32[768,128]{1,0:T(8,128)}, u32[]{:S(2)}, u32[]{:S(2)}) %collective-permute-start.2) | collective-permute-done | bytes 393248 | tf_op jit(solution)/shard_map/ppermute | solution.py:78
  31.9 4.8 %collective-permute-done.6 = f32[1280,128]{1,0:T(8,128)S(1)} collective-permute-done((f32[1280,128]{1,0:T(8,128)S(1)}, f32[1280,128]{1,0:T(8,128)S(1)}, u32[]{:S(2)}, u32[]{:S(2)}) %collective-permute-start.6) | collective-permute-done | bytes 655392 | tf_op jit(solution)/shard_map/ppermute | solution.py:78
  37.9 1.6 collective-permute-start.9
  40.6 8.8 %collective-permute-done.9 = f32[768,128]{1,0:T(8,128)S(1)} collective-permute-done((f32[768,128]{1,0:T(8,128)S(1)}, f32[768,128]{1,0:T(8,128)S(1)}, u32[]{:S(2)}, u32[]{:S(2)}) %collective-permute-start.9) | collective-permute-done | bytes 393248 | tf_op jit(solution)/shard_map/ppermute | solution.py:78
  50.9 6.6 %collective-permute-done.4 = f32[640,128]{1,0:T(8,128)S(1)} collective-permute-done((f32[640,128]{1,0:T(8,128)S(1)}, f32[640,128]{1,0:T(8,128)S(1)}, u32[]{:S(2)}, u32[]{:S(2)}) %collective-permute-start.4) | collective-permute-done | bytes 327712 | tf_op jit(solution)/shard_map/ppermute | solution.py:78
  58.7 1.6 collective-permute-start.13
  60.4 1.6 collective-permute-start.11
  61.9 15.0 %collective-permute-done.14 = f32[384,128]{1,0:T(8,128)S(1)} collective-permute-done((f32[384,128]{1,0:T(8,128)S(1)}, f32[384,128]{1,0:T(8,128)S(1)}, u32[]{:S(2)}, u32[]{:S(2)}) %collective-permute-start.14) | collective-permute-done | bytes 196640 | tf_op jit(solution)/shard_map/ppermute | solution.py:78
  76.9 3.4 %collective-permute-start.12 = (f32[384,128]{1,0:T(8,128)S(1)}, f32[384,128]{1,0:T(8,128)S(1)}, u32[]{:S(2)}, u32[]{:S(2)}) collective-permute-start(f32[384,128]{1,0:T(8,128)S(1)} %get-tuple-element.96), channel_id=1, source_target_pairs={{0,4},{1,5},{2,6},{3,7},{4,0},{5,1},{6,2},{7,3},{8,12},{9,13},{10,... | collective-permute-start | bytes 589832 | tf_op jit(solution)/shard_map/ppermute | solution.py:78
  80.4 9.1 %collective-permute-done.12 = f32[384,128]{1,0:T(8,128)S(1)} collective-permute-done((f32[384,128]{1,0:T(8,128)S(1)}, f32[384,128]{1,0:T(8,128)S(1)}, u32[]{:S(2)}, u32[]{:S(2)}) %collective-permute-start.12) | collective-permute-done | bytes 196640 | tf_op jit(solution)/shard_map/ppermute | solution.py:78
  89.7 1.6 collective-permute-start.17
  92.5 1.5 collective-permute-start.15
  94.1 6.0 %collective-permute-done.18 = f32[384,128]{1,0:T(8,128)S(1)} collective-permute-done((f32[384,128]{1,0:T(8,128)S(1)}, f32[384,128]{1,0:T(8,128)S(1)}, u32[]{:S(2)}, u32[]{:S(2)}) %collective-permute-start.18) | collective-permute-done | bytes 196640 | tf_op jit(solution)/shard_map/ppermute | solution.py:78
  100.2 6.0 %collective-permute-done.17 = f32[1280,128]{1,0:T(8,128)S(1)} collective-permute-done((f32[1280,128]{1,0:T(8,128)S(1)}, f32[1280,128]{1,0:T(8,128)S(1)}, u32[]{:S(2)}, u32[]{:S(2)}) %collective-permute-start.17) | collective-permute-done | bytes 655392 | tf_op jit(solution)/shard_map/ppermute | solution.py:78
  107.8 3.7 %collective-permute-done.20 = f32[384,128]{1,0:T(8,128)S(1)} collective-permute-done((f32[384,128]{1,0:T(8,128)S(1)}, f32[384,128]{1,0:T(8,128)S(1)}, u32[]{:S(2)}, u32[]{:S(2)}) %collective-permute-start.20) | collective-permute-done | bytes 196640 | tf_op jit(solution)/shard_map/ppermute | solution.py:78
  112.5 2.3 %gather_fusion = f32[768,128]{1,0:T(8,128)} fusion(f32[4096,128]{1,0:T(8,128)S(1)} %constant_dynamic-update-slice_fusion, s32[1024]{0:T(1024)S(1)} %pad_clamp_fusion.1), kind=kCustom, calls=%fused_computation | custom fusion | bytes 789504 | tf_op jit(solution)/shard_map/jit(_take)/gather | solution.py:193
  115.9 7.2 %collective-permute-done.21 = f32[256,128]{1,0:T(8,128)S(1)} collective-permute-done((f32[256,128]{1,0:T(8,128)S(1)}, f32[256,128]{1,0:T(8,128)S(1)}, u32[]{:S(2)}, u32[]{:S(2)}) %collective-permute-start.21) | collective-permute-done | bytes 131104 | tf_op jit(solution)/shard_map/ppermute | solution.py:78
  124.9 4.2 %collective-permute-done.22 = f32[256,128]{1,0:T(8,128)S(1)} collective-permute-done((f32[256,128]{1,0:T(8,128)S(1)}, f32[256,128]{1,0:T(8,128)S(1)}, u32[]{:S(2)}, u32[]{:S(2)}) %collective-permute-start.22) | collective-permute-done | bytes 131104 | tf_op jit(solution)/shard_map/ppermute | solution.py:78
  131.3 2.6 %all-to-all-start = ((f32[32,12,128]{2,1,0:T(8,128)}), f32[32,12,128]{2,1,0:T(8,128)S(1)}, u32[]{:S(2)}, u32[]{:S(2)}) async-start(f32[32,12,128]{2,1,0:T(8,128)} %pad_maximum_fusion.2), calls=%async_computation | async-start | bytes 524288 | tf_op jit(solution)/shard_map/all_to_all | solution.py:219
  134.0 2.7 %collective-permute-start.24 = (f32[640,128]{1,0:T(8,128)S(1)}, f32[640,128]{1,0:T(8,128)S(1)}, u32[]{:S(2)}, u32[]{:S(2)}) collective-permute-start(f32[640,128]{1,0:T(8,128)S(1)} %get-tuple-element.64), channel_id=1, source_target_pairs={{0,4},{1,5},{2,6},{3,7},{4,0},{5,1},{6,2},{7,3},{8,12},{9,13},{10,... | collective-permute-start | bytes 983048 | tf_op jit(solution)/shard_map/ppermute | solution.py:78
  136.8 1.5 collective-permute-start.23
  138.3 11.2 %all-to-all-done = f32[32,12,128]{2,1,0:T(8,128)S(1)} async-done(((f32[32,12,128]{2,1,0:T(8,128)}), f32[32,12,128]{2,1,0:T(8,128)S(1)}, u32[]{:S(2)}, u32[]{:S(2)}) %all-to-all-start) | async-done | bytes 196640 | tf_op jit(solution)/shard_map/all_to_all | solution.py:219
  150.1 4.5 %all-to-all-start.1 = ((f32[32,4,128]{2,1,0:T(4,128)}), f32[32,4,128]{2,1,0:T(4,128)S(1)}, u32[]{:S(2)}, u32[]{:S(2)}) async-start(f32[32,4,128]{2,1,0:T(4,128)} %broadcast_in_dim.91), calls=%async_computation.1 | async-start | bytes 131072 | tf_op jit(solution)/shard_map/all_to_all | solution.py:223
  154.7 2.7 %collective-permute-start.26 = (f32[640,128]{1,0:T(8,128)S(1)}, f32[640,128]{1,0:T(8,128)S(1)}, u32[]{:S(2)}, u32[]{:S(2)}) collective-permute-start(f32[640,128]{1,0:T(8,128)S(1)} %get-tuple-element.68), channel_id=1, source_target_pairs={{0,4},{1,5},{2,6},{3,7},{4,0},{5,1},{6,2},{7,3},{8,12},{9,13},{10,... | collective-permute-start | bytes 983048 | tf_op jit(solution)/shard_map/ppermute | solution.py:78
  158.2 1.5 collective-permute-start.25
  162.1 11.9 %collective-permute-done.26 = f32[640,128]{1,0:T(8,128)S(1)} collective-permute-done((f32[640,128]{1,0:T(8,128)S(1)}, f32[640,128]{1,0:T(8,128)S(1)}, u32[]{:S(2)}, u32[]{:S(2)}) %collective-permute-start.26) | collective-permute-done | bytes 327712 | tf_op jit(solution)/shard_map/ppermute | solution.py:78
  (139 shorter events, 37.8 us)
Async XLA Ops:
  4.9 13.2 %collective-permute-start.1 = (f32[768,128]{1,0:T(8,128)S(1)}, f32[768,128]{1,0:T(8,128)}, u32[]{:S(2)}, u32[]{:S(2)}) collective-permute-start(f32[768,128]{1,0:T(8,128)S(1)} %get-tuple-element.38), channel_id=1, source_target_pairs={{0,8},{8,0},{16,24},{24,16},{1,9},{9,1},{17,25},{25,17},{2,10},{10... | collective-permute-start | bytes 1179656 | tf_op jit(solution)/shard_map/ppermute | solution.py:78
  5.4 15.3 %collective-permute-start.3 = (f32[1280,128]{1,0:T(8,128)S(1)}, f32[1280,128]{1,0:T(8,128)S(1)}, u32[]{:S(2)}, u32[]{:S(2)}) collective-permute-start(f32[1280,128]{1,0:T(8,128)S(1)} %get-tuple-element.39), channel_id=1, source_target_pairs={{0,8},{8,0},{16,24},{24,16},{1,9},{9,1},{17,25},{25,17},{2,10},{10... | collective-permute-start | bytes 1966088 | tf_op jit(solution)/shard_map/ppermute | solution.py:78
  6.2 24.6 %collective-permute-start = (f32[640,128]{1,0:T(8,128)}, f32[640,128]{1,0:T(8,128)}, u32[]{:S(2)}, u32[]{:S(2)}) collective-permute-start(f32[640,128]{1,0:T(8,128)} %slice.63), channel_id=1, source_target_pairs={{0,4},{1,5},{2,6},{3,7},{4,0},{5,1},{6,2},{7,3},{8,12},{9,13},{10,... | collective-permute-start | bytes 983048 | tf_op jit(solution)/shard_map/ppermute | solution.py:78
  10.2 26.5 %collective-permute-start.5 = (f32[768,128]{1,0:T(8,128)S(1)}, f32[768,128]{1,0:T(8,128)}, u32[]{:S(2)}, u32[]{:S(2)}) collective-permute-start(f32[768,128]{1,0:T(8,128)S(1)} %get-tuple-element.43), channel_id=1, source_target_pairs={{0,2},{1,3},{2,0},{3,1},{4,6},{5,7},{6,4},{7,5},{8,10},{9,11},{10,... | collective-permute-start | bytes 1179656 | tf_op jit(solution)/shard_map/ppermute | solution.py:78
  19.1 10.7 %collective-permute-start.2 = (f32[768,128]{1,0:T(8,128)S(1)}, f32[768,128]{1,0:T(8,128)}, u32[]{:S(2)}, u32[]{:S(2)}) collective-permute-start(f32[768,128]{1,0:T(8,128)S(1)} %multiply_add_fusion.14), channel_id=1, source_target_pairs={{0,16},{8,24},{16,0},{24,8},{1,17},{9,25},{17,1},{25,9},{2,18},{10... | collective-permute-start | bytes 1179656 | tf_op jit(solution)/shard_map/ppermute | solution.py:78
  20.7 15.9 %collective-permute-start.6 = (f32[1280,128]{1,0:T(8,128)S(1)}, f32[1280,128]{1,0:T(8,128)S(1)}, u32[]{:S(2)}, u32[]{:S(2)}) collective-permute-start(f32[1280,128]{1,0:T(8,128)S(1)} %multiply_add_fusion.6), channel_id=1, source_target_pairs={{0,1},{1,0},{2,3},{3,2},{4,5},{5,4},{6,7},{7,6},{8,9},{9,8},{10,11... | collective-permute-start | bytes 1966088 | tf_op jit(solution)/shard_map/ppermute | solution.py:78
  37.8 1.8 collective-permute-start.7
  37.9 11.5 %collective-permute-start.9 = (f32[768,128]{1,0:T(8,128)S(1)}, f32[768,128]{1,0:T(8,128)S(1)}, u32[]{:S(2)}, u32[]{:S(2)}) collective-permute-start(f32[768,128]{1,0:T(8,128)S(1)} %multiply_add_fusion.13), channel_id=1, source_target_pairs={{0,1},{1,0},{2,3},{3,2},{4,5},{5,4},{6,7},{7,6},{8,9},{9,8},{10,11... | collective-permute-start | bytes 1179656 | tf_op jit(solution)/shard_map/ppermute | solution.py:78
  39.7 11.2 %collective-permute-start.8 = (f32[768,128]{1,0:T(8,128)S(1)}, f32[768,128]{1,0:T(8,128)S(1)}, u32[]{:S(2)}, u32[]{:S(2)}) collective-permute-start(f32[768,128]{1,0:T(8,128)S(1)} %multiply_add_fusion.11), channel_id=1, source_target_pairs={{0,16},{8,24},{16,0},{24,8},{1,17},{9,25},{17,1},{25,9},{2,18},{10... | collective-permute-start | bytes 1179656 | tf_op jit(solution)/shard_map/ppermute | solution.py:78
  40.3 17.3 %collective-permute-start.4 = (f32[640,128]{1,0:T(8,128)S(1)}, f32[640,128]{1,0:T(8,128)S(1)}, u32[]{:S(2)}, u32[]{:S(2)}) collective-permute-start(f32[640,128]{1,0:T(8,128)S(1)} %get-tuple-element.90), channel_id=1, source_target_pairs={{0,4},{1,5},{2,6},{3,7},{4,0},{5,1},{6,2},{7,3},{8,12},{9,13},{10,... | collective-permute-start | bytes 983048 | tf_op jit(solution)/shard_map/ppermute | solution.py:78
  57.6 2.7 %collective-permute-start.10 = (f32[1280,128]{1,0:T(8,128)S(1)}, f32[1280,128]{1,0:T(8,128)S(1)}, u32[]{:S(2)}, u32[]{:S(2)}) collective-permute-start(f32[1280,128]{1,0:T(8,128)S(1)} %pad_maximum_fusion), channel_id=1, source_target_pairs={{0,8},{8,0},{16,24},{24,16},{1,9},{9,1},{17,25},{25,17},{2,10},{10... | collective-permute-start | bytes 1966088 | tf_op jit(solution)/shard_map/ppermute | solution.py:78
  57.7 31.9 %collective-permute-start.16 = (f32[1280,128]{1,0:T(8,128)S(1)}, f32[1280,128]{1,0:T(8,128)S(1)}, u32[]{:S(2)}, u32[]{:S(2)}) collective-permute-start(f32[1280,128]{1,0:T(8,128)S(1)} %multiply_add_fusion.5), channel_id=1, source_target_pairs={{0,2},{1,3},{2,0},{3,1},{4,6},{5,7},{6,4},{7,5},{8,10},{9,11},{10,... | collective-permute-start | bytes 1966088 | tf_op jit(solution)/shard_map/ppermute | solution.py:78
  57.8 19.0 %collective-permute-start.14 = (f32[384,128]{1,0:T(8,128)S(1)}, f32[384,128]{1,0:T(8,128)S(1)}, u32[]{:S(2)}, u32[]{:S(2)}) collective-permute-start(f32[384,128]{1,0:T(8,128)S(1)} %slice.92), channel_id=1, source_target_pairs={{0,4},{1,5},{2,6},{3,7},{4,0},{5,1},{6,2},{7,3},{8,12},{9,13},{10,... | collective-permute-start | bytes 589832 | tf_op jit(solution)/shard_map/ppermute | solution.py:78
  58.7 18.2 %collective-permute-start.13 = (f32[768,128]{1,0:T(8,128)S(1)}, f32[768,128]{1,0:T(8,128)S(1)}, u32[]{:S(2)}, u32[]{:S(2)}) collective-permute-start(f32[768,128]{1,0:T(8,128)S(1)} %multiply_add_fusion.9), channel_id=1, source_target_pairs={{0,1},{1,0},{2,3},{3,2},{4,5},{5,4},{6,7},{7,6},{8,9},{9,8},{10,11... | collective-permute-start | bytes 1179656 | tf_op jit(solution)/shard_map/ppermute | solution.py:78
  60.4 29.2 %collective-permute-start.11 = (f32[1280,128]{1,0:T(8,128)S(1)}, f32[1280,128]{1,0:T(8,128)S(1)}, u32[]{:S(2)}, u32[]{:S(2)}) collective-permute-start(f32[1280,128]{1,0:T(8,128)S(1)} %multiply_add_fusion.4), channel_id=1, source_target_pairs={{0,16},{8,24},{16,0},{24,8},{1,17},{9,25},{17,1},{25,9},{2,18},{10... | collective-permute-start | bytes 1966088 | tf_op jit(solution)/shard_map/ppermute | solution.py:78
  76.9 12.6 %collective-permute-start.12 = (f32[384,128]{1,0:T(8,128)S(1)}, f32[384,128]{1,0:T(8,128)S(1)}, u32[]{:S(2)}, u32[]{:S(2)}) collective-permute-start(f32[384,128]{1,0:T(8,128)S(1)} %get-tuple-element.96), channel_id=1, source_target_pairs={{0,4},{1,5},{2,6},{3,7},{4,0},{5,1},{6,2},{7,3},{8,12},{9,13},{10,... | collective-permute-start | bytes 589832 | tf_op jit(solution)/shard_map/ppermute | solution.py:78
  89.7 16.5 %collective-permute-start.17 = (f32[1280,128]{1,0:T(8,128)S(1)}, f32[1280,128]{1,0:T(8,128)S(1)}, u32[]{:S(2)}, u32[]{:S(2)}) collective-permute-start(f32[1280,128]{1,0:T(8,128)S(1)} %multiply_add_fusion.2), channel_id=1, source_target_pairs={{0,16},{8,24},{16,0},{24,8},{1,17},{9,25},{17,1},{25,9},{2,18},{10... | collective-permute-start | bytes 1966088 | tf_op jit(solution)/shard_map/ppermute | solution.py:78
  91.3 8.8 %collective-permute-start.18 = (f32[384,128]{1,0:T(8,128)S(1)}, f32[384,128]{1,0:T(8,128)S(1)}, u32[]{:S(2)}, u32[]{:S(2)}) collective-permute-start(f32[384,128]{1,0:T(8,128)S(1)} %slice.93), channel_id=1, source_target_pairs={{0,4},{1,5},{2,6},{3,7},{4,0},{5,1},{6,2},{7,3},{8,12},{9,13},{10,... | collective-permute-start | bytes 589832 | tf_op jit(solution)/shard_map/ppermute | solution.py:78
  91.4 20.1 %collective-permute-start.19 = (f32[768,128]{1,0:T(8,128)S(1)}, f32[768,128]{1,0:T(8,128)S(1)}, u32[]{:S(2)}, u32[]{:S(2)}) collective-permute-start(f32[768,128]{1,0:T(8,128)S(1)} %pad_maximum_fusion.1), channel_id=1, source_target_pairs={{0,2},{1,3},{2,0},{3,1},{4,6},{5,7},{6,4},{7,5},{8,10},{9,11},{10,... | collective-permute-start | bytes 1179656 | tf_op jit(solution)/shard_map/ppermute | solution.py:78
  92.5 15.1 %collective-permute-start.15 = (f32[1280,128]{1,0:T(8,128)S(1)}, f32[1280,128]{1,0:T(8,128)S(1)}, u32[]{:S(2)}, u32[]{:S(2)}) collective-permute-start(f32[1280,128]{1,0:T(8,128)S(1)} %multiply_add_fusion.3), channel_id=1, source_target_pairs={{0,1},{1,0},{2,3},{3,2},{4,5},{5,4},{6,7},{7,6},{8,9},{9,8},{10,11... | collective-permute-start | bytes 1966088 | tf_op jit(solution)/shard_map/ppermute | solution.py:78
  100.1 11.4 %collective-permute-start.20 = (f32[384,128]{1,0:T(8,128)S(1)}, f32[384,128]{1,0:T(8,128)S(1)}, u32[]{:S(2)}, u32[]{:S(2)}) collective-permute-start(f32[384,128]{1,0:T(8,128)S(1)} %get-tuple-element.93), channel_id=1, source_target_pairs={{0,4},{1,5},{2,6},{3,7},{4,0},{5,1},{6,2},{7,3},{8,12},{9,13},{10,... | collective-permute-start | bytes 589832 | tf_op jit(solution)/shard_map/ppermute | solution.py:78
  115.7 7.4 %collective-permute-start.21 = (f32[256,128]{1,0:T(8,128)S(1)}, f32[256,128]{1,0:T(8,128)S(1)}, u32[]{:S(2)}, u32[]{:S(2)}) collective-permute-start(f32[256,128]{1,0:T(8,128)S(1)} %slice.96), channel_id=1, source_target_pairs={{0,4},{1,5},{2,6},{3,7},{4,0},{5,1},{6,2},{7,3},{8,12},{9,13},{10,... | collective-permute-start | bytes 393224 | tf_op jit(solution)/shard_map/ppermute | solution.py:78
  124.0 5.0 %collective-permute-start.22 = (f32[256,128]{1,0:T(8,128)S(1)}, f32[256,128]{1,0:T(8,128)S(1)}, u32[]{:S(2)}, u32[]{:S(2)}) collective-permute-start(f32[256,128]{1,0:T(8,128)S(1)} %get-tuple-element.91), channel_id=1, source_target_pairs={{0,2},{1,3},{2,0},{3,1},{4,6},{5,7},{6,4},{7,5},{8,10},{9,11},{10,... | collective-permute-start | bytes 393224 | tf_op jit(solution)/shard_map/ppermute | solution.py:78
  131.3 18.1 %all-to-all-start = ((f32[32,12,128]{2,1,0:T(8,128)}), f32[32,12,128]{2,1,0:T(8,128)S(1)}, u32[]{:S(2)}, u32[]{:S(2)}) async-start(f32[32,12,128]{2,1,0:T(8,128)} %pad_maximum_fusion.2), calls=%async_computation | async-start | bytes 524288 | tf_op jit(solution)/shard_map/all_to_all | solution.py:219
  134.0 23.4 %collective-permute-start.24 = (f32[640,128]{1,0:T(8,128)S(1)}, f32[640,128]{1,0:T(8,128)S(1)}, u32[]{:S(2)}, u32[]{:S(2)}) collective-permute-start(f32[640,128]{1,0:T(8,128)S(1)} %get-tuple-element.64), channel_id=1, source_target_pairs={{0,4},{1,5},{2,6},{3,7},{4,0},{5,1},{6,2},{7,3},{8,12},{9,13},{10,... | collective-permute-start | bytes 983048 | tf_op jit(solution)/shard_map/ppermute | solution.py:78
  136.8 20.7 %collective-permute-start.23 = (f32[640,128]{1,0:T(8,128)S(1)}, f32[640,128]{1,0:T(8,128)S(1)}, u32[]{:S(2)}, u32[]{:S(2)}) collective-permute-start(f32[640,128]{1,0:T(8,128)S(1)} %get-tuple-element.63), channel_id=1, source_target_pairs={{0,2},{1,3},{2,0},{3,1},{4,6},{5,7},{6,4},{7,5},{8,10},{9,11},{10,... | collective-permute-start | bytes 983048 | tf_op jit(solution)/shard_map/ppermute | solution.py:78
  150.1 11.9 %all-to-all-start.1 = ((f32[32,4,128]{2,1,0:T(4,128)}), f32[32,4,128]{2,1,0:T(4,128)S(1)}, u32[]{:S(2)}, u32[]{:S(2)}) async-start(f32[32,4,128]{2,1,0:T(4,128)} %broadcast_in_dim.91), calls=%async_computation.1 | async-start | bytes 131072 | tf_op jit(solution)/shard_map/all_to_all | solution.py:223
  154.7 19.3 %collective-permute-start.26 = (f32[640,128]{1,0:T(8,128)S(1)}, f32[640,128]{1,0:T(8,128)S(1)}, u32[]{:S(2)}, u32[]{:S(2)}) collective-permute-start(f32[640,128]{1,0:T(8,128)S(1)} %get-tuple-element.68), channel_id=1, source_target_pairs={{0,4},{1,5},{2,6},{3,7},{4,0},{5,1},{6,2},{7,3},{8,12},{9,13},{10,... | collective-permute-start | bytes 983048 | tf_op jit(solution)/shard_map/ppermute | solution.py:78
  157.4 17.5 %copy-start.6 = (f32[768,128]{1,0:T(8,128)S(1)}, f32[768,128]{1,0:T(8,128)}, u32[]{:S(2)}) copy-start(f32[768,128]{1,0:T(8,128)} %get-tuple-element.76) | copy-start | bytes 1179652
  158.2 17.5 %copy-start.3 = (f32[384,128]{1,0:T(8,128)S(1)}, f32[384,128]{1,0:T(8,128)}, u32[]{:S(2)}) copy-start(f32[384,128]{1,0:T(8,128)} %copy-done.2) | copy-start | bytes 589828
  158.2 16.0 %collective-permute-start.25 = (f32[640,128]{1,0:T(8,128)S(1)}, f32[640,128]{1,0:T(8,128)S(1)}, u32[]{:S(2)}, u32[]{:S(2)}) collective-permute-start(f32[640,128]{1,0:T(8,128)S(1)} %get-tuple-element.67), channel_id=1, source_target_pairs={{0,2},{1,3},{2,0},{3,1},{4,6},{5,7},{6,4},{7,5},{8,10},{9,11},{10,... | collective-permute-start | bytes 983048 | tf_op jit(solution)/shard_map/ppermute | solution.py:78
  159.7 16.7 %copy-start.5 = (f32[384,128]{1,0:T(8,128)S(1)}, f32[384,128]{1,0:T(8,128)}, u32[]{:S(2)}) copy-start(f32[384,128]{1,0:T(8,128)} %copy-done.4) | copy-start | bytes 589828
  (7 other events, 42.9 us)

commit v4 on v3

--- a/solution.py
+++ b/solution.py
@@ -110,14 +110,38 @@
     return [value[low:high] for low, high in zip(cuts, cuts[1:])]
 
 
-def send_rows(picks, base, rows_here, devices, most):
-    offsets = picks.reshape(devices, -1) - base
-    owned = (offsets >= 0) & (offsets < rows_here)
-    rank = jnp.cumsum(owned.astype(jnp.int32), axis=1) - 1
-    slot = jnp.arange(most, dtype=jnp.int32)
-    hit = owned[:, None, :] & (rank[:, None, :] == slot[None, :, None])
-    rows = jnp.sum(jnp.where(hit, offsets[:, None, :], 0), axis=2)
-    return rows, jnp.any(hit, axis=2)
+def index_kernel(rows_here, most, bases_ref, picks_ref, out_ref):
+    picks = picks_ref[...]
+    devices, per = picks.shape
+    before = lax.broadcasted_iota(jnp.int32, (per, per), 0)
+    earlier = before < lax.broadcasted_iota(jnp.int32, (per, per), 1)
+    earlier = jnp.where(earlier, 1.0, 0.0).astype(jnp.bfloat16)
+    for which in range(out_ref.shape[0]):
+        offsets = picks - bases_ref[which]
+        owned = (offsets >= 0) & (offsets < rows_here)
+        ones = jnp.where(owned, 1.0, 0.0).astype(jnp.bfloat16)
+        rank = jnp.dot(ones, earlier, preferred_element_type=jnp.float32)
+        rank = jnp.where(owned, rank, -1.0)
+        marked = (offsets + 1).astype(jnp.float32)
+        for slot in range(most):
+            hit = jnp.where(rank == float(slot), marked, 0.0)
+            row = jnp.sum(hit, axis=1, keepdims=True).astype(jnp.int32) - 1
+            out_ref[which, :, slot : slot + 1] = row
+
+
+def send_rows(picks, owners, rows_here, devices, most):
+    bases = jnp.stack(owners) * rows_here
+    rows = pl.pallas_call(
+        functools.partial(index_kernel, rows_here, most),
+        out_shape=jax.ShapeDtypeStruct((len(owners), devices, most), jnp.int32),
+        in_specs=[
+            pl.BlockSpec(memory_space=pltpu.SMEM),
+            pl.BlockSpec(memory_space=pltpu.VMEM),
+        ],
+        out_specs=pl.BlockSpec(memory_space=pltpu.VMEM),
+        compiler_params=pltpu.CompilerParams(vmem_limit_bytes=8 * 2**20),
+    )(bases.astype(jnp.int32), picks.reshape(devices, -1))
+    return rows.reshape(len(owners) * devices * most)
 
 
 def landing(block, rows_here, most):
@@ -145,68 +169,59 @@
     me = lax.axis_index(AXES)
     per = picks.shape[0] // devices
     most = -(-per // devices)
-    cuts = [0, 5, 8, 11, 16]
-    cuts = [cut * rows_here // 16 for cut in cuts]
+    cuts = [rows_here * cut // 4 for cut in range(5)]
 
     c = local_transform(panel, flips, scale, [b - a for a, b in zip(cuts, cuts[1:])])
     chain = Chain()
-
-    def halves(value):
-        return [launch(part, far) for part in split(value, 2)]
-
-    far0 = halves(c[0])
-    mid2 = launch(c[2], mid)
-    core1, core3 = chain.begin(c[1], core), chain.begin(c[3], core)
-    rows, filled = send_rows(picks, me * rows_here, rows_here, devices, most)
-    rows, filled = rows.reshape(-1), filled.reshape(-1)
-    rows_mid = send_rows(picks, (me ^ bit_of(mid)) * rows_here, rows_here, devices, most)[0].reshape(-1)
-    rows_far = send_rows(picks, (me ^ bit_of(far)) * rows_here, rows_here, devices, most)[0].reshape(-1)
+    core1, core2, core3 = [chain.begin(c[i], core) for i in (1, 2, 3)]
+    wanted = send_rows(picks, [me ^ bit_of(far), me ^ bit_of(mid), me], rows_here, devices, most)
     spots = landing(lax.dynamic_slice(picks, (me * per,), (per,)), rows_here, most)
-
-    first1 = chain.begin(chain.end(core1), first)
-    second3 = chain.begin(chain.end(core3), second)
-    chain.last = (chain.last, rows, filled, rows_mid, rows_far, spots)
-    second1 = chain.begin(chain.end(first1), second)
-    v0 = [chain.end(far0[0])]
-    mid3 = launch(chain.end(second3), mid)
-    core2 = chain.begin(chain.end(mid2), core)
-    first2 = chain.begin(chain.end(core2), first)
-    far1 = halves(chain.end(second1))
+    v1, v2, v3 = chain.end(core1), chain.end(core2), chain.end(core3)
+    mid1 = launch(v1, mid)
+    far0 = launch(after(c[0], v1), far)
+    first2 = chain.begin(v2, first)
+    second3 = chain.begin(v3, second)
+    chain.last = (chain.last, wanted, spots)
+    first1 = chain.begin(chain.end(mid1), first)
     second2 = chain.begin(chain.end(first2), second)
-    v0 = jnp.concatenate(v0 + [chain.end(far0[1])], axis=0)
-    core0 = chain.begin(v0, core)
-    first0 = chain.begin(chain.end(core0), first)
-    v1 = [chain.end(far1[0])]
-    far2 = halves(chain.end(second2))
-    v1 = jnp.concatenate(v1 + [chain.end(far1[1])], axis=0)
-    mid1 = launch(v1, mid)
-    second0 = chain.begin(chain.end(first0), second)
-    first3 = chain.begin(chain.end(mid3), first)
-    v2 = [chain.end(far2[0])]
+    first3 = chain.begin(chain.end(second3), first)
+    core0 = chain.begin(chain.end(far0), core)
+    v1 = chain.end(first1)
+    v2 = chain.end(second2)
+    mid2 = launch(v2, mid)
+    far1 = launch(after(v1, v2), far)
+    second0 = chain.begin(chain.end(core0), second)
     v3 = chain.end(first3)
-    v0 = chain.end(second0)
-    v2 = jnp.concatenate(v2 + [chain.end(far2[1])], axis=0)
-    v1 = chain.end(mid1)
+    mid3 = launch(v3, mid)
+    second1 = chain.begin(chain.end(far1), second)
+    v2 = chain.end(mid2)
+    far2 = launch(after(v2, v3), far)
+    first0 = chain.begin(chain.end(second0), first)
+    v0 = chain.end(first0)
+    v3 = chain.end(mid3)
+    v1 = chain.end(second1)
 
     held = jnp.concatenate([v0, v1, v2, v3], axis=0)
-    wanted = jnp.concatenate([rows_far, rows_mid, rows])
     taken = jnp.take(held, wanted, axis=0, mode="clip")
     count = devices * most
-    give_far = launch(taken[:count], far)
-    give_mid = launch(taken[count : 2 * count], mid)
-    own = taken[2 * count :]
+    rows, filled = wanted[2 * count :], wanted[2 * count :] >= 0
+    to_far, to_mid, own = lax.optimization_barrier(
+        (taken[:count], taken[count : 2 * count], taken[2 * count :])
+    )
+    give_mid, give_far = launch(to_mid, mid), launch(to_far, far)
     parts0, parts3 = split(v0, 2), split(v3, 2)
     ends0, ends3 = [], []
 
     def more(step, gate):
+        ends0.append(launch(after(parts0[step], gate), mid))
         ends3.append(launch(after(parts3[step], gate), far))
-        ends0.append(launch(after(parts0[step], gate), mid))
-
+
+    got_mid = chain.end((give_mid[0], own, mid))
+    v2 = chain.end(far2)
     got_far = chain.end((give_far[0], own, far))
-    got_mid = chain.end((give_mid[0], own, mid))
     place = rows[:, None]
     chosen = jnp.where(
-        place >= cuts[3], got_far, jnp.where(place < cuts[1], got_mid, own)
+        place >= cuts[2], got_far, jnp.where(place < cuts[1], got_mid, own)
     )
     kept = jnp.where(filled[:, None], chosen, 0.0)
     part = lax.dot_general(
@@ -226,8 +241,8 @@
     chain.last = (chain.last, landed)
     final0, final3 = [], []
     for step in range(2):
+        final0.append(chain.end(ends0[step]))
         final3.append(chain.end(ends3[step]))
-        final0.append(chain.end(ends0[step]))
         chain.last = (chain.last, gram, sketch)
     mixed = jnp.concatenate(final0 + [v1, v2] + final3, axis=0)
     return (mixed, sketch, gram)

time: 180 us -> 155 us (0.86)
  waiting for transfers between devices: 103 us -> 87 us
  other arithmetic: 18.5 us -> 7.89 us
  starting transfers between devices: 39.8 us -> 43.1 us
  local copies, waits for them, and re-layouts: 14.4 us -> 11.9 us
    ppermute x27 -> x24, waiting for transfers between devices: 90.9 us -> 79.7 us  [launch(): return (lax.ppermute(value, axis, pairs), value, stage)]
    all_to_all x1, waiting for transfers between devices: 11.2 us -> 6.23 us  [on_device(): landed = lax.all_to_all(both, AXES, 0, 0, tiled=True)]
    reduce_sum x3 -> x0, other arithmetic: 3.24 us -> none  [send_rows(): rows = jnp.sum(jnp.where(hit, offsets[:, None, :], 0), axis=2)]
    ppermute x27 -> x24, starting transfers between devices: 32.7 us -> 35.3 us  [launch(): return (lax.ppermute(value, axis, pairs), value, stage)]
    another operation x6 -> x0, other arithmetic: 1.87 us -> none
    unnamed x27 -> x18, local copies, waits for them, and re-layouts: 5.89 us -> 6.01 us
  transfers between devices with their start and end apart: 29 -> 26, of which waited for: 18 -> 12; matrix products, arithmetic and copies ran while one was open for 10% -> 9% of each run, Pallas kernels for 0% -> 1%
where the time goes in v4:
time: 155 us; the launch traced here: 154 us
  waiting for transfers between devices  87 us (56%)
  starting transfers between devices  43.1 us (28%)
  local copies, waits for them, and re-layouts  11.9 us (8%)
  other arithmetic  7.89 us (5%)
  Pallas kernels  2.83 us (2%)
    ppermute x24, waiting for transfers between devices, launch(): return (lax.ppermute(value, axis, pairs), value, stage)  79.7 us
    ppermute x24, starting transfers between devices, launch(): return (lax.ppermute(value, axis, pairs), value, stage)  35.3 us
    all_to_all x1, waiting for transfers between devices, on_device(): landed = lax.all_to_all(both, AXES, 0, 0, tiled=True)  6.23 us
    unnamed x18, local copies, waits for them, and re-layouts  6.01 us
    all_to_all x1, starting transfers between devices, on_device(): landed = lax.all_to_all(both, AXES, 0, 0, tiled=True)  4.24 us
    add x20, other arithmetic, end(): self.last = partner + sign_of(stage) * value  4.22 us
    all_to_all x1, starting transfers between devices, on_device(): gram = lax.all_to_all(shared, AXES, 0, 0, tiled=True).reshape(width, width)  3.57 us
  transfers between devices with their start and end apart: 26, of which 12 were waited for; matrix products, arithmetic and copies ran while one was open for 9% of the time, Pallas kernels for 1%

profile of v4, /device:TPU:0, one launch (start us, length us, event | category | flops | bytes accessed | tf_op | source)
XLA Modules:
  0.0 154.2 jit_solution(8258878503406809572)
XLA Ops:
  0.6 1.6 %copy-done = f32[4096,128]{1,0:T(8,128)S(1)} copy-done((f32[4096,128]{1,0:T(8,128)S(1)}, f32[4096,128]{1,0:T(8,128)}, u32[]{:S(2)}) %copy-start) | copy-done | bytes 2097176
  2.9 1.9 %shard_map.58 = (f32[1024,128]{1,0:T(8,128)S(1)}, f32[1024,128]{1,0:T(8,128)S(1)}, f32[1024,128]{1,0:T(8,128)S(1)}, f32[1024,128]{1,0:T(8,128)S(1)}) custom-call(s32[32,128]{1,0:T(8,128)S(1)} %bitcast.9, f32[4096,128]{1,0:T(8,128)S(1)} %copy-done), custom_call_target="tpu_custom_call" | custom-call | tf_op jit(solution)/shard_map/pallas_call | solution.py:65
  8.2 3.0 %collective-permute-start.6 = (f32[1024,128]{1,0:T(8,128)S(1)}, f32[1024,128]{1,0:T(8,128)S(1)}, u32[]{:S(2)}, u32[]{:S(2)}) collective-permute-start(f32[1024,128]{1,0:T(8,128)S(1)} %multiply_add_fusion.17), channel_id=1, source_target_pairs={{0,2},{1,3},{2,0},{3,1},{4,6},{5,7},{6,4},{7,5},{8,10},{9,11},{10,... | collective-permute-start | bytes 1572872 | tf_op jit(solution)/shard_map/ppermute | solution.py:78
  11.2 2.6 %collective-permute-start.1 = (f32[1024,128]{1,0:T(8,128)S(1)}, f32[1024,128]{1,0:T(8,128)S(1)}, u32[]{:S(2)}, u32[]{:S(2)}) collective-permute-start(f32[1024,128]{1,0:T(8,128)S(1)} %get-tuple-element.42), channel_id=1, source_target_pairs={{0,4},{1,5},{2,6},{3,7},{4,0},{5,1},{6,2},{7,3},{8,12},{9,13},{10,... | collective-permute-start | bytes 1572872 | tf_op jit(solution)/shard_map/ppermute | solution.py:78
  13.8 1.6 %collective-permute-start.5 = (f32[1024,128]{1,0:T(8,128)S(1)}, f32[1024,128]{1,0:T(8,128)S(1)}, u32[]{:S(2)}, u32[]{:S(2)}) collective-permute-start(f32[1024,128]{1,0:T(8,128)S(1)} %multiply_add_fusion.16), channel_id=1, source_target_pairs={{0,16},{8,24},{16,0},{24,8},{1,17},{9,25},{17,1},{25,9},{2,18},{10... | collective-permute-start | bytes 1572872 | tf_op jit(solution)/shard_map/ppermute | solution.py:78
  15.5 1.6 %collective-permute-start.4 = (f32[1024,128]{1,0:T(8,128)S(1)}, f32[1024,128]{1,0:T(8,128)S(1)}, u32[]{:S(2)}, u32[]{:S(2)}) collective-permute-start(f32[1024,128]{1,0:T(8,128)S(1)} %multiply_add_fusion.15), channel_id=1, source_target_pairs={{0,1},{1,0},{2,3},{3,2},{4,5},{5,4},{6,7},{7,6},{8,9},{9,8},{10,11... | collective-permute-start | bytes 1572872 | tf_op jit(solution)/shard_map/ppermute | solution.py:78
  17.0 17.5 %collective-permute-done.6 = f32[1024,128]{1,0:T(8,128)S(1)} collective-permute-done((f32[1024,128]{1,0:T(8,128)S(1)}, f32[1024,128]{1,0:T(8,128)S(1)}, u32[]{:S(2)}, u32[]{:S(2)}) %collective-permute-start.6) | collective-permute-done | bytes 524320 | tf_op jit(solution)/shard_map/ppermute | solution.py:78
  34.6 1.7 %collective-permute-start.9 = (f32[1024,128]{1,0:T(8,128)S(1)}, f32[1024,128]{1,0:T(8,128)S(1)}, u32[]{:S(2)}, u32[]{:S(2)}) collective-permute-start(f32[1024,128]{1,0:T(8,128)S(1)} %multiply_add_fusion.14), channel_id=1, source_target_pairs={{0,16},{8,24},{16,0},{24,8},{1,17},{9,25},{17,1},{25,9},{2,18},{10... | collective-permute-start | bytes 1572872 | tf_op jit(solution)/shard_map/ppermute | solution.py:78
  36.4 1.6 %collective-permute-start.8 = (f32[1024,128]{1,0:T(8,128)S(1)}, f32[1024,128]{1,0:T(8,128)S(1)}, u32[]{:S(2)}, u32[]{:S(2)}) collective-permute-start(f32[1024,128]{1,0:T(8,128)S(1)} %multiply_add_fusion.13), channel_id=1, source_target_pairs={{0,1},{1,0},{2,3},{3,2},{4,5},{5,4},{6,7},{7,6},{8,9},{9,8},{10,11... | collective-permute-start | bytes 1572872 | tf_op jit(solution)/shard_map/ppermute | solution.py:78
  38.8 10.7 %collective-permute-done.9 = f32[1024,128]{1,0:T(8,128)S(1)} collective-permute-done((f32[1024,128]{1,0:T(8,128)S(1)}, f32[1024,128]{1,0:T(8,128)S(1)}, u32[]{:S(2)}, u32[]{:S(2)}) %collective-permute-start.9) | collective-permute-done | bytes 524320 | tf_op jit(solution)/shard_map/ppermute | solution.py:78
  49.7 3.2 %collective-permute-start.12 = (f32[1024,128]{1,0:T(8,128)S(1)}, f32[1024,128]{1,0:T(8,128)S(1)}, u32[]{:S(2)}, u32[]{:S(2)}) collective-permute-start(f32[1024,128]{1,0:T(8,128)S(1)} %multiply_add_fusion.10), channel_id=1, source_target_pairs={{0,4},{1,5},{2,6},{3,7},{4,0},{5,1},{6,2},{7,3},{8,12},{9,13},{10,... | collective-permute-start | bytes 1572872 | tf_op jit(solution)/shard_map/ppermute | solution.py:78
  53.0 1.6 %collective-permute-start.10 = (f32[1024,128]{1,0:T(8,128)S(1)}, f32[1024,128]{1,0:T(8,128)S(1)}, u32[]{:S(2)}, u32[]{:S(2)}) collective-permute-start(f32[1024,128]{1,0:T(8,128)S(1)} %multiply_add_fusion.8), channel_id=1, source_target_pairs={{0,1},{1,0},{2,3},{3,2},{4,5},{5,4},{6,7},{7,6},{8,9},{9,8},{10,11... | collective-permute-start | bytes 1572872 | tf_op jit(solution)/shard_map/ppermute | solution.py:78
  54.6 4.8 %collective-permute-done.13 = f32[1024,128]{1,0:T(8,128)S(1)} collective-permute-done((f32[1024,128]{1,0:T(8,128)S(1)}, f32[1024,128]{1,0:T(8,128)S(1)}, u32[]{:S(2)}, u32[]{:S(2)}) %collective-permute-start.13) | collective-permute-done | bytes 524320 | tf_op jit(solution)/shard_map/ppermute | solution.py:78
  59.4 14.3 %collective-permute-done.12 = f32[1024,128]{1,0:T(8,128)S(1)} collective-permute-done((f32[1024,128]{1,0:T(8,128)S(1)}, f32[1024,128]{1,0:T(8,128)S(1)}, u32[]{:S(2)}, u32[]{:S(2)}) %collective-permute-start.12) | collective-permute-done | bytes 524320 | tf_op jit(solution)/shard_map/ppermute | solution.py:78
  76.0 1.5 collective-permute-start.15
  77.5 2.7 %collective-permute-start.18 = (f32[1024,128]{1,0:T(8,128)S(1)}, f32[1024,128]{1,0:T(8,128)}, u32[]{:S(2)}, u32[]{:S(2)}) collective-permute-start(f32[1024,128]{1,0:T(8,128)S(1)} %multiply_add_fusion.5), channel_id=1, source_target_pairs={{0,4},{1,5},{2,6},{3,7},{4,0},{5,1},{6,2},{7,3},{8,12},{9,13},{10,... | collective-permute-start | bytes 1572872 | tf_op jit(solution)/shard_map/ppermute | solution.py:78
  80.1 5.3 %collective-permute-done.14 = f32[1024,128]{1,0:T(8,128)} collective-permute-done((f32[1024,128]{1,0:T(8,128)S(1)}, f32[1024,128]{1,0:T(8,128)}, u32[]{:S(2)}, u32[]{:S(2)}) %collective-permute-start.14) | collective-permute-done | bytes 524320 | tf_op jit(solution)/shard_map/ppermute | solution.py:78
  86.5 7.2 %collective-permute-done.16 = f32[1024,128]{1,0:T(8,128)S(1)} collective-permute-done((f32[1024,128]{1,0:T(8,128)S(1)}, f32[1024,128]{1,0:T(8,128)S(1)}, u32[]{:S(2)}, u32[]{:S(2)}) %collective-permute-start.16) | collective-permute-done | bytes 524320 | tf_op jit(solution)/shard_map/ppermute | solution.py:78
  94.8 2.3 %gather_fusion = f32[768,128]{1,0:T(8,128)} fusion(f32[4096,128]{1,0:T(8,128)S(1)} %pad_maximum_fusion, s32[1024]{0:T(1024)S(1)} %pad_clamp_fusion.1), kind=kCustom, calls=%fused_computation | custom fusion | bytes 789504 | tf_op jit(solution)/shard_map/jit(_take)/gather | solution.py:205
  98.6 3.0 %collective-permute-start.17 = (f32[256,128]{1,0:T(8,128)S(1)}, f32[256,128]{1,0:T(8,128)S(1)}, u32[]{:S(2)}, u32[]{:S(2)}) collective-permute-start(f32[256,128]{1,0:T(8,128)S(1)} %get-tuple-element.62), channel_id=1, source_target_pairs={{0,4},{1,5},{2,6},{3,7},{4,0},{5,1},{6,2},{7,3},{8,12},{9,13},{10,... | collective-permute-start | bytes 393224 | tf_op jit(solution)/shard_map/ppermute | solution.py:78
  101.5 4.3 %collective-permute-done.19 = f32[256,128]{1,0:T(8,128)S(1)} collective-permute-done((f32[256,128]{1,0:T(8,128)S(1)}, f32[256,128]{1,0:T(8,128)S(1)}, u32[]{:S(2)}, u32[]{:S(2)}) %collective-permute-start.19) | collective-permute-done | bytes 131104 | tf_op jit(solution)/shard_map/ppermute | solution.py:78
  105.8 1.2 multiply_add_fusion
  108.4 4.2 %all-to-all-start = ((f32[32,12,128]{2,1,0:T(8,128)}), f32[32,12,128]{2,1,0:T(8,128)S(1)}, u32[]{:S(2)}, u32[]{:S(2)}) async-start(f32[32,12,128]{2,1,0:T(8,128)} %pad_maximum_fusion.1), calls=%async_computation | async-start | bytes 524288 | tf_op jit(solution)/shard_map/all_to_all | solution.py:234
  112.7 1.8 %collective-permute-start.20 = (f32[512,128]{1,0:T(8,128)S(1)}, f32[512,128]{1,0:T(8,128)S(1)}, u32[]{:S(2)}, u32[]{:S(2)}) collective-permute-start(f32[512,128]{1,0:T(8,128)S(1)} %get-tuple-element.69), channel_id=1, source_target_pairs={{0,2},{1,3},{2,0},{3,1},{4,6},{5,7},{6,4},{7,5},{8,10},{9,11},{10,... | collective-permute-start | bytes 786440 | tf_op jit(solution)/shard_map/ppermute | solution.py:78
  114.6 2.4 %collective-permute-start.22 = (f32[512,128]{1,0:T(8,128)S(1)}, f32[512,128]{1,0:T(8,128)S(1)}, u32[]{:S(2)}, u32[]{:S(2)}) collective-permute-start(f32[512,128]{1,0:T(8,128)S(1)} %get-tuple-element.72), channel_id=1, source_target_pairs={{0,4},{1,5},{2,6},{3,7},{4,0},{5,1},{6,2},{7,3},{8,12},{9,13},{10,... | collective-permute-start | bytes 786440 | tf_op jit(solution)/shard_map/ppermute | solution.py:78
  117.0 6.2 %all-to-all-done = f32[32,12,128]{2,1,0:T(8,128)S(1)} async-done(((f32[32,12,128]{2,1,0:T(8,128)}), f32[32,12,128]{2,1,0:T(8,128)S(1)}, u32[]{:S(2)}, u32[]{:S(2)}) %all-to-all-start) | async-done | bytes 196640 | tf_op jit(solution)/shard_map/all_to_all | solution.py:234
  123.2 7.3 %collective-permute-done.20 = f32[512,128]{1,0:T(8,128)S(1)} collective-permute-done((f32[512,128]{1,0:T(8,128)S(1)}, f32[512,128]{1,0:T(8,128)S(1)}, u32[]{:S(2)}, u32[]{:S(2)}) %collective-permute-start.20) | collective-permute-done | bytes 262176 | tf_op jit(solution)/shard_map/ppermute | solution.py:78
  131.2 3.6 %all-to-all-start.1 = ((f32[32,4,128]{2,1,0:T(4,128)}), f32[32,4,128]{2,1,0:T(4,128)S(1)}, u32[]{:S(2)}, u32[]{:S(2)}) async-start(f32[32,4,128]{2,1,0:T(4,128)} %broadcast_in_dim.50), calls=%async_computation.1 | async-start | bytes 131072 | tf_op jit(solution)/shard_map/all_to_all | solution.py:238
  134.8 1.8 %collective-permute-start.21 = (f32[512,128]{1,0:T(8,128)S(1)}, f32[512,128]{1,0:T(8,128)S(1)}, u32[]{:S(2)}, u32[]{:S(2)}) collective-permute-start(f32[512,128]{1,0:T(8,128)S(1)} %get-tuple-element.71), channel_id=1, source_target_pairs={{0,2},{1,3},{2,0},{3,1},{4,6},{5,7},{6,4},{7,5},{8,10},{9,11},{10,... | collective-permute-start | bytes 786440 | tf_op jit(solution)/shard_map/ppermute | solution.py:78
  137.4 2.4 %collective-permute-start.23 = (f32[512,128]{1,0:T(8,128)S(1)}, f32[512,128]{1,0:T(8,128)S(1)}, u32[]{:S(2)}, u32[]{:S(2)}) collective-permute-start(f32[512,128]{1,0:T(8,128)S(1)} %get-tuple-element.75), channel_id=1, source_target_pairs={{0,4},{1,5},{2,6},{3,7},{4,0},{5,1},{6,2},{7,3},{8,12},{9,13},{10,... | collective-permute-start | bytes 786440 | tf_op jit(solution)/shard_map/ppermute | solution.py:78
  139.8 1.3 gather_fusion.1
  142.2 7.6 %collective-permute-done.21 = f32[512,128]{1,0:T(8,128)S(1)} collective-permute-done((f32[512,128]{1,0:T(8,128)S(1)}, f32[512,128]{1,0:T(8,128)S(1)}, u32[]{:S(2)}, u32[]{:S(2)}) %collective-permute-start.21) | collective-permute-done | bytes 262176 | tf_op jit(solution)/shard_map/ppermute | solution.py:78
  (88 shorter events, 19.5 us)
Async XLA Ops:
  0.6 1.6 %copy-start = (f32[4096,128]{1,0:T(8,128)S(1)}, f32[4096,128]{1,0:T(8,128)}, u32[]{:S(2)}) copy-start(f32[4096,128]{1,0:T(8,128)} %panel_ref.1) | copy-start | bytes 6291460
  2.9 3.0 %copy-start.6 = (s32[8192]{0:T(1024)S(1)}, s32[8192]{0:T(1024)}, u32[]{:S(2)}) copy-start(s32[8192]{0:T(1024)} %param.5) | copy-start | bytes 98308
  4.9 2.2 %collective-permute-start = (f32[1024,128]{1,0:T(8,128)S(1)}, f32[1024,128]{1,0:T(8,128)}, u32[]{:S(2)}, u32[]{:S(2)}) collective-permute-start(f32[1024,128]{1,0:T(8,128)S(1)} %get-tuple-element.41), channel_id=1, source_target_pairs={{0,8},{8,0},{16,24},{24,16},{1,9},{9,1},{17,25},{25,17},{2,10},{10... | collective-permute-start | bytes 1572872 | tf_op jit(solution)/shard_map/ppermute | solution.py:78
  5.4 10.0 %collective-permute-start.2 = (f32[1024,128]{1,0:T(8,128)S(1)}, f32[1024,128]{1,0:T(8,128)S(1)}, u32[]{:S(2)}, u32[]{:S(2)}) collective-permute-start(f32[1024,128]{1,0:T(8,128)S(1)} %get-tuple-element.43), channel_id=1, source_target_pairs={{0,8},{8,0},{16,24},{24,16},{1,9},{9,1},{17,25},{25,17},{2,10},{10... | collective-permute-start | bytes 1572872 | tf_op jit(solution)/shard_map/ppermute | solution.py:78
  5.5 8.3 %collective-permute-start.3 = (f32[1024,128]{1,0:T(8,128)S(1)}, f32[1024,128]{1,0:T(8,128)S(1)}, u32[]{:S(2)}, u32[]{:S(2)}) collective-permute-start(f32[1024,128]{1,0:T(8,128)S(1)} %get-tuple-element.44), channel_id=1, source_target_pairs={{0,8},{8,0},{16,24},{24,16},{1,9},{9,1},{17,25},{25,17},{2,10},{10... | collective-permute-start | bytes 1572872 | tf_op jit(solution)/shard_map/ppermute | solution.py:78
  8.2 26.4 %collective-permute-start.6 = (f32[1024,128]{1,0:T(8,128)S(1)}, f32[1024,128]{1,0:T(8,128)S(1)}, u32[]{:S(2)}, u32[]{:S(2)}) collective-permute-start(f32[1024,128]{1,0:T(8,128)S(1)} %multiply_add_fusion.17), channel_id=1, source_target_pairs={{0,2},{1,3},{2,0},{3,1},{4,6},{5,7},{6,4},{7,5},{8,10},{9,11},{10,... | collective-permute-start | bytes 1572872 | tf_op jit(solution)/shard_map/ppermute | solution.py:78
  11.2 27.4 %collective-permute-start.1 = (f32[1024,128]{1,0:T(8,128)S(1)}, f32[1024,128]{1,0:T(8,128)S(1)}, u32[]{:S(2)}, u32[]{:S(2)}) collective-permute-start(f32[1024,128]{1,0:T(8,128)S(1)} %get-tuple-element.42), channel_id=1, source_target_pairs={{0,4},{1,5},{2,6},{3,7},{4,0},{5,1},{6,2},{7,3},{8,12},{9,13},{10,... | collective-permute-start | bytes 1572872 | tf_op jit(solution)/shard_map/ppermute | solution.py:78
  13.8 22.5 %collective-permute-start.5 = (f32[1024,128]{1,0:T(8,128)S(1)}, f32[1024,128]{1,0:T(8,128)S(1)}, u32[]{:S(2)}, u32[]{:S(2)}) collective-permute-start(f32[1024,128]{1,0:T(8,128)S(1)} %multiply_add_fusion.16), channel_id=1, source_target_pairs={{0,16},{8,24},{16,0},{24,8},{1,17},{9,25},{17,1},{25,9},{2,18},{10... | collective-permute-start | bytes 1572872 | tf_op jit(solution)/shard_map/ppermute | solution.py:78
  15.5 22.5 %collective-permute-start.4 = (f32[1024,128]{1,0:T(8,128)S(1)}, f32[1024,128]{1,0:T(8,128)S(1)}, u32[]{:S(2)}, u32[]{:S(2)}) collective-permute-start(f32[1024,128]{1,0:T(8,128)S(1)} %multiply_add_fusion.15), channel_id=1, source_target_pairs={{0,1},{1,0},{2,3},{3,2},{4,5},{5,4},{6,7},{7,6},{8,9},{9,8},{10,11... | collective-permute-start | bytes 1572872 | tf_op jit(solution)/shard_map/ppermute | solution.py:78
  34.6 14.9 %collective-permute-start.9 = (f32[1024,128]{1,0:T(8,128)S(1)}, f32[1024,128]{1,0:T(8,128)S(1)}, u32[]{:S(2)}, u32[]{:S(2)}) collective-permute-start(f32[1024,128]{1,0:T(8,128)S(1)} %multiply_add_fusion.14), channel_id=1, source_target_pairs={{0,16},{8,24},{16,0},{24,8},{1,17},{9,25},{17,1},{25,9},{2,18},{10... | collective-permute-start | bytes 1572872 | tf_op jit(solution)/shard_map/ppermute | solution.py:78
  36.4 13.2 %collective-permute-start.8 = (f32[1024,128]{1,0:T(8,128)S(1)}, f32[1024,128]{1,0:T(8,128)S(1)}, u32[]{:S(2)}, u32[]{:S(2)}) collective-permute-start(f32[1024,128]{1,0:T(8,128)S(1)} %multiply_add_fusion.13), channel_id=1, source_target_pairs={{0,1},{1,0},{2,3},{3,2},{4,5},{5,4},{6,7},{7,6},{8,9},{9,8},{10,11... | collective-permute-start | bytes 1572872 | tf_op jit(solution)/shard_map/ppermute | solution.py:78
  38.0 21.3 %collective-permute-start.13 = (f32[1024,128]{1,0:T(8,128)S(1)}, f32[1024,128]{1,0:T(8,128)S(1)}, u32[]{:S(2)}, u32[]{:S(2)}) collective-permute-start(f32[1024,128]{1,0:T(8,128)S(1)} %multiply_add_fusion.12), channel_id=1, source_target_pairs={{0,16},{8,24},{16,0},{24,8},{1,17},{9,25},{17,1},{25,9},{2,18},{10... | collective-permute-start | bytes 1572872 | tf_op jit(solution)/shard_map/ppermute | solution.py:78
  38.7 11.0 %collective-permute-start.7 = (f32[1024,128]{1,0:T(8,128)S(1)}, f32[1024,128]{1,0:T(8,128)S(1)}, u32[]{:S(2)}, u32[]{:S(2)}) collective-permute-start(f32[1024,128]{1,0:T(8,128)S(1)} %multiply_add_fusion.11), channel_id=1, source_target_pairs={{0,8},{8,0},{16,24},{24,16},{1,9},{9,1},{17,25},{25,17},{2,10},{10... | collective-permute-start | bytes 1572872 | tf_op jit(solution)/shard_map/ppermute | solution.py:78
  49.6 24.1 %collective-permute-start.11 = (f32[1024,128]{1,0:T(8,128)S(1)}, f32[1024,128]{1,0:T(8,128)S(1)}, u32[]{:S(2)}, u32[]{:S(2)}) collective-permute-start(f32[1024,128]{1,0:T(8,128)S(1)} %multiply_add_fusion.9), channel_id=1, source_target_pairs={{0,2},{1,3},{2,0},{3,1},{4,6},{5,7},{6,4},{7,5},{8,10},{9,11},{10,... | collective-permute-start | bytes 1572872 | tf_op jit(solution)/shard_map/ppermute | solution.py:78
  49.7 23.9 %collective-permute-start.12 = (f32[1024,128]{1,0:T(8,128)S(1)}, f32[1024,128]{1,0:T(8,128)S(1)}, u32[]{:S(2)}, u32[]{:S(2)}) collective-permute-start(f32[1024,128]{1,0:T(8,128)S(1)} %multiply_add_fusion.10), channel_id=1, source_target_pairs={{0,4},{1,5},{2,6},{3,7},{4,0},{5,1},{6,2},{7,3},{8,12},{9,13},{10,... | collective-permute-start | bytes 1572872 | tf_op jit(solution)/shard_map/ppermute | solution.py:78
  53.0 20.8 %collective-permute-start.10 = (f32[1024,128]{1,0:T(8,128)S(1)}, f32[1024,128]{1,0:T(8,128)S(1)}, u32[]{:S(2)}, u32[]{:S(2)}) collective-permute-start(f32[1024,128]{1,0:T(8,128)S(1)} %multiply_add_fusion.8), channel_id=1, source_target_pairs={{0,1},{1,0},{2,3},{3,2},{4,5},{5,4},{6,7},{7,6},{8,9},{9,8},{10,11... | collective-permute-start | bytes 1572872 | tf_op jit(solution)/shard_map/ppermute | solution.py:78
  73.9 11.6 %collective-permute-start.14 = (f32[1024,128]{1,0:T(8,128)S(1)}, f32[1024,128]{1,0:T(8,128)}, u32[]{:S(2)}, u32[]{:S(2)}) collective-permute-start(f32[1024,128]{1,0:T(8,128)S(1)} %multiply_add_fusion.4), channel_id=1, source_target_pairs={{0,16},{8,24},{16,0},{24,8},{1,17},{9,25},{17,1},{25,9},{2,18},{10... | collective-permute-start | bytes 1572872 | tf_op jit(solution)/shard_map/ppermute | solution.py:78
  74.9 18.9 %collective-permute-start.16 = (f32[1024,128]{1,0:T(8,128)S(1)}, f32[1024,128]{1,0:T(8,128)S(1)}, u32[]{:S(2)}, u32[]{:S(2)}) collective-permute-start(f32[1024,128]{1,0:T(8,128)S(1)} %multiply_add_fusion.7), channel_id=1, source_target_pairs={{0,2},{1,3},{2,0},{3,1},{4,6},{5,7},{6,4},{7,5},{8,10},{9,11},{10,... | collective-permute-start | bytes 1572872 | tf_op jit(solution)/shard_map/ppermute | solution.py:78
  76.0 17.8 %collective-permute-start.15 = (f32[1024,128]{1,0:T(8,128)S(1)}, f32[1024,128]{1,0:T(8,128)S(1)}, u32[]{:S(2)}, u32[]{:S(2)}) collective-permute-start(f32[1024,128]{1,0:T(8,128)S(1)} %multiply_add_fusion.6), channel_id=1, source_target_pairs={{0,1},{1,0},{2,3},{3,2},{4,5},{5,4},{6,7},{7,6},{8,9},{9,8},{10,11... | collective-permute-start | bytes 1572872 | tf_op jit(solution)/shard_map/ppermute | solution.py:78
  77.5 28.4 %collective-permute-start.18 = (f32[1024,128]{1,0:T(8,128)S(1)}, f32[1024,128]{1,0:T(8,128)}, u32[]{:S(2)}, u32[]{:S(2)}) collective-permute-start(f32[1024,128]{1,0:T(8,128)S(1)} %multiply_add_fusion.5), channel_id=1, source_target_pairs={{0,4},{1,5},{2,6},{3,7},{4,0},{5,1},{6,2},{7,3},{8,12},{9,13},{10,... | collective-permute-start | bytes 1572872 | tf_op jit(solution)/shard_map/ppermute | solution.py:78
  86.5 7.4 %copy-start.2 = (f32[1024,128]{1,0:T(8,128)}, f32[1024,128]{1,0:T(8,128)S(1)}, u32[]{:S(2)}) copy-start(f32[1024,128]{1,0:T(8,128)S(1)} %multiply_add_fusion.3) | copy-start | bytes 1572868
  93.8 0.8 copy-start.4
  97.1 15.6 %copy-start.3 = (f32[1024,128]{1,0:T(8,128)S(1)}, f32[1024,128]{1,0:T(8,128)}, u32[]{:S(2)}) copy-start(f32[1024,128]{1,0:T(8,128)} %copy-done.2) | copy-start | bytes 1572868
  98.2 7.6 %collective-permute-start.19 = (f32[256,128]{1,0:T(8,128)S(1)}, f32[256,128]{1,0:T(8,128)S(1)}, u32[]{:S(2)}, u32[]{:S(2)}) collective-permute-start(f32[256,128]{1,0:T(8,128)S(1)} %get-tuple-element.64), channel_id=1, source_target_pairs={{0,2},{1,3},{2,0},{3,1},{4,6},{5,7},{6,4},{7,5},{8,10},{9,11},{10,... | collective-permute-start | bytes 393224 | tf_op jit(solution)/shard_map/ppermute | solution.py:78
  98.6 8.4 %collective-permute-start.17 = (f32[256,128]{1,0:T(8,128)S(1)}, f32[256,128]{1,0:T(8,128)S(1)}, u32[]{:S(2)}, u32[]{:S(2)}) collective-permute-start(f32[256,128]{1,0:T(8,128)S(1)} %get-tuple-element.62), channel_id=1, source_target_pairs={{0,4},{1,5},{2,6},{3,7},{4,0},{5,1},{6,2},{7,3},{8,12},{9,13},{10,... | collective-permute-start | bytes 393224 | tf_op jit(solution)/shard_map/ppermute | solution.py:78
  105.8 6.8 %copy-start.5 = (f32[1024,128]{1,0:T(8,128)S(1)}, f32[1024,128]{1,0:T(8,128)}, u32[]{:S(2)}) copy-start(f32[1024,128]{1,0:T(8,128)} %copy-done.4) | copy-start | bytes 1572868
  108.4 14.8 %all-to-all-start = ((f32[32,12,128]{2,1,0:T(8,128)}), f32[32,12,128]{2,1,0:T(8,128)S(1)}, u32[]{:S(2)}, u32[]{:S(2)}) async-start(f32[32,12,128]{2,1,0:T(8,128)} %pad_maximum_fusion.1), calls=%async_computation | async-start | bytes 524288 | tf_op jit(solution)/shard_map/all_to_all | solution.py:234
  112.7 17.8 %collective-permute-start.20 = (f32[512,128]{1,0:T(8,128)S(1)}, f32[512,128]{1,0:T(8,128)S(1)}, u32[]{:S(2)}, u32[]{:S(2)}) collective-permute-start(f32[512,128]{1,0:T(8,128)S(1)} %get-tuple-element.69), channel_id=1, source_target_pairs={{0,2},{1,3},{2,0},{3,1},{4,6},{5,7},{6,4},{7,5},{8,10},{9,11},{10,... | collective-permute-start | bytes 786440 | tf_op jit(solution)/shard_map/ppermute | solution.py:78
  114.6 22.8 %collective-permute-start.22 = (f32[512,128]{1,0:T(8,128)S(1)}, f32[512,128]{1,0:T(8,128)S(1)}, u32[]{:S(2)}, u32[]{:S(2)}) collective-permute-start(f32[512,128]{1,0:T(8,128)S(1)} %get-tuple-element.72), channel_id=1, source_target_pairs={{0,4},{1,5},{2,6},{3,7},{4,0},{5,1},{6,2},{7,3},{8,12},{9,13},{10,... | collective-permute-start | bytes 786440 | tf_op jit(solution)/shard_map/ppermute | solution.py:78
  131.2 11.0 %all-to-all-start.1 = ((f32[32,4,128]{2,1,0:T(4,128)}), f32[32,4,128]{2,1,0:T(4,128)S(1)}, u32[]{:S(2)}, u32[]{:S(2)}) async-start(f32[32,4,128]{2,1,0:T(4,128)} %broadcast_in_dim.50), calls=%async_computation.1 | async-start | bytes 131072 | tf_op jit(solution)/shard_map/all_to_all | solution.py:238
  134.8 15.0 %collective-permute-start.21 = (f32[512,128]{1,0:T(8,128)S(1)}, f32[512,128]{1,0:T(8,128)S(1)}, u32[]{:S(2)}, u32[]{:S(2)}) collective-permute-start(f32[512,128]{1,0:T(8,128)S(1)} %get-tuple-element.71), channel_id=1, source_target_pairs={{0,2},{1,3},{2,0},{3,1},{4,6},{5,7},{6,4},{7,5},{8,10},{9,11},{10,... | collective-permute-start | bytes 786440 | tf_op jit(solution)/shard_map/ppermute | solution.py:78
  137.4 15.5 %collective-permute-start.23 = (f32[512,128]{1,0:T(8,128)S(1)}, f32[512,128]{1,0:T(8,128)S(1)}, u32[]{:S(2)}, u32[]{:S(2)}) collective-permute-start(f32[512,128]{1,0:T(8,128)S(1)} %get-tuple-element.75), channel_id=1, source_target_pairs={{0,4},{1,5},{2,6},{3,7},{4,0},{5,1},{6,2},{7,3},{8,12},{9,13},{10,... | collective-permute-start | bytes 786440 | tf_op jit(solution)/shard_map/ppermute | solution.py:78
  (1 other events, 0.7 us)

commit v5 on v4

--- a/solution.py
+++ b/solution.py
@@ -21,16 +21,23 @@
 
 
 def local_kernel(scale, flips_ref, panel_ref, *refs):
-    *outs, held = refs
+    *outs, flags, held, arrived = refs
     blocks = panel_ref.shape[0] // BLOCK
     width = panel_ref.shape[1]
-    lanes = flips_ref.shape[1]
-    per = BLOCK // lanes
+    per = BLOCK // flips_ref.shape[1]
+    loads = [pltpu.make_async_copy(flips_ref, flags, arrived.at[blocks])]
+    for b in range(blocks):
+        source = panel_ref.at[pl.ds(b * BLOCK, BLOCK), :]
+        loads.append(pltpu.make_async_copy(source, held.at[b], arrived.at[b]))
+    for load in loads:
+        load.start()
     base = signs(BLOCK)
+    loads[0].wait()
     for b in range(blocks):
-        row = jnp.concatenate([flips_ref[b * per + i : b * per + i + 1, :] for i in range(per)], axis=1)
+        row = jnp.concatenate([flags[b * per + i : b * per + i + 1, :] for i in range(per)], axis=1)
         mixer = (base * (1 - 2 * row).astype(jnp.float32)).astype(jnp.bfloat16)
-        values = panel_ref[b * BLOCK : (b + 1) * BLOCK, :]
+        loads[b + 1].wait()
+        values = held[b]
         high = values.astype(jnp.bfloat16)
         rest = values - high.astype(jnp.float32)
         middle = rest.astype(jnp.bfloat16)
@@ -65,10 +72,14 @@
     return pl.pallas_call(
         functools.partial(local_kernel, scale),
         out_shape=[jax.ShapeDtypeStruct((share, width), jnp.float32) for share in shares],
-        in_specs=[pl.BlockSpec(memory_space=pltpu.VMEM)] * 2,
+        in_specs=[pl.BlockSpec(memory_space=pltpu.HBM)] * 2,
         out_specs=[pl.BlockSpec(memory_space=pltpu.VMEM)] * len(shares),
-        scratch_shapes=[pltpu.VMEM((rows // BLOCK, BLOCK, width), jnp.float32)],
-        compiler_params=pltpu.CompilerParams(vmem_limit_bytes=32 * 2**20),
+        scratch_shapes=[
+            pltpu.VMEM((rows // 128, 128), jnp.int32),
+            pltpu.VMEM((rows // BLOCK, BLOCK, width), jnp.float32),
+            pltpu.SemaphoreType.DMA((rows // BLOCK + 1,)),
+        ],
+        compiler_params=pltpu.CompilerParams(vmem_limit_bytes=60 * 2**20),
     )(flips.reshape(rows // 128, 128), panel)
 
 
@@ -86,6 +97,55 @@
 def bit_of(stage):
     axis, level = stage
     return 2**level * (lax.axis_size("wide") if axis == "narrow" else 1)
+
+
+def store_kernel(*refs):
+    *values, out_ref, sent = refs
+    copies, at = [], 0
+    for i, value in enumerate(values):
+        rows = value.shape[0]
+        copies.append(pltpu.make_async_copy(value, out_ref.at[pl.ds(at, rows), :], sent.at[i]))
+        at += rows
+    for copy in copies:
+        copy.start()
+    for copy in copies:
+        copy.wait()
+
+
+def store_rows(values, rows):
+    return pl.pallas_call(
+        store_kernel,
+        out_shape=jax.ShapeDtypeStruct((rows, values[0].shape[1]), jnp.float32),
+        in_specs=[pl.BlockSpec(memory_space=pltpu.VMEM)] * len(values),
+        out_specs=pl.BlockSpec(memory_space=pl.ANY),
+        scratch_shapes=[pltpu.SemaphoreType.DMA((len(values),))],
+        compiler_params=pltpu.CompilerParams(vmem_limit_bytes=8 * 2**20),
+    )(*values)
+
+
+def finish_kernel(at, sign_ref, partner_ref, value_ref, whole_ref, out_ref, held, sent):
+    del whole_ref
+    held[...] = partner_ref[...] + sign_ref[0] * value_ref[...]
+    rows = held.shape[0]
+    copy = pltpu.make_async_copy(held, out_ref.at[pl.ds(at, rows), :], sent)
+    copy.start()
+    copy.wait()
+
+
+def finish(whole, sent, at, *others):
+    partner, value, stage = sent
+    partner = after(partner, others)
+    return pl.pallas_call(
+        functools.partial(finish_kernel, at),
+        out_shape=jax.ShapeDtypeStruct(whole.shape, jnp.float32),
+        in_specs=[pl.BlockSpec(memory_space=pltpu.SMEM)]
+        + [pl.BlockSpec(memory_space=pltpu.VMEM)] * 2
+        + [pl.BlockSpec(memory_space=pl.ANY)],
+        out_specs=pl.BlockSpec(memory_space=pl.ANY),
+        scratch_shapes=[pltpu.VMEM(value.shape, jnp.float32), pltpu.SemaphoreType.DMA],
+        input_output_aliases={3: 0},
+        compiler_params=pltpu.CompilerParams(vmem_limit_bytes=8 * 2**20),
+    )(sign_of(stage).reshape(1), partner, value, whole)
 
 
 class Chain:
@@ -169,37 +229,34 @@
     me = lax.axis_index(AXES)
     per = picks.shape[0] // devices
     most = -(-per // devices)
-    cuts = [rows_here * cut // 4 for cut in range(5)]
+    cuts = [rows_here * cut // 16 for cut in (0, 3, 6, 11, 16)]
 
     c = local_transform(panel, flips, scale, [b - a for a, b in zip(cuts, cuts[1:])])
     chain = Chain()
-    core1, core2, core3 = [chain.begin(c[i], core) for i in (1, 2, 3)]
+    far0, mid1 = launch(c[0], far), launch(c[1], mid)
+    core2, core3 = chain.begin(c[2], core), chain.begin(c[3], core)
     wanted = send_rows(picks, [me ^ bit_of(far), me ^ bit_of(mid), me], rows_here, devices, most)
     spots = landing(lax.dynamic_slice(picks, (me * per,), (per,)), rows_here, most)
-    v1, v2, v3 = chain.end(core1), chain.end(core2), chain.end(core3)
-    mid1 = launch(v1, mid)
-    far0 = launch(after(c[0], v1), far)
-    first2 = chain.begin(v2, first)
-    second3 = chain.begin(v3, second)
-    chain.last = (chain.last, wanted, spots)
-    first1 = chain.begin(chain.end(mid1), first)
+    first2 = chain.begin(chain.end(core2), first)
+    second3 = chain.begin(chain.end(core3), second)
+    mid0 = launch(chain.end(far0), mid)
+    far1 = launch(chain.end(mid1), far)
     second2 = chain.begin(chain.end(first2), second)
     first3 = chain.begin(chain.end(second3), first)
-    core0 = chain.begin(chain.end(far0), core)
-    v1 = chain.end(first1)
-    v2 = chain.end(second2)
-    mid2 = launch(v2, mid)
-    far1 = launch(after(v1, v2), far)
-    second0 = chain.begin(chain.end(core0), second)
-    v3 = chain.end(first3)
-    mid3 = launch(v3, mid)
-    second1 = chain.begin(chain.end(far1), second)
-    v2 = chain.end(mid2)
-    far2 = launch(after(v2, v3), far)
-    first0 = chain.begin(chain.end(second0), first)
-    v0 = chain.end(first0)
-    v3 = chain.end(mid3)
-    v1 = chain.end(second1)
+    v2 = split(chain.end(second2), 2)
+    far2 = [launch(part, far) for part in v2]
+    v3 = split(chain.end(first3), 2)
+    mid3 = [launch(part, mid) for part in v3]
+    core0 = chain.begin(chain.end(mid0), core)
+    core1 = chain.begin(chain.end(far1), core)
+    first0 = chain.begin(chain.end(core0), first)
+    second1 = chain.begin(chain.end(core1), second)
+    v2, v3 = [chain.end(far2[0])], [chain.end(mid3[0])]
+    second0 = chain.begin(chain.end(first0), second)
+    first1 = chain.begin(chain.end(second1), first)
+    v0, v1 = chain.end(second0), chain.end(first1)
+    v2, v3 = v2 + [chain.end(far2[1])], v3 + [chain.end(mid3[1])]
+    v2, v3 = jnp.concatenate(v2, axis=0), jnp.concatenate(v3, axis=0)
 
     held = jnp.concatenate([v0, v1, v2, v3], axis=0)
     taken = jnp.take(held, wanted, axis=0, mode="clip")
@@ -209,19 +266,20 @@
         (taken[:count], taken[count : 2 * count], taken[2 * count :])
     )
     give_mid, give_far = launch(to_mid, mid), launch(to_far, far)
-    parts0, parts3 = split(v0, 2), split(v3, 2)
-    ends0, ends3 = [], []
+    whole = store_rows([v0, v1], rows_here)
+    parts2, parts3 = split(v2, 2), split(v3, 2)
+    ends = []
 
     def more(step, gate):
-        ends0.append(launch(after(parts0[step], gate), mid))
-        ends3.append(launch(after(parts3[step], gate), far))
-
+        ends.append(launch(after(parts2[step], gate), mid))
+        ends.append(launch(after(parts3[step], gate), far))
+
+    more(0, to_far)
     got_mid = chain.end((give_mid[0], own, mid))
-    v2 = chain.end(far2)
     got_far = chain.end((give_far[0], own, far))
     place = rows[:, None]
     chosen = jnp.where(
-        place >= cuts[2], got_far, jnp.where(place < cuts[1], got_mid, own)
+        place >= cuts[3], got_far, jnp.where(place >= cuts[2], got_mid, own)
     )
     kept = jnp.where(filled[:, None], chosen, 0.0)
     part = lax.dot_general(
@@ -232,20 +290,17 @@
         [chosen.reshape(devices, most, width), part.reshape(devices, -1, width)], axis=1
     )
     landed = lax.all_to_all(both, AXES, 0, 0, tiled=True)
-    more(0, both)
+    more(1, both)
     mine = jnp.sum(landed[:, most:], axis=0) / float(picks.shape[0])
     shared = jnp.broadcast_to(mine[None], (devices,) + mine.shape)
     gram = lax.all_to_all(shared, AXES, 0, 0, tiled=True).reshape(width, width)
-    more(1, shared)
     sketch = jnp.take(landed[:, :most].reshape(devices * most, width), spots, axis=0, mode="clip")
-    chain.last = (chain.last, landed)
-    final0, final3 = [], []
-    for step in range(2):
-        final0.append(chain.end(ends0[step]))
-        final3.append(chain.end(ends3[step]))
-        chain.last = (chain.last, gram, sketch)
-    mixed = jnp.concatenate(final0 + [v1, v2] + final3, axis=0)
-    return (mixed, sketch, gram)
+    half = parts2[0].shape[0]
+    whole = finish(whole, ends[0], cuts[2], chain.last, landed)
+    whole = finish(whole, ends[1], cuts[3], chain.last, landed)
+    whole = finish(whole, ends[2], cuts[2] + half, gram, sketch)
+    whole = finish(whole, ends[3], cuts[3] + half, gram, sketch)
+    return (whole, sketch, gram)
 
 
 def solution(mesh):

time: 155 us -> 157 us (1.013)
  Pallas kernels: 2.83 us -> 11.7 us
  waiting for transfers between devices: 87 us -> 82.3 us
  local copies, waits for them, and re-layouts: 11.9 us -> 7.75 us
  other arithmetic: 7.89 us -> 10.9 us
    ppermute x24 -> x26, waiting for transfers between devices: 79.7 us -> 66.4 us  [launch(): return (lax.ppermute(value, axis, pairs), value, stage)]
    all_to_all x1, waiting for transfers between devices: 1.02 us -> 6.56 us  [on_device(): gram = lax.all_to_all(shared, AXES, 0, 0, tiled=True).reshape(width, width)]
    pallas_call x1, Pallas kernels: 1.95 us -> 6.83 us  [local_transform(): pl.pallas_call(functools.partial(local_kernel, scale), out_shape=[jax.Sha...]
    pallas_call x0 -> x5, Pallas kernels: none -> 3.97 us  [the longest x4 3.07 us: finish(): pl.pallas_call(functools.partial(finish_kernel, at), out_shape=jax.ShapeD...]
    unnamed x18 -> x11, local copies, waits for them, and re-layouts: 6.01 us -> 2.14 us
    all_to_all x1, waiting for transfers between devices: 6.23 us -> 9.37 us  [on_device(): landed = lax.all_to_all(both, AXES, 0, 0, tiled=True)]
    unnamed x2 -> x3, other arithmetic: 1.46 us -> 4.36 us
    ppermute x24 -> x26, starting transfers between devices: 35.3 us -> 33.1 us  [launch(): return (lax.ppermute(value, axis, pairs), value, stage)]
  transfers between devices with their start and end apart: 26 -> 28, of which waited for: 12 -> 15; matrix products, arithmetic and copies ran while one was open for 9% -> 8% of each run, Pallas kernels for 1% -> 2%
where the time goes in v5:
time: 157 us; the launch traced here: 156 us
  waiting for transfers between devices  82.3 us (52%)
  starting transfers between devices  42.4 us (27%)
  Pallas kernels  11.7 us (7%)
  other arithmetic  10.9 us (7%)
  local copies, waits for them, and re-layouts  7.75 us (5%)
    ppermute x26, waiting for transfers between devices, launch(): return (lax.ppermute(value, axis, pairs), value, stage)  66.4 us
    ppermute x26, starting transfers between devices, launch(): return (lax.ppermute(value, axis, pairs), value, stage)  33.1 us
    all_to_all x1, waiting for transfers between devices, on_device(): landed = lax.all_to_all(both, AXES, 0, 0, tiled=True)  9.37 us
    pallas_call x1, Pallas kernels, local_transform(): pl.pallas_call(functools.partial(local_kernel, scale), out_shape=[jax.Sha...  6.83 us
    all_to_all x1, waiting for transfers between devices, on_device(): gram = lax.all_to_all(shared, AXES, 0, 0, tiled=True).reshape(width, width)  6.56 us
    all_to_all x1, starting transfers between devices, on_device(): gram = lax.all_to_all(shared, AXES, 0, 0, tiled=True).reshape(width, width)  4.65 us
    all_to_all x1, starting transfers between devices, on_device(): landed = lax.all_to_all(both, AXES, 0, 0, tiled=True)  4.61 us
    unnamed x3, other arithmetic  4.36 us
  transfers between devices with their start and end apart: 28, of which 15 were waited for; matrix products, arithmetic and copies ran while one was open for 8% of the time, Pallas kernels for 2%

profile of v5, /device:TPU:0, one launch (start us, length us, event | category | flops | bytes accessed | tf_op | source)
XLA Modules:
  0.0 156.4 jit_solution(4122394455384325962)
XLA Ops:
  0.6 6.8 %shard_map.58 = (f32[768,128]{1,0:T(8,128)}, f32[768,128]{1,0:T(8,128)}, f32[1280,128]{1,0:T(8,128)}, f32[1280,128]{1,0:T(8,128)}) custom-call(s32[32,128]{1,0:T(8,128)} %bitcast.14, f32[4096,128]{1,0:T(8,128)} %panel_ref.1), custom_call_target="tpu_custom_call" | custom-call | tf_op jit(solution)/shard_map/pallas_call | solution.py:72
  8.1 4.0 %collective-permute-start.5 = (f32[768,128]{1,0:T(8,128)}, f32[768,128]{1,0:T(8,128)S(1)}, u32[]{:S(2)}, u32[]{:S(2)}) collective-permute-start(f32[768,128]{1,0:T(8,128)} %get-tuple-element.43), channel_id=1, source_target_pairs={{0,4},{1,5},{2,6},{3,7},{4,0},{5,1},{6,2},{7,3},{8,12},{9,13},{10,... | collective-permute-start | bytes 1179656 | tf_op jit(solution)/shard_map/ppermute | solution.py:89
  12.1 1.6 %collective-permute-start.4 = (f32[768,128]{1,0:T(8,128)}, f32[768,128]{1,0:T(8,128)S(1)}, u32[]{:S(2)}, u32[]{:S(2)}) collective-permute-start(f32[768,128]{1,0:T(8,128)} %get-tuple-element.42), channel_id=1, source_target_pairs={{0,2},{1,3},{2,0},{3,1},{4,6},{5,7},{6,4},{7,5},{8,10},{9,11},{10,... | collective-permute-start | bytes 1179656 | tf_op jit(solution)/shard_map/ppermute | solution.py:89
  13.7 1.2 multiply_add_fusion.5
  14.9 1.6 collective-permute-start.3
  16.5 1.6 %collective-permute-start.2 = (f32[1280,128]{1,0:T(8,128)S(1)}, f32[1280,128]{1,0:T(8,128)S(1)}, u32[]{:S(2)}, u32[]{:S(2)}) collective-permute-start(f32[1280,128]{1,0:T(8,128)S(1)} %multiply_add_fusion.4), channel_id=1, source_target_pairs={{0,1},{1,0},{2,3},{3,2},{4,5},{5,4},{6,7},{7,6},{8,9},{9,8},{10,11... | collective-permute-start | bytes 1966088 | tf_op jit(solution)/shard_map/ppermute | solution.py:89
  18.1 12.1 %collective-permute-done.5 = f32[768,128]{1,0:T(8,128)S(1)} collective-permute-done((f32[768,128]{1,0:T(8,128)}, f32[768,128]{1,0:T(8,128)S(1)}, u32[]{:S(2)}, u32[]{:S(2)}) %collective-permute-start.5) | collective-permute-done | bytes 393248 | tf_op jit(solution)/shard_map/ppermute | solution.py:89
  31.2 1.6 %collective-permute-start.7 = (f32[1280,128]{1,0:T(8,128)S(1)}, f32[1280,128]{1,0:T(8,128)S(1)}, u32[]{:S(2)}, u32[]{:S(2)}) collective-permute-start(f32[1280,128]{1,0:T(8,128)S(1)} %multiply_add_fusion.3), channel_id=1, source_target_pairs={{0,1},{1,0},{2,3},{3,2},{4,5},{5,4},{6,7},{7,6},{8,9},{9,8},{10,11... | collective-permute-start | bytes 1966088 | tf_op jit(solution)/shard_map/ppermute | solution.py:89
  32.8 1.6 collective-permute-start.6
  35.2 2.4 %collective-permute-start.10 = (f32[768,128]{1,0:T(8,128)S(1)}, f32[768,128]{1,0:T(8,128)S(1)}, u32[]{:S(2)}, u32[]{:S(2)}) collective-permute-start(f32[768,128]{1,0:T(8,128)S(1)} %multiply_add_fusion.14), channel_id=1, source_target_pairs={{0,4},{1,5},{2,6},{3,7},{4,0},{5,1},{6,2},{7,3},{8,12},{9,13},{10,... | collective-permute-start | bytes 1179656 | tf_op jit(solution)/shard_map/ppermute | solution.py:89
  37.6 9.0 %collective-permute-done.7 = f32[1280,128]{1,0:T(8,128)S(1)} collective-permute-done((f32[1280,128]{1,0:T(8,128)S(1)}, f32[1280,128]{1,0:T(8,128)S(1)}, u32[]{:S(2)}, u32[]{:S(2)}) %collective-permute-start.7) | collective-permute-done | bytes 655392 | tf_op jit(solution)/shard_map/ppermute | solution.py:89
  47.9 3.7 %collective-permute-done.11 = f32[768,128]{1,0:T(8,128)S(1)} collective-permute-done((f32[768,128]{1,0:T(8,128)S(1)}, f32[768,128]{1,0:T(8,128)S(1)}, u32[]{:S(2)}, u32[]{:S(2)}) %collective-permute-start.11) | collective-permute-done | bytes 393248 | tf_op jit(solution)/shard_map/ppermute | solution.py:89
  51.8 2.8 %collective-permute-done.10 = f32[768,128]{1,0:T(8,128)S(1)} collective-permute-done((f32[768,128]{1,0:T(8,128)S(1)}, f32[768,128]{1,0:T(8,128)S(1)}, u32[]{:S(2)}, u32[]{:S(2)}) %collective-permute-start.10) | collective-permute-done | bytes 393248 | tf_op jit(solution)/shard_map/ppermute | solution.py:89
  55.2 2.6 %collective-permute-start.17 = (f32[640,128]{1,0:T(8,128)S(1)}, f32[640,128]{1,0:T(8,128)S(1)}, u32[]{:S(2)}, u32[]{:S(2)}) collective-permute-start(f32[640,128]{1,0:T(8,128)S(1)} %slice.49), channel_id=1, source_target_pairs={{0,4},{1,5},{2,6},{3,7},{4,0},{5,1},{6,2},{7,3},{8,12},{9,13},{10,... | collective-permute-start | bytes 983048 | tf_op jit(solution)/shard_map/ppermute | solution.py:89
  60.0 13.0 %collective-permute-done.17 = f32[640,128]{1,0:T(8,128)S(1)} collective-permute-done((f32[640,128]{1,0:T(8,128)S(1)}, f32[640,128]{1,0:T(8,128)S(1)}, u32[]{:S(2)}, u32[]{:S(2)}) %collective-permute-start.17) | collective-permute-done | bytes 327712 | tf_op jit(solution)/shard_map/ppermute | solution.py:89
  77.3 2.6 %collective-permute-start.8 = (f32[640,128]{1,0:T(8,128)}, f32[640,128]{1,0:T(8,128)S(1)}, u32[]{:S(2)}, u32[]{:S(2)}) collective-permute-start(f32[640,128]{1,0:T(8,128)} %get-tuple-element.85), channel_id=1, source_target_pairs={{0,2},{1,3},{2,0},{3,1},{4,6},{5,7},{6,4},{7,5},{8,10},{9,11},{10,... | collective-permute-start | bytes 983048 | tf_op jit(solution)/shard_map/ppermute | solution.py:89
  79.9 3.5 %collective-permute-done.19 = f32[768,128]{1,0:T(8,128)} collective-permute-done((f32[768,128]{1,0:T(8,128)S(1)}, f32[768,128]{1,0:T(8,128)}, u32[]{:S(2)}, u32[]{:S(2)}) %collective-permute-start.19) | collective-permute-done | bytes 393248 | tf_op jit(solution)/shard_map/ppermute | solution.py:89
  83.4 1.8 %constant_dynamic-update-slice_fusion.5 = (f32[4096,128]{1,0:T(8,128)}, f32[768,128]{1,0:T(8,128)S(1)}) fusion(f32[768,128]{1,0:T(8,128)} %collective-permute-done.19, f32[768,128]{1,0:T(8,128)S(1)} %multiply_add_fusion.9, f32[]{:T(128)S(6)} %convert_element_type.16), kind=kLoop, calls=%fused_computation.43 | loop fusion | flops 196607 | bytes 1572868
  85.2 1.8 %constant_dynamic-update-slice_fusion.4 = (f32[4096,128]{1,0:T(8,128)}, f32[768,128]{1,0:T(8,128)S(1)}) fusion(f32[4096,128]{1,0:T(8,128)} %get-tuple-element.83, f32[768,128]{1,0:T(8,128)} %collective-permute-done.18, f32[768,128]{1,0:T(8,128)S(1)} %multiply_add_fusion.8, f32[]{:T(128)S(6)} %convert_element_type.15), kind=kLoop, calls=%fused_computation.42 | loop fusion | flops 196608 | bytes 1572868
  87.7 4.1 %collective-permute-done.9 = f32[640,128]{1,0:T(8,128)S(1)} collective-permute-done((f32[640,128]{1,0:T(8,128)}, f32[640,128]{1,0:T(8,128)S(1)}, u32[]{:S(2)}, u32[]{:S(2)}) %collective-permute-start.9) | collective-permute-done | bytes 327712 | tf_op jit(solution)/shard_map/ppermute | solution.py:89
  94.1 3.2 %gather_fusion = f32[768,128]{1,0:T(8,128)S(1)} fusion(f32[4096,128]{1,0:T(8,128)} %get-tuple-element.77, s32[1024]{0:T(1024)S(1)} %pad_clamp_fusion.1), kind=kCustom, calls=%fused_computation | custom fusion | bytes 789504 | tf_op jit(solution)/shard_map/jit(_take)/gather | solution.py:262
  98.3 3.3 %collective-permute-start.20 = (f32[256,128]{1,0:T(8,128)S(1)}, f32[256,128]{1,0:T(8,128)S(1)}, u32[]{:S(2)}, u32[]{:S(2)}) collective-permute-start(f32[256,128]{1,0:T(8,128)S(1)} %get-tuple-element.62), channel_id=1, source_target_pairs={{0,4},{1,5},{2,6},{3,7},{4,0},{5,1},{6,2},{7,3},{8,12},{9,13},{10,... | collective-permute-start | bytes 393224 | tf_op jit(solution)/shard_map/ppermute | solution.py:89
  101.6 2.2 %collective-permute-done.21 = f32[256,128]{1,0:T(8,128)S(1)} collective-permute-done((f32[256,128]{1,0:T(8,128)S(1)}, f32[256,128]{1,0:T(8,128)S(1)}, u32[]{:S(2)}, u32[]{:S(2)}) %collective-permute-start.21) | collective-permute-done | bytes 131104 | tf_op jit(solution)/shard_map/ppermute | solution.py:89
  103.8 4.0 %collective-permute-done.20 = f32[256,128]{1,0:T(8,128)S(1)} collective-permute-done((f32[256,128]{1,0:T(8,128)S(1)}, f32[256,128]{1,0:T(8,128)S(1)}, u32[]{:S(2)}, u32[]{:S(2)}) %collective-permute-start.20) | collective-permute-done | bytes 131104 | tf_op jit(solution)/shard_map/ppermute | solution.py:89
  109.2 4.6 %all-to-all-start = ((f32[32,12,128]{2,1,0:T(8,128)}), f32[32,12,128]{2,1,0:T(8,128)S(1)}, u32[]{:S(2)}, u32[]{:S(2)}) async-start(f32[32,12,128]{2,1,0:T(8,128)} %pad_maximum_fusion), calls=%async_computation | async-start | bytes 524288 | tf_op jit(solution)/shard_map/all_to_all | solution.py:292
  115.0 2.7 %collective-permute-start.24 = (f32[640,128]{1,0:T(8,128)S(1)}, f32[640,128]{1,0:T(8,128)S(1)}, u32[]{:S(2)}, u32[]{:S(2)}) collective-permute-start(f32[640,128]{1,0:T(8,128)S(1)} %get-tuple-element.71.value_ref), channel_id=1, source_target_pairs={{0,4},{1,5},{2,6},{3,7},{4,0},{5,1},{6,2},{7,3},{8,12},{9,13},{10,... | collective-permute-start | bytes 983048 | tf_op jit(solution)/shard_map/ppermute | solution.py:89
  117.7 1.5 collective-permute-start.25
  120.0 9.4 %all-to-all-done = f32[32,12,128]{2,1,0:T(8,128)S(1)} async-done(((f32[32,12,128]{2,1,0:T(8,128)}), f32[32,12,128]{2,1,0:T(8,128)S(1)}, u32[]{:S(2)}, u32[]{:S(2)}) %all-to-all-start) | async-done | bytes 196640 | tf_op jit(solution)/shard_map/all_to_all | solution.py:292
  130.1 4.6 %all-to-all-start.1 = ((f32[32,4,128]{2,1,0:T(4,128)}), f32[32,4,128]{2,1,0:T(4,128)S(1)}, u32[]{:S(2)}, u32[]{:S(2)}) async-start(f32[32,4,128]{2,1,0:T(4,128)} %broadcast_in_dim.50), calls=%async_computation.1 | async-start | bytes 131072 | tf_op jit(solution)/shard_map/all_to_all | solution.py:296
  134.7 10.1 %collective-permute-done.24.partner_ref = f32[640,128]{1,0:T(8,128)S(1)} collective-permute-done((f32[640,128]{1,0:T(8,128)S(1)}, f32[640,128]{1,0:T(8,128)S(1)}, u32[]{:S(2)}, u32[]{:S(2)}) %collective-permute-start.24) | collective-permute-done | bytes 327712 | tf_op jit(solution)/shard_map/ppermute | solution.py:89
  144.8 1.3 gather_fusion.1
  147.7 6.6 %all-to-all-done.1 = f32[32,4,128]{2,1,0:T(4,128)S(1)} async-done(((f32[32,4,128]{2,1,0:T(4,128)}), f32[32,4,128]{2,1,0:T(4,128)S(1)}, u32[]{:S(2)}, u32[]{:S(2)}) %all-to-all-start.1) | async-done | bytes 65568 | tf_op jit(solution)/shard_map/all_to_all | solution.py:296
  (87 shorter events, 22.8 us)
Async XLA Ops:
  7.5 9.0 %copy-start = (f32[1280,128]{1,0:T(8,128)S(1)}, f32[1280,128]{1,0:T(8,128)}, u32[]{:S(2)}) copy-start(f32[1280,128]{1,0:T(8,128)} %get-tuple-element.39) | copy-start | bytes 1966084
  7.5 22.7 %copy-start.2 = (f32[768,128]{1,0:T(8,128)S(1)}, f32[768,128]{1,0:T(8,128)}, u32[]{:S(2)}) copy-start(f32[768,128]{1,0:T(8,128)} %get-tuple-element.43) | copy-start | bytes 1179652
  7.5 6.2 %collective-permute-start.1 = (f32[1280,128]{1,0:T(8,128)}, f32[1280,128]{1,0:T(8,128)S(1)}, u32[]{:S(2)}, u32[]{:S(2)}) collective-permute-start(f32[1280,128]{1,0:T(8,128)} %get-tuple-element.40), channel_id=1, source_target_pairs={{0,8},{8,0},{16,24},{24,16},{1,9},{9,1},{17,25},{25,17},{2,10},{10... | collective-permute-start | bytes 1966088 | tf_op jit(solution)/shard_map/ppermute | solution.py:89
  8.0 8.4 %collective-permute-start = (f32[1280,128]{1,0:T(8,128)}, f32[1280,128]{1,0:T(8,128)S(1)}, u32[]{:S(2)}, u32[]{:S(2)}) collective-permute-start(f32[1280,128]{1,0:T(8,128)} %get-tuple-element.39), channel_id=1, source_target_pairs={{0,8},{8,0},{16,24},{24,16},{1,9},{9,1},{17,25},{25,17},{2,10},{10... | collective-permute-start | bytes 1966088 | tf_op jit(solution)/shard_map/ppermute | solution.py:89
  8.1 22.1 %collective-permute-start.5 = (f32[768,128]{1,0:T(8,128)}, f32[768,128]{1,0:T(8,128)S(1)}, u32[]{:S(2)}, u32[]{:S(2)}) collective-permute-start(f32[768,128]{1,0:T(8,128)} %get-tuple-element.43), channel_id=1, source_target_pairs={{0,4},{1,5},{2,6},{3,7},{4,0},{5,1},{6,2},{7,3},{8,12},{9,13},{10,... | collective-permute-start | bytes 1179656 | tf_op jit(solution)/shard_map/ppermute | solution.py:89
  12.1 18.3 %collective-permute-start.4 = (f32[768,128]{1,0:T(8,128)}, f32[768,128]{1,0:T(8,128)S(1)}, u32[]{:S(2)}, u32[]{:S(2)}) collective-permute-start(f32[768,128]{1,0:T(8,128)} %get-tuple-element.42), channel_id=1, source_target_pairs={{0,2},{1,3},{2,0},{3,1},{4,6},{5,7},{6,4},{7,5},{8,10},{9,11},{10,... | collective-permute-start | bytes 1179656 | tf_op jit(solution)/shard_map/ppermute | solution.py:89
  13.7 16.7 %copy-start.1 = (f32[768,128]{1,0:T(8,128)S(1)}, f32[768,128]{1,0:T(8,128)}, u32[]{:S(2)}) copy-start(f32[768,128]{1,0:T(8,128)} %get-tuple-element.42) | copy-start | bytes 1179652
  14.9 16.2 %collective-permute-start.3 = (f32[1280,128]{1,0:T(8,128)S(1)}, f32[1280,128]{1,0:T(8,128)S(1)}, u32[]{:S(2)}, u32[]{:S(2)}) collective-permute-start(f32[1280,128]{1,0:T(8,128)S(1)} %multiply_add_fusion.5), channel_id=1, source_target_pairs={{0,16},{8,24},{16,0},{24,8},{1,17},{9,25},{17,1},{25,9},{2,18},{10... | collective-permute-start | bytes 1966088 | tf_op jit(solution)/shard_map/ppermute | solution.py:89
  16.5 16.2 %collective-permute-start.2 = (f32[1280,128]{1,0:T(8,128)S(1)}, f32[1280,128]{1,0:T(8,128)S(1)}, u32[]{:S(2)}, u32[]{:S(2)}) collective-permute-start(f32[1280,128]{1,0:T(8,128)S(1)} %multiply_add_fusion.4), channel_id=1, source_target_pairs={{0,1},{1,0},{2,3},{3,2},{4,5},{5,4},{6,7},{7,6},{8,9},{9,8},{10,11... | collective-permute-start | bytes 1966088 | tf_op jit(solution)/shard_map/ppermute | solution.py:89
  31.2 15.4 %collective-permute-start.7 = (f32[1280,128]{1,0:T(8,128)S(1)}, f32[1280,128]{1,0:T(8,128)S(1)}, u32[]{:S(2)}, u32[]{:S(2)}) collective-permute-start(f32[1280,128]{1,0:T(8,128)S(1)} %multiply_add_fusion.3), channel_id=1, source_target_pairs={{0,1},{1,0},{2,3},{3,2},{4,5},{5,4},{6,7},{7,6},{8,9},{9,8},{10,11... | collective-permute-start | bytes 1966088 | tf_op jit(solution)/shard_map/ppermute | solution.py:89
  32.8 15.0 %collective-permute-start.6 = (f32[1280,128]{1,0:T(8,128)S(1)}, f32[1280,128]{1,0:T(8,128)S(1)}, u32[]{:S(2)}, u32[]{:S(2)}) collective-permute-start(f32[1280,128]{1,0:T(8,128)S(1)} %multiply_add_fusion.2), channel_id=1, source_target_pairs={{0,16},{8,24},{16,0},{24,8},{1,17},{9,25},{17,1},{25,9},{2,18},{10... | collective-permute-start | bytes 1966088 | tf_op jit(solution)/shard_map/ppermute | solution.py:89
  34.4 17.3 %collective-permute-start.11 = (f32[768,128]{1,0:T(8,128)S(1)}, f32[768,128]{1,0:T(8,128)S(1)}, u32[]{:S(2)}, u32[]{:S(2)}) collective-permute-start(f32[768,128]{1,0:T(8,128)S(1)} %multiply_add_fusion.15), channel_id=1, source_target_pairs={{0,2},{1,3},{2,0},{3,1},{4,6},{5,7},{6,4},{7,5},{8,10},{9,11},{10,... | collective-permute-start | bytes 1179656 | tf_op jit(solution)/shard_map/ppermute | solution.py:89
  35.2 19.3 %collective-permute-start.10 = (f32[768,128]{1,0:T(8,128)S(1)}, f32[768,128]{1,0:T(8,128)S(1)}, u32[]{:S(2)}, u32[]{:S(2)}) collective-permute-start(f32[768,128]{1,0:T(8,128)S(1)} %multiply_add_fusion.14), channel_id=1, source_target_pairs={{0,4},{1,5},{2,6},{3,7},{4,0},{5,1},{6,2},{7,3},{8,12},{9,13},{10,... | collective-permute-start | bytes 1179656 | tf_op jit(solution)/shard_map/ppermute | solution.py:89
  51.7 6.0 %collective-permute-start.13 = (f32[768,128]{1,0:T(8,128)S(1)}, f32[768,128]{1,0:T(8,128)}, u32[]{:S(2)}, u32[]{:S(2)}) collective-permute-start(f32[768,128]{1,0:T(8,128)S(1)} %multiply_add_fusion.13), channel_id=1, source_target_pairs={{0,8},{8,0},{16,24},{24,16},{1,9},{9,1},{17,25},{25,17},{2,10},{10... | collective-permute-start | bytes 1179656 | tf_op jit(solution)/shard_map/ppermute | solution.py:89
  54.6 4.8 %collective-permute-start.12 = (f32[768,128]{1,0:T(8,128)S(1)}, f32[768,128]{1,0:T(8,128)S(1)}, u32[]{:S(2)}, u32[]{:S(2)}) collective-permute-start(f32[768,128]{1,0:T(8,128)S(1)} %multiply_add_fusion.12), channel_id=1, source_target_pairs={{0,8},{8,0},{16,24},{24,16},{1,9},{9,1},{17,25},{25,17},{2,10},{10... | collective-permute-start | bytes 1179656 | tf_op jit(solution)/shard_map/ppermute | solution.py:89
  54.8 19.0 %collective-permute-start.16 = (f32[640,128]{1,0:T(8,128)S(1)}, f32[640,128]{1,0:T(8,128)S(1)}, u32[]{:S(2)}, u32[]{:S(2)}) collective-permute-start(f32[640,128]{1,0:T(8,128)S(1)} %slice.48), channel_id=1, source_target_pairs={{0,2},{1,3},{2,0},{3,1},{4,6},{5,7},{6,4},{7,5},{8,10},{9,11},{10,... | collective-permute-start | bytes 983048 | tf_op jit(solution)/shard_map/ppermute | solution.py:89
  55.2 17.8 %collective-permute-start.17 = (f32[640,128]{1,0:T(8,128)S(1)}, f32[640,128]{1,0:T(8,128)S(1)}, u32[]{:S(2)}, u32[]{:S(2)}) collective-permute-start(f32[640,128]{1,0:T(8,128)S(1)} %slice.49), channel_id=1, source_target_pairs={{0,4},{1,5},{2,6},{3,7},{4,0},{5,1},{6,2},{7,3},{8,12},{9,13},{10,... | collective-permute-start | bytes 983048 | tf_op jit(solution)/shard_map/ppermute | solution.py:89
  58.8 15.8 %collective-permute-start.15 = (f32[768,128]{1,0:T(8,128)S(1)}, f32[768,128]{1,0:T(8,128)S(1)}, u32[]{:S(2)}, u32[]{:S(2)}) collective-permute-start(f32[768,128]{1,0:T(8,128)S(1)} %multiply_add_fusion.11), channel_id=1, source_target_pairs={{0,16},{8,24},{16,0},{24,8},{1,17},{9,25},{17,1},{25,9},{2,18},{10... | collective-permute-start | bytes 1179656 | tf_op jit(solution)/shard_map/ppermute | solution.py:89
  59.4 15.7 %collective-permute-start.14 = (f32[768,128]{1,0:T(8,128)S(1)}, f32[768,128]{1,0:T(8,128)S(1)}, u32[]{:S(2)}, u32[]{:S(2)}) collective-permute-start(f32[768,128]{1,0:T(8,128)S(1)} %multiply_add_fusion.10), channel_id=1, source_target_pairs={{0,1},{1,0},{2,3},{3,2},{4,5},{5,4},{6,7},{7,6},{8,9},{9,8},{10,11... | collective-permute-start | bytes 1179656 | tf_op jit(solution)/shard_map/ppermute | solution.py:89
  73.7 2.1 %copy-start.3 = (s32[8192]{0:T(1024)S(1)}, s32[8192]{0:T(1024)}, u32[]{:S(2)}) copy-start(s32[8192]{0:T(1024)} %param.5) | copy-start | bytes 98308
  74.6 8.8 %collective-permute-start.19 = (f32[768,128]{1,0:T(8,128)S(1)}, f32[768,128]{1,0:T(8,128)}, u32[]{:S(2)}, u32[]{:S(2)}) collective-permute-start(f32[768,128]{1,0:T(8,128)S(1)} %multiply_add_fusion.9), channel_id=1, source_target_pairs={{0,1},{1,0},{2,3},{3,2},{4,5},{5,4},{6,7},{7,6},{8,9},{9,8},{10,11... | collective-permute-start | bytes 1179656 | tf_op jit(solution)/shard_map/ppermute | solution.py:89
  75.2 10.0 %collective-permute-start.18 = (f32[768,128]{1,0:T(8,128)S(1)}, f32[768,128]{1,0:T(8,128)}, u32[]{:S(2)}, u32[]{:S(2)}) collective-permute-start(f32[768,128]{1,0:T(8,128)S(1)} %multiply_add_fusion.8), channel_id=1, source_target_pairs={{0,16},{8,24},{16,0},{24,8},{1,17},{9,25},{17,1},{25,9},{2,18},{10... | collective-permute-start | bytes 1179656 | tf_op jit(solution)/shard_map/ppermute | solution.py:89
  76.9 14.9 %collective-permute-start.9 = (f32[640,128]{1,0:T(8,128)}, f32[640,128]{1,0:T(8,128)S(1)}, u32[]{:S(2)}, u32[]{:S(2)}) collective-permute-start(f32[640,128]{1,0:T(8,128)} %get-tuple-element.87), channel_id=1, source_target_pairs={{0,4},{1,5},{2,6},{3,7},{4,0},{5,1},{6,2},{7,3},{8,12},{9,13},{10,... | collective-permute-start | bytes 983048 | tf_op jit(solution)/shard_map/ppermute | solution.py:89
  77.3 16.0 %collective-permute-start.8 = (f32[640,128]{1,0:T(8,128)}, f32[640,128]{1,0:T(8,128)S(1)}, u32[]{:S(2)}, u32[]{:S(2)}) collective-permute-start(f32[640,128]{1,0:T(8,128)} %get-tuple-element.85), channel_id=1, source_target_pairs={{0,2},{1,3},{2,0},{3,1},{4,6},{5,7},{6,4},{7,5},{8,10},{9,11},{10,... | collective-permute-start | bytes 983048 | tf_op jit(solution)/shard_map/ppermute | solution.py:89
  97.3 6.5 %collective-permute-start.21 = (f32[256,128]{1,0:T(8,128)S(1)}, f32[256,128]{1,0:T(8,128)S(1)}, u32[]{:S(2)}, u32[]{:S(2)}) collective-permute-start(f32[256,128]{1,0:T(8,128)S(1)} %get-tuple-element.63), channel_id=1, source_target_pairs={{0,2},{1,3},{2,0},{3,1},{4,6},{5,7},{6,4},{7,5},{8,10},{9,11},{10,... | collective-permute-start | bytes 393224 | tf_op jit(solution)/shard_map/ppermute | solution.py:89
  98.3 9.5 %collective-permute-start.20 = (f32[256,128]{1,0:T(8,128)S(1)}, f32[256,128]{1,0:T(8,128)S(1)}, u32[]{:S(2)}, u32[]{:S(2)}) collective-permute-start(f32[256,128]{1,0:T(8,128)S(1)} %get-tuple-element.62), channel_id=1, source_target_pairs={{0,4},{1,5},{2,6},{3,7},{4,0},{5,1},{6,2},{7,3},{8,12},{9,13},{10,... | collective-permute-start | bytes 393224 | tf_op jit(solution)/shard_map/ppermute | solution.py:89
  109.2 20.2 %all-to-all-start = ((f32[32,12,128]{2,1,0:T(8,128)}), f32[32,12,128]{2,1,0:T(8,128)S(1)}, u32[]{:S(2)}, u32[]{:S(2)}) async-start(f32[32,12,128]{2,1,0:T(8,128)} %pad_maximum_fusion), calls=%async_computation | async-start | bytes 524288 | tf_op jit(solution)/shard_map/all_to_all | solution.py:292
  115.0 29.8 %collective-permute-start.24 = (f32[640,128]{1,0:T(8,128)S(1)}, f32[640,128]{1,0:T(8,128)S(1)}, u32[]{:S(2)}, u32[]{:S(2)}) collective-permute-start(f32[640,128]{1,0:T(8,128)S(1)} %get-tuple-element.71.value_ref), channel_id=1, source_target_pairs={{0,4},{1,5},{2,6},{3,7},{4,0},{5,1},{6,2},{7,3},{8,12},{9,13},{10,... | collective-permute-start | bytes 983048 | tf_op jit(solution)/shard_map/ppermute | solution.py:89
  117.7 27.0 %collective-permute-start.25 = (f32[640,128]{1,0:T(8,128)S(1)}, f32[640,128]{1,0:T(8,128)S(1)}, u32[]{:S(2)}, u32[]{:S(2)}) collective-permute-start(f32[640,128]{1,0:T(8,128)S(1)} %get-tuple-element.73.value_ref), channel_id=1, source_target_pairs={{0,2},{1,3},{2,0},{3,1},{4,6},{5,7},{6,4},{7,5},{8,10},{9,11},{10,... | collective-permute-start | bytes 983048 | tf_op jit(solution)/shard_map/ppermute | solution.py:89
  119.2 35.0 %collective-permute-start.22 = (f32[640,128]{1,0:T(8,128)S(1)}, f32[640,128]{1,0:T(8,128)S(1)}, u32[]{:S(2)}, u32[]{:S(2)}) collective-permute-start(f32[640,128]{1,0:T(8,128)S(1)} %get-tuple-element.67.value_ref), channel_id=1, source_target_pairs={{0,4},{1,5},{2,6},{3,7},{4,0},{5,1},{6,2},{7,3},{8,12},{9,13},{10,... | collective-permute-start | bytes 983048 | tf_op jit(solution)/shard_map/ppermute | solution.py:89
  119.7 34.5 %collective-permute-start.23 = (f32[640,128]{1,0:T(8,128)S(1)}, f32[640,128]{1,0:T(8,128)S(1)}, u32[]{:S(2)}, u32[]{:S(2)}) collective-permute-start(f32[640,128]{1,0:T(8,128)S(1)} %get-tuple-element.69.value_ref), channel_id=1, source_target_pairs={{0,2},{1,3},{2,0},{3,1},{4,6},{5,7},{6,4},{7,5},{8,10},{9,11},{10,... | collective-permute-start | bytes 983048 | tf_op jit(solution)/shard_map/ppermute | solution.py:89
  130.1 24.2 %all-to-all-start.1 = ((f32[32,4,128]{2,1,0:T(4,128)}), f32[32,4,128]{2,1,0:T(4,128)S(1)}, u32[]{:S(2)}, u32[]{:S(2)}) async-start(f32[32,4,128]{2,1,0:T(4,128)} %broadcast_in_dim.50), calls=%async_computation.1 | async-start | bytes 131072 | tf_op jit(solution)/shard_map/all_to_all | solution.py:296

commit v6 on v5

--- a/solution.py
+++ b/solution.py
@@ -21,23 +21,16 @@
 
 
 def local_kernel(scale, flips_ref, panel_ref, *refs):
-    *outs, flags, held, arrived = refs
+    *outs, held = refs
     blocks = panel_ref.shape[0] // BLOCK
     width = panel_ref.shape[1]
-    per = BLOCK // flips_ref.shape[1]
-    loads = [pltpu.make_async_copy(flips_ref, flags, arrived.at[blocks])]
+    lanes = flips_ref.shape[1]
+    per = BLOCK // lanes
+    base = signs(BLOCK)
     for b in range(blocks):
-        source = panel_ref.at[pl.ds(b * BLOCK, BLOCK), :]
-        loads.append(pltpu.make_async_copy(source, held.at[b], arrived.at[b]))
-    for load in loads:
-        load.start()
-    base = signs(BLOCK)
-    loads[0].wait()
-    for b in range(blocks):
-        row = jnp.concatenate([flags[b * per + i : b * per + i + 1, :] for i in range(per)], axis=1)
+        row = jnp.concatenate([flips_ref[b * per + i : b * per + i + 1, :] for i in range(per)], axis=1)
         mixer = (base * (1 - 2 * row).astype(jnp.float32)).astype(jnp.bfloat16)
-        loads[b + 1].wait()
-        values = held[b]
+        values = panel_ref[b * BLOCK : (b + 1) * BLOCK, :]
         high = values.astype(jnp.bfloat16)
         rest = values - high.astype(jnp.float32)
         middle = rest.astype(jnp.bfloat16)
@@ -72,14 +65,10 @@
     return pl.pallas_call(
         functools.partial(local_kernel, scale),
         out_shape=[jax.ShapeDtypeStruct((share, width), jnp.float32) for share in shares],
-        in_specs=[pl.BlockSpec(memory_space=pltpu.HBM)] * 2,
+        in_specs=[pl.BlockSpec(memory_space=pltpu.VMEM)] * 2,
         out_specs=[pl.BlockSpec(memory_space=pltpu.VMEM)] * len(shares),
-        scratch_shapes=[
-            pltpu.VMEM((rows // 128, 128), jnp.int32),
-            pltpu.VMEM((rows // BLOCK, BLOCK, width), jnp.float32),
-            pltpu.SemaphoreType.DMA((rows // BLOCK + 1,)),
-        ],
-        compiler_params=pltpu.CompilerParams(vmem_limit_bytes=60 * 2**20),
+        scratch_shapes=[pltpu.VMEM((rows // BLOCK, BLOCK, width), jnp.float32)],
+        compiler_params=pltpu.CompilerParams(vmem_limit_bytes=32 * 2**20),
     )(flips.reshape(rows // 128, 128), panel)
 
 
@@ -162,12 +151,6 @@
         for stage in stages[:-1]:
             value = self.end(launch(value, stage))
         return launch(value, stages[-1])
-
-
-def split(value, parts):
-    units = value.shape[0] // 16
-    cuts = [16 * (units * i // parts) for i in range(parts + 1)]
-    return [value[low:high] for low, high in zip(cuts, cuts[1:])]
 
 
 def index_kernel(rows_here, most, bases_ref, picks_ref, out_ref):
@@ -229,58 +212,41 @@
     me = lax.axis_index(AXES)
     per = picks.shape[0] // devices
     most = -(-per // devices)
-    cuts = [rows_here * cut // 16 for cut in (0, 3, 6, 11, 16)]
+    cuts = [rows_here * cut // 16 for cut in (0, 5, 8, 12, 16)]
 
     c = local_transform(panel, flips, scale, [b - a for a, b in zip(cuts, cuts[1:])])
     chain = Chain()
-    far0, mid1 = launch(c[0], far), launch(c[1], mid)
+    half = cuts[1] // 2
+    far0 = [launch(c[0][:half], far), launch(c[0][half:], far)]
+    far1 = launch(c[1], far)
     core2, core3 = chain.begin(c[2], core), chain.begin(c[3], core)
-    wanted = send_rows(picks, [me ^ bit_of(far), me ^ bit_of(mid), me], rows_here, devices, most)
+    wanted = send_rows(picks, [me], rows_here, devices, most)
     spots = landing(lax.dynamic_slice(picks, (me * per,), (per,)), rows_here, most)
     first2 = chain.begin(chain.end(core2), first)
-    second3 = chain.begin(chain.end(core3), second)
-    mid0 = launch(chain.end(far0), mid)
-    far1 = launch(chain.end(mid1), far)
+    mid3 = launch(chain.end(core3), mid)
+    v0 = [chain.end(far0[0])]
     second2 = chain.begin(chain.end(first2), second)
+    second3 = chain.begin(chain.end(mid3), second)
+    mid2 = launch(chain.end(second2), mid)
+    v0 = jnp.concatenate(v0 + [chain.end(far0[1])], axis=0)
+    core0 = chain.begin(v0, core)
     first3 = chain.begin(chain.end(second3), first)
-    v2 = split(chain.end(second2), 2)
-    far2 = [launch(part, far) for part in v2]
-    v3 = split(chain.end(first3), 2)
-    mid3 = [launch(part, mid) for part in v3]
-    core0 = chain.begin(chain.end(mid0), core)
+    second0 = chain.begin(chain.end(core0), second)
+    far2 = launch(chain.end(mid2), far)
+    far3 = launch(chain.end(first3), far)
     core1 = chain.begin(chain.end(far1), core)
-    first0 = chain.begin(chain.end(core0), first)
-    second1 = chain.begin(chain.end(core1), second)
-    v2, v3 = [chain.end(far2[0])], [chain.end(mid3[0])]
-    second0 = chain.begin(chain.end(first0), second)
+    first0 = chain.begin(chain.end(second0), first)
+    mid1 = launch(chain.end(core1), mid)
+    mid0 = launch(chain.end(first0), mid)
+    second1 = chain.begin(chain.end(mid1), second)
+    v2 = chain.end(far2)
     first1 = chain.begin(chain.end(second1), first)
-    v0, v1 = chain.end(second0), chain.end(first1)
-    v2, v3 = v2 + [chain.end(far2[1])], v3 + [chain.end(mid3[1])]
-    v2, v3 = jnp.concatenate(v2, axis=0), jnp.concatenate(v3, axis=0)
-
-    held = jnp.concatenate([v0, v1, v2, v3], axis=0)
-    taken = jnp.take(held, wanted, axis=0, mode="clip")
-    count = devices * most
-    rows, filled = wanted[2 * count :], wanted[2 * count :] >= 0
-    to_far, to_mid, own = lax.optimization_barrier(
-        (taken[:count], taken[count : 2 * count], taken[2 * count :])
-    )
-    give_mid, give_far = launch(to_mid, mid), launch(to_far, far)
-    whole = store_rows([v0, v1], rows_here)
-    parts2, parts3 = split(v2, 2), split(v3, 2)
-    ends = []
-
-    def more(step, gate):
-        ends.append(launch(after(parts2[step], gate), mid))
-        ends.append(launch(after(parts3[step], gate), far))
-
-    more(0, to_far)
-    got_mid = chain.end((give_mid[0], own, mid))
-    got_far = chain.end((give_far[0], own, far))
-    place = rows[:, None]
-    chosen = jnp.where(
-        place >= cuts[3], got_far, jnp.where(place >= cuts[2], got_mid, own)
-    )
+    v0, v1 = chain.end(mid0), chain.end(first1)
+    whole = store_rows([v0, v1, v2], rows_here)
+    whole = finish(whole, far3, cuts[3], chain.last, wanted, spots)
+
+    filled = wanted >= 0
+    chosen = jnp.take(whole, wanted, axis=0, mode="clip")
     kept = jnp.where(filled[:, None], chosen, 0.0)
     part = lax.dot_general(
         kept, kept, (((0,), (0,)), ((), ())),
@@ -290,16 +256,10 @@
         [chosen.reshape(devices, most, width), part.reshape(devices, -1, width)], axis=1
     )
     landed = lax.all_to_all(both, AXES, 0, 0, tiled=True)
-    more(1, both)
     mine = jnp.sum(landed[:, most:], axis=0) / float(picks.shape[0])
     shared = jnp.broadcast_to(mine[None], (devices,) + mine.shape)
     gram = lax.all_to_all(shared, AXES, 0, 0, tiled=True).reshape(width, width)
     sketch = jnp.take(landed[:, :most].reshape(devices * most, width), spots, axis=0, mode="clip")
-    half = parts2[0].shape[0]
-    whole = finish(whole, ends[0], cuts[2], chain.last, landed)
-    whole = finish(whole, ends[1], cuts[3], chain.last, landed)
-    whole = finish(whole, ends[2], cuts[2] + half, gram, sketch)
-    whole = finish(whole, ends[3], cuts[3] + half, gram, sketch)
     return (whole, sketch, gram)
 
 

time: 157 us -> 155 us (0.987)
  waiting for transfers between devices: 82.3 us -> 93.4 us
  starting transfers between devices: 42.4 us -> 34.3 us
  Pallas kernels: 11.7 us -> 4.23 us
  other arithmetic: 10.9 us -> 12.5 us
    ppermute x26 -> x21, waiting for transfers between devices: 66.4 us -> 76.8 us  [launch(): return (lax.ppermute(value, axis, pairs), value, stage)]
    add x15 -> x19, other arithmetic: 2.87 us -> 10.2 us  [end(): self.last = partner + sign_of(stage) * value]
    pallas_call x1, Pallas kernels: 6.83 us -> 1.94 us  [local_transform(): pl.pallas_call(functools.partial(local_kernel, scale), out_shape=[jax.Sha...]
    unnamed x3 -> x0, other arithmetic: 4.36 us -> none
    ppermute x26 -> x21, starting transfers between devices: 33.1 us -> 28.9 us  [launch(): return (lax.ppermute(value, axis, pairs), value, stage)]
    pallas_call x4 -> x1, Pallas kernels: 3.07 us -> 0.86 us  [finish(): pl.pallas_call(functools.partial(finish_kernel, at), out_shape=jax.ShapeD...]
    all_to_all x1, starting transfers between devices: 4.65 us -> 2.57 us  [on_device(): gram = lax.all_to_all(shared, AXES, 0, 0, tiled=True).reshape(width, width)]
    all_to_all x1, starting transfers between devices: 4.61 us -> 2.86 us  [on_device(): landed = lax.all_to_all(both, AXES, 0, 0, tiled=True)]
  transfers between devices with their start and end apart: 28 -> 23, of which waited for: 15 -> 12; matrix products, arithmetic and copies ran while one was open for 8% -> 9% of each run, Pallas kernels for 2% -> 1%
where the time goes in v6:
time: 155 us; the launch traced here: 154 us
  waiting for transfers between devices  93.4 us (60%)
  starting transfers between devices  34.3 us (22%)
  other arithmetic  12.5 us (8%)
  local copies, waits for them, and re-layouts  8.18 us (5%)
  Pallas kernels  4.23 us (3%)
    ppermute x21, waiting for transfers between devices, launch(): return (lax.ppermute(value, axis, pairs), value, stage)  76.8 us
    ppermute x21, starting transfers between devices, launch(): return (lax.ppermute(value, axis, pairs), value, stage)  28.9 us
    all_to_all x1, waiting for transfers between devices, on_device(): landed = lax.all_to_all(both, AXES, 0, 0, tiled=True)  10.6 us
    add x19, other arithmetic, end(): self.last = partner + sign_of(stage) * value  10.2 us
    all_to_all x1, waiting for transfers between devices, on_device(): gram = lax.all_to_all(shared, AXES, 0, 0, tiled=True).reshape(width, width)  5.91 us
  transfers between devices with their start and end apart: 23, of which 12 were waited for; matrix products, arithmetic and copies ran while one was open for 9% of the time, Pallas kernels for 1%

profile of v6, /device:TPU:0, one launch (start us, length us, event | category | flops | bytes accessed | tf_op | source)
XLA Modules:
  0.0 154.0 jit_solution(3685071338843717591)
XLA Ops:
  0.6 1.6 %copy-done = f32[4096,128]{1,0:T(8,128)S(1)} copy-done((f32[4096,128]{1,0:T(8,128)S(1)}, f32[4096,128]{1,0:T(8,128)}, u32[]{:S(2)}) %copy-start) | copy-done | bytes 2097176
  2.9 1.9 %shard_map.58 = (f32[1280,128]{1,0:T(8,128)S(1)}, f32[768,128]{1,0:T(8,128)S(1)}, f32[1024,128]{1,0:T(8,128)S(1)}, f32[1024,128]{1,0:T(8,128)S(1)}) custom-call(s32[32,128]{1,0:T(8,128)S(1)} %bitcast.8, f32[4096,128]{1,0:T(8,128)S(1)} %copy-done), custom_call_target="tpu_custom_call" | custom-call | tf_op jit(solution)/shard_map/pallas_call | solution.py:65
  6.2 4.0 %collective-permute-start.4 = (f32[640,128]{1,0:T(8,128)}, f32[640,128]{1,0:T(8,128)}, u32[]{:S(2)}, u32[]{:S(2)}) collective-permute-start(f32[640,128]{1,0:T(8,128)} %slice.12), channel_id=1, source_target_pairs={{0,4},{1,5},{2,6},{3,7},{4,0},{5,1},{6,2},{7,3},{8,12},{9,13},{10,... | collective-permute-start | bytes 983048 | tf_op jit(solution)/shard_map/ppermute | solution.py:78
  11.4 1.6 %collective-permute-start.3 = (f32[1024,128]{1,0:T(8,128)S(1)}, f32[1024,128]{1,0:T(8,128)}, u32[]{:S(2)}, u32[]{:S(2)}) collective-permute-start(f32[1024,128]{1,0:T(8,128)S(1)} %multiply_add_fusion.12), channel_id=1, source_target_pairs={{0,16},{8,24},{16,0},{24,8},{1,17},{9,25},{17,1},{25,9},{2,18},{10... | collective-permute-start | bytes 1572872 | tf_op jit(solution)/shard_map/ppermute | solution.py:78
  13.0 1.6 %collective-permute-start.2 = (f32[1024,128]{1,0:T(8,128)S(1)}, f32[1024,128]{1,0:T(8,128)}, u32[]{:S(2)}, u32[]{:S(2)}) collective-permute-start(f32[1024,128]{1,0:T(8,128)S(1)} %multiply_add_fusion.11), channel_id=1, source_target_pairs={{0,2},{1,3},{2,0},{3,1},{4,6},{5,7},{6,4},{7,5},{8,10},{9,11},{10,... | collective-permute-start | bytes 1572872 | tf_op jit(solution)/shard_map/ppermute | solution.py:78
  14.6 11.0 %collective-permute-done.4 = f32[640,128]{1,0:T(8,128)} collective-permute-done((f32[640,128]{1,0:T(8,128)}, f32[640,128]{1,0:T(8,128)}, u32[]{:S(2)}, u32[]{:S(2)}) %collective-permute-start.4) | collective-permute-done | bytes 327712 | tf_op jit(solution)/shard_map/ppermute | solution.py:78
  26.7 1.1 multiply_add_fusion.10
  27.8 1.6 %collective-permute-start.7 = (f32[1024,128]{1,0:T(8,128)S(1)}, f32[1024,128]{1,0:T(8,128)}, u32[]{:S(2)}, u32[]{:S(2)}) collective-permute-start(f32[1024,128]{1,0:T(8,128)S(1)} %multiply_add_fusion.10), channel_id=1, source_target_pairs={{0,1},{1,0},{2,3},{3,2},{4,5},{5,4},{6,7},{7,6},{8,9},{9,8},{10,11... | collective-permute-start | bytes 1572872 | tf_op jit(solution)/shard_map/ppermute | solution.py:78
  29.4 4.6 %collective-permute-done.2 = f32[1024,128]{1,0:T(8,128)} collective-permute-done((f32[1024,128]{1,0:T(8,128)S(1)}, f32[1024,128]{1,0:T(8,128)}, u32[]{:S(2)}, u32[]{:S(2)}) %collective-permute-start.2) | collective-permute-done | bytes 524320 | tf_op jit(solution)/shard_map/ppermute | solution.py:78
  35.1 1.4 collective-permute-start.5
  36.5 6.3 %collective-permute-done.7 = f32[1024,128]{1,0:T(8,128)} collective-permute-done((f32[1024,128]{1,0:T(8,128)S(1)}, f32[1024,128]{1,0:T(8,128)}, u32[]{:S(2)}, u32[]{:S(2)}) %collective-permute-start.7) | collective-permute-done | bytes 524320 | tf_op jit(solution)/shard_map/ppermute | solution.py:78
  43.9 2.0 %collective-permute-done.6 = f32[640,128]{1,0:T(8,128)S(1)} collective-permute-done((f32[640,128]{1,0:T(8,128)S(1)}, f32[640,128]{1,0:T(8,128)S(1)}, u32[]{:S(2)}, u32[]{:S(2)}) %collective-permute-start.6) | collective-permute-done | bytes 327712 | tf_op jit(solution)/shard_map/ppermute | solution.py:78
  46.2 2.0 %collective-permute-start.9 = (f32[1024,128]{1,0:T(8,128)S(1)}, f32[1024,128]{1,0:T(8,128)S(1)}, u32[]{:S(2)}, u32[]{:S(2)}) collective-permute-start(f32[1024,128]{1,0:T(8,128)S(1)} %multiply_add_fusion.8), channel_id=1, source_target_pairs={{0,2},{1,3},{2,0},{3,1},{4,6},{5,7},{6,4},{7,5},{8,10},{9,11},{10,... | collective-permute-start | bytes 1572872 | tf_op jit(solution)/shard_map/ppermute | solution.py:78
  48.2 4.3 %collective-permute-done.5 = f32[1024,128]{1,0:T(8,128)} collective-permute-done((f32[1024,128]{1,0:T(8,128)S(1)}, f32[1024,128]{1,0:T(8,128)}, u32[]{:S(2)}, u32[]{:S(2)}) %collective-permute-start.5) | collective-permute-done | bytes 524320 | tf_op jit(solution)/shard_map/ppermute | solution.py:78
  53.6 1.3 collective-permute-start.8
  55.0 1.6 %collective-permute-start.14 = (f32[1280,128]{1,0:T(8,128)S(1)}, f32[1280,128]{1,0:T(8,128)S(1)}, u32[]{:S(2)}, u32[]{:S(2)}) collective-permute-start(f32[1280,128]{1,0:T(8,128)S(1)} %multiply_add_fusion.3), channel_id=1, source_target_pairs={{0,1},{1,0},{2,3},{3,2},{4,5},{5,4},{6,7},{7,6},{8,9},{9,8},{10,11... | collective-permute-start | bytes 1966088 | tf_op jit(solution)/shard_map/ppermute | solution.py:78
  56.6 12.3 %collective-permute-done.9 = f32[1024,128]{1,0:T(8,128)S(1)} collective-permute-done((f32[1024,128]{1,0:T(8,128)S(1)}, f32[1024,128]{1,0:T(8,128)S(1)}, u32[]{:S(2)}, u32[]{:S(2)}) %collective-permute-start.9) | collective-permute-done | bytes 524320 | tf_op jit(solution)/shard_map/ppermute | solution.py:78
  70.3 1.6 %collective-permute-start.16 = (f32[1280,128]{1,0:T(8,128)S(1)}, f32[1280,128]{1,0:T(8,128)S(1)}, u32[]{:S(2)}, u32[]{:S(2)}) collective-permute-start(f32[1280,128]{1,0:T(8,128)S(1)} %multiply_add_fusion.2), channel_id=1, source_target_pairs={{0,16},{8,24},{16,0},{24,8},{1,17},{9,25},{17,1},{25,9},{2,18},{10... | collective-permute-start | bytes 1966088 | tf_op jit(solution)/shard_map/ppermute | solution.py:78
  73.8 3.9 %collective-permute-start.15 = (f32[768,128]{1,0:T(8,128)S(1)}, f32[768,128]{1,0:T(8,128)S(1)}, u32[]{:S(2)}, u32[]{:S(2)}) collective-permute-start(f32[768,128]{1,0:T(8,128)S(1)} %multiply_add_fusion.16), channel_id=1, source_target_pairs={{0,2},{1,3},{2,0},{3,1},{4,6},{5,7},{6,4},{7,5},{8,10},{9,11},{10,... | collective-permute-start | bytes 1179656 | tf_op jit(solution)/shard_map/ppermute | solution.py:78
  77.8 9.7 %collective-permute-done.16 = f32[1280,128]{1,0:T(8,128)S(1)} collective-permute-done((f32[1280,128]{1,0:T(8,128)S(1)}, f32[1280,128]{1,0:T(8,128)S(1)}, u32[]{:S(2)}, u32[]{:S(2)}) %collective-permute-start.16) | collective-permute-done | bytes 655392 | tf_op jit(solution)/shard_map/ppermute | solution.py:78
  87.8 5.7 %collective-permute-done.15 = f32[768,128]{1,0:T(8,128)S(1)} collective-permute-done((f32[768,128]{1,0:T(8,128)S(1)}, f32[768,128]{1,0:T(8,128)S(1)}, u32[]{:S(2)}, u32[]{:S(2)}) %collective-permute-start.15) | collective-permute-done | bytes 393248 | tf_op jit(solution)/shard_map/ppermute | solution.py:78
  93.6 1.5 collective-permute-start.17
  95.4 4.5 %collective-permute-start.11 = (f32[1024,128]{1,0:T(8,128)S(1)}, f32[1024,128]{1,0:T(8,128)S(1)}, u32[]{:S(2)}, u32[]{:S(2)}) collective-permute-start(f32[1024,128]{1,0:T(8,128)S(1)} %multiply_add_fusion.5.value_ref), channel_id=1, source_target_pairs={{0,4},{1,5},{2,6},{3,7},{4,0},{5,1},{6,2},{7,3},{8,12},{9,13},{10,... | collective-permute-start | bytes 1572872 | tf_op jit(solution)/shard_map/ppermute | solution.py:78
  101.0 2.4 %collective-permute-done.17 = f32[768,128]{1,0:T(8,128)} collective-permute-done((f32[768,128]{1,0:T(8,128)S(1)}, f32[768,128]{1,0:T(8,128)}, u32[]{:S(2)}, u32[]{:S(2)}) %collective-permute-start.17) | collective-permute-done | bytes 393248 | tf_op jit(solution)/shard_map/ppermute | solution.py:78
  105.1 18.4 %collective-permute-done.20 = f32[1280,128]{1,0:T(8,128)S(1)} collective-permute-done((f32[1280,128]{1,0:T(8,128)S(1)}, f32[1280,128]{1,0:T(8,128)S(1)}, u32[]{:S(2)}, u32[]{:S(2)}) %collective-permute-start.20) | collective-permute-done | bytes 655392 | tf_op jit(solution)/shard_map/ppermute | solution.py:78
  123.7 1.2 shard_map.59.whole_ref
  125.7 2.3 %gather_fusion = f32[256,128]{1,0:T(8,128)S(1)} fusion(f32[4096,128]{1,0:T(8,128)} %shard_map.60, s32[1024]{0:T(1024)S(1)} %pad_clamp_fusion.1), kind=kCustom, calls=%fused_computation | custom fusion | bytes 263168 | tf_op jit(solution)/shard_map/jit(_take)/gather | solution.py:249
  129.3 2.9 %all-to-all-start = ((f32[32,12,128]{2,1,0:T(8,128)}), f32[32,12,128]{2,1,0:T(8,128)S(1)}, u32[]{:S(2)}, u32[]{:S(2)}) async-start(f32[32,12,128]{2,1,0:T(8,128)} %pad_maximum_fusion.1), calls=%async_computation | async-start | bytes 524288 | tf_op jit(solution)/shard_map/all_to_all | solution.py:258
  132.2 10.6 %all-to-all-done = f32[32,12,128]{2,1,0:T(8,128)S(1)} async-done(((f32[32,12,128]{2,1,0:T(8,128)}), f32[32,12,128]{2,1,0:T(8,128)S(1)}, u32[]{:S(2)}, u32[]{:S(2)}) %all-to-all-start) | async-done | bytes 196640 | tf_op jit(solution)/shard_map/all_to_all | solution.py:258
  143.5 2.6 %all-to-all-start.1 = ((f32[32,4,128]{2,1,0:T(4,128)}), f32[32,4,128]{2,1,0:T(4,128)S(1)}, u32[]{:S(2)}, u32[]{:S(2)}) async-start(f32[32,4,128]{2,1,0:T(4,128)} %broadcast_in_dim.35), calls=%async_computation.1 | async-start | bytes 131072 | tf_op jit(solution)/shard_map/all_to_all | solution.py:261
  146.1 1.3 gather_fusion.1
  147.4 5.9 %all-to-all-done.1 = f32[32,4,128]{2,1,0:T(4,128)S(1)} async-done(((f32[32,4,128]{2,1,0:T(4,128)}), f32[32,4,128]{2,1,0:T(4,128)S(1)}, u32[]{:S(2)}, u32[]{:S(2)}) %all-to-all-start.1) | async-done | bytes 65568 | tf_op jit(solution)/shard_map/all_to_all | solution.py:261
  (64 shorter events, 18.2 us)
Async XLA Ops:
  0.6 1.6 %copy-start = (f32[4096,128]{1,0:T(8,128)S(1)}, f32[4096,128]{1,0:T(8,128)}, u32[]{:S(2)}) copy-start(f32[4096,128]{1,0:T(8,128)} %panel_ref.1) | copy-start | bytes 6291460
  2.2 0.7 copy-start.1
  4.9 5.4 %collective-permute-start.1 = (f32[1024,128]{1,0:T(8,128)S(1)}, f32[1024,128]{1,0:T(8,128)}, u32[]{:S(2)}, u32[]{:S(2)}) collective-permute-start(f32[1024,128]{1,0:T(8,128)S(1)} %get-tuple-element.28), channel_id=1, source_target_pairs={{0,8},{8,0},{16,24},{24,16},{1,9},{9,1},{17,25},{25,17},{2,10},{10... | collective-permute-start | bytes 1572872 | tf_op jit(solution)/shard_map/ppermute | solution.py:78
  5.4 7.5 %collective-permute-start = (f32[1024,128]{1,0:T(8,128)S(1)}, f32[1024,128]{1,0:T(8,128)S(1)}, u32[]{:S(2)}, u32[]{:S(2)}) collective-permute-start(f32[1024,128]{1,0:T(8,128)S(1)} %get-tuple-element.27), channel_id=1, source_target_pairs={{0,8},{8,0},{16,24},{24,16},{1,9},{9,1},{17,25},{25,17},{2,10},{10... | collective-permute-start | bytes 1572872 | tf_op jit(solution)/shard_map/ppermute | solution.py:78
  6.2 19.4 %collective-permute-start.4 = (f32[640,128]{1,0:T(8,128)}, f32[640,128]{1,0:T(8,128)}, u32[]{:S(2)}, u32[]{:S(2)}) collective-permute-start(f32[640,128]{1,0:T(8,128)} %slice.12), channel_id=1, source_target_pairs={{0,4},{1,5},{2,6},{3,7},{4,0},{5,1},{6,2},{7,3},{8,12},{9,13},{10,... | collective-permute-start | bytes 983048 | tf_op jit(solution)/shard_map/ppermute | solution.py:78
  11.4 15.3 %collective-permute-start.3 = (f32[1024,128]{1,0:T(8,128)S(1)}, f32[1024,128]{1,0:T(8,128)}, u32[]{:S(2)}, u32[]{:S(2)}) collective-permute-start(f32[1024,128]{1,0:T(8,128)S(1)} %multiply_add_fusion.12), channel_id=1, source_target_pairs={{0,16},{8,24},{16,0},{24,8},{1,17},{9,25},{17,1},{25,9},{2,18},{10... | collective-permute-start | bytes 1572872 | tf_op jit(solution)/shard_map/ppermute | solution.py:78
  13.0 21.1 %collective-permute-start.2 = (f32[1024,128]{1,0:T(8,128)S(1)}, f32[1024,128]{1,0:T(8,128)}, u32[]{:S(2)}, u32[]{:S(2)}) collective-permute-start(f32[1024,128]{1,0:T(8,128)S(1)} %multiply_add_fusion.11), channel_id=1, source_target_pairs={{0,2},{1,3},{2,0},{3,1},{4,6},{5,7},{6,4},{7,5},{8,10},{9,11},{10,... | collective-permute-start | bytes 1572872 | tf_op jit(solution)/shard_map/ppermute | solution.py:78
  27.8 15.0 %collective-permute-start.7 = (f32[1024,128]{1,0:T(8,128)S(1)}, f32[1024,128]{1,0:T(8,128)}, u32[]{:S(2)}, u32[]{:S(2)}) collective-permute-start(f32[1024,128]{1,0:T(8,128)S(1)} %multiply_add_fusion.10), channel_id=1, source_target_pairs={{0,1},{1,0},{2,3},{3,2},{4,5},{5,4},{6,7},{7,6},{8,9},{9,8},{10,11... | collective-permute-start | bytes 1572872 | tf_op jit(solution)/shard_map/ppermute | solution.py:78
  29.4 16.5 %collective-permute-start.6 = (f32[640,128]{1,0:T(8,128)S(1)}, f32[640,128]{1,0:T(8,128)S(1)}, u32[]{:S(2)}, u32[]{:S(2)}) collective-permute-start(f32[640,128]{1,0:T(8,128)S(1)} %get-tuple-element.51), channel_id=1, source_target_pairs={{0,4},{1,5},{2,6},{3,7},{4,0},{5,1},{6,2},{7,3},{8,12},{9,13},{10,... | collective-permute-start | bytes 983048 | tf_op jit(solution)/shard_map/ppermute | solution.py:78
  35.1 17.4 %collective-permute-start.5 = (f32[1024,128]{1,0:T(8,128)S(1)}, f32[1024,128]{1,0:T(8,128)}, u32[]{:S(2)}, u32[]{:S(2)}) collective-permute-start(f32[1024,128]{1,0:T(8,128)S(1)} %multiply_add_fusion.9), channel_id=1, source_target_pairs={{0,1},{1,0},{2,3},{3,2},{4,5},{5,4},{6,7},{7,6},{8,9},{9,8},{10,11... | collective-permute-start | bytes 1572872 | tf_op jit(solution)/shard_map/ppermute | solution.py:78
  46.0 8.9 %collective-permute-start.10 = (f32[1280,128]{1,0:T(8,128)S(1)}, f32[1280,128]{1,0:T(8,128)S(1)}, u32[]{:S(2)}, u32[]{:S(2)}) collective-permute-start(f32[1280,128]{1,0:T(8,128)S(1)} %pad_maximum_fusion), channel_id=1, source_target_pairs={{0,8},{8,0},{16,24},{24,16},{1,9},{9,1},{17,25},{25,17},{2,10},{10... | collective-permute-start | bytes 1966088 | tf_op jit(solution)/shard_map/ppermute | solution.py:78
  46.1 23.0 %collective-permute-start.12 = (f32[768,128]{1,0:T(8,128)S(1)}, f32[768,128]{1,0:T(8,128)}, u32[]{:S(2)}, u32[]{:S(2)}) collective-permute-start(f32[768,128]{1,0:T(8,128)S(1)} %get-tuple-element.40), channel_id=1, source_target_pairs={{0,4},{1,5},{2,6},{3,7},{4,0},{5,1},{6,2},{7,3},{8,12},{9,13},{10,... | collective-permute-start | bytes 1179656 | tf_op jit(solution)/shard_map/ppermute | solution.py:78
  46.2 22.7 %collective-permute-start.9 = (f32[1024,128]{1,0:T(8,128)S(1)}, f32[1024,128]{1,0:T(8,128)S(1)}, u32[]{:S(2)}, u32[]{:S(2)}) collective-permute-start(f32[1024,128]{1,0:T(8,128)S(1)} %multiply_add_fusion.8), channel_id=1, source_target_pairs={{0,2},{1,3},{2,0},{3,1},{4,6},{5,7},{6,4},{7,5},{8,10},{9,11},{10,... | collective-permute-start | bytes 1572872 | tf_op jit(solution)/shard_map/ppermute | solution.py:78
  53.6 15.3 %collective-permute-start.8 = (f32[1024,128]{1,0:T(8,128)S(1)}, f32[1024,128]{1,0:T(8,128)S(1)}, u32[]{:S(2)}, u32[]{:S(2)}) collective-permute-start(f32[1024,128]{1,0:T(8,128)S(1)} %multiply_add_fusion.7), channel_id=1, source_target_pairs={{0,16},{8,24},{16,0},{24,8},{1,17},{9,25},{17,1},{25,9},{2,18},{10... | collective-permute-start | bytes 1572872 | tf_op jit(solution)/shard_map/ppermute | solution.py:78
  55.0 15.2 %collective-permute-start.14 = (f32[1280,128]{1,0:T(8,128)S(1)}, f32[1280,128]{1,0:T(8,128)S(1)}, u32[]{:S(2)}, u32[]{:S(2)}) collective-permute-start(f32[1280,128]{1,0:T(8,128)S(1)} %multiply_add_fusion.3), channel_id=1, source_target_pairs={{0,1},{1,0},{2,3},{3,2},{4,5},{5,4},{6,7},{7,6},{8,9},{9,8},{10,11... | collective-permute-start | bytes 1966088 | tf_op jit(solution)/shard_map/ppermute | solution.py:78
  69.0 2.9 %copy-start.2 = (s32[8192]{0:T(1024)S(1)}, s32[8192]{0:T(1024)}, u32[]{:S(2)}) copy-start(s32[8192]{0:T(1024)} %param.5) | copy-start | bytes 98308
  70.1 2.7 %collective-permute-start.13 = (f32[768,128]{1,0:T(8,128)S(1)}, f32[768,128]{1,0:T(8,128)}, u32[]{:S(2)}, u32[]{:S(2)}) collective-permute-start(f32[768,128]{1,0:T(8,128)S(1)} %multiply_add_fusion.17), channel_id=1, source_target_pairs={{0,8},{8,0},{16,24},{24,16},{1,9},{9,1},{17,25},{25,17},{2,10},{10... | collective-permute-start | bytes 1179656 | tf_op jit(solution)/shard_map/ppermute | solution.py:78
  70.3 17.2 %collective-permute-start.16 = (f32[1280,128]{1,0:T(8,128)S(1)}, f32[1280,128]{1,0:T(8,128)S(1)}, u32[]{:S(2)}, u32[]{:S(2)}) collective-permute-start(f32[1280,128]{1,0:T(8,128)S(1)} %multiply_add_fusion.2), channel_id=1, source_target_pairs={{0,16},{8,24},{16,0},{24,8},{1,17},{9,25},{17,1},{25,9},{2,18},{10... | collective-permute-start | bytes 1966088 | tf_op jit(solution)/shard_map/ppermute | solution.py:78
  72.4 27.6 %collective-permute-start.18 = (f32[1024,128]{1,0:T(8,128)S(1)}, f32[1024,128]{1,0:T(8,128)}, u32[]{:S(2)}, u32[]{:S(2)}) collective-permute-start(f32[1024,128]{1,0:T(8,128)S(1)} %multiply_add_fusion.6), channel_id=1, source_target_pairs={{0,4},{1,5},{2,6},{3,7},{4,0},{5,1},{6,2},{7,3},{8,12},{9,13},{10,... | collective-permute-start | bytes 1572872 | tf_op jit(solution)/shard_map/ppermute | solution.py:78
  73.8 19.7 %collective-permute-start.15 = (f32[768,128]{1,0:T(8,128)S(1)}, f32[768,128]{1,0:T(8,128)S(1)}, u32[]{:S(2)}, u32[]{:S(2)}) collective-permute-start(f32[768,128]{1,0:T(8,128)S(1)} %multiply_add_fusion.16), channel_id=1, source_target_pairs={{0,2},{1,3},{2,0},{3,1},{4,6},{5,7},{6,4},{7,5},{8,10},{9,11},{10,... | collective-permute-start | bytes 1179656 | tf_op jit(solution)/shard_map/ppermute | solution.py:78
  87.5 36.0 %collective-permute-start.20 = (f32[1280,128]{1,0:T(8,128)S(1)}, f32[1280,128]{1,0:T(8,128)S(1)}, u32[]{:S(2)}, u32[]{:S(2)}) collective-permute-start(f32[1280,128]{1,0:T(8,128)S(1)} %multiply_add_fusion.1), channel_id=1, source_target_pairs={{0,2},{1,3},{2,0},{3,1},{4,6},{5,7},{6,4},{7,5},{8,10},{9,11},{10,... | collective-permute-start | bytes 1966088 | tf_op jit(solution)/shard_map/ppermute | solution.py:78
  93.6 9.8 %collective-permute-start.17 = (f32[768,128]{1,0:T(8,128)S(1)}, f32[768,128]{1,0:T(8,128)}, u32[]{:S(2)}, u32[]{:S(2)}) collective-permute-start(f32[768,128]{1,0:T(8,128)S(1)} %multiply_add_fusion.15), channel_id=1, source_target_pairs={{0,1},{1,0},{2,3},{3,2},{4,5},{5,4},{6,7},{7,6},{8,9},{9,8},{10,11... | collective-permute-start | bytes 1179656 | tf_op jit(solution)/shard_map/ppermute | solution.py:78
  95.4 29.5 %collective-permute-start.11 = (f32[1024,128]{1,0:T(8,128)S(1)}, f32[1024,128]{1,0:T(8,128)S(1)}, u32[]{:S(2)}, u32[]{:S(2)}) collective-permute-start(f32[1024,128]{1,0:T(8,128)S(1)} %multiply_add_fusion.5.value_ref), channel_id=1, source_target_pairs={{0,4},{1,5},{2,6},{3,7},{4,0},{5,1},{6,2},{7,3},{8,12},{9,13},{10,... | collective-permute-start | bytes 1572872 | tf_op jit(solution)/shard_map/ppermute | solution.py:78
  104.5 19.1 %collective-permute-start.19 = (f32[768,128]{1,0:T(8,128)S(1)}, f32[768,128]{1,0:T(8,128)S(1)}, u32[]{:S(2)}, u32[]{:S(2)}) collective-permute-start(f32[768,128]{1,0:T(8,128)S(1)} %multiply_add_fusion.14), channel_id=1, source_target_pairs={{0,16},{8,24},{16,0},{24,8},{1,17},{9,25},{17,1},{25,9},{2,18},{10... | collective-permute-start | bytes 1179656 | tf_op jit(solution)/shard_map/ppermute | solution.py:78
  129.3 13.5 %all-to-all-start = ((f32[32,12,128]{2,1,0:T(8,128)}), f32[32,12,128]{2,1,0:T(8,128)S(1)}, u32[]{:S(2)}, u32[]{:S(2)}) async-start(f32[32,12,128]{2,1,0:T(8,128)} %pad_maximum_fusion.1), calls=%async_computation | async-start | bytes 524288 | tf_op jit(solution)/shard_map/all_to_all | solution.py:258
  143.5 9.9 %all-to-all-start.1 = ((f32[32,4,128]{2,1,0:T(4,128)}), f32[32,4,128]{2,1,0:T(4,128)S(1)}, u32[]{:S(2)}, u32[]{:S(2)}) async-start(f32[32,4,128]{2,1,0:T(4,128)} %broadcast_in_dim.35), calls=%async_computation.1 | async-start | bytes 131072 | tf_op jit(solution)/shard_map/all_to_all | solution.py:261

commit v7 on v6

--- a/solution.py
+++ b/solution.py
@@ -83,58 +83,38 @@
     return (1 - 2 * (lax.axis_index(axis) >> level & 1)).astype(jnp.float32)
 
 
-def bit_of(stage):
-    axis, level = stage
-    return 2**level * (lax.axis_size("wide") if axis == "narrow" else 1)
-
-
-def store_kernel(*refs):
-    *values, out_ref, sent = refs
-    copies, at = [], 0
-    for i, value in enumerate(values):
-        rows = value.shape[0]
-        copies.append(pltpu.make_async_copy(value, out_ref.at[pl.ds(at, rows), :], sent.at[i]))
-        at += rows
-    for copy in copies:
-        copy.start()
-    for copy in copies:
-        copy.wait()
-
-
-def store_rows(values, rows):
-    return pl.pallas_call(
-        store_kernel,
-        out_shape=jax.ShapeDtypeStruct((rows, values[0].shape[1]), jnp.float32),
-        in_specs=[pl.BlockSpec(memory_space=pltpu.VMEM)] * len(values),
-        out_specs=pl.BlockSpec(memory_space=pl.ANY),
-        scratch_shapes=[pltpu.SemaphoreType.DMA((len(values),))],
-        compiler_params=pltpu.CompilerParams(vmem_limit_bytes=8 * 2**20),
-    )(*values)
-
-
-def finish_kernel(at, sign_ref, partner_ref, value_ref, whole_ref, out_ref, held, sent):
-    del whole_ref
-    held[...] = partner_ref[...] + sign_ref[0] * value_ref[...]
-    rows = held.shape[0]
-    copy = pltpu.make_async_copy(held, out_ref.at[pl.ds(at, rows), :], sent)
+def store_kernel(at, *refs):
+    value_ref, out_ref, sent = refs[0], refs[-2], refs[-1]
+    rows = value_ref.shape[0]
+    copy = pltpu.make_async_copy(value_ref, out_ref.at[pl.ds(at, rows), :], sent)
     copy.start()
     copy.wait()
 
 
-def finish(whole, sent, at, *others):
-    partner, value, stage = sent
-    partner = after(partner, others)
+def store(whole, value, at, rows):
+    operands = [value] if whole is None else [value, whole]
     return pl.pallas_call(
-        functools.partial(finish_kernel, at),
-        out_shape=jax.ShapeDtypeStruct(whole.shape, jnp.float32),
-        in_specs=[pl.BlockSpec(memory_space=pltpu.SMEM)]
-        + [pl.BlockSpec(memory_space=pltpu.VMEM)] * 2
-        + [pl.BlockSpec(memory_space=pl.ANY)],
+        functools.partial(store_kernel, at),
+        out_shape=jax.ShapeDtypeStruct((rows, value.shape[1]), jnp.float32),
+        in_specs=[pl.BlockSpec(memory_space=pl.ANY)] * len(operands),
         out_specs=pl.BlockSpec(memory_space=pl.ANY),
-        scratch_shapes=[pltpu.VMEM(value.shape, jnp.float32), pltpu.SemaphoreType.DMA],
-        input_output_aliases={3: 0},
-        compiler_params=pltpu.CompilerParams(vmem_limit_bytes=8 * 2**20),
-    )(sign_of(stage).reshape(1), partner, value, whole)
+        scratch_shapes=[pltpu.SemaphoreType.DMA],
+        input_output_aliases={} if whole is None else {1: 0},
+    )(*operands)
+
+
+def turn(value, groups):
+    rows, width = value.shape
+    value = value.reshape(4, rows // 4, width)
+    value = lax.all_to_all(value, "wide", 0, 0, axis_index_groups=groups, tiled=True)
+    return value.reshape(rows, width)
+
+
+def sums_of_four(value):
+    rows, width = value.shape
+    a, b, c, d = value.reshape(4, rows // 4, width)
+    a, b, c, d = a + b, a - b, c + d, c - d
+    return jnp.concatenate([a + c, b + d, a - c, b - d], axis=0)
 
 
 class Chain:
@@ -204,46 +184,42 @@
     devices = narrow * wide
     scale = 1.0 / float(rows_here * devices) ** 0.5
     levels = wide.bit_length() - 1
-    far, mid = ("wide", levels - 1), ("wide", levels - 2)
     near = [("narrow", l) for l in range(narrow.bit_length() - 1)]
     near += [("wide", l) for l in range(levels - 2)]
     core, first, second = near[:1], near[1:2], near[2:]
+    low = wide // 4
+    groups = [[place * low + group for place in range(4)] for group in range(low)]
 
     me = lax.axis_index(AXES)
     per = picks.shape[0] // devices
     most = -(-per // devices)
-    cuts = [rows_here * cut // 16 for cut in (0, 5, 8, 12, 16)]
-
-    c = local_transform(panel, flips, scale, [b - a for a, b in zip(cuts, cuts[1:])])
+    count = 4
+    size = rows_here // count
+
+    c = local_transform(panel, flips, scale, [size] * count)
     chain = Chain()
-    half = cuts[1] // 2
-    far0 = [launch(c[0][:half], far), launch(c[0][half:], far)]
-    far1 = launch(c[1], far)
-    core2, core3 = chain.begin(c[2], core), chain.begin(c[3], core)
     wanted = send_rows(picks, [me], rows_here, devices, most)
     spots = landing(lax.dynamic_slice(picks, (me * per,), (per,)), rows_here, most)
-    first2 = chain.begin(chain.end(core2), first)
-    mid3 = launch(chain.end(core3), mid)
-    v0 = [chain.end(far0[0])]
-    second2 = chain.begin(chain.end(first2), second)
-    second3 = chain.begin(chain.end(mid3), second)
-    mid2 = launch(chain.end(second2), mid)
-    v0 = jnp.concatenate(v0 + [chain.end(far0[1])], axis=0)
-    core0 = chain.begin(v0, core)
-    first3 = chain.begin(chain.end(second3), first)
-    second0 = chain.begin(chain.end(core0), second)
-    far2 = launch(chain.end(mid2), far)
-    far3 = launch(chain.end(first3), far)
-    core1 = chain.begin(chain.end(far1), core)
-    first0 = chain.begin(chain.end(second0), first)
-    mid1 = launch(chain.end(core1), mid)
-    mid0 = launch(chain.end(first0), mid)
-    second1 = chain.begin(chain.end(mid1), second)
-    v2 = chain.end(far2)
-    first1 = chain.begin(chain.end(second1), first)
-    v0, v1 = chain.end(mid0), chain.end(first1)
-    whole = store_rows([v0, v1, v2], rows_here)
-    whole = finish(whole, far3, cuts[3], chain.last, wanted, spots)
+    turned = [turn(value, groups) for value in c]
+    sent_core, sent_first, sent_second, back = {}, {}, {}, {}
+    whole = None
+    for step in range(2 * count):
+        if step < count:
+            value = sums_of_four(after(turned[step], chain.last))
+            chain.last = value
+            sent_core[step] = chain.begin(value, core)
+        i = step - 1
+        if 0 <= i < count:
+            sent_second[i] = chain.begin(chain.end(sent_first[i]), second)
+        if step < count:
+            sent_first[step] = chain.begin(chain.end(sent_core[step]), first)
+        i = step - 2
+        if 0 <= i < count:
+            back[i] = turn(chain.end(sent_second[i]), groups)
+        i = step - 4
+        if 0 <= i < count:
+            whole = store(whole, after(back[i], chain.last), i * size, rows_here)
+            chain.last = whole
 
     filled = wanted >= 0
     chosen = jnp.take(whole, wanted, axis=0, mode="clip")

time: 155 us -> 231 us (1.49)
  Pallas kernels: 4.23 us -> 71.4 us
  waiting for transfers between devices: 93.4 us -> 69.7 us
  blocking collectives: 0 us -> 20.6 us
  starting transfers between devices: 34.3 us -> 46 us
    pallas_call x2 -> x4, Pallas kernels: 2.03 us -> 68 us  [store(): pl.pallas_call(functools.partial(store_kernel, at), out_shape=jax.ShapeDt...]
    ppermute x21 -> x12, waiting for transfers between devices: 76.8 us -> 17.5 us  [launch(): return (lax.ppermute(value, axis, pairs), value, stage)]
    all_to_all x0 -> x7, waiting for transfers between devices: none -> 35.9 us  [turn(): lax.all_to_all(value, 'wide', 0, 0, axis_index_groups=groups, tiled=True)]
    all_to_all x0 -> x7, starting transfers between devices: none -> 25.9 us  [turn(): lax.all_to_all(value, 'wide', 0, 0, axis_index_groups=groups, tiled=True)]
    all_to_all x0 -> x1, blocking collectives: none -> 20.6 us  [turn(): lax.all_to_all(value, 'wide', 0, 0, axis_index_groups=groups, tiled=True)]
    ppermute x21 -> x12, starting transfers between devices: 28.9 us -> 11.5 us  [launch(): return (lax.ppermute(value, axis, pairs), value, stage)]
    all_to_all x1, starting transfers between devices: 2.86 us -> 6.09 us  [on_device(): landed = lax.all_to_all(both, AXES, 0, 0, tiled=True)]
    concatenate x1 -> x4, other arithmetic: 0.04 us -> 2.52 us  [sums_of_four(): return jnp.concatenate([a + c, b + d, a - c, b - d], axis=0)]
  transfers between devices with their start and end apart: 23 -> 21, of which waited for: 12 -> 12; matrix products, arithmetic and copies ran while one was open for 9% -> 6% of each run, Pallas kernels for 1% -> 22%
where the time goes in v7:
time: 231 us; the launch traced here: 230 us
  Pallas kernels  71.4 us (31%)
  waiting for transfers between devices  69.7 us (30%)
  starting transfers between devices  46 us (20%)
  blocking collectives  20.6 us (9%)
  other arithmetic  12.9 us (6%)
  local copies, waits for them, and re-layouts  8.24 us (4%)
    pallas_call x4, Pallas kernels, store(): pl.pallas_call(functools.partial(store_kernel, at), out_shape=jax.ShapeDt...  68 us
    all_to_all x7, waiting for transfers between devices, turn(): lax.all_to_all(value, 'wide', 0, 0, axis_index_groups=groups, tiled=True)  35.9 us
    all_to_all x7, starting transfers between devices, turn(): lax.all_to_all(value, 'wide', 0, 0, axis_index_groups=groups, tiled=True)  25.9 us
    all_to_all x1, blocking collectives, turn(): lax.all_to_all(value, 'wide', 0, 0, axis_index_groups=groups, tiled=True)  20.6 us
    ppermute x12, waiting for transfers between devices, launch(): return (lax.ppermute(value, axis, pairs), value, stage)  17.5 us
    ppermute x12, starting transfers between devices, launch(): return (lax.ppermute(value, axis, pairs), value, stage)  11.5 us
    all_to_all x1, waiting for transfers between devices, on_device(): landed = lax.all_to_all(both, AXES, 0, 0, tiled=True)  10.4 us
    add x12, other arithmetic, end(): self.last = partner + sign_of(stage) * value  9.03 us
  transfers between devices with their start and end apart: 21, of which 12 were waited for; matrix products, arithmetic and copies ran while one was open for 6% of the time, Pallas kernels for 22%

profile of v7, /device:TPU:0, one launch (start us, length us, event | category | flops | bytes accessed | tf_op | source)
XLA Modules:
  0.0 230.2 jit_solution(17271268095602024461)
XLA Ops:
  0.6 1.6 copy-done
  2.9 3.1 %shard_map.58 = (f32[1024,128]{1,0:T(8,128)S(1)}, f32[1024,128]{1,0:T(8,128)}, f32[1024,128]{1,0:T(8,128)}, f32[1024,128]{1,0:T(8,128)}) custom-call(s32[32,128]{1,0:T(8,128)S(1)} %bitcast.24, f32[4096,128]{1,0:T(8,128)S(1)} %copy-done), custom_call_target="tpu_custom_call" | custom-call | tf_op jit(solution)/shard_map/pallas_call | solution.py:65
  6.1 20.6 %all_to_all.50 = f32[4,256,128]{2,1,0:T(8,128)S(1)} all-to-all(f32[4,256,128]{2,1,0:T(8,128)S(1)} %bitcast.23), channel_id=1, replica_groups={{0,2,4,6},{1,3,5,7},{8,10,12,14},{9,11,13,15},{16,18,20,22},{17,19,21,2..., dimensions={0} | all-to-all | bytes 1048576 | tf_op jit(solution)/shard_map/all_to_all | solution.py:109
  26.7 3.5 %all-to-all-start.2 = ((f32[4,256,128]{2,1,0:T(8,128)}), f32[4,256,128]{2,1,0:T(8,128)S(1)}, u32[]{:S(2)}, u32[]{:S(2)}) async-start(f32[4,256,128]{2,1,0:T(8,128)} %bitcast.5), calls=%async_computation.2 | async-start | bytes 1048576 | tf_op jit(solution)/shard_map/all_to_all | solution.py:109
  30.3 1.9 collective-permute-done
  33.8 9.9 %all-to-all-done.2 = f32[4,256,128]{2,1,0:T(8,128)S(1)} async-done(((f32[4,256,128]{2,1,0:T(8,128)}), f32[4,256,128]{2,1,0:T(8,128)S(1)}, u32[]{:S(2)}, u32[]{:S(2)}) %all-to-all-start.2) | async-done | bytes 524320 | tf_op jit(solution)/shard_map/all_to_all | solution.py:109
  43.7 3.5 %all-to-all-start.3 = ((f32[4,256,128]{2,1,0:T(8,128)}), f32[4,256,128]{2,1,0:T(8,128)S(1)}, u32[]{:S(2)}, u32[]{:S(2)}) async-start(f32[4,256,128]{2,1,0:T(8,128)} %bitcast.7), calls=%async_computation.3 | async-start | bytes 1048576 | tf_op jit(solution)/shard_map/all_to_all | solution.py:109
  48.2 2.1 collective-permute-done.3
  51.8 9.3 %all-to-all-done.3 = f32[4,256,128]{2,1,0:T(8,128)S(1)} async-done(((f32[4,256,128]{2,1,0:T(8,128)}), f32[4,256,128]{2,1,0:T(8,128)S(1)}, u32[]{:S(2)}, u32[]{:S(2)}) %all-to-all-start.3) | async-done | bytes 524320 | tf_op jit(solution)/shard_map/all_to_all | solution.py:109
  63.6 3.5 %all-to-all-start = ((f32[4,256,128]{2,1,0:T(8,128)}), f32[4,256,128]{2,1,0:T(8,128)S(1)}, u32[]{:S(2)}, u32[]{:S(2)}) async-start(f32[4,256,128]{2,1,0:T(8,128)} %bitcast.1), calls=%async_computation | async-start | bytes 1048576 | tf_op jit(solution)/shard_map/all_to_all | solution.py:109
  68.2 1.6 collective-permute-start.7
  69.8 6.7 %collective-permute-done.2 = f32[1024,128]{1,0:T(8,128)} collective-permute-done((f32[1024,128]{1,0:T(8,128)S(1)}, f32[1024,128]{1,0:T(8,128)}, u32[]{:S(2)}, u32[]{:S(2)}) %collective-permute-start.2) | collective-permute-done | bytes 524320 | tf_op jit(solution)/shard_map/ppermute | solution.py:78
  76.5 1.9 multiply_add_fusion.6
  78.4 3.8 %all-to-all-done = f32[4,256,128]{2,1,0:T(8,128)S(1)} async-done(((f32[4,256,128]{2,1,0:T(8,128)}), f32[4,256,128]{2,1,0:T(8,128)S(1)}, u32[]{:S(2)}, u32[]{:S(2)}) %all-to-all-start) | async-done | bytes 524320 | tf_op jit(solution)/shard_map/all_to_all | solution.py:109
  83.5 3.5 %all-to-all-start.4 = ((f32[4,256,128]{2,1,0:T(8,128)}), f32[4,256,128]{2,1,0:T(8,128)S(1)}, u32[]{:S(2)}, u32[]{:S(2)}) async-start(f32[4,256,128]{2,1,0:T(8,128)} %bitcast.9), calls=%async_computation.4 | async-start | bytes 1048576 | tf_op jit(solution)/shard_map/all_to_all | solution.py:109
  91.3 6.6 %collective-permute-done.9 = f32[1024,128]{1,0:T(8,128)} collective-permute-done((f32[1024,128]{1,0:T(8,128)S(1)}, f32[1024,128]{1,0:T(8,128)}, u32[]{:S(2)}, u32[]{:S(2)}) %collective-permute-start.9) | collective-permute-done | bytes 524320 | tf_op jit(solution)/shard_map/ppermute | solution.py:78
  97.9 1.9 multiply_add_fusion.3
  99.8 2.4 %all-to-all-done.4 = f32[4,256,128]{2,1,0:T(8,128)S(1)} async-done(((f32[4,256,128]{2,1,0:T(8,128)}), f32[4,256,128]{2,1,0:T(8,128)S(1)}, u32[]{:S(2)}, u32[]{:S(2)}) %all-to-all-start.4) | async-done | bytes 524320 | tf_op jit(solution)/shard_map/all_to_all | solution.py:109
  102.2 3.5 %all-to-all-start.7 = ((f32[4,256,128]{2,1,0:T(8,128)}), f32[4,256,128]{2,1,0:T(8,128)S(1)}, u32[]{:S(2)}, u32[]{:S(2)}) async-start(f32[4,256,128]{2,1,0:T(8,128)} %bitcast.15), calls=%async_computation.7 | async-start | bytes 1048576 | tf_op jit(solution)/shard_map/all_to_all | solution.py:109
  106.7 1.6 collective-permute-start.10
  109.5 10.5 %all-to-all-done.7 = f32[4,256,128]{2,1,0:T(8,128)S(1)} async-done(((f32[4,256,128]{2,1,0:T(8,128)}), f32[4,256,128]{2,1,0:T(8,128)S(1)}, u32[]{:S(2)}, u32[]{:S(2)}) %all-to-all-start.7) | async-done | bytes 524320 | tf_op jit(solution)/shard_map/all_to_all | solution.py:109
  119.9 3.5 %all-to-all-start.6 = ((f32[4,256,128]{2,1,0:T(8,128)}), f32[4,256,128]{2,1,0:T(8,128)S(1)}, u32[]{:S(2)}, u32[]{:S(2)}) async-start(f32[4,256,128]{2,1,0:T(8,128)} %bitcast.13), calls=%async_computation.6 | async-start | bytes 1048576 | tf_op jit(solution)/shard_map/all_to_all | solution.py:109
  123.4 17.0 %shard_map.59.refs_1_ = f32[4096,128]{1,0:T(8,128)} custom-call(f32[1024,128]{1,0:T(8,128)} %bitcast.26), custom_call_target="tpu_custom_call" | custom-call | tf_op jit(solution)/shard_map/pallas_call | solution.py:96
  141.3 5.1 %all-to-all-start.5 = ((f32[4,256,128]{2,1,0:T(8,128)}), f32[4,256,128]{2,1,0:T(8,128)S(1)}, u32[]{:S(2)}, u32[]{:S(2)}) async-start(f32[4,256,128]{2,1,0:T(8,128)} %bitcast.11), calls=%async_computation.5 | async-start | bytes 1048576 | tf_op jit(solution)/shard_map/all_to_all | solution.py:109
  146.9 17.0 %shard_map.60.refs_1_ = f32[4096,128]{1,0:T(8,128)} custom-call(f32[1024,128]{1,0:T(8,128)} %bitcast.25, f32[4096,128]{1,0:T(8,128)} %shard_map.59.refs_1_), custom_call_target="tpu_custom_call", output_to_operand_aliasing={{}: (1, {})} | custom-call | tf_op jit(solution)/shard_map/pallas_call | solution.py:96
  163.9 17.0 %shard_map.61.refs_1_ = f32[4096,128]{1,0:T(8,128)} custom-call(f32[1024,128]{1,0:T(8,128)} %bitcast.27, f32[4096,128]{1,0:T(8,128)} %shard_map.60.refs_1_), custom_call_target="tpu_custom_call", output_to_operand_aliasing={{}: (1, {})} | custom-call | tf_op jit(solution)/shard_map/pallas_call | solution.py:96
  181.8 17.0 %shard_map.62 = f32[4096,128]{1,0:T(8,128)} custom-call(f32[1024,128]{1,0:T(8,128)} %bitcast.28, f32[4096,128]{1,0:T(8,128)} %shard_map.61.refs_1_), custom_call_target="tpu_custom_call", output_to_operand_aliasing={{}: (1, {})} | custom-call | tf_op jit(solution)/shard_map/pallas_call | solution.py:96
  198.8 2.3 %gather_fusion = f32[256,128]{1,0:T(8,128)S(1)} fusion(f32[4096,128]{1,0:T(8,128)} %shard_map.62, s32[1024]{0:T(1024)S(1)} %pad_clamp_fusion.1), kind=kCustom, calls=%fused_computation | custom fusion | bytes 263168 | tf_op jit(solution)/shard_map/jit(_take)/gather | solution.py:225
  202.3 6.1 %all-to-all-start.8 = ((f32[32,12,128]{2,1,0:T(8,128)}), f32[32,12,128]{2,1,0:T(8,128)S(1)}, u32[]{:S(2)}, u32[]{:S(2)}) async-start(f32[32,12,128]{2,1,0:T(8,128)} %pad_maximum_fusion.4), calls=%async_computation.8 | async-start | bytes 524288 | tf_op jit(solution)/shard_map/all_to_all | solution.py:234
  208.7 10.4 %all-to-all-done.8 = f32[32,12,128]{2,1,0:T(8,128)S(1)} async-done(((f32[32,12,128]{2,1,0:T(8,128)}), f32[32,12,128]{2,1,0:T(8,128)S(1)}, u32[]{:S(2)}, u32[]{:S(2)}) %all-to-all-start.8) | async-done | bytes 196640 | tf_op jit(solution)/shard_map/all_to_all | solution.py:234
  219.7 2.6 %all-to-all-start.9 = ((f32[32,4,128]{2,1,0:T(4,128)}), f32[32,4,128]{2,1,0:T(4,128)S(1)}, u32[]{:S(2)}, u32[]{:S(2)}) async-start(f32[32,4,128]{2,1,0:T(4,128)} %broadcast_in_dim.35), calls=%async_computation.9 | async-start | bytes 131072 | tf_op jit(solution)/shard_map/all_to_all | solution.py:237
  223.7 5.9 %all-to-all-done.9 = f32[32,4,128]{2,1,0:T(4,128)S(1)} async-done(((f32[32,4,128]{2,1,0:T(4,128)}), f32[32,4,128]{2,1,0:T(4,128)S(1)}, u32[]{:S(2)}, u32[]{:S(2)}) %all-to-all-start.9) | async-done | bytes 65568 | tf_op jit(solution)/shard_map/all_to_all | solution.py:237
  (69 shorter events, 22.8 us)
Async XLA Ops:
  0.6 1.6 copy-start
  2.2 0.7 copy-start.1
  26.7 17.1 %all-to-all-start.2 = ((f32[4,256,128]{2,1,0:T(8,128)}), f32[4,256,128]{2,1,0:T(8,128)S(1)}, u32[]{:S(2)}, u32[]{:S(2)}) async-start(f32[4,256,128]{2,1,0:T(8,128)} %bitcast.5), calls=%async_computation.2 | async-start | bytes 1048576 | tf_op jit(solution)/shard_map/all_to_all | solution.py:109
  30.2 2.0 collective-permute-start
  32.3 15.8 %collective-permute-start.1 = (f32[1024,128]{1,0:T(8,128)S(1)}, f32[1024,128]{1,0:T(8,128)S(1)}, u32[]{:S(2)}, u32[]{:S(2)}) collective-permute-start(f32[1024,128]{1,0:T(8,128)S(1)} %multiply_add_fusion.11), channel_id=1, source_target_pairs={{0,16},{8,24},{16,0},{24,8},{1,17},{9,25},{17,1},{25,9},{2,18},{10... | collective-permute-start | bytes 1572872 | tf_op jit(solution)/shard_map/ppermute | solution.py:78
  43.7 17.4 %all-to-all-start.3 = ((f32[4,256,128]{2,1,0:T(8,128)}), f32[4,256,128]{2,1,0:T(8,128)S(1)}, u32[]{:S(2)}, u32[]{:S(2)}) async-start(f32[4,256,128]{2,1,0:T(8,128)} %bitcast.7), calls=%async_computation.3 | async-start | bytes 1048576 | tf_op jit(solution)/shard_map/all_to_all | solution.py:109
  48.1 2.1 collective-permute-start.3
  50.3 16.8 %collective-permute-start.5 = (f32[1024,128]{1,0:T(8,128)S(1)}, f32[1024,128]{1,0:T(8,128)S(1)}, u32[]{:S(2)}, u32[]{:S(2)}) collective-permute-start(f32[1024,128]{1,0:T(8,128)S(1)} %multiply_add_fusion.9), channel_id=1, source_target_pairs={{0,16},{8,24},{16,0},{24,8},{1,17},{9,25},{17,1},{25,9},{2,18},{10... | collective-permute-start | bytes 1572872 | tf_op jit(solution)/shard_map/ppermute | solution.py:78
  62.0 5.1 %collective-permute-start.4 = (f32[1024,128]{1,0:T(8,128)}, f32[1024,128]{1,0:T(8,128)}, u32[]{:S(2)}, u32[]{:S(2)}) collective-permute-start(f32[1024,128]{1,0:T(8,128)} %pad_maximum_fusion.2), channel_id=1, source_target_pairs={{0,8},{8,0},{16,24},{24,16},{1,9},{9,1},{17,25},{25,17},{2,10},{10... | collective-permute-start | bytes 1572872 | tf_op jit(solution)/shard_map/ppermute | solution.py:78
  62.0 14.4 %collective-permute-start.2 = (f32[1024,128]{1,0:T(8,128)S(1)}, f32[1024,128]{1,0:T(8,128)}, u32[]{:S(2)}, u32[]{:S(2)}) collective-permute-start(f32[1024,128]{1,0:T(8,128)S(1)} %multiply_add_fusion.10), channel_id=1, source_target_pairs={{0,1},{1,0},{2,3},{3,2},{4,5},{5,4},{6,7},{7,6},{8,9},{9,8},{10,11... | collective-permute-start | bytes 1572872 | tf_op jit(solution)/shard_map/ppermute | solution.py:78
  63.6 18.6 %all-to-all-start = ((f32[4,256,128]{2,1,0:T(8,128)}), f32[4,256,128]{2,1,0:T(8,128)S(1)}, u32[]{:S(2)}, u32[]{:S(2)}) async-start(f32[4,256,128]{2,1,0:T(8,128)} %bitcast.1), calls=%async_computation | async-start | bytes 1048576 | tf_op jit(solution)/shard_map/all_to_all | solution.py:109
  68.2 18.8 %collective-permute-start.7 = (f32[1024,128]{1,0:T(8,128)S(1)}, f32[1024,128]{1,0:T(8,128)S(1)}, u32[]{:S(2)}, u32[]{:S(2)}) collective-permute-start(f32[1024,128]{1,0:T(8,128)S(1)} %multiply_add_fusion.7), channel_id=1, source_target_pairs={{0,16},{8,24},{16,0},{24,8},{1,17},{9,25},{17,1},{25,9},{2,18},{10... | collective-permute-start | bytes 1572872 | tf_op jit(solution)/shard_map/ppermute | solution.py:78
  83.0 4.1 %collective-permute-start.6 = (f32[1024,128]{1,0:T(8,128)}, f32[1024,128]{1,0:T(8,128)}, u32[]{:S(2)}, u32[]{:S(2)}) collective-permute-start(f32[1024,128]{1,0:T(8,128)} %pad_maximum_fusion.3), channel_id=1, source_target_pairs={{0,8},{8,0},{16,24},{24,16},{1,9},{9,1},{17,25},{25,17},{2,10},{10... | collective-permute-start | bytes 1572872 | tf_op jit(solution)/shard_map/ppermute | solution.py:78
  83.0 14.8 %collective-permute-start.9 = (f32[1024,128]{1,0:T(8,128)S(1)}, f32[1024,128]{1,0:T(8,128)}, u32[]{:S(2)}, u32[]{:S(2)}) collective-permute-start(f32[1024,128]{1,0:T(8,128)S(1)} %multiply_add_fusion.8), channel_id=1, source_target_pairs={{0,1},{1,0},{2,3},{3,2},{4,5},{5,4},{6,7},{7,6},{8,9},{9,8},{10,11... | collective-permute-start | bytes 1572872 | tf_op jit(solution)/shard_map/ppermute | solution.py:78
  83.5 18.6 %all-to-all-start.4 = ((f32[4,256,128]{2,1,0:T(8,128)}), f32[4,256,128]{2,1,0:T(8,128)S(1)}, u32[]{:S(2)}, u32[]{:S(2)}) async-start(f32[4,256,128]{2,1,0:T(8,128)} %bitcast.9), calls=%async_computation.4 | async-start | bytes 1048576 | tf_op jit(solution)/shard_map/all_to_all | solution.py:109
  88.2 17.4 %collective-permute-start.8 = (f32[1024,128]{1,0:T(8,128)S(1)}, f32[1024,128]{1,0:T(8,128)}, u32[]{:S(2)}, u32[]{:S(2)}) collective-permute-start(f32[1024,128]{1,0:T(8,128)S(1)} %multiply_add_fusion.4), channel_id=1, source_target_pairs={{0,16},{8,24},{16,0},{24,8},{1,17},{9,25},{17,1},{25,9},{2,18},{10... | collective-permute-start | bytes 1572872 | tf_op jit(solution)/shard_map/ppermute | solution.py:78
  89.8 18.8 %collective-permute-start.11 = (f32[1024,128]{1,0:T(8,128)S(1)}, f32[1024,128]{1,0:T(8,128)S(1)}, u32[]{:S(2)}, u32[]{:S(2)}) collective-permute-start(f32[1024,128]{1,0:T(8,128)S(1)} %multiply_add_fusion.5), channel_id=1, source_target_pairs={{0,1},{1,0},{2,3},{3,2},{4,5},{5,4},{6,7},{7,6},{8,9},{9,8},{10,11... | collective-permute-start | bytes 1572872 | tf_op jit(solution)/shard_map/ppermute | solution.py:78
  102.2 7.3 %copy-start.3 = (f32[4,256,128]{2,1,0:T(8,128)}, f32[4,256,128]{2,1,0:T(8,128)S(1)}, u32[]{:S(2)}) copy-start(f32[4,256,128]{2,1,0:T(8,128)S(1)} %all-to-all-done.4) | copy-start | bytes 1572868
  102.2 17.8 %all-to-all-start.7 = ((f32[4,256,128]{2,1,0:T(8,128)}), f32[4,256,128]{2,1,0:T(8,128)S(1)}, u32[]{:S(2)}, u32[]{:S(2)}) async-start(f32[4,256,128]{2,1,0:T(8,128)} %bitcast.15), calls=%async_computation.7 | async-start | bytes 1048576 | tf_op jit(solution)/shard_map/all_to_all | solution.py:109
  106.7 33.7 %collective-permute-start.10 = (f32[1024,128]{1,0:T(8,128)S(1)}, f32[1024,128]{1,0:T(8,128)S(1)}, u32[]{:S(2)}, u32[]{:S(2)}) collective-permute-start(f32[1024,128]{1,0:T(8,128)S(1)} %multiply_add_fusion.2), channel_id=1, source_target_pairs={{0,1},{1,0},{2,3},{3,2},{4,5},{5,4},{6,7},{7,6},{8,9},{9,8},{10,11... | collective-permute-start | bytes 1572872 | tf_op jit(solution)/shard_map/ppermute | solution.py:78
  119.9 21.4 %copy-start.2 = (f32[4,256,128]{2,1,0:T(8,128)}, f32[4,256,128]{2,1,0:T(8,128)S(1)}, u32[]{:S(2)}) copy-start(f32[4,256,128]{2,1,0:T(8,128)S(1)} %all-to-all-done.7) | copy-start | bytes 1572868
  119.9 21.4 %all-to-all-start.6 = ((f32[4,256,128]{2,1,0:T(8,128)}), f32[4,256,128]{2,1,0:T(8,128)S(1)}, u32[]{:S(2)}, u32[]{:S(2)}) async-start(f32[4,256,128]{2,1,0:T(8,128)} %bitcast.13), calls=%async_computation.6 | async-start | bytes 1048576 | tf_op jit(solution)/shard_map/all_to_all | solution.py:109
  123.4 22.9 %copy-start.6 = (s32[8192]{0:T(1024)S(1)}, s32[8192]{0:T(1024)}, u32[]{:S(2)}) copy-start(s32[8192]{0:T(1024)} %param.5) | copy-start | bytes 98308
  141.3 22.6 %copy-start.4 = (f32[4,256,128]{2,1,0:T(8,128)}, f32[4,256,128]{2,1,0:T(8,128)S(1)}, u32[]{:S(2)}) copy-start(f32[4,256,128]{2,1,0:T(8,128)S(1)} %all-to-all-done.6) | copy-start | bytes 1572868
  141.3 39.6 %all-to-all-start.5 = ((f32[4,256,128]{2,1,0:T(8,128)}), f32[4,256,128]{2,1,0:T(8,128)S(1)}, u32[]{:S(2)}, u32[]{:S(2)}) async-start(f32[4,256,128]{2,1,0:T(8,128)} %bitcast.11), calls=%async_computation.5 | async-start | bytes 1048576 | tf_op jit(solution)/shard_map/all_to_all | solution.py:109
  181.0 0.8 copy-start.5
  202.3 16.7 %all-to-all-start.8 = ((f32[32,12,128]{2,1,0:T(8,128)}), f32[32,12,128]{2,1,0:T(8,128)S(1)}, u32[]{:S(2)}, u32[]{:S(2)}) async-start(f32[32,12,128]{2,1,0:T(8,128)} %pad_maximum_fusion.4), calls=%async_computation.8 | async-start | bytes 524288 | tf_op jit(solution)/shard_map/all_to_all | solution.py:234
  219.7 9.9 %all-to-all-start.9 = ((f32[32,4,128]{2,1,0:T(4,128)}), f32[32,4,128]{2,1,0:T(4,128)S(1)}, u32[]{:S(2)}, u32[]{:S(2)}) async-start(f32[32,4,128]{2,1,0:T(4,128)} %broadcast_in_dim.35), calls=%async_computation.9 | async-start | bytes 131072 | tf_op jit(solution)/shard_map/all_to_all | solution.py:237

commit v8 on v7

--- a/solution.py
+++ b/solution.py
@@ -20,7 +20,7 @@
     return (1 - 2 * parity).astype(jnp.float32)
 
 
-def local_kernel(scale, flips_ref, panel_ref, *refs):
+def local_kernel(scale, turns_ref, flips_ref, panel_ref, *refs):
     *outs, held = refs
     blocks = panel_ref.shape[0] // BLOCK
     width = panel_ref.shape[1]
@@ -29,7 +29,8 @@
     base = signs(BLOCK)
     for b in range(blocks):
         row = jnp.concatenate([flips_ref[b * per + i : b * per + i + 1, :] for i in range(per)], axis=1)
-        mixer = (base * (1 - 2 * row).astype(jnp.float32)).astype(jnp.bfloat16)
+        turned = (1 - 2 * row) * turns_ref[b % 4]
+        mixer = (base * turned.astype(jnp.float32)).astype(jnp.bfloat16)
         values = panel_ref[b * BLOCK : (b + 1) * BLOCK, :]
         high = values.astype(jnp.bfloat16)
         rest = values - high.astype(jnp.float32)
@@ -60,16 +61,18 @@
     lax.fori_loop(0, BLOCK // strip, body, 0)
 
 
-def local_transform(panel, flips, scale, shares):
+def local_transform(panel, flips, turns, scale):
     rows, width = panel.shape
+    blocks = rows // BLOCK
     return pl.pallas_call(
         functools.partial(local_kernel, scale),
-        out_shape=[jax.ShapeDtypeStruct((share, width), jnp.float32) for share in shares],
-        in_specs=[pl.BlockSpec(memory_space=pltpu.VMEM)] * 2,
-        out_specs=[pl.BlockSpec(memory_space=pltpu.VMEM)] * len(shares),
-        scratch_shapes=[pltpu.VMEM((rows // BLOCK, BLOCK, width), jnp.float32)],
+        out_shape=[jax.ShapeDtypeStruct((BLOCK, width), jnp.float32)] * blocks,
+        in_specs=[pl.BlockSpec(memory_space=pltpu.SMEM)]
+        + [pl.BlockSpec(memory_space=pltpu.VMEM)] * 2,
+        out_specs=[pl.BlockSpec(memory_space=pltpu.VMEM)] * blocks,
+        scratch_shapes=[pltpu.VMEM((blocks, BLOCK, width), jnp.float32)],
         compiler_params=pltpu.CompilerParams(vmem_limit_bytes=32 * 2**20),
-    )(flips.reshape(rows // 128, 128), panel)
+    )(turns, flips.reshape(rows // 128, 128), panel)
 
 
 def launch(value, stage):
@@ -83,38 +86,47 @@
     return (1 - 2 * (lax.axis_index(axis) >> level & 1)).astype(jnp.float32)
 
 
-def store_kernel(at, *refs):
-    value_ref, out_ref, sent = refs[0], refs[-2], refs[-1]
-    rows = value_ref.shape[0]
-    copy = pltpu.make_async_copy(value_ref, out_ref.at[pl.ds(at, rows), :], sent)
-    copy.start()
-    copy.wait()
-
-
-def store(whole, value, at, rows):
-    operands = [value] if whole is None else [value, whole]
+def store_kernel(ats_ref, *refs):
+    values, out_ref, sent = refs[:4], refs[-2], refs[-1]
+    rows = values[0].shape[0]
+    copies = []
+    for i, value in enumerate(values):
+        at = pl.multiple_of(ats_ref[i], rows)
+        copies.append(pltpu.make_async_copy(value, out_ref.at[pl.ds(at, rows), :], sent.at[i]))
+    for copy in copies:
+        copy.start()
+    for copy in copies:
+        copy.wait()
+
+
+def store(whole, values, ats, rows):
+    operands = list(values) + ([] if whole is None else [whole])
+    kinds = [pltpu.SMEM] + [pltpu.VMEM] * 4 + ([] if whole is None else [pl.ANY])
     return pl.pallas_call(
-        functools.partial(store_kernel, at),
-        out_shape=jax.ShapeDtypeStruct((rows, value.shape[1]), jnp.float32),
-        in_specs=[pl.BlockSpec(memory_space=pl.ANY)] * len(operands),
+        store_kernel,
+        out_shape=jax.ShapeDtypeStruct((rows, values[0].shape[1]), jnp.float32),
+        in_specs=[pl.BlockSpec(memory_space=kind) for kind in kinds],
         out_specs=pl.BlockSpec(memory_space=pl.ANY),
-        scratch_shapes=[pltpu.SemaphoreType.DMA],
-        input_output_aliases={} if whole is None else {1: 0},
-    )(*operands)
-
-
-def turn(value, groups):
-    rows, width = value.shape
-    value = value.reshape(4, rows // 4, width)
-    value = lax.all_to_all(value, "wide", 0, 0, axis_index_groups=groups, tiled=True)
-    return value.reshape(rows, width)
-
-
-def sums_of_four(value):
-    rows, width = value.shape
-    a, b, c, d = value.reshape(4, rows // 4, width)
+        scratch_shapes=[pltpu.SemaphoreType.DMA((4,))],
+        input_output_aliases={} if whole is None else {5: 0},
+        compiler_params=pltpu.CompilerParams(vmem_limit_bytes=8 * 2**20),
+    )(ats, *operands)
+
+
+def turn(parts, low):
+    size = lax.axis_size("wide")
+    sent = [parts[0]]
+    for j in (1, 2, 3):
+        pairs = [(source, source ^ j * low) for source in range(size)]
+        sent.append(lax.ppermute(parts[j], "wide", pairs))
+    return sent
+
+
+def sums_of_four(parts, turns, whole_turn):
+    a, b, c, d = [part * turns[k] for k, part in enumerate(parts)]
     a, b, c, d = a + b, a - b, c + d, c - d
-    return jnp.concatenate([a + c, b + d, a - c, b - d], axis=0)
+    outs = [a + c, b + d, a - c, b - d]
+    return jnp.concatenate([out * (turns[j] * whole_turn) for j, out in enumerate(outs)], axis=0)
 
 
 class Chain:
@@ -188,26 +200,38 @@
     near += [("wide", l) for l in range(levels - 2)]
     core, first, second = near[:1], near[1:2], near[2:]
     low = wide // 4
-    groups = [[place * low + group for place in range(4)] for group in range(low)]
+    place = lax.axis_index("wide") // low
+    turns = [1 - 2 * ((place & j & 1) ^ ((place & j) >> 1)) for j in range(4)]
+    real_turns = [turn_j.astype(jnp.float32) for turn_j in turns]
+    whole_turn = real_turns[3]
 
     me = lax.axis_index(AXES)
     per = picks.shape[0] // devices
     most = -(-per // devices)
-    count = 4
-    size = rows_here // count
-
-    c = local_transform(panel, flips, scale, [size] * count)
+    count = rows_here // (4 * BLOCK)
+
+    blocks = local_transform(panel, flips, jnp.stack(turns), scale)
     chain = Chain()
     wanted = send_rows(picks, [me], rows_here, devices, most)
     spots = landing(lax.dynamic_slice(picks, (me * per,), (per,)), rows_here, most)
-    turned = [turn(value, groups) for value in c]
+    away = [turn(blocks[4 * i : 4 * i + 4], low) for i in range(count)]
     sent_core, sent_first, sent_second, back = {}, {}, {}, {}
     whole = None
+
+    def arrive(parts):
+        out = lax.optimization_barrier((list(parts), chain.last))[0]
+        return out
+
     for step in range(2 * count):
         if step < count:
-            value = sums_of_four(after(turned[step], chain.last))
+            value = sums_of_four(arrive(away[step]), real_turns, whole_turn)
             chain.last = value
             sent_core[step] = chain.begin(value, core)
+        i = step - 4
+        if 0 <= i < count:
+            ats = jnp.stack([((place ^ j) + 4 * i) * BLOCK for j in range(4)])
+            whole = store(whole, arrive(back[i]), ats.astype(jnp.int32), rows_here)
+            chain.last = whole
         i = step - 1
         if 0 <= i < count:
             sent_second[i] = chain.begin(chain.end(sent_first[i]), second)
@@ -215,11 +239,8 @@
             sent_first[step] = chain.begin(chain.end(sent_core[step]), first)
         i = step - 2
         if 0 <= i < count:
-            back[i] = turn(chain.end(sent_second[i]), groups)
-        i = step - 4
-        if 0 <= i < count:
-            whole = store(whole, after(back[i], chain.last), i * size, rows_here)
-            chain.last = whole
+            value = chain.end(sent_second[i])
+            back[i] = turn([value[j * BLOCK : (j + 1) * BLOCK] for j in range(4)], low)
 
     filled = wanted >= 0
     chosen = jnp.take(whole, wanted, axis=0, mode="clip")

time: 231 us -> 166 us (0.72)
  Pallas kernels: 71.4 us -> 8.2 us
  blocking collectives: 20.6 us -> 0 us
  starting transfers between devices: 46 us -> 56.9 us
  waiting for transfers between devices: 69.7 us -> 78.5 us
    pallas_call x4, Pallas kernels: 68 us -> 5.45 us  [store(): pl.pallas_call(store_kernel, out_shape=jax.ShapeDtypeStruct((rows, values...]
    ppermute x0 -> x24, waiting for transfers between devices: none -> 45.7 us  [turn(): sent.append(lax.ppermute(parts[j], 'wide', pairs))]
    ppermute x0 -> x24, starting transfers between devices: none -> 38.8 us  [turn(): sent.append(lax.ppermute(parts[j], 'wide', pairs))]
    all_to_all x7 -> x0, waiting for transfers between devices: 35.9 us -> none  [turn(): lax.all_to_all(value, 'wide', 0, 0, axis_index_groups=groups, tiled=True)]
    all_to_all x7 -> x0, starting transfers between devices: 25.9 us -> none  [turn(): lax.all_to_all(value, 'wide', 0, 0, axis_index_groups=groups, tiled=True)]
    all_to_all x1 -> x0, blocking collectives: 20.6 us -> none  [turn(): lax.all_to_all(value, 'wide', 0, 0, axis_index_groups=groups, tiled=True)]
    add x12, other arithmetic: 9.03 us -> 5.86 us  [end(): self.last = partner + sign_of(stage) * value]
    all_to_all x1, starting transfers between devices: 6.09 us -> 3.66 us  [on_device(): landed = lax.all_to_all(both, AXES, 0, 0, tiled=True)]
  transfers between devices with their start and end apart: 21 -> 38, of which waited for: 12 -> 16; matrix products, arithmetic and copies ran while one was open for 6% -> 8% of each run, Pallas kernels for 22% -> 3%
where the time goes in v8:
time: 166 us; the launch traced here: 165 us
  waiting for transfers between devices  78.5 us (47%)
  starting transfers between devices  56.9 us (34%)
  other arithmetic  11.6 us (7%)
  local copies, waits for them, and re-layouts  8.34 us (5%)
  Pallas kernels  8.2 us (5%)
    ppermute x24, waiting for transfers between devices, turn(): sent.append(lax.ppermute(parts[j], 'wide', pairs))  45.7 us
    ppermute x24, starting transfers between devices, turn(): sent.append(lax.ppermute(parts[j], 'wide', pairs))  38.8 us
    ppermute x12, waiting for transfers between devices, launch(): return (lax.ppermute(value, axis, pairs), value, stage)  17.2 us
    ppermute x12, starting transfers between devices, launch(): return (lax.ppermute(value, axis, pairs), value, stage)  11.8 us
    all_to_all x1, waiting for transfers between devices, on_device(): landed = lax.all_to_all(both, AXES, 0, 0, tiled=True)  9.68 us
    all_to_all x1, waiting for transfers between devices, on_device(): gram = lax.all_to_all(shared, AXES, 0, 0, tiled=True).reshape(width, width)  5.91 us
    add x12, other arithmetic, end(): self.last = partner + sign_of(stage) * value  5.86 us
    pallas_call x4, Pallas kernels, store(): pl.pallas_call(store_kernel, out_shape=jax.ShapeDtypeStruct((rows, values...  5.45 us
  transfers between devices with their start and end apart: 38, of which 16 were waited for; matrix products, arithmetic and copies ran while one was open for 8% of the time, Pallas kernels for 3%

profile of v8, /device:TPU:0, one launch (start us, length us, event | category | flops | bytes accessed | tf_op | source)
XLA Modules:
  0.0 165.1 jit_solution(10589411135221975137)
XLA Ops:
  0.7 1.6 copy-done
  3.0 2.5 %shard_map.58 = (f32[256,128]{1,0:T(8,128)S(1)}, f32[256,128]{1,0:T(8,128)S(1)}, f32[256,128]{1,0:T(8,128)S(1)}, f32[256,128]{1,0:T(8,128)S(1)}, f32[256,128]{1,...) custom-call(s32[4]{0:T(128)S(1)} %pad_add_fusion.1.turns_ref, ...), custom_call_target="tpu_custom_call" | custom-call | tf_op jit(solution)/shard_map/pallas_call | solution.py:67
  5.5 3.1 %collective-permute-start.3 = (f32[256,128]{1,0:T(8,128)S(1)}, f32[256,128]{1,0:T(8,128)S(1)}, u32[]{:S(2)}, u32[]{:S(2)}) collective-permute-start(f32[256,128]{1,0:T(8,128)S(1)} %get-tuple-element.68), channel_id=1, source_target_pairs={{0,2},{1,3},{2,0},{3,1},{4,6},{5,7},{6,4},{7,5},{8,10},{9,11},{10,... | collective-permute-start | bytes 393224 | tf_op jit(solution)/shard_map/ppermute | solution.py:121
  8.6 2.6 %collective-permute-start.4 = (f32[256,128]{1,0:T(8,128)S(1)}, f32[256,128]{1,0:T(8,128)S(1)}, u32[]{:S(2)}, u32[]{:S(2)}) collective-permute-start(f32[256,128]{1,0:T(8,128)S(1)} %get-tuple-element.69), channel_id=1, source_target_pairs={{0,4},{1,5},{2,6},{3,7},{4,0},{5,1},{6,2},{7,3},{8,12},{9,13},{10,... | collective-permute-start | bytes 393224 | tf_op jit(solution)/shard_map/ppermute | solution.py:121
  11.2 2.5 %collective-permute-done.3 = f32[256,128]{1,0:T(8,128)S(1)} collective-permute-done((f32[256,128]{1,0:T(8,128)S(1)}, f32[256,128]{1,0:T(8,128)S(1)}, u32[]{:S(2)}, u32[]{:S(2)}) %collective-permute-start.3) | collective-permute-done | bytes 131104 | tf_op jit(solution)/shard_map/ppermute | solution.py:121
  13.7 7.9 %collective-permute-done.4 = f32[256,128]{1,0:T(8,128)S(1)} collective-permute-done((f32[256,128]{1,0:T(8,128)S(1)}, f32[256,128]{1,0:T(8,128)S(1)}, u32[]{:S(2)}, u32[]{:S(2)}) %collective-permute-start.4) | collective-permute-done | bytes 131104 | tf_op jit(solution)/shard_map/ppermute | solution.py:121
  21.8 2.4 %collective-permute-start.10 = (f32[256,128]{1,0:T(8,128)S(1)}, f32[256,128]{1,0:T(8,128)S(1)}, u32[]{:S(2)}, u32[]{:S(2)}) collective-permute-start(f32[256,128]{1,0:T(8,128)S(1)} %get-tuple-element.79), channel_id=1, source_target_pairs={{0,6},{1,7},{2,4},{3,5},{4,2},{5,3},{6,0},{7,1},{8,14},{9,15},{10,... | collective-permute-start | bytes 393224 | tf_op jit(solution)/shard_map/ppermute | solution.py:121
  27.8 2.1 %collective-permute-done.10 = f32[256,128]{1,0:T(8,128)S(1)} collective-permute-done((f32[256,128]{1,0:T(8,128)S(1)}, f32[256,128]{1,0:T(8,128)S(1)}, u32[]{:S(2)}, u32[]{:S(2)}) %collective-permute-start.10) | collective-permute-done | bytes 131104 | tf_op jit(solution)/shard_map/ppermute | solution.py:121
  30.0 2.9 %collective-permute-done.8 = f32[256,128]{1,0:T(8,128)S(1)} collective-permute-done((f32[256,128]{1,0:T(8,128)S(1)}, f32[256,128]{1,0:T(8,128)S(1)}, u32[]{:S(2)}, u32[]{:S(2)}) %collective-permute-start.8) | collective-permute-done | bytes 131104 | tf_op jit(solution)/shard_map/ppermute | solution.py:121
  32.9 4.7 %collective-permute-done.9 = f32[256,128]{1,0:T(8,128)S(1)} collective-permute-done((f32[256,128]{1,0:T(8,128)S(1)}, f32[256,128]{1,0:T(8,128)S(1)}, u32[]{:S(2)}, u32[]{:S(2)}) %collective-permute-start.9) | collective-permute-done | bytes 131104 | tf_op jit(solution)/shard_map/ppermute | solution.py:121
  38.4 3.0 %collective-permute-start.13 = (f32[256,128]{1,0:T(8,128)S(1)}, f32[256,128]{1,0:T(8,128)S(1)}, u32[]{:S(2)}, u32[]{:S(2)}) collective-permute-start(f32[256,128]{1,0:T(8,128)S(1)} %get-tuple-element.87), channel_id=1, source_target_pairs={{0,4},{1,5},{2,6},{3,7},{4,0},{5,1},{6,2},{7,3},{8,12},{9,13},{10,... | collective-permute-start | bytes 393224 | tf_op jit(solution)/shard_map/ppermute | solution.py:121
  46.8 4.6 %collective-permute-done.13 = f32[256,128]{1,0:T(8,128)S(1)} collective-permute-done((f32[256,128]{1,0:T(8,128)S(1)}, f32[256,128]{1,0:T(8,128)S(1)}, u32[]{:S(2)}, u32[]{:S(2)}) %collective-permute-start.13) | collective-permute-done | bytes 131104 | tf_op jit(solution)/shard_map/ppermute | solution.py:121
  52.3 3.0 %collective-permute-start = (f32[256,128]{1,0:T(8,128)S(1)}, f32[256,128]{1,0:T(8,128)S(1)}, u32[]{:S(2)}, u32[]{:S(2)}) collective-permute-start(f32[256,128]{1,0:T(8,128)S(1)} %get-tuple-element.64), channel_id=1, source_target_pairs={{0,2},{1,3},{2,0},{3,1},{4,6},{5,7},{6,4},{7,5},{8,10},{9,11},{10,... | collective-permute-start | bytes 393224 | tf_op jit(solution)/shard_map/ppermute | solution.py:121
  62.8 8.3 %collective-permute-done.11 = f32[1024,128]{1,0:T(8,128)} collective-permute-done((f32[1024,128]{1,0:T(8,128)S(1)}, f32[1024,128]{1,0:T(8,128)}, u32[]{:S(2)}, u32[]{:S(2)}) %collective-permute-start.11) | collective-permute-done | bytes 524320 | tf_op jit(solution)/shard_map/ppermute | solution.py:81
  78.8 1.8 %collective-permute-start.21 = (f32[256,128]{1,0:T(8,128)S(1)}, f32[256,128]{1,0:T(8,128)S(1)}, u32[]{:S(2)}, u32[]{:S(2)}) collective-permute-start(f32[256,128]{1,0:T(8,128)S(1)} %get-tuple-element.137), channel_id=1, source_target_pairs={{0,2},{1,3},{2,0},{3,1},{4,6},{5,7},{6,4},{7,5},{8,10},{9,11},{10,... | collective-permute-start | bytes 393224 | tf_op jit(solution)/shard_map/ppermute | solution.py:121
  80.9 2.4 %collective-permute-start.23 = (f32[256,128]{1,0:T(8,128)S(1)}, f32[256,128]{1,0:T(8,128)S(1)}, u32[]{:S(2)}, u32[]{:S(2)}) collective-permute-start(f32[256,128]{1,0:T(8,128)S(1)} %get-tuple-element.135), channel_id=1, source_target_pairs={{0,6},{1,7},{2,4},{3,5},{4,2},{5,3},{6,0},{7,1},{8,14},{9,15},{10,... | collective-permute-start | bytes 393224 | tf_op jit(solution)/shard_map/ppermute | solution.py:121
  83.2 5.6 %collective-permute-done.24 = f32[1024,128]{1,0:T(8,128)} collective-permute-done((f32[1024,128]{1,0:T(8,128)S(1)}, f32[1024,128]{1,0:T(8,128)}, u32[]{:S(2)}, u32[]{:S(2)}) %collective-permute-start.24) | collective-permute-done | bytes 524320 | tf_op jit(solution)/shard_map/ppermute | solution.py:81
  91.5 1.7 %collective-permute-done.22.refs_2_ = f32[256,128]{1,0:T(8,128)S(1)} collective-permute-done((f32[256,128]{1,0:T(8,128)S(1)}, f32[256,128]{1,0:T(8,128)S(1)}, u32[]{:S(2)}, u32[]{:S(2)}) %collective-permute-start.22) | collective-permute-done | bytes 131104 | tf_op jit(solution)/shard_map/ppermute | solution.py:121
  95.6 2.4 %collective-permute-start.26 = (f32[256,128]{1,0:T(8,128)S(1)}, f32[256,128]{1,0:T(8,128)S(1)}, u32[]{:S(2)}, u32[]{:S(2)}) collective-permute-start(f32[256,128]{1,0:T(8,128)S(1)} %get-tuple-element.133), channel_id=1, source_target_pairs={{0,2},{1,3},{2,0},{3,1},{4,6},{5,7},{6,4},{7,5},{8,10},{9,11},{10,... | collective-permute-start | bytes 393224 | tf_op jit(solution)/shard_map/ppermute | solution.py:121
  98.1 2.3 %collective-permute-start.28 = (f32[256,128]{1,0:T(8,128)S(1)}, f32[256,128]{1,0:T(8,128)S(1)}, u32[]{:S(2)}, u32[]{:S(2)}) collective-permute-start(f32[256,128]{1,0:T(8,128)S(1)} %get-tuple-element.131), channel_id=1, source_target_pairs={{0,6},{1,7},{2,4},{3,5},{4,2},{5,3},{6,0},{7,1},{8,14},{9,15},{10,... | collective-permute-start | bytes 393224 | tf_op jit(solution)/shard_map/ppermute | solution.py:121
  100.5 3.2 %collective-permute-done.29 = f32[1024,128]{1,0:T(8,128)S(1)} collective-permute-done((f32[1024,128]{1,0:T(8,128)S(1)}, f32[1024,128]{1,0:T(8,128)S(1)}, u32[]{:S(2)}, u32[]{:S(2)}) %collective-permute-start.29) | collective-permute-done | bytes 524320 | tf_op jit(solution)/shard_map/ppermute | solution.py:81
  103.7 5.3 %collective-permute-done.27.refs_2_ = f32[256,128]{1,0:T(8,128)S(1)} collective-permute-done((f32[256,128]{1,0:T(8,128)S(1)}, f32[256,128]{1,0:T(8,128)S(1)}, u32[]{:S(2)}, u32[]{:S(2)}) %collective-permute-start.27) | collective-permute-done | bytes 131104 | tf_op jit(solution)/shard_map/ppermute | solution.py:121
  109.1 2.7 %collective-permute-start.33 = (f32[256,128]{1,0:T(8,128)S(1)}, f32[256,128]{1,0:T(8,128)S(1)}, u32[]{:S(2)}, u32[]{:S(2)}) collective-permute-start(f32[256,128]{1,0:T(8,128)S(1)} %get-tuple-element.125), channel_id=1, source_target_pairs={{0,2},{1,3},{2,0},{3,1},{4,6},{5,7},{6,4},{7,5},{8,10},{9,11},{10,... | collective-permute-start | bytes 393224 | tf_op jit(solution)/shard_map/ppermute | solution.py:121
  111.8 2.4 %collective-permute-start.35 = (f32[256,128]{1,0:T(8,128)S(1)}, f32[256,128]{1,0:T(8,128)S(1)}, u32[]{:S(2)}, u32[]{:S(2)}) collective-permute-start(f32[256,128]{1,0:T(8,128)S(1)} %get-tuple-element.123), channel_id=1, source_target_pairs={{0,6},{1,7},{2,4},{3,5},{4,2},{5,3},{6,0},{7,1},{8,14},{9,15},{10,... | collective-permute-start | bytes 393224 | tf_op jit(solution)/shard_map/ppermute | solution.py:121
  117.7 2.4 %collective-permute-start.32 = (f32[256,128]{1,0:T(8,128)S(1)}, f32[256,128]{1,0:T(8,128)S(1)}, u32[]{:S(2)}, u32[]{:S(2)}) collective-permute-start(f32[256,128]{1,0:T(8,128)S(1)} %get-tuple-element.127), channel_id=1, source_target_pairs={{0,6},{1,7},{2,4},{3,5},{4,2},{5,3},{6,0},{7,1},{8,14},{9,15},{10,... | collective-permute-start | bytes 393224 | tf_op jit(solution)/shard_map/ppermute | solution.py:121
  120.4 4.4 %collective-permute-done.34.refs_2_ = f32[256,128]{1,0:T(8,128)S(1)} collective-permute-done((f32[256,128]{1,0:T(8,128)S(1)}, f32[256,128]{1,0:T(8,128)S(1)}, u32[]{:S(2)}, u32[]{:S(2)}) %collective-permute-start.34) | collective-permute-done | bytes 131104 | tf_op jit(solution)/shard_map/ppermute | solution.py:121
  126.2 8.5 %collective-permute-done.31.refs_2_ = f32[256,128]{1,0:T(8,128)S(1)} collective-permute-done((f32[256,128]{1,0:T(8,128)S(1)}, f32[256,128]{1,0:T(8,128)S(1)}, u32[]{:S(2)}, u32[]{:S(2)}) %collective-permute-start.31) | collective-permute-done | bytes 131104 | tf_op jit(solution)/shard_map/ppermute | solution.py:121
  136.0 2.3 %gather_fusion = f32[256,128]{1,0:T(8,128)S(1)} fusion(f32[4096,128]{1,0:T(8,128)} %shard_map.62, s32[1024]{0:T(1024)S(1)} %pad_clamp_fusion.1), kind=kCustom, calls=%fused_computation | custom fusion | bytes 263168 | tf_op jit(solution)/shard_map/jit(_take)/gather | solution.py:246
  139.6 3.7 %all-to-all-start = ((f32[32,12,128]{2,1,0:T(8,128)}), f32[32,12,128]{2,1,0:T(8,128)S(1)}, u32[]{:S(2)}, u32[]{:S(2)}) async-start(f32[32,12,128]{2,1,0:T(8,128)} %pad_maximum_fusion.4), calls=%async_computation | async-start | bytes 524288 | tf_op jit(solution)/shard_map/all_to_all | solution.py:255
  144.2 9.7 %all-to-all-done = f32[32,12,128]{2,1,0:T(8,128)S(1)} async-done(((f32[32,12,128]{2,1,0:T(8,128)}), f32[32,12,128]{2,1,0:T(8,128)S(1)}, u32[]{:S(2)}, u32[]{:S(2)}) %all-to-all-start) | async-done | bytes 196640 | tf_op jit(solution)/shard_map/all_to_all | solution.py:255
  154.6 2.6 %all-to-all-start.1 = ((f32[32,4,128]{2,1,0:T(4,128)}), f32[32,4,128]{2,1,0:T(4,128)S(1)}, u32[]{:S(2)}, u32[]{:S(2)}) async-start(f32[32,4,128]{2,1,0:T(4,128)} %broadcast_in_dim.35), calls=%async_computation.1 | async-start | bytes 131072 | tf_op jit(solution)/shard_map/all_to_all | solution.py:258
  158.5 5.9 %all-to-all-done.1 = f32[32,4,128]{2,1,0:T(4,128)S(1)} async-done(((f32[32,4,128]{2,1,0:T(4,128)}), f32[32,4,128]{2,1,0:T(4,128)S(1)}, u32[]{:S(2)}, u32[]{:S(2)}) %all-to-all-start.1) | async-done | bytes 65568 | tf_op jit(solution)/shard_map/all_to_all | solution.py:258
  (101 shorter events, 43.7 us)
Async XLA Ops:
  8.6 12.9 %collective-permute-start.4 = (f32[256,128]{1,0:T(8,128)S(1)}, f32[256,128]{1,0:T(8,128)S(1)}, u32[]{:S(2)}, u32[]{:S(2)}) collective-permute-start(f32[256,128]{1,0:T(8,128)S(1)} %get-tuple-element.69), channel_id=1, source_target_pairs={{0,4},{1,5},{2,6},{3,7},{4,0},{5,1},{6,2},{7,3},{8,12},{9,13},{10,... | collective-permute-start | bytes 393224 | tf_op jit(solution)/shard_map/ppermute | solution.py:121
  11.2 10.3 %collective-permute-start.5 = (f32[256,128]{1,0:T(8,128)S(1)}, f32[256,128]{1,0:T(8,128)S(1)}, u32[]{:S(2)}, u32[]{:S(2)}) collective-permute-start(f32[256,128]{1,0:T(8,128)S(1)} %get-tuple-element.70), channel_id=1, source_target_pairs={{0,6},{1,7},{2,4},{3,5},{4,2},{5,3},{6,0},{7,1},{8,14},{9,15},{10,... | collective-permute-start | bytes 393224 | tf_op jit(solution)/shard_map/ppermute | solution.py:121
  21.8 8.2 %collective-permute-start.10 = (f32[256,128]{1,0:T(8,128)S(1)}, f32[256,128]{1,0:T(8,128)S(1)}, u32[]{:S(2)}, u32[]{:S(2)}) collective-permute-start(f32[256,128]{1,0:T(8,128)S(1)} %get-tuple-element.79), channel_id=1, source_target_pairs={{0,6},{1,7},{2,4},{3,5},{4,2},{5,3},{6,0},{7,1},{8,14},{9,15},{10,... | collective-permute-start | bytes 393224 | tf_op jit(solution)/shard_map/ppermute | solution.py:121
  24.1 8.7 %collective-permute-start.8 = (f32[256,128]{1,0:T(8,128)S(1)}, f32[256,128]{1,0:T(8,128)S(1)}, u32[]{:S(2)}, u32[]{:S(2)}) collective-permute-start(f32[256,128]{1,0:T(8,128)S(1)} %get-tuple-element.77), channel_id=1, source_target_pairs={{0,2},{1,3},{2,0},{3,1},{4,6},{5,7},{6,4},{7,5},{8,10},{9,11},{10,... | collective-permute-start | bytes 393224 | tf_op jit(solution)/shard_map/ppermute | solution.py:121
  25.4 12.1 %collective-permute-start.9 = (f32[256,128]{1,0:T(8,128)S(1)}, f32[256,128]{1,0:T(8,128)S(1)}, u32[]{:S(2)}, u32[]{:S(2)}) collective-permute-start(f32[256,128]{1,0:T(8,128)S(1)} %get-tuple-element.78), channel_id=1, source_target_pairs={{0,4},{1,5},{2,6},{3,7},{4,0},{5,1},{6,2},{7,3},{8,12},{9,13},{10,... | collective-permute-start | bytes 393224 | tf_op jit(solution)/shard_map/ppermute | solution.py:121
  26.3 16.5 %collective-permute-start.7 = (f32[1024,128]{1,0:T(8,128)S(1)}, f32[1024,128]{1,0:T(8,128)S(1)}, u32[]{:S(2)}, u32[]{:S(2)}) collective-permute-start(f32[1024,128]{1,0:T(8,128)S(1)} %multiply_add_fusion.11), channel_id=1, source_target_pairs={{0,16},{8,24},{16,0},{24,8},{1,17},{9,25},{17,1},{25,9},{2,18},{10... | collective-permute-start | bytes 1572872 | tf_op jit(solution)/shard_map/ppermute | solution.py:81
  38.4 8.4 %collective-permute-start.12 = (f32[256,128]{1,0:T(8,128)S(1)}, f32[256,128]{1,0:T(8,128)S(1)}, u32[]{:S(2)}, u32[]{:S(2)}) collective-permute-start(f32[256,128]{1,0:T(8,128)S(1)} %get-tuple-element.86), channel_id=1, source_target_pairs={{0,2},{1,3},{2,0},{3,1},{4,6},{5,7},{6,4},{7,5},{8,10},{9,11},{10,... | collective-permute-start | bytes 393224 | tf_op jit(solution)/shard_map/ppermute | solution.py:121
  38.4 13.0 %collective-permute-start.13 = (f32[256,128]{1,0:T(8,128)S(1)}, f32[256,128]{1,0:T(8,128)S(1)}, u32[]{:S(2)}, u32[]{:S(2)}) collective-permute-start(f32[256,128]{1,0:T(8,128)S(1)} %get-tuple-element.87), channel_id=1, source_target_pairs={{0,4},{1,5},{2,6},{3,7},{4,0},{5,1},{6,2},{7,3},{8,12},{9,13},{10,... | collective-permute-start | bytes 393224 | tf_op jit(solution)/shard_map/ppermute | solution.py:121
  41.5 9.9 %collective-permute-start.14 = (f32[256,128]{1,0:T(8,128)S(1)}, f32[256,128]{1,0:T(8,128)S(1)}, u32[]{:S(2)}, u32[]{:S(2)}) collective-permute-start(f32[256,128]{1,0:T(8,128)S(1)} %get-tuple-element.88), channel_id=1, source_target_pairs={{0,6},{1,7},{2,4},{3,5},{4,2},{5,3},{6,0},{7,1},{8,14},{9,15},{10,... | collective-permute-start | bytes 393224 | tf_op jit(solution)/shard_map/ppermute | solution.py:121
  44.0 14.6 %collective-permute-start.17 = (f32[1024,128]{1,0:T(8,128)S(1)}, f32[1024,128]{1,0:T(8,128)S(1)}, u32[]{:S(2)}, u32[]{:S(2)}) collective-permute-start(f32[1024,128]{1,0:T(8,128)S(1)} %multiply_add_fusion.9), channel_id=1, source_target_pairs={{0,16},{8,24},{16,0},{24,8},{1,17},{9,25},{17,1},{25,9},{2,18},{10... | collective-permute-start | bytes 1572872 | tf_op jit(solution)/shard_map/ppermute | solution.py:81
  52.3 19.9 %collective-permute-start = (f32[256,128]{1,0:T(8,128)S(1)}, f32[256,128]{1,0:T(8,128)S(1)}, u32[]{:S(2)}, u32[]{:S(2)}) collective-permute-start(f32[256,128]{1,0:T(8,128)S(1)} %get-tuple-element.64), channel_id=1, source_target_pairs={{0,2},{1,3},{2,0},{3,1},{4,6},{5,7},{6,4},{7,5},{8,10},{9,11},{10,... | collective-permute-start | bytes 393224 | tf_op jit(solution)/shard_map/ppermute | solution.py:121
  55.3 16.9 %collective-permute-start.1 = (f32[256,128]{1,0:T(8,128)S(1)}, f32[256,128]{1,0:T(8,128)S(1)}, u32[]{:S(2)}, u32[]{:S(2)}) collective-permute-start(f32[256,128]{1,0:T(8,128)S(1)} %get-tuple-element.65), channel_id=1, source_target_pairs={{0,4},{1,5},{2,6},{3,7},{4,0},{5,1},{6,2},{7,3},{8,12},{9,13},{10,... | collective-permute-start | bytes 393224 | tf_op jit(solution)/shard_map/ppermute | solution.py:121
  57.0 14.2 %collective-permute-start.11 = (f32[1024,128]{1,0:T(8,128)S(1)}, f32[1024,128]{1,0:T(8,128)}, u32[]{:S(2)}, u32[]{:S(2)}) collective-permute-start(f32[1024,128]{1,0:T(8,128)S(1)} %multiply_add_fusion.10), channel_id=1, source_target_pairs={{0,1},{1,0},{2,3},{3,2},{4,5},{5,4},{6,7},{7,6},{8,9},{9,8},{10,11... | collective-permute-start | bytes 1572872 | tf_op jit(solution)/shard_map/ppermute | solution.py:81
  58.6 13.7 %collective-permute-start.2 = (f32[256,128]{1,0:T(8,128)S(1)}, f32[256,128]{1,0:T(8,128)S(1)}, u32[]{:S(2)}, u32[]{:S(2)}) collective-permute-start(f32[256,128]{1,0:T(8,128)S(1)} %get-tuple-element.66), channel_id=1, source_target_pairs={{0,6},{1,7},{2,4},{3,5},{4,2},{5,3},{6,0},{7,1},{8,14},{9,15},{10,... | collective-permute-start | bytes 393224 | tf_op jit(solution)/shard_map/ppermute | solution.py:121
  61.2 14.7 %collective-permute-start.19 = (f32[1024,128]{1,0:T(8,128)S(1)}, f32[1024,128]{1,0:T(8,128)S(1)}, u32[]{:S(2)}, u32[]{:S(2)}) collective-permute-start(f32[1024,128]{1,0:T(8,128)S(1)} %multiply_add_fusion.7), channel_id=1, source_target_pairs={{0,16},{8,24},{16,0},{24,8},{1,17},{9,25},{17,1},{25,9},{2,18},{10... | collective-permute-start | bytes 1572872 | tf_op jit(solution)/shard_map/ppermute | solution.py:81
  74.3 14.5 %collective-permute-start.24 = (f32[1024,128]{1,0:T(8,128)S(1)}, f32[1024,128]{1,0:T(8,128)}, u32[]{:S(2)}, u32[]{:S(2)}) collective-permute-start(f32[1024,128]{1,0:T(8,128)S(1)} %multiply_add_fusion.8), channel_id=1, source_target_pairs={{0,1},{1,0},{2,3},{3,2},{4,5},{5,4},{6,7},{7,6},{8,9},{9,8},{10,11... | collective-permute-start | bytes 1572872 | tf_op jit(solution)/shard_map/ppermute | solution.py:81
  77.1 17.4 %collective-permute-start.20 = (f32[1024,128]{1,0:T(8,128)S(1)}, f32[1024,128]{1,0:T(8,128)S(1)}, u32[]{:S(2)}, u32[]{:S(2)}) collective-permute-start(f32[1024,128]{1,0:T(8,128)S(1)} %multiply_add_fusion.4), channel_id=1, source_target_pairs={{0,16},{8,24},{16,0},{24,8},{1,17},{9,25},{17,1},{25,9},{2,18},{10... | collective-permute-start | bytes 1572872 | tf_op jit(solution)/shard_map/ppermute | solution.py:81
  78.8 12.7 %collective-permute-start.21 = (f32[256,128]{1,0:T(8,128)S(1)}, f32[256,128]{1,0:T(8,128)S(1)}, u32[]{:S(2)}, u32[]{:S(2)}) collective-permute-start(f32[256,128]{1,0:T(8,128)S(1)} %get-tuple-element.137), channel_id=1, source_target_pairs={{0,2},{1,3},{2,0},{3,1},{4,6},{5,7},{6,4},{7,5},{8,10},{9,11},{10,... | collective-permute-start | bytes 393224 | tf_op jit(solution)/shard_map/ppermute | solution.py:121
  80.6 12.6 %collective-permute-start.22 = (f32[256,128]{1,0:T(8,128)S(1)}, f32[256,128]{1,0:T(8,128)S(1)}, u32[]{:S(2)}, u32[]{:S(2)}) collective-permute-start(f32[256,128]{1,0:T(8,128)S(1)} %get-tuple-element.136), channel_id=1, source_target_pairs={{0,4},{1,5},{2,6},{3,7},{4,0},{5,1},{6,2},{7,3},{8,12},{9,13},{10,... | collective-permute-start | bytes 393224 | tf_op jit(solution)/shard_map/ppermute | solution.py:121
  80.9 12.3 %collective-permute-start.23 = (f32[256,128]{1,0:T(8,128)S(1)}, f32[256,128]{1,0:T(8,128)S(1)}, u32[]{:S(2)}, u32[]{:S(2)}) collective-permute-start(f32[256,128]{1,0:T(8,128)S(1)} %get-tuple-element.135), channel_id=1, source_target_pairs={{0,6},{1,7},{2,4},{3,5},{4,2},{5,3},{6,0},{7,1},{8,14},{9,15},{10,... | collective-permute-start | bytes 393224 | tf_op jit(solution)/shard_map/ppermute | solution.py:121
  88.9 14.8 %collective-permute-start.29 = (f32[1024,128]{1,0:T(8,128)S(1)}, f32[1024,128]{1,0:T(8,128)S(1)}, u32[]{:S(2)}, u32[]{:S(2)}) collective-permute-start(f32[1024,128]{1,0:T(8,128)S(1)} %multiply_add_fusion.5), channel_id=1, source_target_pairs={{0,1},{1,0},{2,3},{3,2},{4,5},{5,4},{6,7},{7,6},{8,9},{9,8},{10,11... | collective-permute-start | bytes 1572872 | tf_op jit(solution)/shard_map/ppermute | solution.py:81
  94.6 21.0 %collective-permute-start.25 = (f32[1024,128]{1,0:T(8,128)S(1)}, f32[1024,128]{1,0:T(8,128)S(1)}, u32[]{:S(2)}, u32[]{:S(2)}) collective-permute-start(f32[1024,128]{1,0:T(8,128)S(1)} %multiply_add_fusion.2), channel_id=1, source_target_pairs={{0,1},{1,0},{2,3},{3,2},{4,5},{5,4},{6,7},{7,6},{8,9},{9,8},{10,11... | collective-permute-start | bytes 1572872 | tf_op jit(solution)/shard_map/ppermute | solution.py:81
  98.0 11.0 %collective-permute-start.27 = (f32[256,128]{1,0:T(8,128)S(1)}, f32[256,128]{1,0:T(8,128)S(1)}, u32[]{:S(2)}, u32[]{:S(2)}) collective-permute-start(f32[256,128]{1,0:T(8,128)S(1)} %get-tuple-element.132), channel_id=1, source_target_pairs={{0,4},{1,5},{2,6},{3,7},{4,0},{5,1},{6,2},{7,3},{8,12},{9,13},{10,... | collective-permute-start | bytes 393224 | tf_op jit(solution)/shard_map/ppermute | solution.py:121
  98.1 10.9 %collective-permute-start.28 = (f32[256,128]{1,0:T(8,128)S(1)}, f32[256,128]{1,0:T(8,128)S(1)}, u32[]{:S(2)}, u32[]{:S(2)}) collective-permute-start(f32[256,128]{1,0:T(8,128)S(1)} %get-tuple-element.131), channel_id=1, source_target_pairs={{0,6},{1,7},{2,4},{3,5},{4,2},{5,3},{6,0},{7,1},{8,14},{9,15},{10,... | collective-permute-start | bytes 393224 | tf_op jit(solution)/shard_map/ppermute | solution.py:121
  109.1 8.6 %collective-permute-start.33 = (f32[256,128]{1,0:T(8,128)S(1)}, f32[256,128]{1,0:T(8,128)S(1)}, u32[]{:S(2)}, u32[]{:S(2)}) collective-permute-start(f32[256,128]{1,0:T(8,128)S(1)} %get-tuple-element.125), channel_id=1, source_target_pairs={{0,2},{1,3},{2,0},{3,1},{4,6},{5,7},{6,4},{7,5},{8,10},{9,11},{10,... | collective-permute-start | bytes 393224 | tf_op jit(solution)/shard_map/ppermute | solution.py:121
  111.8 13.0 %collective-permute-start.34 = (f32[256,128]{1,0:T(8,128)S(1)}, f32[256,128]{1,0:T(8,128)S(1)}, u32[]{:S(2)}, u32[]{:S(2)}) collective-permute-start(f32[256,128]{1,0:T(8,128)S(1)} %get-tuple-element.124), channel_id=1, source_target_pairs={{0,4},{1,5},{2,6},{3,7},{4,0},{5,1},{6,2},{7,3},{8,12},{9,13},{10,... | collective-permute-start | bytes 393224 | tf_op jit(solution)/shard_map/ppermute | solution.py:121
  111.8 13.0 %collective-permute-start.35 = (f32[256,128]{1,0:T(8,128)S(1)}, f32[256,128]{1,0:T(8,128)S(1)}, u32[]{:S(2)}, u32[]{:S(2)}) collective-permute-start(f32[256,128]{1,0:T(8,128)S(1)} %get-tuple-element.123), channel_id=1, source_target_pairs={{0,6},{1,7},{2,4},{3,5},{4,2},{5,3},{6,0},{7,1},{8,14},{9,15},{10,... | collective-permute-start | bytes 393224 | tf_op jit(solution)/shard_map/ppermute | solution.py:121
  115.7 10.5 %collective-permute-start.30 = (f32[256,128]{1,0:T(8,128)S(1)}, f32[256,128]{1,0:T(8,128)S(1)}, u32[]{:S(2)}, u32[]{:S(2)}) collective-permute-start(f32[256,128]{1,0:T(8,128)S(1)} %get-tuple-element.129), channel_id=1, source_target_pairs={{0,2},{1,3},{2,0},{3,1},{4,6},{5,7},{6,4},{7,5},{8,10},{9,11},{10,... | collective-permute-start | bytes 393224 | tf_op jit(solution)/shard_map/ppermute | solution.py:121
  116.8 17.8 %collective-permute-start.31 = (f32[256,128]{1,0:T(8,128)S(1)}, f32[256,128]{1,0:T(8,128)S(1)}, u32[]{:S(2)}, u32[]{:S(2)}) collective-permute-start(f32[256,128]{1,0:T(8,128)S(1)} %get-tuple-element.128), channel_id=1, source_target_pairs={{0,4},{1,5},{2,6},{3,7},{4,0},{5,1},{6,2},{7,3},{8,12},{9,13},{10,... | collective-permute-start | bytes 393224 | tf_op jit(solution)/shard_map/ppermute | solution.py:121
  117.7 16.9 %collective-permute-start.32 = (f32[256,128]{1,0:T(8,128)S(1)}, f32[256,128]{1,0:T(8,128)S(1)}, u32[]{:S(2)}, u32[]{:S(2)}) collective-permute-start(f32[256,128]{1,0:T(8,128)S(1)} %get-tuple-element.127), channel_id=1, source_target_pairs={{0,6},{1,7},{2,4},{3,5},{4,2},{5,3},{6,0},{7,1},{8,14},{9,15},{10,... | collective-permute-start | bytes 393224 | tf_op jit(solution)/shard_map/ppermute | solution.py:121
  139.6 14.3 %all-to-all-start = ((f32[32,12,128]{2,1,0:T(8,128)}), f32[32,12,128]{2,1,0:T(8,128)S(1)}, u32[]{:S(2)}, u32[]{:S(2)}) async-start(f32[32,12,128]{2,1,0:T(8,128)} %pad_maximum_fusion.4), calls=%async_computation | async-start | bytes 524288 | tf_op jit(solution)/shard_map/all_to_all | solution.py:255
  154.6 9.9 %all-to-all-start.1 = ((f32[32,4,128]{2,1,0:T(4,128)}), f32[32,4,128]{2,1,0:T(4,128)S(1)}, u32[]{:S(2)}, u32[]{:S(2)}) async-start(f32[32,4,128]{2,1,0:T(4,128)} %broadcast_in_dim.35), calls=%async_computation.1 | async-start | bytes 131072 | tf_op jit(solution)/shard_map/all_to_all | solution.py:258
  (8 other events, 38.2 us)

commit v9 on v8

--- a/solution.py
+++ b/solution.py
@@ -66,10 +66,11 @@
     blocks = rows // BLOCK
     return pl.pallas_call(
         functools.partial(local_kernel, scale),
-        out_shape=[jax.ShapeDtypeStruct((BLOCK, width), jnp.float32)] * blocks,
+        out_shape=[jax.ShapeDtypeStruct((BLOCK, width), jnp.float32)] * 4
+        + [jax.ShapeDtypeStruct((rows - 4 * BLOCK, width), jnp.float32)],
         in_specs=[pl.BlockSpec(memory_space=pltpu.SMEM)]
         + [pl.BlockSpec(memory_space=pltpu.VMEM)] * 2,
-        out_specs=[pl.BlockSpec(memory_space=pltpu.VMEM)] * blocks,
+        out_specs=[pl.BlockSpec(memory_space=pltpu.VMEM)] * 5,
         scratch_shapes=[pltpu.VMEM((blocks, BLOCK, width), jnp.float32)],
         compiler_params=pltpu.CompilerParams(vmem_limit_bytes=32 * 2**20),
     )(turns, flips.reshape(rows // 128, 128), panel)
@@ -115,11 +116,11 @@
 
 def turn(parts, low):
     size = lax.axis_size("wide")
-    sent = [parts[0]]
-    for j in (1, 2, 3):
+    sent = {0: parts[0]}
+    for j in (3, 2, 1):
         pairs = [(source, source ^ j * low) for source in range(size)]
-        sent.append(lax.ppermute(parts[j], "wide", pairs))
-    return sent
+        sent[j] = lax.ppermute(parts[j], "wide", pairs)
+    return [sent[j] for j in range(4)]
 
 
 def sums_of_four(parts, turns, whole_turn):
@@ -210,40 +211,58 @@
     most = -(-per // devices)
     count = rows_here // (4 * BLOCK)
 
-    blocks = local_transform(panel, flips, jnp.stack(turns), scale)
+    *chunk, rest = local_transform(panel, flips, jnp.stack(turns), scale)
     chain = Chain()
+
+    def pieces(value):
+        return [value[j * BLOCK : (j + 1) * BLOCK] for j in range(value.shape[0] // BLOCK)]
+
+    def arrive(parts):
+        return lax.optimization_barrier((list(parts), chain.last))[0]
+
+    def gather_z(parts):
+        chain.last = sums_of_four(arrive(parts), real_turns, whole_turn)
+        return chain.last
+
+    away = [turn(chunk, low)]
+    sent_rest = chain.begin(rest, core)
     wanted = send_rows(picks, [me], rows_here, devices, most)
     spots = landing(lax.dynamic_slice(picks, (me * per,), (per,)), rows_here, most)
-    away = [turn(blocks[4 * i : 4 * i + 4], low) for i in range(count)]
-    sent_core, sent_first, sent_second, back = {}, {}, {}, {}
+    rest = pieces(chain.end(sent_rest))
+    away += [turn(rest[4 * i : 4 * i + 4], low) for i in range(count - 1)]
+
+    back, one, two = {}, {}, {}
     whole = None
 
-    def arrive(parts):
-        out = lax.optimization_barrier((list(parts), chain.last))[0]
-        return out
-
-    for step in range(2 * count):
-        if step < count:
-            value = sums_of_four(arrive(away[step]), real_turns, whole_turn)
-            chain.last = value
-            sent_core[step] = chain.begin(value, core)
-        i = step - 4
-        if 0 <= i < count:
-            ats = jnp.stack([((place ^ j) + 4 * i) * BLOCK for j in range(4)])
-            whole = store(whole, arrive(back[i]), ats.astype(jnp.int32), rows_here)
-            chain.last = whole
-        i = step - 1
-        if 0 <= i < count:
-            sent_second[i] = chain.begin(chain.end(sent_first[i]), second)
-        if step < count:
-            sent_first[step] = chain.begin(chain.end(sent_core[step]), first)
-        i = step - 2
-        if 0 <= i < count:
-            value = chain.end(sent_second[i])
-            back[i] = turn([value[j * BLOCK : (j + 1) * BLOCK] for j in range(4)], low)
+    def keep(i):
+        nonlocal whole
+        ats = jnp.stack([((place ^ j) + 4 * i) * BLOCK for j in range(4)])
+        back[i] = arrive(back[i])
+        whole = store(whole, back[i], ats.astype(jnp.int32), rows_here)
+        chain.last = whole
+
+    one[0] = chain.begin(gather_z(away[0]), first)
+    one[1] = chain.begin(gather_z(away[1]), first)
+    two[0] = chain.begin(chain.end(one[0]), second)
+    one[2] = chain.begin(gather_z(away[2]), first)
+    chain.last = (chain.last, wanted, spots)
+    two[1] = chain.begin(chain.end(one[1]), second)
+    sent0 = chain.begin(chain.end(two[0]), core)
+    one[3] = chain.begin(gather_z(away[3]), first)
+    back[0] = turn(pieces(chain.end(sent0)), low)
+    two[2] = chain.begin(chain.end(one[2]), second)
+    keep(0)
+    back[1] = turn(pieces(chain.end(two[1])), low)
+    two[3] = chain.begin(chain.end(one[3]), second)
+    back[2] = turn(pieces(chain.end(two[2])), low)
+    keep(1)
+    back[3] = turn(pieces(chain.end(two[3])), low)
+    keep(2)
+    keep(3)
 
     filled = wanted >= 0
-    chosen = jnp.take(whole, wanted, axis=0, mode="clip")
+    held = jnp.concatenate([part for i in range(count) for part in back[i]], axis=0)
+    chosen = jnp.take(held, wanted ^ place * BLOCK, axis=0, mode="clip")
     kept = jnp.where(filled[:, None], chosen, 0.0)
     part = lax.dot_general(
         kept, kept, (((0,), (0,)), ((), ())),

time: 166 us -> 162 us (0.976)
  starting transfers between devices: 56.9 us -> 63 us
  other arithmetic: 11.6 us -> 6.04 us
  waiting for transfers between devices: 78.5 us -> 75.3 us
    ppermute x24, starting transfers between devices: 38.8 us -> 43.3 us  [turn(): sent[j] = lax.ppermute(parts[j], 'wide', pairs)]
    add x12 -> x10, other arithmetic: 5.86 us -> 2.1 us  [end(): self.last = partner + sign_of(stage) * value]
    ppermute x24, waiting for transfers between devices: 45.7 us -> 42.7 us  [turn(): sent[j] = lax.ppermute(parts[j], 'wide', pairs)]
    concatenate x4, other arithmetic: 2.52 us -> 0.15 us  [sums_of_four(): jnp.concatenate([out * (turns[j] * whole_turn) for j, out in enumerate(ou...]
    mul x4, other arithmetic: 0.32 us -> 2.25 us  [sums_of_four(): out * (turns[j] * whole_turn)]
    ppermute x12 -> x10, waiting for transfers between devices: 17.2 us -> 17.5 us  [launch(): return (lax.ppermute(value, axis, pairs), value, stage)]
    ppermute x12 -> x10, starting transfers between devices: 11.8 us -> 12 us  [launch(): return (lax.ppermute(value, axis, pairs), value, stage)]
  transfers between devices with their start and end apart: 38 -> 36, of which waited for: 16 -> 15; matrix products, arithmetic and copies ran while one was open for 8% -> 5% of each run, Pallas kernels for 3% -> 4%
where the time goes in v9:
time: 162 us; the launch traced here: 161 us
  waiting for transfers between devices  75.3 us (46%)
  starting transfers between devices  63 us (39%)
  Pallas kernels  8.24 us (5%)
  local copies, waits for them, and re-layouts  7 us (4%)
  other arithmetic  6.04 us (4%)
    ppermute x24, starting transfers between devices, turn(): sent[j] = lax.ppermute(parts[j], 'wide', pairs)  43.3 us
    ppermute x24, waiting for transfers between devices, turn(): sent[j] = lax.ppermute(parts[j], 'wide', pairs)  42.7 us
    ppermute x10, waiting for transfers between devices, launch(): return (lax.ppermute(value, axis, pairs), value, stage)  17.5 us
    ppermute x10, starting transfers between devices, launch(): return (lax.ppermute(value, axis, pairs), value, stage)  12 us
    all_to_all x1, waiting for transfers between devices, on_device(): landed = lax.all_to_all(both, AXES, 0, 0, tiled=True)  9.18 us
    all_to_all x1, waiting for transfers between devices, on_device(): gram = lax.all_to_all(shared, AXES, 0, 0, tiled=True).reshape(width, width)  5.91 us
    pallas_call x4, Pallas kernels, store(): pl.pallas_call(store_kernel, out_shape=jax.ShapeDtypeStruct((rows, values...  5.45 us
    all_to_all x1, starting transfers between devices, on_device(): landed = lax.all_to_all(both, AXES, 0, 0, tiled=True)  5.13 us
  transfers between devices with their start and end apart: 36, of which 15 were waited for; matrix products, arithmetic and copies ran while one was open for 5% of the time, Pallas kernels for 4%

profile of v9, /device:TPU:0, one launch (start us, length us, event | category | flops | bytes accessed | tf_op | source)
XLA Modules:
  0.0 161.1 jit_solution(6893675249649517734)
XLA Ops:
  0.7 1.6 copy-done
  3.1 2.5 %shard_map.58 = (f32[256,128]{1,0:T(8,128)S(1)}, f32[256,128]{1,0:T(8,128)S(1)}, f32[256,128]{1,0:T(8,128)S(1)}, f32[256,128]{1,0:T(8,128)S(1)}, f32[3072,128]{1,0:T(8,128)S(1)}) custom-call(s32[4]{0:T(128)S(1)} %pad_add_fusion.1.turns_ref, s32[32,128]{1,0:T(8,128)S(1)} %bitcast.26, f32[4096,128]{1,0:T(8,128)S(1)} %copy-done), custom_call_target="tpu_custom_call" | custom-call | tf_op jit(solution)/shard_map/pallas_call | solution.py:67
  6.1 2.6 %collective-permute-start.4 = (f32[256,128]{1,0:T(8,128)S(1)}, f32[256,128]{1,0:T(8,128)S(1)}, u32[]{:S(2)}, u32[]{:S(2)}) collective-permute-start(f32[256,128]{1,0:T(8,128)S(1)} %get-tuple-element.51), channel_id=1, source_target_pairs={{0,2},{1,3},{2,0},{3,1},{4,6},{5,7},{6,4},{7,5},{8,10},{9,11},{10,... | collective-permute-start | bytes 393224 | tf_op jit(solution)/shard_map/ppermute | solution.py:122
  8.8 2.6 %collective-permute-start.5 = (f32[256,128]{1,0:T(8,128)S(1)}, f32[256,128]{1,0:T(8,128)S(1)}, u32[]{:S(2)}, u32[]{:S(2)}) collective-permute-start(f32[256,128]{1,0:T(8,128)S(1)} %get-tuple-element.52), channel_id=1, source_target_pairs={{0,4},{1,5},{2,6},{3,7},{4,0},{5,1},{6,2},{7,3},{8,12},{9,13},{10,... | collective-permute-start | bytes 393224 | tf_op jit(solution)/shard_map/ppermute | solution.py:122
  12.0 1.6 multiply_add_fusion
  15.0 6.6 %collective-permute-done.5 = f32[256,128]{1,0:T(8,128)S(1)} collective-permute-done((f32[256,128]{1,0:T(8,128)S(1)}, f32[256,128]{1,0:T(8,128)S(1)}, u32[]{:S(2)}, u32[]{:S(2)}) %collective-permute-start.5) | collective-permute-done | bytes 131104 | tf_op jit(solution)/shard_map/ppermute | solution.py:122
  21.7 2.5 %collective-permute-start.10 = (f32[256,128]{1,0:T(8,128)S(1)}, f32[256,128]{1,0:T(8,128)}, u32[]{:S(2)}, u32[]{:S(2)}) collective-permute-start(f32[256,128]{1,0:T(8,128)S(1)} %get-tuple-element.99), channel_id=1, source_target_pairs={{0,6},{1,7},{2,4},{3,5},{4,2},{5,3},{6,0},{7,1},{8,14},{9,15},{10,... | collective-permute-start | bytes 393224 | tf_op jit(solution)/shard_map/ppermute | solution.py:122
  24.1 1.7 %collective-permute-start.8 = (f32[256,128]{1,0:T(8,128)S(1)}, f32[256,128]{1,0:T(8,128)}, u32[]{:S(2)}, u32[]{:S(2)}) collective-permute-start(f32[256,128]{1,0:T(8,128)S(1)} %get-tuple-element.101), channel_id=1, source_target_pairs={{0,2},{1,3},{2,0},{3,1},{4,6},{5,7},{6,4},{7,5},{8,10},{9,11},{10,... | collective-permute-start | bytes 393224 | tf_op jit(solution)/shard_map/ppermute | solution.py:122
  26.2 1.6 collective-permute-start.7
  27.9 1.7 %collective-permute-start.13 = (f32[256,128]{1,0:T(8,128)S(1)}, f32[256,128]{1,0:T(8,128)S(1)}, u32[]{:S(2)}, u32[]{:S(2)}) collective-permute-start(f32[256,128]{1,0:T(8,128)S(1)} %get-tuple-element.97), channel_id=1, source_target_pairs={{0,2},{1,3},{2,0},{3,1},{4,6},{5,7},{6,4},{7,5},{8,10},{9,11},{10,... | collective-permute-start | bytes 393224 | tf_op jit(solution)/shard_map/ppermute | solution.py:122
  30.0 4.6 %collective-permute-start.14 = (f32[256,128]{1,0:T(8,128)S(1)}, f32[256,128]{1,0:T(8,128)S(1)}, u32[]{:S(2)}, u32[]{:S(2)}) collective-permute-start(f32[256,128]{1,0:T(8,128)S(1)} %get-tuple-element.96), channel_id=1, source_target_pairs={{0,4},{1,5},{2,6},{3,7},{4,0},{5,1},{6,2},{7,3},{8,12},{9,13},{10,... | collective-permute-start | bytes 393224 | tf_op jit(solution)/shard_map/ppermute | solution.py:122
  36.0 5.5 %collective-permute-done.9 = f32[256,128]{1,0:T(8,128)} collective-permute-done((f32[256,128]{1,0:T(8,128)S(1)}, f32[256,128]{1,0:T(8,128)}, u32[]{:S(2)}, u32[]{:S(2)}) %collective-permute-start.9) | collective-permute-done | bytes 131104 | tf_op jit(solution)/shard_map/ppermute | solution.py:122
  42.7 1.6 collective-permute-start.12
  44.3 3.1 %collective-permute-start.2 = (f32[256,128]{1,0:T(8,128)}, f32[256,128]{1,0:T(8,128)S(1)}, u32[]{:S(2)}, u32[]{:S(2)}) collective-permute-start(f32[256,128]{1,0:T(8,128)} %get-tuple-element.104), channel_id=1, source_target_pairs={{0,4},{1,5},{2,6},{3,7},{4,0},{5,1},{6,2},{7,3},{8,12},{9,13},{10,... | collective-permute-start | bytes 393224 | tf_op jit(solution)/shard_map/ppermute | solution.py:122
  47.4 1.9 %collective-permute-start.3 = (f32[256,128]{1,0:T(8,128)S(1)}, f32[256,128]{1,0:T(8,128)S(1)}, u32[]{:S(2)}, u32[]{:S(2)}) collective-permute-start(f32[256,128]{1,0:T(8,128)S(1)} %get-tuple-element.103), channel_id=1, source_target_pairs={{0,6},{1,7},{2,4},{3,5},{4,2},{5,3},{6,0},{7,1},{8,14},{9,15},{10,... | collective-permute-start | bytes 393224 | tf_op jit(solution)/shard_map/ppermute | solution.py:122
  49.3 1.6 collective-permute-start.11
  52.0 6.6 %collective-permute-done.11 = f32[1024,128]{1,0:T(8,128)S(1)} collective-permute-done((f32[1024,128]{1,0:T(8,128)S(1)}, f32[1024,128]{1,0:T(8,128)S(1)}, u32[]{:S(2)}, u32[]{:S(2)}) %collective-permute-start.11) | collective-permute-done | bytes 524320 | tf_op jit(solution)/shard_map/ppermute | solution.py:82
  59.0 1.6 collective-permute-start.22
  63.8 10.0 %collective-permute-done.22 = f32[1024,128]{1,0:T(8,128)S(1)} collective-permute-done((f32[1024,128]{1,0:T(8,128)S(1)}, f32[1024,128]{1,0:T(8,128)S(1)}, u32[]{:S(2)}, u32[]{:S(2)}) %collective-permute-start.22) | collective-permute-done | bytes 524320 | tf_op jit(solution)/shard_map/ppermute | solution.py:82
  73.8 4.9 %collective-permute-start.19 = (f32[256,128]{1,0:T(8,128)S(1)}, f32[256,128]{1,0:T(8,128)S(1)}, u32[]{:S(2)}, u32[]{:S(2)}) collective-permute-start(f32[256,128]{1,0:T(8,128)S(1)} %get-tuple-element.121), channel_id=1, source_target_pairs={{0,2},{1,3},{2,0},{3,1},{4,6},{5,7},{6,4},{7,5},{8,10},{9,11},{10,... | collective-permute-start | bytes 393224 | tf_op jit(solution)/shard_map/ppermute | solution.py:122
  81.4 1.7 %collective-permute-done.19.refs_1_ = f32[256,128]{1,0:T(8,128)S(1)} collective-permute-done((f32[256,128]{1,0:T(8,128)S(1)}, f32[256,128]{1,0:T(8,128)S(1)}, u32[]{:S(2)}, u32[]{:S(2)}) %collective-permute-start.19) | collective-permute-done | bytes 131104 | tf_op jit(solution)/shard_map/ppermute | solution.py:122
  84.6 6.5 %collective-permute-done.20.refs_2_ = f32[256,128]{1,0:T(8,128)S(1)} collective-permute-done((f32[256,128]{1,0:T(8,128)S(1)}, f32[256,128]{1,0:T(8,128)S(1)}, u32[]{:S(2)}, u32[]{:S(2)}) %collective-permute-start.20) | collective-permute-done | bytes 131104 | tf_op jit(solution)/shard_map/ppermute | solution.py:122
  92.7 2.0 %collective-permute-start.24 = (f32[256,128]{1,0:T(8,128)S(1)}, f32[256,128]{1,0:T(8,128)S(1)}, u32[]{:S(2)}, u32[]{:S(2)}) collective-permute-start(f32[256,128]{1,0:T(8,128)S(1)} %get-tuple-element.117), channel_id=1, source_target_pairs={{0,2},{1,3},{2,0},{3,1},{4,6},{5,7},{6,4},{7,5},{8,10},{9,11},{10,... | collective-permute-start | bytes 393224 | tf_op jit(solution)/shard_map/ppermute | solution.py:122
  99.1 7.8 %collective-permute-done.25.refs_2_ = f32[256,128]{1,0:T(8,128)S(1)} collective-permute-done((f32[256,128]{1,0:T(8,128)S(1)}, f32[256,128]{1,0:T(8,128)S(1)}, u32[]{:S(2)}, u32[]{:S(2)}) %collective-permute-start.25) | collective-permute-done | bytes 131104 | tf_op jit(solution)/shard_map/ppermute | solution.py:122
  106.9 2.0 %collective-permute-start.31 = (f32[256,128]{1,0:T(8,128)S(1)}, f32[256,128]{1,0:T(8,128)S(1)}, u32[]{:S(2)}, u32[]{:S(2)}) collective-permute-start(f32[256,128]{1,0:T(8,128)S(1)} %get-tuple-element.109), channel_id=1, source_target_pairs={{0,2},{1,3},{2,0},{3,1},{4,6},{5,7},{6,4},{7,5},{8,10},{9,11},{10,... | collective-permute-start | bytes 393224 | tf_op jit(solution)/shard_map/ppermute | solution.py:122
  114.0 1.9 %collective-permute-start.29 = (f32[256,128]{1,0:T(8,128)S(1)}, f32[256,128]{1,0:T(8,128)S(1)}, u32[]{:S(2)}, u32[]{:S(2)}) collective-permute-start(f32[256,128]{1,0:T(8,128)S(1)} %get-tuple-element.112), channel_id=1, source_target_pairs={{0,4},{1,5},{2,6},{3,7},{4,0},{5,1},{6,2},{7,3},{8,12},{9,13},{10,... | collective-permute-start | bytes 393224 | tf_op jit(solution)/shard_map/ppermute | solution.py:122
  117.3 4.4 %collective-permute-done.32.refs_2_ = f32[256,128]{1,0:T(8,128)S(1)} collective-permute-done((f32[256,128]{1,0:T(8,128)S(1)}, f32[256,128]{1,0:T(8,128)S(1)}, u32[]{:S(2)}, u32[]{:S(2)}) %collective-permute-start.32) | collective-permute-done | bytes 131104 | tf_op jit(solution)/shard_map/ppermute | solution.py:122
  123.2 8.9 %collective-permute-done.29.refs_2_ = f32[256,128]{1,0:T(8,128)S(1)} collective-permute-done((f32[256,128]{1,0:T(8,128)S(1)}, f32[256,128]{1,0:T(8,128)S(1)}, u32[]{:S(2)}, u32[]{:S(2)}) %collective-permute-start.29) | collective-permute-done | bytes 131104 | tf_op jit(solution)/shard_map/ppermute | solution.py:122
  134.2 5.1 %all-to-all-start = ((f32[32,12,128]{2,1,0:T(8,128)}), f32[32,12,128]{2,1,0:T(8,128)S(1)}, u32[]{:S(2)}, u32[]{:S(2)}) async-start(f32[32,12,128]{2,1,0:T(8,128)} %pad_maximum_fusion.4), calls=%async_computation | async-start | bytes 524288 | tf_op jit(solution)/shard_map/all_to_all | solution.py:274
  140.8 9.2 %all-to-all-done = f32[32,12,128]{2,1,0:T(8,128)S(1)} async-done(((f32[32,12,128]{2,1,0:T(8,128)}), f32[32,12,128]{2,1,0:T(8,128)S(1)}, u32[]{:S(2)}, u32[]{:S(2)}) %all-to-all-start) | async-done | bytes 196640 | tf_op jit(solution)/shard_map/all_to_all | solution.py:274
  150.7 2.6 %all-to-all-start.1 = ((f32[32,4,128]{2,1,0:T(4,128)}), f32[32,4,128]{2,1,0:T(4,128)S(1)}, u32[]{:S(2)}, u32[]{:S(2)}) async-start(f32[32,4,128]{2,1,0:T(4,128)} %broadcast_in_dim.32), calls=%async_computation.1 | async-start | bytes 131072 | tf_op jit(solution)/shard_map/all_to_all | solution.py:277
  154.6 5.9 %all-to-all-done.1 = f32[32,4,128]{2,1,0:T(4,128)S(1)} async-done(((f32[32,4,128]{2,1,0:T(4,128)}), f32[32,4,128]{2,1,0:T(4,128)S(1)}, u32[]{:S(2)}, u32[]{:S(2)}) %all-to-all-start.1) | async-done | bytes 65568 | tf_op jit(solution)/shard_map/all_to_all | solution.py:277
  (115 shorter events, 35.7 us)
Async XLA Ops:
  6.1 8.9 %collective-permute-start.4 = (f32[256,128]{1,0:T(8,128)S(1)}, f32[256,128]{1,0:T(8,128)S(1)}, u32[]{:S(2)}, u32[]{:S(2)}) collective-permute-start(f32[256,128]{1,0:T(8,128)S(1)} %get-tuple-element.51), channel_id=1, source_target_pairs={{0,2},{1,3},{2,0},{3,1},{4,6},{5,7},{6,4},{7,5},{8,10},{9,11},{10,... | collective-permute-start | bytes 393224 | tf_op jit(solution)/shard_map/ppermute | solution.py:122
  8.8 12.9 %collective-permute-start.5 = (f32[256,128]{1,0:T(8,128)S(1)}, f32[256,128]{1,0:T(8,128)S(1)}, u32[]{:S(2)}, u32[]{:S(2)}) collective-permute-start(f32[256,128]{1,0:T(8,128)S(1)} %get-tuple-element.52), channel_id=1, source_target_pairs={{0,4},{1,5},{2,6},{3,7},{4,0},{5,1},{6,2},{7,3},{8,12},{9,13},{10,... | collective-permute-start | bytes 393224 | tf_op jit(solution)/shard_map/ppermute | solution.py:122
  11.3 10.3 %collective-permute-start.6 = (f32[256,128]{1,0:T(8,128)S(1)}, f32[256,128]{1,0:T(8,128)S(1)}, u32[]{:S(2)}, u32[]{:S(2)}) collective-permute-start(f32[256,128]{1,0:T(8,128)S(1)} %get-tuple-element.53), channel_id=1, source_target_pairs={{0,6},{1,7},{2,4},{3,5},{4,2},{5,3},{6,0},{7,1},{8,14},{9,15},{10,... | collective-permute-start | bytes 393224 | tf_op jit(solution)/shard_map/ppermute | solution.py:122
  24.1 10.5 %collective-permute-start.8 = (f32[256,128]{1,0:T(8,128)S(1)}, f32[256,128]{1,0:T(8,128)}, u32[]{:S(2)}, u32[]{:S(2)}) collective-permute-start(f32[256,128]{1,0:T(8,128)S(1)} %get-tuple-element.101), channel_id=1, source_target_pairs={{0,2},{1,3},{2,0},{3,1},{4,6},{5,7},{6,4},{7,5},{8,10},{9,11},{10,... | collective-permute-start | bytes 393224 | tf_op jit(solution)/shard_map/ppermute | solution.py:122
  25.8 15.7 %collective-permute-start.9 = (f32[256,128]{1,0:T(8,128)S(1)}, f32[256,128]{1,0:T(8,128)}, u32[]{:S(2)}, u32[]{:S(2)}) collective-permute-start(f32[256,128]{1,0:T(8,128)S(1)} %get-tuple-element.100), channel_id=1, source_target_pairs={{0,4},{1,5},{2,6},{3,7},{4,0},{5,1},{6,2},{7,3},{8,12},{9,13},{10,... | collective-permute-start | bytes 393224 | tf_op jit(solution)/shard_map/ppermute | solution.py:122
  26.2 16.5 %collective-permute-start.7 = (f32[1024,128]{1,0:T(8,128)S(1)}, f32[1024,128]{1,0:T(8,128)S(1)}, u32[]{:S(2)}, u32[]{:S(2)}) collective-permute-start(f32[1024,128]{1,0:T(8,128)S(1)} %pad_maximum_fusion), channel_id=1, source_target_pairs={{0,16},{8,24},{16,0},{24,8},{1,17},{9,25},{17,1},{25,9},{2,18},{10... | collective-permute-start | bytes 1572872 | tf_op jit(solution)/shard_map/ppermute | solution.py:82
  27.9 16.4 %collective-permute-start.13 = (f32[256,128]{1,0:T(8,128)S(1)}, f32[256,128]{1,0:T(8,128)S(1)}, u32[]{:S(2)}, u32[]{:S(2)}) collective-permute-start(f32[256,128]{1,0:T(8,128)S(1)} %get-tuple-element.97), channel_id=1, source_target_pairs={{0,2},{1,3},{2,0},{3,1},{4,6},{5,7},{6,4},{7,5},{8,10},{9,11},{10,... | collective-permute-start | bytes 393224 | tf_op jit(solution)/shard_map/ppermute | solution.py:122
  30.0 17.4 %collective-permute-start.14 = (f32[256,128]{1,0:T(8,128)S(1)}, f32[256,128]{1,0:T(8,128)S(1)}, u32[]{:S(2)}, u32[]{:S(2)}) collective-permute-start(f32[256,128]{1,0:T(8,128)S(1)} %get-tuple-element.96), channel_id=1, source_target_pairs={{0,4},{1,5},{2,6},{3,7},{4,0},{5,1},{6,2},{7,3},{8,12},{9,13},{10,... | collective-permute-start | bytes 393224 | tf_op jit(solution)/shard_map/ppermute | solution.py:122
  34.7 14.7 %collective-permute-start.15 = (f32[256,128]{1,0:T(8,128)S(1)}, f32[256,128]{1,0:T(8,128)S(1)}, u32[]{:S(2)}, u32[]{:S(2)}) collective-permute-start(f32[256,128]{1,0:T(8,128)S(1)} %get-tuple-element.95), channel_id=1, source_target_pairs={{0,6},{1,7},{2,4},{3,5},{4,2},{5,3},{6,0},{7,1},{8,14},{9,15},{10,... | collective-permute-start | bytes 393224 | tf_op jit(solution)/shard_map/ppermute | solution.py:122
  41.5 19.1 %collective-permute-start.1 = (f32[256,128]{1,0:T(8,128)}, f32[256,128]{1,0:T(8,128)}, u32[]{:S(2)}, u32[]{:S(2)}) collective-permute-start(f32[256,128]{1,0:T(8,128)} %get-tuple-element.105), channel_id=1, source_target_pairs={{0,2},{1,3},{2,0},{3,1},{4,6},{5,7},{6,4},{7,5},{8,10},{9,11},{10,... | collective-permute-start | bytes 393224 | tf_op jit(solution)/shard_map/ppermute | solution.py:122
  42.7 9.2 %collective-permute-start.12 = (f32[1024,128]{1,0:T(8,128)S(1)}, f32[1024,128]{1,0:T(8,128)S(1)}, u32[]{:S(2)}, u32[]{:S(2)}) collective-permute-start(f32[1024,128]{1,0:T(8,128)S(1)} %pad_maximum_fusion.1), channel_id=1, source_target_pairs={{0,16},{8,24},{16,0},{24,8},{1,17},{9,25},{17,1},{25,9},{2,18},{10... | collective-permute-start | bytes 1572872 | tf_op jit(solution)/shard_map/ppermute | solution.py:82
  44.3 17.8 %collective-permute-start.2 = (f32[256,128]{1,0:T(8,128)}, f32[256,128]{1,0:T(8,128)S(1)}, u32[]{:S(2)}, u32[]{:S(2)}) collective-permute-start(f32[256,128]{1,0:T(8,128)} %get-tuple-element.104), channel_id=1, source_target_pairs={{0,4},{1,5},{2,6},{3,7},{4,0},{5,1},{6,2},{7,3},{8,12},{9,13},{10,... | collective-permute-start | bytes 393224 | tf_op jit(solution)/shard_map/ppermute | solution.py:122
  47.4 14.7 %collective-permute-start.3 = (f32[256,128]{1,0:T(8,128)S(1)}, f32[256,128]{1,0:T(8,128)S(1)}, u32[]{:S(2)}, u32[]{:S(2)}) collective-permute-start(f32[256,128]{1,0:T(8,128)S(1)} %get-tuple-element.103), channel_id=1, source_target_pairs={{0,6},{1,7},{2,4},{3,5},{4,2},{5,3},{6,0},{7,1},{8,14},{9,15},{10,... | collective-permute-start | bytes 393224 | tf_op jit(solution)/shard_map/ppermute | solution.py:122
  49.3 9.3 %collective-permute-start.11 = (f32[1024,128]{1,0:T(8,128)S(1)}, f32[1024,128]{1,0:T(8,128)S(1)}, u32[]{:S(2)}, u32[]{:S(2)}) collective-permute-start(f32[1024,128]{1,0:T(8,128)S(1)} %multiply_add_fusion.9), channel_id=1, source_target_pairs={{0,1},{1,0},{2,3},{3,2},{4,5},{5,4},{6,7},{7,6},{8,9},{9,8},{10,11... | collective-permute-start | bytes 1572872 | tf_op jit(solution)/shard_map/ppermute | solution.py:82
  59.0 14.8 %collective-permute-start.22 = (f32[1024,128]{1,0:T(8,128)S(1)}, f32[1024,128]{1,0:T(8,128)S(1)}, u32[]{:S(2)}, u32[]{:S(2)}) collective-permute-start(f32[1024,128]{1,0:T(8,128)S(1)} %pad_maximum_fusion.2), channel_id=1, source_target_pairs={{0,16},{8,24},{16,0},{24,8},{1,17},{9,25},{17,1},{25,9},{2,18},{10... | collective-permute-start | bytes 1572872 | tf_op jit(solution)/shard_map/ppermute | solution.py:82
  60.6 31.9 %collective-permute-start.17 = (f32[1024,128]{1,0:T(8,128)S(1)}, f32[1024,128]{1,0:T(8,128)S(1)}, u32[]{:S(2)}, u32[]{:S(2)}) collective-permute-start(f32[1024,128]{1,0:T(8,128)S(1)} %multiply_add_fusion.8), channel_id=1, source_target_pairs={{0,1},{1,0},{2,3},{3,2},{4,5},{5,4},{6,7},{7,6},{8,9},{9,8},{10,11... | collective-permute-start | bytes 1572872 | tf_op jit(solution)/shard_map/ppermute | solution.py:82
  63.2 29.4 %collective-permute-start.16 = (f32[1024,128]{1,0:T(8,128)S(1)}, f32[1024,128]{1,0:T(8,128)S(1)}, u32[]{:S(2)}, u32[]{:S(2)}) collective-permute-start(f32[1024,128]{1,0:T(8,128)S(1)} %pad_maximum_fusion.3), channel_id=1, source_target_pairs={{0,16},{8,24},{16,0},{24,8},{1,17},{9,25},{17,1},{25,9},{2,18},{10... | collective-permute-start | bytes 1572872 | tf_op jit(solution)/shard_map/ppermute | solution.py:82
  73.8 9.3 %collective-permute-start.19 = (f32[256,128]{1,0:T(8,128)S(1)}, f32[256,128]{1,0:T(8,128)S(1)}, u32[]{:S(2)}, u32[]{:S(2)}) collective-permute-start(f32[256,128]{1,0:T(8,128)S(1)} %get-tuple-element.121), channel_id=1, source_target_pairs={{0,2},{1,3},{2,0},{3,1},{4,6},{5,7},{6,4},{7,5},{8,10},{9,11},{10,... | collective-permute-start | bytes 393224 | tf_op jit(solution)/shard_map/ppermute | solution.py:122
  78.7 12.4 %collective-permute-start.20 = (f32[256,128]{1,0:T(8,128)S(1)}, f32[256,128]{1,0:T(8,128)S(1)}, u32[]{:S(2)}, u32[]{:S(2)}) collective-permute-start(f32[256,128]{1,0:T(8,128)S(1)} %get-tuple-element.120), channel_id=1, source_target_pairs={{0,4},{1,5},{2,6},{3,7},{4,0},{5,1},{6,2},{7,3},{8,12},{9,13},{10,... | collective-permute-start | bytes 393224 | tf_op jit(solution)/shard_map/ppermute | solution.py:122
  79.8 11.3 %collective-permute-start.21 = (f32[256,128]{1,0:T(8,128)S(1)}, f32[256,128]{1,0:T(8,128)S(1)}, u32[]{:S(2)}, u32[]{:S(2)}) collective-permute-start(f32[256,128]{1,0:T(8,128)S(1)} %get-tuple-element.119), channel_id=1, source_target_pairs={{0,6},{1,7},{2,4},{3,5},{4,2},{5,3},{6,0},{7,1},{8,14},{9,15},{10,... | collective-permute-start | bytes 393224 | tf_op jit(solution)/shard_map/ppermute | solution.py:122
  83.1 15.8 %collective-permute-start.27 = (f32[1024,128]{1,0:T(8,128)S(1)}, f32[1024,128]{1,0:T(8,128)S(1)}, u32[]{:S(2)}, u32[]{:S(2)}) collective-permute-start(f32[1024,128]{1,0:T(8,128)S(1)} %multiply_add_fusion.5), channel_id=1, source_target_pairs={{0,1},{1,0},{2,3},{3,2},{4,5},{5,4},{6,7},{7,6},{8,9},{9,8},{10,11... | collective-permute-start | bytes 1572872 | tf_op jit(solution)/shard_map/ppermute | solution.py:82
  94.7 12.2 %collective-permute-start.25 = (f32[256,128]{1,0:T(8,128)S(1)}, f32[256,128]{1,0:T(8,128)S(1)}, u32[]{:S(2)}, u32[]{:S(2)}) collective-permute-start(f32[256,128]{1,0:T(8,128)S(1)} %get-tuple-element.116), channel_id=1, source_target_pairs={{0,4},{1,5},{2,6},{3,7},{4,0},{5,1},{6,2},{7,3},{8,12},{9,13},{10,... | collective-permute-start | bytes 393224 | tf_op jit(solution)/shard_map/ppermute | solution.py:122
  95.9 11.0 %collective-permute-start.26 = (f32[256,128]{1,0:T(8,128)S(1)}, f32[256,128]{1,0:T(8,128)S(1)}, u32[]{:S(2)}, u32[]{:S(2)}) collective-permute-start(f32[256,128]{1,0:T(8,128)S(1)} %get-tuple-element.115), channel_id=1, source_target_pairs={{0,6},{1,7},{2,4},{3,5},{4,2},{5,3},{6,0},{7,1},{8,14},{9,15},{10,... | collective-permute-start | bytes 393224 | tf_op jit(solution)/shard_map/ppermute | solution.py:122
  97.3 15.5 %collective-permute-start.23 = (f32[1024,128]{1,0:T(8,128)S(1)}, f32[1024,128]{1,0:T(8,128)S(1)}, u32[]{:S(2)}, u32[]{:S(2)}) collective-permute-start(f32[1024,128]{1,0:T(8,128)S(1)} %multiply_add_fusion.3), channel_id=1, source_target_pairs={{0,1},{1,0},{2,3},{3,2},{4,5},{5,4},{6,7},{7,6},{8,9},{9,8},{10,11... | collective-permute-start | bytes 1572872 | tf_op jit(solution)/shard_map/ppermute | solution.py:82
  106.9 9.0 %collective-permute-start.31 = (f32[256,128]{1,0:T(8,128)S(1)}, f32[256,128]{1,0:T(8,128)S(1)}, u32[]{:S(2)}, u32[]{:S(2)}) collective-permute-start(f32[256,128]{1,0:T(8,128)S(1)} %get-tuple-element.109), channel_id=1, source_target_pairs={{0,2},{1,3},{2,0},{3,1},{4,6},{5,7},{6,4},{7,5},{8,10},{9,11},{10,... | collective-permute-start | bytes 393224 | tf_op jit(solution)/shard_map/ppermute | solution.py:122
  108.9 12.9 %collective-permute-start.32 = (f32[256,128]{1,0:T(8,128)S(1)}, f32[256,128]{1,0:T(8,128)S(1)}, u32[]{:S(2)}, u32[]{:S(2)}) collective-permute-start(f32[256,128]{1,0:T(8,128)S(1)} %get-tuple-element.108), channel_id=1, source_target_pairs={{0,4},{1,5},{2,6},{3,7},{4,0},{5,1},{6,2},{7,3},{8,12},{9,13},{10,... | collective-permute-start | bytes 393224 | tf_op jit(solution)/shard_map/ppermute | solution.py:122
  109.9 11.9 %collective-permute-start.33 = (f32[256,128]{1,0:T(8,128)S(1)}, f32[256,128]{1,0:T(8,128)S(1)}, u32[]{:S(2)}, u32[]{:S(2)}) collective-permute-start(f32[256,128]{1,0:T(8,128)S(1)} %get-tuple-element.107), channel_id=1, source_target_pairs={{0,6},{1,7},{2,4},{3,5},{4,2},{5,3},{6,0},{7,1},{8,14},{9,15},{10,... | collective-permute-start | bytes 393224 | tf_op jit(solution)/shard_map/ppermute | solution.py:122
  112.9 10.3 %collective-permute-start.28 = (f32[256,128]{1,0:T(8,128)S(1)}, f32[256,128]{1,0:T(8,128)S(1)}, u32[]{:S(2)}, u32[]{:S(2)}) collective-permute-start(f32[256,128]{1,0:T(8,128)S(1)} %get-tuple-element.113), channel_id=1, source_target_pairs={{0,2},{1,3},{2,0},{3,1},{4,6},{5,7},{6,4},{7,5},{8,10},{9,11},{10,... | collective-permute-start | bytes 393224 | tf_op jit(solution)/shard_map/ppermute | solution.py:122
  114.0 18.2 %collective-permute-start.29 = (f32[256,128]{1,0:T(8,128)S(1)}, f32[256,128]{1,0:T(8,128)S(1)}, u32[]{:S(2)}, u32[]{:S(2)}) collective-permute-start(f32[256,128]{1,0:T(8,128)S(1)} %get-tuple-element.112), channel_id=1, source_target_pairs={{0,4},{1,5},{2,6},{3,7},{4,0},{5,1},{6,2},{7,3},{8,12},{9,13},{10,... | collective-permute-start | bytes 393224 | tf_op jit(solution)/shard_map/ppermute | solution.py:122
  115.9 16.3 %collective-permute-start.30 = (f32[256,128]{1,0:T(8,128)S(1)}, f32[256,128]{1,0:T(8,128)S(1)}, u32[]{:S(2)}, u32[]{:S(2)}) collective-permute-start(f32[256,128]{1,0:T(8,128)S(1)} %get-tuple-element.111), channel_id=1, source_target_pairs={{0,6},{1,7},{2,4},{3,5},{4,2},{5,3},{6,0},{7,1},{8,14},{9,15},{10,... | collective-permute-start | bytes 393224 | tf_op jit(solution)/shard_map/ppermute | solution.py:122
  134.2 15.8 %all-to-all-start = ((f32[32,12,128]{2,1,0:T(8,128)}), f32[32,12,128]{2,1,0:T(8,128)S(1)}, u32[]{:S(2)}, u32[]{:S(2)}) async-start(f32[32,12,128]{2,1,0:T(8,128)} %pad_maximum_fusion.4), calls=%async_computation | async-start | bytes 524288 | tf_op jit(solution)/shard_map/all_to_all | solution.py:274
  150.7 9.9 %all-to-all-start.1 = ((f32[32,4,128]{2,1,0:T(4,128)}), f32[32,4,128]{2,1,0:T(4,128)S(1)}, u32[]{:S(2)}, u32[]{:S(2)}) async-start(f32[32,4,128]{2,1,0:T(4,128)} %broadcast_in_dim.32), calls=%async_computation.1 | async-start | bytes 131072 | tf_op jit(solution)/shard_map/all_to_all | solution.py:277
  (7 other events, 39.4 us)

commit v10 on v7

--- a/solution.py
+++ b/solution.py
@@ -72,65 +72,35 @@
     )(flips.reshape(rows // 128, 128), panel)
 
 
-def launch(value, stage):
-    axis, level = stage
-    pairs = [(source, source ^ 2**level) for source in range(lax.axis_size(axis))]
-    return lax.ppermute(value, axis, pairs), value, stage
+def device_kernel(in_ref, out_ref):
+    devices, rows, _ = in_ref.shape
+    strip = 8
+
+    def body(step, carry):
+        at = pl.multiple_of(step * strip, strip)
+        items = [in_ref[d, pl.ds(at, strip), :] for d in range(devices)]
+        apart = 1
+        while apart < devices:
+            items = [
+                items[d] + items[d ^ apart] if d & apart == 0 else items[d ^ apart] - items[d]
+                for d in range(devices)
+            ]
+            apart *= 2
+        for d in range(devices):
+            out_ref[d, pl.ds(at, strip), :] = items[d]
+        return carry
+
+    lax.fori_loop(0, rows // strip, body, 0)
 
 
-def sign_of(stage):
-    axis, level = stage
-    return (1 - 2 * (lax.axis_index(axis) >> level & 1)).astype(jnp.float32)
-
-
-def store_kernel(at, *refs):
-    value_ref, out_ref, sent = refs[0], refs[-2], refs[-1]
-    rows = value_ref.shape[0]
-    copy = pltpu.make_async_copy(value_ref, out_ref.at[pl.ds(at, rows), :], sent)
-    copy.start()
-    copy.wait()
-
-
-def store(whole, value, at, rows):
-    operands = [value] if whole is None else [value, whole]
+def device_sums(value):
     return pl.pallas_call(
-        functools.partial(store_kernel, at),
-        out_shape=jax.ShapeDtypeStruct((rows, value.shape[1]), jnp.float32),
-        in_specs=[pl.BlockSpec(memory_space=pl.ANY)] * len(operands),
-        out_specs=pl.BlockSpec(memory_space=pl.ANY),
-        scratch_shapes=[pltpu.SemaphoreType.DMA],
-        input_output_aliases={} if whole is None else {1: 0},
-    )(*operands)
-
-
-def turn(value, groups):
-    rows, width = value.shape
-    value = value.reshape(4, rows // 4, width)
-    value = lax.all_to_all(value, "wide", 0, 0, axis_index_groups=groups, tiled=True)
-    return value.reshape(rows, width)
-
-
-def sums_of_four(value):
-    rows, width = value.shape
-    a, b, c, d = value.reshape(4, rows // 4, width)
-    a, b, c, d = a + b, a - b, c + d, c - d
-    return jnp.concatenate([a + c, b + d, a - c, b - d], axis=0)
-
-
-class Chain:
-    def __init__(self):
-        self.last = ()
-
-    def end(self, sent):
-        partner, value, stage = sent
-        partner = after(partner, self.last)
-        self.last = partner + sign_of(stage) * value
-        return self.last
-
-    def begin(self, value, stages):
-        for stage in stages[:-1]:
-            value = self.end(launch(value, stage))
-        return launch(value, stages[-1])
+        device_kernel,
+        out_shape=jax.ShapeDtypeStruct(value.shape, jnp.float32),
+        in_specs=[pl.BlockSpec(memory_space=pltpu.VMEM)],
+        out_specs=pl.BlockSpec(memory_space=pltpu.VMEM),
+        compiler_params=pltpu.CompilerParams(vmem_limit_bytes=32 * 2**20),
+    )(value)
 
 
 def index_kernel(rows_here, most, bases_ref, picks_ref, out_ref):
@@ -174,52 +144,22 @@
     return owners * most + jnp.sum(earlier.astype(jnp.int32), axis=1)
 
 
-def after(value, *others):
-    return lax.optimization_barrier((value, others))[0]
-
-
 def on_device(panel, flips, picks):
     rows_here, width = panel.shape
-    narrow, wide = lax.axis_size("narrow"), lax.axis_size("wide")
-    devices = narrow * wide
+    devices = lax.axis_size("narrow") * lax.axis_size("wide")
     scale = 1.0 / float(rows_here * devices) ** 0.5
-    levels = wide.bit_length() - 1
-    near = [("narrow", l) for l in range(narrow.bit_length() - 1)]
-    near += [("wide", l) for l in range(levels - 2)]
-    core, first, second = near[:1], near[1:2], near[2:]
-    low = wide // 4
-    groups = [[place * low + group for place in range(4)] for group in range(low)]
-
     me = lax.axis_index(AXES)
     per = picks.shape[0] // devices
     most = -(-per // devices)
-    count = 4
-    size = rows_here // count
 
-    c = local_transform(panel, flips, scale, [size] * count)
-    chain = Chain()
+    local = local_transform(panel, flips, scale, [rows_here])[0]
+    local = local.reshape(devices, rows_here // devices, width)
     wanted = send_rows(picks, [me], rows_here, devices, most)
     spots = landing(lax.dynamic_slice(picks, (me * per,), (per,)), rows_here, most)
-    turned = [turn(value, groups) for value in c]
-    sent_core, sent_first, sent_second, back = {}, {}, {}, {}
-    whole = None
-    for step in range(2 * count):
-        if step < count:
-            value = sums_of_four(after(turned[step], chain.last))
-            chain.last = value
-            sent_core[step] = chain.begin(value, core)
-        i = step - 1
-        if 0 <= i < count:
-            sent_second[i] = chain.begin(chain.end(sent_first[i]), second)
-        if step < count:
-            sent_first[step] = chain.begin(chain.end(sent_core[step]), first)
-        i = step - 2
-        if 0 <= i < count:
-            back[i] = turn(chain.end(sent_second[i]), groups)
-        i = step - 4
-        if 0 <= i < count:
-            whole = store(whole, after(back[i], chain.last), i * size, rows_here)
-            chain.last = whole
+    slices = lax.all_to_all(local, AXES, 0, 0, tiled=True)
+    slices, wanted, spots = lax.optimization_barrier((slices, wanted, spots))
+    mixed = lax.all_to_all(device_sums(slices), AXES, 0, 0, tiled=True)
+    whole = mixed.reshape(rows_here, width)
 
     filled = wanted >= 0
     chosen = jnp.take(whole, wanted, axis=0, mode="clip")

time: 231 us -> 147 us (0.64)
  Pallas kernels: 71.4 us -> 2.86 us
  waiting for transfers between devices: 69.7 us -> 116 us
  starting transfers between devices: 46 us -> 15.2 us
  blocking collectives: 20.6 us -> 0 us
  other arithmetic: 12.9 us -> 1.14 us
    pallas_call x4 -> x1, Pallas kernels: 68 us -> 0.66 us  [device_sums(): pl.pallas_call(device_kernel, out_shape=jax.ShapeDtypeStruct(value.shape,...]
    all_to_all x7 -> x2, waiting for transfers between devices: 35.9 us -> 99.4 us  [the longest x1 50.1 us: on_device(): mixed = lax.all_to_all(device_sums(slices), AXES, 0, 0, tiled=True)]
    all_to_all x1 -> x0, blocking collectives: 20.6 us -> none  [turn(): lax.all_to_all(value, 'wide', 0, 0, axis_index_groups=groups, tiled=True)]
    ppermute x12 -> x0, waiting for transfers between devices: 17.5 us -> none  [launch(): return (lax.ppermute(value, axis, pairs), value, stage)]
    all_to_all x7 -> x2, starting transfers between devices: 25.9 us -> 10 us  [the longest x1 7.3 us: on_device(): slices = lax.all_to_all(local, AXES, 0, 0, tiled=True)]
    ppermute x12 -> x0, starting transfers between devices: 11.5 us -> none  [launch(): return (lax.ppermute(value, axis, pairs), value, stage)]
    add x16 -> x0, other arithmetic: 9.22 us -> none  [the longest x12 9.03 us: end(): self.last = partner + sign_of(stage) * value]
    all_to_all x1, starting transfers between devices: 6.09 us -> 2.59 us  [on_device(): landed = lax.all_to_all(both, AXES, 0, 0, tiled=True)]
  transfers between devices with their start and end apart: 21 -> 4, of which waited for: 12 -> 4; matrix products, arithmetic and copies ran while one was open for 6% -> 1% of each run, Pallas kernels for 22% -> 0%
where the time goes in v10:
time: 147 us; the launch traced here: 146 us
  waiting for transfers between devices  116 us (79%)
  starting transfers between devices  15.2 us (10%)
  local copies, waits for them, and re-layouts  9.7 us (7%)
  Pallas kernels  2.86 us (2%)
    all_to_all x1, waiting for transfers between devices, on_device(): mixed = lax.all_to_all(device_sums(slices), AXES, 0, 0, tiled=True)  50.1 us
    all_to_all x1, waiting for transfers between devices, on_device(): slices = lax.all_to_all(local, AXES, 0, 0, tiled=True)  49.3 us
    all_to_all x1, waiting for transfers between devices, on_device(): landed = lax.all_to_all(both, AXES, 0, 0, tiled=True)  10.6 us
    all_to_all x1, starting transfers between devices, on_device(): slices = lax.all_to_all(local, AXES, 0, 0, tiled=True)  7.3 us
    unnamed x12, local copies, waits for them, and re-layouts  6.88 us
    all_to_all x1, waiting for transfers between devices, on_device(): gram = lax.all_to_all(shared, AXES, 0, 0, tiled=True).reshape(width, width)  5.91 us
  transfers between devices with their start and end apart: 4, of which 4 were waited for; matrix products, arithmetic and copies ran while one was open for 1% of the time, Pallas kernels for 0%

profile of v10, /device:TPU:0, one launch (start us, length us, event | category | flops | bytes accessed | tf_op | source)
XLA Modules:
  0.0 146.1 jit_solution(4983290328215943517)
XLA Ops:
  0.6 0.0 copy-start.2
  0.6 1.6 %copy-done.2 = f32[4096,128]{1,0:T(8,128)S(1)} copy-done((f32[4096,128]{1,0:T(8,128)S(1)}, f32[4096,128]{1,0:T(8,128)}, u32[]{:S(2)}) %copy-start.2) | copy-done | bytes 2097176
  2.2 0.0 copy-start.3
  2.2 0.7 copy-done.3
  2.9 1.9 %shard_map.58 = f32[4096,128]{1,0:T(8,128)S(1)} custom-call(s32[32,128]{1,0:T(8,128)S(1)} %bitcast.10, f32[4096,128]{1,0:T(8,128)S(1)} %copy-done.2), custom_call_target="tpu_custom_call" | custom-call | tf_op jit(solution)/shard_map/pallas_call | solution.py:65
  4.9 0.0 copy-start
  4.9 1.3 copy-done
  6.2 0.0 copy-start.4
  6.2 7.3 %all-to-all-start = ((f32[32,128,128]{2,1,0:T(8,128)}), f32[32,128,128]{2,1,0:T(8,128)S(1)}, u32[]{:S(2)}, u32[]{:S(2)}) async-start(f32[32,128,128]{2,1,0:T(8,128)} %bitcast.9), calls=%async_computation | async-start | bytes 4194304 | tf_op jit(solution)/shard_map/all_to_all | solution.py:159
  13.5 0.0 copy-done.4
  13.6 0.3 shard_map.59
  13.8 0.1 reshape.44
  13.9 0.1 and_select_fusion
  14.0 0.2 convert_reduce_fusion
  14.2 0.1 multiply_add_fusion
  14.3 49.3 %all-to-all-done.in_ref = f32[32,128,128]{2,1,0:T(8,128)S(1)} async-done(((f32[32,128,128]{2,1,0:T(8,128)}), f32[32,128,128]{2,1,0:T(8,128)S(1)}, u32[]{:S(2)}, u32[]{:S(2)}) %all-to-all-start) | async-done | bytes 2097184 | tf_op jit(solution)/shard_map/all_to_all | solution.py:159
  63.6 0.7 shard_map.60
  64.3 0.0 copy-start.1
  64.3 1.3 copy-done.1
  65.6 2.7 %all-to-all-start.1 = ((f32[32,128,128]{2,1,0:T(8,128)}), f32[32,128,128]{2,1,0:T(8,128)S(1)}, u32[]{:S(2)}, u32[]{:S(2)}) async-start(f32[32,128,128]{2,1,0:T(8,128)} %copy-done.1), calls=%async_computation.1 | async-start | bytes 4194304 | tf_op jit(solution)/shard_map/all_to_all | solution.py:161
  68.4 50.1 %all-to-all-done.1 = f32[32,128,128]{2,1,0:T(8,128)S(1)} async-done(((f32[32,128,128]{2,1,0:T(8,128)}), f32[32,128,128]{2,1,0:T(8,128)S(1)}, u32[]{:S(2)}, u32[]{:S(2)}) %all-to-all-start.1) | async-done | bytes 2097184 | tf_op jit(solution)/shard_map/all_to_all | solution.py:161
  118.4 0.7 gather_fusion
  119.2 0.5 fusion.1
  119.7 0.7 pad_maximum_fusion
  120.4 2.6 %all-to-all-start.2 = ((f32[32,12,128]{2,1,0:T(8,128)}), f32[32,12,128]{2,1,0:T(8,128)S(1)}, u32[]{:S(2)}, u32[]{:S(2)}) async-start(f32[32,12,128]{2,1,0:T(8,128)} %pad_maximum_fusion), calls=%async_computation.2 | async-start | bytes 524288 | tf_op jit(solution)/shard_map/all_to_all | solution.py:174
  123.0 10.6 %all-to-all-done.2 = f32[32,12,128]{2,1,0:T(8,128)S(1)} async-done(((f32[32,12,128]{2,1,0:T(8,128)}), f32[32,12,128]{2,1,0:T(8,128)S(1)}, u32[]{:S(2)}, u32[]{:S(2)}) %all-to-all-start.2) | async-done | bytes 196640 | tf_op jit(solution)/shard_map/all_to_all | solution.py:174
  133.7 0.6 broadcast_in_dim.35
  134.3 2.6 %all-to-all-start.3 = ((f32[32,4,128]{2,1,0:T(4,128)}), f32[32,4,128]{2,1,0:T(4,128)S(1)}, u32[]{:S(2)}, u32[]{:S(2)}) async-start(f32[32,4,128]{2,1,0:T(4,128)} %broadcast_in_dim.35), calls=%async_computation.3 | async-start | bytes 131072 | tf_op jit(solution)/shard_map/all_to_all | solution.py:177
  136.9 1.3 gather_fusion.1
  138.2 5.9 %all-to-all-done.3 = f32[32,4,128]{2,1,0:T(4,128)S(1)} async-done(((f32[32,4,128]{2,1,0:T(4,128)}), f32[32,4,128]{2,1,0:T(4,128)S(1)}, u32[]{:S(2)}, u32[]{:S(2)}) %all-to-all-start.3) | async-done | bytes 65568 | tf_op jit(solution)/shard_map/all_to_all | solution.py:177
  144.2 1.3 copy.8
  145.5 0.6 copy.9
  (7 shorter events, 0.1 us)
Async XLA Ops:
  0.6 1.6 %copy-start.2 = (f32[4096,128]{1,0:T(8,128)S(1)}, f32[4096,128]{1,0:T(8,128)}, u32[]{:S(2)}) copy-start(f32[4096,128]{1,0:T(8,128)} %panel_ref.1) | copy-start | bytes 6291460
  2.2 0.7 copy-start.3
  4.9 1.3 copy-start
  6.2 7.3 %copy-start.4 = (s32[8192]{0:T(1024)S(1)}, s32[8192]{0:T(1024)}, u32[]{:S(2)}) copy-start(s32[8192]{0:T(1024)} %param.5) | copy-start | bytes 98308
  6.2 57.4 %all-to-all-start = ((f32[32,128,128]{2,1,0:T(8,128)}), f32[32,128,128]{2,1,0:T(8,128)S(1)}, u32[]{:S(2)}, u32[]{:S(2)}) async-start(f32[32,128,128]{2,1,0:T(8,128)} %bitcast.9), calls=%async_computation | async-start | bytes 4194304 | tf_op jit(solution)/shard_map/all_to_all | solution.py:159
  64.3 1.3 copy-start.1
  65.6 52.8 %all-to-all-start.1 = ((f32[32,128,128]{2,1,0:T(8,128)}), f32[32,128,128]{2,1,0:T(8,128)S(1)}, u32[]{:S(2)}, u32[]{:S(2)}) async-start(f32[32,128,128]{2,1,0:T(8,128)} %copy-done.1), calls=%async_computation.1 | async-start | bytes 4194304 | tf_op jit(solution)/shard_map/all_to_all | solution.py:161
  120.4 13.2 %all-to-all-start.2 = ((f32[32,12,128]{2,1,0:T(8,128)}), f32[32,12,128]{2,1,0:T(8,128)S(1)}, u32[]{:S(2)}, u32[]{:S(2)}) async-start(f32[32,12,128]{2,1,0:T(8,128)} %pad_maximum_fusion), calls=%async_computation.2 | async-start | bytes 524288 | tf_op jit(solution)/shard_map/all_to_all | solution.py:174
  134.3 9.9 %all-to-all-start.3 = ((f32[32,4,128]{2,1,0:T(4,128)}), f32[32,4,128]{2,1,0:T(4,128)S(1)}, u32[]{:S(2)}, u32[]{:S(2)}) async-start(f32[32,4,128]{2,1,0:T(4,128)} %broadcast_in_dim.35), calls=%async_computation.3 | async-start | bytes 131072 | tf_op jit(solution)/shard_map/all_to_all | solution.py:177

commit v11 on v10

--- a/solution.py
+++ b/solution.py
@@ -137,6 +137,73 @@
     return rows.reshape(len(owners) * devices * most)
 
 
+def count_kernel(rows_here, me_ref, picks_ref, out_ref):
+    picks = picks_ref[...]
+    rows, devices = out_ref.shape
+    owner = picks >> rows_here.bit_length() - 1
+    local = picks & rows_here - 1
+    held = local >> rows.bit_length() - 1 == me_ref[0]
+    place = jnp.where(held, local & rows - 1, -1)
+    shape = (devices, picks.shape[1])
+    owners = jnp.where(lax.broadcasted_iota(jnp.int32, shape, 0) == owner, 1.0, 0.0)
+    shape = (rows, picks.shape[1])
+    places = jnp.where(lax.broadcasted_iota(jnp.int32, shape, 0) == place, 1.0, 0.0)
+    out_ref[...] = lax.dot_general(
+        places.astype(jnp.bfloat16),
+        owners.astype(jnp.bfloat16),
+        (((1,), (1,)), ((), ())),
+        preferred_element_type=jnp.float32,
+    )
+
+
+def count_picks(picks, me, rows_here, devices):
+    return pl.pallas_call(
+        functools.partial(count_kernel, rows_here),
+        out_shape=jax.ShapeDtypeStruct((rows_here // devices, devices), jnp.float32),
+        in_specs=[
+            pl.BlockSpec(memory_space=pltpu.SMEM),
+            pl.BlockSpec(memory_space=pltpu.VMEM),
+        ],
+        out_specs=pl.BlockSpec(memory_space=pltpu.VMEM),
+        compiler_params=pltpu.CompilerParams(vmem_limit_bytes=32 * 2**20),
+    )(me.reshape(1).astype(jnp.int32), picks.reshape(1, -1))
+
+
+def part_kernel(counts_ref, held_ref, out_ref):
+    devices, _, width = held_ref.shape
+    total = jnp.zeros((width, width), jnp.float32)
+    for d in range(devices):
+        rows = held_ref[d]
+        total = total + lax.dot_general(
+            rows,
+            rows * counts_ref[:, d : d + 1],
+            (((0,), (0,)), ((), ())),
+            precision=lax.Precision.HIGHEST,
+            preferred_element_type=jnp.float32,
+        )
+    out_ref[...] = total
+
+
+def gram_part(counts, held):
+    width = held.shape[2]
+    return pl.pallas_call(
+        part_kernel,
+        out_shape=jax.ShapeDtypeStruct((width, width), jnp.float32),
+        in_specs=[pl.BlockSpec(memory_space=pltpu.VMEM)] * 2,
+        out_specs=pl.BlockSpec(memory_space=pltpu.VMEM),
+        compiler_params=pltpu.CompilerParams(vmem_limit_bytes=32 * 2**20),
+    )(counts, held)
+
+
+def sum_over_devices(value):
+    for axis in AXES:
+        size = lax.axis_size(axis)
+        for level in range(size.bit_length() - 1):
+            pairs = [(source, source ^ 2**level) for source in range(size)]
+            value = value + lax.ppermute(value, axis, pairs)
+    return value
+
+
 def landing(block, rows_here, most):
     owners = block // rows_here
     order = jnp.arange(block.shape[0], dtype=jnp.int32)
@@ -156,27 +223,19 @@
     local = local.reshape(devices, rows_here // devices, width)
     wanted = send_rows(picks, [me], rows_here, devices, most)
     spots = landing(lax.dynamic_slice(picks, (me * per,), (per,)), rows_here, most)
+    counts = count_picks(picks, me, rows_here, devices)
     slices = lax.all_to_all(local, AXES, 0, 0, tiled=True)
-    slices, wanted, spots = lax.optimization_barrier((slices, wanted, spots))
-    mixed = lax.all_to_all(device_sums(slices), AXES, 0, 0, tiled=True)
-    whole = mixed.reshape(rows_here, width)
-
-    filled = wanted >= 0
-    chosen = jnp.take(whole, wanted, axis=0, mode="clip")
-    kept = jnp.where(filled[:, None], chosen, 0.0)
-    part = lax.dot_general(
-        kept, kept, (((0,), (0,)), ((), ())),
-        precision=lax.Precision.HIGHEST, preferred_element_type=jnp.float32,
-    )
-    both = jnp.concatenate(
-        [chosen.reshape(devices, most, width), part.reshape(devices, -1, width)], axis=1
-    )
-    landed = lax.all_to_all(both, AXES, 0, 0, tiled=True)
-    mine = jnp.sum(landed[:, most:], axis=0) / float(picks.shape[0])
-    shared = jnp.broadcast_to(mine[None], (devices,) + mine.shape)
-    gram = lax.all_to_all(shared, AXES, 0, 0, tiled=True).reshape(width, width)
-    sketch = jnp.take(landed[:, :most].reshape(devices * most, width), spots, axis=0, mode="clip")
-    return (whole, sketch, gram)
+    slices, wanted, spots, counts = lax.optimization_barrier((slices, wanted, spots, counts))
+    slices = device_sums(slices)
+    mixed = lax.all_to_all(slices, AXES, 0, 0, tiled=True)
+    gram = sum_over_devices(gram_part(counts, slices)) / float(picks.shape[0])
+    mixed, gram = lax.optimization_barrier((mixed, gram))
+    mixed = mixed.reshape(rows_here, width)
+
+    chosen = jnp.take(mixed, wanted, axis=0, mode="clip")
+    landed = lax.all_to_all(chosen.reshape(devices, most, width), AXES, 0, 0, tiled=True)
+    sketch = jnp.take(landed.reshape(devices * most, width), spots, axis=0, mode="clip")
+    return (mixed, sketch, gram)
 
 
 def solution(mesh):

time: 147 us -> 136 us (0.925)
  waiting for transfers between devices: 116 us -> 92.8 us
  starting transfers between devices: 15.2 us -> 24.7 us
  Pallas kernels: 2.86 us -> 8.85 us
  local copies, waits for them, and re-layouts: 9.7 us -> 7.72 us
    all_to_all x3 -> x2, waiting for transfers between devices: 66.6 us -> 7.73 us  [the longest x1 7.73 us: on_device(): lax.all_to_all(chosen.reshape(devices, most, width), AXES, 0, 0, tiled=True)]
    ppermute x0 -> x5, waiting for transfers between devices: none -> 36.5 us  [sum_over_devices(): value = value + lax.ppermute(value, axis, pairs)]
    ppermute x0 -> x5, starting transfers between devices: none -> 11 us  [sum_over_devices(): value = value + lax.ppermute(value, axis, pairs)]
    pallas_call x0 -> x2, Pallas kernels: none -> 4.65 us  [the longest x1 3.97 us: gram_part(): pl.pallas_call(part_kernel, out_shape=jax.ShapeDtypeStruct((width, width)...]
    unnamed x12 -> x9, local copies, waits for them, and re-layouts: 6.88 us -> 4.94 us
    all_to_all x3 -> x2, starting transfers between devices: 7.88 us -> 6.41 us  [the longest x1 3.69 us: on_device(): lax.all_to_all(chosen.reshape(devices, most, width), AXES, 0, 0, tiled=True)]
  transfers between devices with their start and end apart: 4 -> 8, of which waited for: 4 -> 7; matrix products, arithmetic and copies ran while one was open for 1% -> 1% of each run, Pallas kernels for 0% -> 4%
where the time goes in v11:
time: 136 us
  waiting for transfers between devices  92.8 us (68%)
  starting transfers between devices  24.7 us (18%)
  Pallas kernels  8.85 us (7%)
  local copies, waits for them, and re-layouts  7.72 us (6%)
    all_to_all x1, waiting for transfers between devices, on_device(): slices = lax.all_to_all(local, AXES, 0, 0, tiled=True)  48.6 us
    ppermute x5, waiting for transfers between devices, sum_over_devices(): value = value + lax.ppermute(value, axis, pairs)  36.5 us
    ppermute x5, starting transfers between devices, sum_over_devices(): value = value + lax.ppermute(value, axis, pairs)  11 us
    all_to_all x1, waiting for transfers between devices, on_device(): lax.all_to_all(chosen.reshape(devices, most, width), AXES, 0, 0, tiled=True)  7.73 us
    all_to_all x1, starting transfers between devices, on_device(): slices = lax.all_to_all(local, AXES, 0, 0, tiled=True)  7.3 us
    unnamed x9, local copies, waits for them, and re-layouts  4.94 us
    pallas_call x1, Pallas kernels, gram_part(): pl.pallas_call(part_kernel, out_shape=jax.ShapeDtypeStruct((width, width)...  3.97 us
    all_to_all x1, starting transfers between devices, on_device(): lax.all_to_all(chosen.reshape(devices, most, width), AXES, 0, 0, tiled=True)  3.69 us
  transfers between devices with their start and end apart: 8, of which 7 were waited for; matrix products, arithmetic and copies ran while one was open for 1% of the time, Pallas kernels for 4%

profile of v11, /device:TPU:0, one launch (start us, length us, event | category | flops | bytes accessed | tf_op | source)
XLA Modules:
  0.0 135.9 jit_solution(13750637791117042491)
XLA Ops:
  0.6 1.6 %copy-done.1 = f32[4096,128]{1,0:T(8,128)S(1)} copy-done((f32[4096,128]{1,0:T(8,128)S(1)}, f32[4096,128]{1,0:T(8,128)}, u32[]{:S(2)}) %copy-start.1) | copy-done | bytes 2097176
  2.2 0.7 copy-done.3
  2.9 1.9 %shard_map.58 = f32[4096,128]{1,0:T(8,128)S(1)} custom-call(s32[32,128]{1,0:T(8,128)S(1)} %bitcast.9, f32[4096,128]{1,0:T(8,128)S(1)} %copy-done.1), custom_call_target="tpu_custom_call" | custom-call | tf_op jit(solution)/shard_map/pallas_call | solution.py:65
  4.9 0.0 copy-start
  4.9 1.3 copy-done
  6.2 7.3 %all-to-all-start = ((f32[32,128,128]{2,1,0:T(8,128)}), f32[32,128,128]{2,1,0:T(8,128)S(1)}, u32[]{:S(2)}, u32[]{:S(2)}) async-start(f32[32,128,128]{2,1,0:T(8,128)} %bitcast.7), calls=%async_computation | async-start | bytes 4194304 | tf_op jit(solution)/shard_map/all_to_all | solution.py:227
  13.6 0.7 shard_map.60.counts_ref
  14.3 0.3 shard_map.59
  14.5 0.1 reshape.36
  14.6 0.1 and_select_fusion
  14.7 0.2 convert_reduce_fusion
  14.9 0.1 multiply_add_fusion
  15.0 48.6 %all-to-all-done.in_ref = f32[32,128,128]{2,1,0:T(8,128)S(1)} async-done(((f32[32,128,128]{2,1,0:T(8,128)}), f32[32,128,128]{2,1,0:T(8,128)S(1)}, u32[]{:S(2)}, u32[]{:S(2)}) %all-to-all-start) | async-done | bytes 2097184 | tf_op jit(solution)/shard_map/all_to_all | solution.py:227
  63.6 2.0 %shard_map.61.held_ref = f32[32,128,128]{2,1,0:T(8,128)} custom-call(f32[32,128,128]{2,1,0:T(8,128)S(1)} %all-to-all-done.in_ref), custom_call_target="tpu_custom_call" | custom-call | tf_op jit(solution)/shard_map/pallas_call | solution.py:97
  65.6 2.7 %all-to-all-start.1 = ((f32[32,128,128]{2,1,0:T(8,128)}), f32[32,128,128]{2,1,0:T(8,128)S(1)}, u32[]{:S(2)}, u32[]{:S(2)}) async-start(f32[32,128,128]{2,1,0:T(8,128)} %shard_map.61.held_ref), calls=%async_computation.1 | async-start | bytes 4194304 | tf_op jit(solution)/shard_map/all_to_all | solution.py:230
  68.3 4.0 %shard_map.62 = f32[128,128]{1,0:T(8,128)S(1)} custom-call(f32[128,32]{1,0:T(8,128)S(1)} %shard_map.60.counts_ref, f32[32,128,128]{2,1,0:T(8,128)} %shard_map.61.held_ref), custom_call_target="tpu_custom_call" | custom-call | tf_op jit(solution)/shard_map/pallas_call | solution.py:189
  72.3 0.2 collective-permute-start
  72.5 1.1 collective-permute-done
  73.7 1.7 %collective-permute-start.1 = (f32[128,128]{1,0:T(8,128)S(1)}, f32[128,128]{1,0:T(8,128)S(1)}, u32[]{:S(2)}, u32[]{:S(2)}) collective-permute-start(f32[128,128]{1,0:T(8,128)S(1)} %add.28), channel_id=1, source_target_pairs={{0,16},{8,24},{16,0},{24,8},{1,17},{9,25},{17,1},{25,9},{2,18},{10... | collective-permute-start | bytes 196616 | tf_op jit(solution)/shard_map/ppermute | solution.py:203
  75.4 7.9 %collective-permute-done.1 = f32[128,128]{1,0:T(8,128)S(1)} collective-permute-done((f32[128,128]{1,0:T(8,128)S(1)}, f32[128,128]{1,0:T(8,128)S(1)}, u32[]{:S(2)}, u32[]{:S(2)}) %collective-permute-start.1) | collective-permute-done | bytes 65568 | tf_op jit(solution)/shard_map/ppermute | solution.py:203
  83.2 4.2 %collective-permute-start.2 = (f32[128,128]{1,0:T(8,128)S(1)}, f32[128,128]{1,0:T(8,128)S(1)}, u32[]{:S(2)}, u32[]{:S(2)}) collective-permute-start(f32[128,128]{1,0:T(8,128)S(1)} %add.29), channel_id=1, source_target_pairs={{0,1},{1,0},{2,3},{3,2},{4,5},{5,4},{6,7},{7,6},{8,9},{9,8},{10,11... | collective-permute-start | bytes 196616 | tf_op jit(solution)/shard_map/ppermute | solution.py:203
  87.4 7.7 %collective-permute-done.2 = f32[128,128]{1,0:T(8,128)S(1)} collective-permute-done((f32[128,128]{1,0:T(8,128)S(1)}, f32[128,128]{1,0:T(8,128)S(1)}, u32[]{:S(2)}, u32[]{:S(2)}) %collective-permute-start.2) | collective-permute-done | bytes 65568 | tf_op jit(solution)/shard_map/ppermute | solution.py:203
  95.1 0.1 collective-permute-start.3
  95.2 9.0 %collective-permute-done.3 = f32[128,128]{1,0:T(8,128)S(1)} collective-permute-done((f32[128,128]{1,0:T(8,128)S(1)}, f32[128,128]{1,0:T(8,128)S(1)}, u32[]{:S(2)}, u32[]{:S(2)}) %collective-permute-start.3) | collective-permute-done | bytes 65568 | tf_op jit(solution)/shard_map/ppermute | solution.py:203
  104.2 4.8 %collective-permute-start.4 = (f32[128,128]{1,0:T(8,128)S(1)}, f32[128,128]{1,0:T(8,128)S(1)}, u32[]{:S(2)}, u32[]{:S(2)}) collective-permute-start(f32[128,128]{1,0:T(8,128)S(1)} %add.31), channel_id=1, source_target_pairs={{0,4},{1,5},{2,6},{3,7},{4,0},{5,1},{6,2},{7,3},{8,12},{9,13},{10,... | collective-permute-start | bytes 196616 | tf_op jit(solution)/shard_map/ppermute | solution.py:203
  109.1 10.8 %collective-permute-done.4 = f32[128,128]{1,0:T(8,128)S(1)} collective-permute-done((f32[128,128]{1,0:T(8,128)S(1)}, f32[128,128]{1,0:T(8,128)S(1)}, u32[]{:S(2)}, u32[]{:S(2)}) %collective-permute-start.4) | collective-permute-done | bytes 65568 | tf_op jit(solution)/shard_map/ppermute | solution.py:203
  119.8 0.6 add_multiply_fusion
  120.5 1.3 gather_fusion
  121.8 3.7 %all-to-all-start.2 = ((f32[32,8,128]{2,1,0:T(8,128)}), f32[32,8,128]{2,1,0:T(8,128)S(1)}, u32[]{:S(2)}, u32[]{:S(2)}) async-start(f32[32,8,128]{2,1,0:T(8,128)} %bitcast.5), calls=%async_computation.2 | async-start | bytes 262144 | tf_op jit(solution)/shard_map/all_to_all | solution.py:236
  125.5 7.7 %all-to-all-done.2 = f32[32,8,128]{2,1,0:T(8,128)S(1)} async-done(((f32[32,8,128]{2,1,0:T(8,128)}), f32[32,8,128]{2,1,0:T(8,128)S(1)}, u32[]{:S(2)}, u32[]{:S(2)}) %all-to-all-start.2) | async-done | bytes 131104 | tf_op jit(solution)/shard_map/all_to_all | solution.py:236
  133.3 1.3 gather_fusion.1
  134.6 1.3 copy.7
  (12 shorter events, 0.1 us)
Async XLA Ops:
  0.6 1.6 %copy-start.1 = (f32[4096,128]{1,0:T(8,128)S(1)}, f32[4096,128]{1,0:T(8,128)}, u32[]{:S(2)}) copy-start(f32[4096,128]{1,0:T(8,128)} %panel_ref.1) | copy-start | bytes 6291460
  2.2 0.7 copy-start.3
  4.9 1.3 copy-start
  6.2 7.3 %copy-start.2 = (s32[8192]{0:T(1024)S(1)}, s32[8192]{0:T(1024)}, u32[]{:S(2)}) copy-start(s32[8192]{0:T(1024)} %param.5) | copy-start | bytes 98308
  6.2 57.4 %all-to-all-start = ((f32[32,128,128]{2,1,0:T(8,128)}), f32[32,128,128]{2,1,0:T(8,128)S(1)}, u32[]{:S(2)}, u32[]{:S(2)}) async-start(f32[32,128,128]{2,1,0:T(8,128)} %bitcast.7), calls=%async_computation | async-start | bytes 4194304 | tf_op jit(solution)/shard_map/all_to_all | solution.py:227
  65.6 54.9 %all-to-all-start.1 = ((f32[32,128,128]{2,1,0:T(8,128)}), f32[32,128,128]{2,1,0:T(8,128)S(1)}, u32[]{:S(2)}, u32[]{:S(2)}) async-start(f32[32,128,128]{2,1,0:T(8,128)} %shard_map.61.held_ref), calls=%async_computation.1 | async-start | bytes 4194304 | tf_op jit(solution)/shard_map/all_to_all | solution.py:230
  72.3 1.3 collective-permute-start
  73.7 9.6 %collective-permute-start.1 = (f32[128,128]{1,0:T(8,128)S(1)}, f32[128,128]{1,0:T(8,128)S(1)}, u32[]{:S(2)}, u32[]{:S(2)}) collective-permute-start(f32[128,128]{1,0:T(8,128)S(1)} %add.28), channel_id=1, source_target_pairs={{0,16},{8,24},{16,0},{24,8},{1,17},{9,25},{17,1},{25,9},{2,18},{10... | collective-permute-start | bytes 196616 | tf_op jit(solution)/shard_map/ppermute | solution.py:203
  83.2 11.9 %collective-permute-start.2 = (f32[128,128]{1,0:T(8,128)S(1)}, f32[128,128]{1,0:T(8,128)S(1)}, u32[]{:S(2)}, u32[]{:S(2)}) collective-permute-start(f32[128,128]{1,0:T(8,128)S(1)} %add.29), channel_id=1, source_target_pairs={{0,1},{1,0},{2,3},{3,2},{4,5},{5,4},{6,7},{7,6},{8,9},{9,8},{10,11... | collective-permute-start | bytes 196616 | tf_op jit(solution)/shard_map/ppermute | solution.py:203
  95.1 9.1 %collective-permute-start.3 = (f32[128,128]{1,0:T(8,128)S(1)}, f32[128,128]{1,0:T(8,128)S(1)}, u32[]{:S(2)}, u32[]{:S(2)}) collective-permute-start(f32[128,128]{1,0:T(8,128)S(1)} %add.30), channel_id=1, source_target_pairs={{0,2},{1,3},{2,0},{3,1},{4,6},{5,7},{6,4},{7,5},{8,10},{9,11},{10,... | collective-permute-start | bytes 196616 | tf_op jit(solution)/shard_map/ppermute | solution.py:203
  104.2 15.6 %collective-permute-start.4 = (f32[128,128]{1,0:T(8,128)S(1)}, f32[128,128]{1,0:T(8,128)S(1)}, u32[]{:S(2)}, u32[]{:S(2)}) collective-permute-start(f32[128,128]{1,0:T(8,128)S(1)} %add.31), channel_id=1, source_target_pairs={{0,4},{1,5},{2,6},{3,7},{4,0},{5,1},{6,2},{7,3},{8,12},{9,13},{10,... | collective-permute-start | bytes 196616 | tf_op jit(solution)/shard_map/ppermute | solution.py:203
  121.8 11.4 %all-to-all-start.2 = ((f32[32,8,128]{2,1,0:T(8,128)}), f32[32,8,128]{2,1,0:T(8,128)S(1)}, u32[]{:S(2)}, u32[]{:S(2)}) async-start(f32[32,8,128]{2,1,0:T(8,128)} %bitcast.5), calls=%async_computation.2 | async-start | bytes 262144 | tf_op jit(solution)/shard_map/all_to_all | solution.py:236

commit v12 on v11

--- a/solution.py
+++ b/solution.py
@@ -72,9 +72,10 @@
     )(flips.reshape(rows // 128, 128), panel)
 
 
-def device_kernel(in_ref, out_ref):
+def device_kernel(in_ref, out_ref, held, sent):
     devices, rows, _ = in_ref.shape
     strip = 8
+    quarter = rows // 4
 
     def body(step, carry):
         at = pl.multiple_of(step * strip, strip)
@@ -87,10 +88,20 @@
             ]
             apart *= 2
         for d in range(devices):
-            out_ref[d, pl.ds(at, strip), :] = items[d]
+            held[d, pl.ds(at, strip), :] = items[d]
         return carry
 
-    lax.fori_loop(0, rows // strip, body, 0)
+    copies = []
+    for part in range(4):
+        first = part * quarter // strip
+        lax.fori_loop(first, first + quarter // strip, body, 0)
+        span = pl.ds(part * quarter, quarter)
+        copies.append(
+            pltpu.make_async_copy(held.at[:, span, :], out_ref.at[:, span, :], sent.at[part])
+        )
+        copies[-1].start()
+    for copy in copies:
+        copy.wait()
 
 
 def device_sums(value):
@@ -98,8 +109,29 @@
         device_kernel,
         out_shape=jax.ShapeDtypeStruct(value.shape, jnp.float32),
         in_specs=[pl.BlockSpec(memory_space=pltpu.VMEM)],
-        out_specs=pl.BlockSpec(memory_space=pltpu.VMEM),
-        compiler_params=pltpu.CompilerParams(vmem_limit_bytes=32 * 2**20),
+        out_specs=pl.BlockSpec(memory_space=pl.ANY),
+        scratch_shapes=[
+            pltpu.VMEM(value.shape, jnp.float32),
+            pltpu.SemaphoreType.DMA((4,)),
+        ],
+        compiler_params=pltpu.CompilerParams(vmem_limit_bytes=32 * 2**20),
+    )(value)
+
+
+def store_kernel(value_ref, out_ref, sent):
+    copy = pltpu.make_async_copy(value_ref, out_ref, sent)
+    copy.start()
+    copy.wait()
+
+
+def store(value):
+    return pl.pallas_call(
+        store_kernel,
+        out_shape=jax.ShapeDtypeStruct(value.shape, jnp.float32),
+        in_specs=[pl.BlockSpec(memory_space=pltpu.VMEM)],
+        out_specs=pl.BlockSpec(memory_space=pl.ANY),
+        scratch_shapes=[pltpu.SemaphoreType.DMA],
+        compiler_params=pltpu.CompilerParams(vmem_limit_bytes=8 * 2**20),
     )(value)
 
 
@@ -169,19 +201,24 @@
     )(me.reshape(1).astype(jnp.int32), picks.reshape(1, -1))
 
 
+def halves(value):
+    high = value.astype(jnp.bfloat16)
+    return high, (value - high.astype(jnp.float32)).astype(jnp.bfloat16)
+
+
 def part_kernel(counts_ref, held_ref, out_ref):
     devices, _, width = held_ref.shape
-    total = jnp.zeros((width, width), jnp.float32)
+    total = jnp.zeros((width, 2 * width), jnp.float32)
+    rest = jnp.zeros((width, width), jnp.float32)
     for d in range(devices):
         rows = held_ref[d]
-        total = total + lax.dot_general(
-            rows,
-            rows * counts_ref[:, d : d + 1],
-            (((0,), (0,)), ((), ())),
-            precision=lax.Precision.HIGHEST,
-            preferred_element_type=jnp.float32,
-        )
-    out_ref[...] = total
+        high, low = halves(rows)
+        weighted, spare = halves(rows * counts_ref[:, d : d + 1])
+        over_rows = (((0,), (0,)), ((), ()))
+        both = jnp.concatenate([weighted, spare], axis=1)
+        total += lax.dot_general(high, both, over_rows, preferred_element_type=jnp.float32)
+        rest += lax.dot_general(low, weighted, over_rows, preferred_element_type=jnp.float32)
+    out_ref[...] = total[:, :width] + total[:, width:] + rest
 
 
 def gram_part(counts, held):
@@ -195,13 +232,9 @@
     )(counts, held)
 
 
-def sum_over_devices(value):
-    for axis in AXES:
-        size = lax.axis_size(axis)
-        for level in range(size.bit_length() - 1):
-            pairs = [(source, source ^ 2**level) for source in range(size)]
-            value = value + lax.ppermute(value, axis, pairs)
-    return value
+def add_partner(value, axis, level):
+    pairs = [(source, source ^ 2**level) for source in range(lax.axis_size(axis))]
+    return value + lax.ppermute(value, axis, pairs)
 
 
 def landing(block, rows_here, most):
@@ -228,12 +261,17 @@
     slices, wanted, spots, counts = lax.optimization_barrier((slices, wanted, spots, counts))
     slices = device_sums(slices)
     mixed = lax.all_to_all(slices, AXES, 0, 0, tiled=True)
-    gram = sum_over_devices(gram_part(counts, slices)) / float(picks.shape[0])
+    gram = gram_part(counts, slices)
+    levels = [(axis, l) for axis in AXES for l in range(lax.axis_size(axis).bit_length() - 1)]
+    for axis, level in levels[:-1]:
+        gram = add_partner(gram, axis, level)
     mixed, gram = lax.optimization_barrier((mixed, gram))
     mixed = mixed.reshape(rows_here, width)
-
     chosen = jnp.take(mixed, wanted, axis=0, mode="clip")
     landed = lax.all_to_all(chosen.reshape(devices, most, width), AXES, 0, 0, tiled=True)
+    gram = add_partner(gram, *levels[-1]) / float(picks.shape[0])
+    mixed = store(mixed)
+    landed, mixed, gram = lax.optimization_barrier((landed, mixed, gram))
     sketch = jnp.take(landed.reshape(devices * most, width), spots, axis=0, mode="clip")
     return (mixed, sketch, gram)
 

time: 136 us -> 134 us (0.985)
  starting transfers between devices: 24.7 us -> 21.5 us
  waiting for transfers between devices: 92.8 us -> 94.8 us
    all_to_all x1, waiting for transfers between devices: 0.01 us -> 14.2 us  [on_device(): mixed = lax.all_to_all(slices, AXES, 0, 0, tiled=True)]
    all_to_all x1, waiting for transfers between devices: 7.73 us -> 0.01 us  [on_device(): lax.all_to_all(chosen.reshape(devices, most, width), AXES, 0, 0, tiled=True)]
    ppermute x5, waiting for transfers between devices: 36.5 us -> 31.9 us  [add_partner(): return value + lax.ppermute(value, axis, pairs)]
    ppermute x5, starting transfers between devices: 11 us -> 8.86 us  [add_partner(): return value + lax.ppermute(value, axis, pairs)]
    unnamed x9 -> x8, local copies, waits for them, and re-layouts: 4.94 us -> 3.62 us
where the time goes in v12:
time: 134 us; the launch traced here: 133 us
  waiting for transfers between devices  94.8 us (71%)
  starting transfers between devices  21.5 us (16%)
  Pallas kernels  8.78 us (7%)
  local copies, waits for them, and re-layouts  6.4 us (5%)
    all_to_all x1, waiting for transfers between devices, on_device(): slices = lax.all_to_all(local, AXES, 0, 0, tiled=True)  48.6 us
    ppermute x5, waiting for transfers between devices, add_partner(): return value + lax.ppermute(value, axis, pairs)  31.9 us
    all_to_all x1, waiting for transfers between devices, on_device(): mixed = lax.all_to_all(slices, AXES, 0, 0, tiled=True)  14.2 us
    ppermute x5, starting transfers between devices, add_partner(): return value + lax.ppermute(value, axis, pairs)  8.86 us
    all_to_all x1, starting transfers between devices, on_device(): slices = lax.all_to_all(local, AXES, 0, 0, tiled=True)  7.3 us
    unnamed x8, local copies, waits for them, and re-layouts  3.62 us
    pallas_call x1, Pallas kernels, gram_part(): pl.pallas_call(part_kernel, out_shape=jax.ShapeDtypeStruct((width, width)...  3.06 us
    all_to_all x1, starting transfers between devices, on_device(): mixed = lax.all_to_all(slices, AXES, 0, 0, tiled=True)  2.75 us
  transfers between devices with their start and end apart: 8, of which 7 were waited for; matrix products, arithmetic and copies ran while one was open for 1% of the time, Pallas kernels for 4%

profile of v12, /device:TPU:0, one launch (start us, length us, event | category | flops | bytes accessed | tf_op | source)
XLA Modules:
  0.0 133.3 jit_solution(7847531075561520390)
XLA Ops:
  0.6 1.6 %copy-done.1 = f32[4096,128]{1,0:T(8,128)S(1)} copy-done((f32[4096,128]{1,0:T(8,128)S(1)}, f32[4096,128]{1,0:T(8,128)}, u32[]{:S(2)}) %copy-start.1) | copy-done | bytes 2097176
  2.2 0.7 copy-done.3
  2.9 1.9 %shard_map.58 = f32[4096,128]{1,0:T(8,128)S(1)} custom-call(s32[32,128]{1,0:T(8,128)S(1)} %bitcast.11, f32[4096,128]{1,0:T(8,128)S(1)} %copy-done.1), custom_call_target="tpu_custom_call" | custom-call | tf_op jit(solution)/shard_map/pallas_call | solution.py:65
  4.9 0.0 copy-start
  4.9 1.3 copy-done
  6.2 7.3 %all-to-all-start = ((f32[32,128,128]{2,1,0:T(8,128)}), f32[32,128,128]{2,1,0:T(8,128)S(1)}, u32[]{:S(2)}, u32[]{:S(2)}) async-start(f32[32,128,128]{2,1,0:T(8,128)} %bitcast.9), calls=%async_computation | async-start | bytes 4194304 | tf_op jit(solution)/shard_map/all_to_all | solution.py:260
  13.6 0.3 shard_map.59
  13.8 0.1 reshape.36
  13.9 0.7 shard_map.60.counts_ref
  14.6 0.1 and_select_fusion
  14.7 0.2 convert_reduce_fusion
  14.9 0.1 multiply_add_fusion
  15.0 48.6 %all-to-all-done.in_ref = f32[32,128,128]{2,1,0:T(8,128)S(1)} async-done(((f32[32,128,128]{2,1,0:T(8,128)}), f32[32,128,128]{2,1,0:T(8,128)S(1)}, u32[]{:S(2)}, u32[]{:S(2)}) %all-to-all-start) | async-done | bytes 2097184 | tf_op jit(solution)/shard_map/all_to_all | solution.py:260
  63.6 1.5 %shard_map.61.held_ref = f32[32,128,128]{2,1,0:T(8,128)} custom-call(f32[32,128,128]{2,1,0:T(8,128)S(1)} %all-to-all-done.in_ref), custom_call_target="tpu_custom_call" | custom-call | tf_op jit(solution)/shard_map/pallas_call | solution.py:108
  65.1 2.7 %all-to-all-start.1 = ((f32[32,128,128]{2,1,0:T(8,128)}), f32[32,128,128]{2,1,0:T(8,128)S(1)}, u32[]{:S(2)}, u32[]{:S(2)}) async-start(f32[32,128,128]{2,1,0:T(8,128)} %shard_map.61.held_ref), calls=%async_computation.1 | async-start | bytes 4194304 | tf_op jit(solution)/shard_map/all_to_all | solution.py:263
  67.9 3.1 %shard_map.62 = f32[128,128]{1,0:T(8,128)S(1)} custom-call(f32[128,32]{1,0:T(8,128)S(1)} %shard_map.60.counts_ref, f32[32,128,128]{2,1,0:T(8,128)} %shard_map.61.held_ref), custom_call_target="tpu_custom_call" | custom-call | tf_op jit(solution)/shard_map/pallas_call | solution.py:226
  70.9 0.2 collective-permute-start
  71.1 1.1 collective-permute-done
  72.3 1.7 %collective-permute-start.1 = (f32[128,128]{1,0:T(8,128)S(1)}, f32[128,128]{1,0:T(8,128)S(1)}, u32[]{:S(2)}, u32[]{:S(2)}) collective-permute-start(f32[128,128]{1,0:T(8,128)S(1)} %add.28), channel_id=1, source_target_pairs={{0,16},{8,24},{16,0},{24,8},{1,17},{9,25},{17,1},{25,9},{2,18},{10... | collective-permute-start | bytes 196616 | tf_op jit(solution)/shard_map/ppermute | solution.py:237
  74.0 8.8 %collective-permute-done.1 = f32[128,128]{1,0:T(8,128)S(1)} collective-permute-done((f32[128,128]{1,0:T(8,128)S(1)}, f32[128,128]{1,0:T(8,128)S(1)}, u32[]{:S(2)}, u32[]{:S(2)}) %collective-permute-start.1) | collective-permute-done | bytes 65568 | tf_op jit(solution)/shard_map/ppermute | solution.py:237
  82.8 4.2 %collective-permute-start.2 = (f32[128,128]{1,0:T(8,128)S(1)}, f32[128,128]{1,0:T(8,128)S(1)}, u32[]{:S(2)}, u32[]{:S(2)}) collective-permute-start(f32[128,128]{1,0:T(8,128)S(1)} %add.29), channel_id=1, source_target_pairs={{0,1},{1,0},{2,3},{3,2},{4,5},{5,4},{6,7},{7,6},{8,9},{9,8},{10,11... | collective-permute-start | bytes 196616 | tf_op jit(solution)/shard_map/ppermute | solution.py:237
  87.0 7.7 %collective-permute-done.2 = f32[128,128]{1,0:T(8,128)S(1)} collective-permute-done((f32[128,128]{1,0:T(8,128)S(1)}, f32[128,128]{1,0:T(8,128)S(1)}, u32[]{:S(2)}, u32[]{:S(2)}) %collective-permute-start.2) | collective-permute-done | bytes 65568 | tf_op jit(solution)/shard_map/ppermute | solution.py:237
  94.7 0.1 collective-permute-start.3
  94.7 9.0 %collective-permute-done.3 = f32[128,128]{1,0:T(8,128)S(1)} collective-permute-done((f32[128,128]{1,0:T(8,128)S(1)}, f32[128,128]{1,0:T(8,128)S(1)}, u32[]{:S(2)}, u32[]{:S(2)}) %collective-permute-start.3) | collective-permute-done | bytes 65568 | tf_op jit(solution)/shard_map/ppermute | solution.py:237
  103.8 14.2 %all-to-all-done.1 = f32[32,128,128]{2,1,0:T(8,128)S(1)} async-done(((f32[32,128,128]{2,1,0:T(8,128)}), f32[32,128,128]{2,1,0:T(8,128)S(1)}, u32[]{:S(2)}, u32[]{:S(2)}) %all-to-all-start.1) | async-done | bytes 2097184 | tf_op jit(solution)/shard_map/all_to_all | solution.py:263
  118.0 1.3 %gather_fusion = f32[256,128]{1,0:T(8,128)} fusion(f32[4096,128]{1,0:T(8,128)S(1)} %bitcast.7, s32[1024]{0:T(1024)S(1)} %pad_clamp_fusion.1), kind=kCustom, calls=%fused_computation | custom fusion | bytes 263168 | tf_op jit(solution)/shard_map/jit(_take)/gather | solution.py:270
  119.3 2.6 %all-to-all-start.2 = ((f32[32,8,128]{2,1,0:T(8,128)}), f32[32,8,128]{2,1,0:T(8,128)S(1)}, u32[]{:S(2)}, u32[]{:S(2)}) async-start(f32[32,8,128]{2,1,0:T(8,128)} %bitcast.5), calls=%async_computation.2 | async-start | bytes 262144 | tf_op jit(solution)/shard_map/all_to_all | solution.py:271
  121.9 2.7 %collective-permute-start.4 = (f32[128,128]{1,0:T(8,128)S(1)}, f32[128,128]{1,0:T(8,128)S(1)}, u32[]{:S(2)}, u32[]{:S(2)}) collective-permute-start(f32[128,128]{1,0:T(8,128)S(1)} %add.31), channel_id=1, source_target_pairs={{0,4},{1,5},{2,6},{3,7},{4,0},{5,1},{6,2},{7,3},{8,12},{9,13},{10,... | collective-permute-start | bytes 196616 | tf_op jit(solution)/shard_map/ppermute | solution.py:237
  124.6 1.3 shard_map.63
  126.0 5.3 %collective-permute-done.4 = f32[128,128]{1,0:T(8,128)S(1)} collective-permute-done((f32[128,128]{1,0:T(8,128)S(1)}, f32[128,128]{1,0:T(8,128)S(1)}, u32[]{:S(2)}, u32[]{:S(2)}) %collective-permute-start.4) | collective-permute-done | bytes 65568 | tf_op jit(solution)/shard_map/ppermute | solution.py:237
  131.3 0.6 add_multiply_fusion
  131.9 1.3 %gather_fusion.1 = f32[256,128]{1,0:T(8,128)} fusion(f32[256,128]{1,0:T(8,128)S(1)} %bitcast.12, s32[1024]{0:T(1024)S(1)} %pad_clamp_fusion), kind=kCustom, calls=%fused_computation.1 | custom fusion | bytes 263168 | tf_op jit(solution)/shard_map/jit(_take)/gather | solution.py:275
  (12 shorter events, 0.1 us)
Async XLA Ops:
  0.6 1.6 %copy-start.1 = (f32[4096,128]{1,0:T(8,128)S(1)}, f32[4096,128]{1,0:T(8,128)}, u32[]{:S(2)}) copy-start(f32[4096,128]{1,0:T(8,128)} %panel_ref.1) | copy-start | bytes 6291460
  2.2 0.7 copy-start.3
  4.9 1.3 copy-start
  6.2 7.3 %copy-start.2 = (s32[8192]{0:T(1024)S(1)}, s32[8192]{0:T(1024)}, u32[]{:S(2)}) copy-start(s32[8192]{0:T(1024)} %param.5) | copy-start | bytes 98308
  6.2 57.4 %all-to-all-start = ((f32[32,128,128]{2,1,0:T(8,128)}), f32[32,128,128]{2,1,0:T(8,128)S(1)}, u32[]{:S(2)}, u32[]{:S(2)}) async-start(f32[32,128,128]{2,1,0:T(8,128)} %bitcast.9), calls=%async_computation | async-start | bytes 4194304 | tf_op jit(solution)/shard_map/all_to_all | solution.py:260
  65.1 52.8 %all-to-all-start.1 = ((f32[32,128,128]{2,1,0:T(8,128)}), f32[32,128,128]{2,1,0:T(8,128)S(1)}, u32[]{:S(2)}, u32[]{:S(2)}) async-start(f32[32,128,128]{2,1,0:T(8,128)} %shard_map.61.held_ref), calls=%async_computation.1 | async-start | bytes 4194304 | tf_op jit(solution)/shard_map/all_to_all | solution.py:263
  70.9 1.3 collective-permute-start
  72.3 10.5 %collective-permute-start.1 = (f32[128,128]{1,0:T(8,128)S(1)}, f32[128,128]{1,0:T(8,128)S(1)}, u32[]{:S(2)}, u32[]{:S(2)}) collective-permute-start(f32[128,128]{1,0:T(8,128)S(1)} %add.28), channel_id=1, source_target_pairs={{0,16},{8,24},{16,0},{24,8},{1,17},{9,25},{17,1},{25,9},{2,18},{10... | collective-permute-start | bytes 196616 | tf_op jit(solution)/shard_map/ppermute | solution.py:237
  82.8 11.9 %collective-permute-start.2 = (f32[128,128]{1,0:T(8,128)S(1)}, f32[128,128]{1,0:T(8,128)S(1)}, u32[]{:S(2)}, u32[]{:S(2)}) collective-permute-start(f32[128,128]{1,0:T(8,128)S(1)} %add.29), channel_id=1, source_target_pairs={{0,1},{1,0},{2,3},{3,2},{4,5},{5,4},{6,7},{7,6},{8,9},{9,8},{10,11... | collective-permute-start | bytes 196616 | tf_op jit(solution)/shard_map/ppermute | solution.py:237
  94.7 9.1 %collective-permute-start.3 = (f32[128,128]{1,0:T(8,128)S(1)}, f32[128,128]{1,0:T(8,128)S(1)}, u32[]{:S(2)}, u32[]{:S(2)}) collective-permute-start(f32[128,128]{1,0:T(8,128)S(1)} %add.30), channel_id=1, source_target_pairs={{0,2},{1,3},{2,0},{3,1},{4,6},{5,7},{6,4},{7,5},{8,10},{9,11},{10,... | collective-permute-start | bytes 196616 | tf_op jit(solution)/shard_map/ppermute | solution.py:237
  119.3 12.6 %all-to-all-start.2 = ((f32[32,8,128]{2,1,0:T(8,128)}), f32[32,8,128]{2,1,0:T(8,128)S(1)}, u32[]{:S(2)}, u32[]{:S(2)}) async-start(f32[32,8,128]{2,1,0:T(8,128)} %bitcast.5), calls=%async_computation.2 | async-start | bytes 262144 | tf_op jit(solution)/shard_map/all_to_all | solution.py:271
  121.9 9.4 %collective-permute-start.4 = (f32[128,128]{1,0:T(8,128)S(1)}, f32[128,128]{1,0:T(8,128)S(1)}, u32[]{:S(2)}, u32[]{:S(2)}) collective-permute-start(f32[128,128]{1,0:T(8,128)S(1)} %add.31), channel_id=1, source_target_pairs={{0,4},{1,5},{2,6},{3,7},{4,0},{5,1},{6,2},{7,3},{8,12},{9,13},{10,... | collective-permute-start | bytes 196616 | tf_op jit(solution)/shard_map/ppermute | solution.py:237

commit v13 on v12

--- a/solution.py
+++ b/solution.py
@@ -9,6 +9,7 @@
 
 BLOCK = 256
 AXES = ("narrow", "wide")
+TURNED = ("wide", "narrow")
 
 
 def signs(order):
@@ -169,10 +170,11 @@
     return rows.reshape(len(owners) * devices * most)
 
 
-def count_kernel(rows_here, me_ref, picks_ref, out_ref):
+def count_kernel(rows_here, wide, me_ref, picks_ref, out_ref):
     picks = picks_ref[...]
     rows, devices = out_ref.shape
     owner = picks >> rows_here.bit_length() - 1
+    owner = (owner & wide - 1) * (devices // wide) + (owner >> wide.bit_length() - 1)
     local = picks & rows_here - 1
     held = local >> rows.bit_length() - 1 == me_ref[0]
     place = jnp.where(held, local & rows - 1, -1)
@@ -190,7 +192,7 @@
 
 def count_picks(picks, me, rows_here, devices):
     return pl.pallas_call(
-        functools.partial(count_kernel, rows_here),
+        functools.partial(count_kernel, rows_here, lax.axis_size("wide")),
         out_shape=jax.ShapeDtypeStruct((rows_here // devices, devices), jnp.float32),
         in_specs=[
             pl.BlockSpec(memory_space=pltpu.SMEM),
@@ -256,13 +258,14 @@
     local = local.reshape(devices, rows_here // devices, width)
     wanted = send_rows(picks, [me], rows_here, devices, most)
     spots = landing(lax.dynamic_slice(picks, (me * per,), (per,)), rows_here, most)
-    counts = count_picks(picks, me, rows_here, devices)
-    slices = lax.all_to_all(local, AXES, 0, 0, tiled=True)
+    counts = count_picks(picks, lax.axis_index(TURNED), rows_here, devices)
+    slices = lax.all_to_all(local, TURNED, 0, 0, tiled=True)
     slices, wanted, spots, counts = lax.optimization_barrier((slices, wanted, spots, counts))
     slices = device_sums(slices)
-    mixed = lax.all_to_all(slices, AXES, 0, 0, tiled=True)
+    mixed = lax.all_to_all(slices, TURNED, 0, 0, tiled=True)
     gram = gram_part(counts, slices)
     levels = [(axis, l) for axis in AXES for l in range(lax.axis_size(axis).bit_length() - 1)]
+    levels = levels[::-1]
     for axis, level in levels[:-1]:
         gram = add_partner(gram, axis, level)
     mixed, gram = lax.optimization_barrier((mixed, gram))

time: 134 us -> 148 us (1.10)
  waiting for transfers between devices: 94.8 us -> 109 us
    ppermute x5, waiting for transfers between devices: 31.9 us -> 56 us  [add_partner(): return value + lax.ppermute(value, axis, pairs)]
    all_to_all x2, waiting for transfers between devices: 62.8 us -> 47.4 us  [the longest x1 47.4 us: on_device(): slices = lax.all_to_all(local, TURNED, 0, 0, tiled=True)]
    all_to_all x1, waiting for transfers between devices: 0.01 us -> 5.43 us  [on_device(): lax.all_to_all(chosen.reshape(devices, most, width), AXES, 0, 0, tiled=True)]
    ppermute x5, starting transfers between devices: 8.86 us -> 5.93 us  [add_partner(): return value + lax.ppermute(value, axis, pairs)]
  transfers between devices with their start and end apart: 8 -> 8, of which waited for: 7 -> 6; matrix products, arithmetic and copies ran while one was open for 1% -> 1% of each run, Pallas kernels for 4% -> 4%
where the time goes in v13:
time: 148 us; the launch traced here: 147 us
  waiting for transfers between devices  109 us (74%)
  starting transfers between devices  21.3 us (14%)
  Pallas kernels  8.78 us (6%)
  local copies, waits for them, and re-layouts  6.4 us (4%)
    ppermute x5, waiting for transfers between devices, add_partner(): return value + lax.ppermute(value, axis, pairs)  56 us
    all_to_all x1, waiting for transfers between devices, on_device(): slices = lax.all_to_all(local, TURNED, 0, 0, tiled=True)  47.4 us
    all_to_all x1, starting transfers between devices, on_device(): slices = lax.all_to_all(local, TURNED, 0, 0, tiled=True)  7.3 us
    ppermute x5, starting transfers between devices, add_partner(): return value + lax.ppermute(value, axis, pairs)  5.93 us
    all_to_all x1, waiting for transfers between devices, on_device(): lax.all_to_all(chosen.reshape(devices, most, width), AXES, 0, 0, tiled=True)  5.43 us
    all_to_all x1, starting transfers between devices, on_device(): mixed = lax.all_to_all(slices, TURNED, 0, 0, tiled=True)  4.02 us
    all_to_all x1, starting transfers between devices, on_device(): lax.all_to_all(chosen.reshape(devices, most, width), AXES, 0, 0, tiled=True)  4.01 us
    unnamed x8, local copies, waits for them, and re-layouts  3.62 us
  transfers between devices with their start and end apart: 8, of which 6 were waited for; matrix products, arithmetic and copies ran while one was open for 1% of the time, Pallas kernels for 4%

profile of v13, /device:TPU:0, one launch (start us, length us, event | category | flops | bytes accessed | tf_op | source)
XLA Modules:
  0.0 147.2 jit_solution(8684836985761850999)
XLA Ops:
  0.6 1.6 %copy-done.1 = f32[4096,128]{1,0:T(8,128)S(1)} copy-done((f32[4096,128]{1,0:T(8,128)S(1)}, f32[4096,128]{1,0:T(8,128)}, u32[]{:S(2)}) %copy-start.1) | copy-done | bytes 2097176
  2.2 0.7 copy-done.3
  2.9 1.9 %shard_map.58 = f32[4096,128]{1,0:T(8,128)S(1)} custom-call(s32[32,128]{1,0:T(8,128)S(1)} %bitcast.12, f32[4096,128]{1,0:T(8,128)S(1)} %copy-done.1), custom_call_target="tpu_custom_call" | custom-call | tf_op jit(solution)/shard_map/pallas_call | solution.py:66
  4.9 0.0 copy-start
  4.9 1.3 copy-done
  6.2 7.3 %all-to-all-start = ((f32[32,128,128]{2,1,0:T(8,128)}), f32[32,128,128]{2,1,0:T(8,128)S(1)}, u32[]{:S(2)}, u32[]{:S(2)}) async-start(f32[32,128,128]{2,1,0:T(8,128)} %bitcast.10), calls=%async_computation | async-start | bytes 4194304 | tf_op jit(solution)/shard_map/all_to_all | solution.py:262
  13.6 0.3 shard_map.59
  13.8 0.1 reshape.40
  13.9 0.7 shard_map.60.counts_ref
  14.6 0.1 and_select_fusion
  14.7 0.2 convert_reduce_fusion
  14.9 0.1 multiply_add_fusion
  15.0 47.4 %all-to-all-done.in_ref = f32[32,128,128]{2,1,0:T(8,128)S(1)} async-done(((f32[32,128,128]{2,1,0:T(8,128)}), f32[32,128,128]{2,1,0:T(8,128)S(1)}, u32[]{:S(2)}, u32[]{:S(2)}) %all-to-all-start) | async-done | bytes 2097184 | tf_op jit(solution)/shard_map/all_to_all | solution.py:262
  62.4 1.5 %shard_map.61.held_ref = f32[32,128,128]{2,1,0:T(8,128)} custom-call(f32[32,128,128]{2,1,0:T(8,128)S(1)} %all-to-all-done.in_ref), custom_call_target="tpu_custom_call" | custom-call | tf_op jit(solution)/shard_map/pallas_call | solution.py:109
  63.9 4.0 %all-to-all-start.1 = ((f32[32,128,128]{2,1,0:T(8,128)}), f32[32,128,128]{2,1,0:T(8,128)S(1)}, u32[]{:S(2)}, u32[]{:S(2)}) async-start(f32[32,128,128]{2,1,0:T(8,128)} %shard_map.61.held_ref), calls=%async_computation.1 | async-start | bytes 4194304 | tf_op jit(solution)/shard_map/all_to_all | solution.py:265
  68.0 3.1 %shard_map.62 = f32[128,128]{1,0:T(8,128)S(1)} custom-call(f32[128,32]{1,0:T(8,128)S(1)} %shard_map.60.counts_ref, f32[32,128,128]{2,1,0:T(8,128)} %shard_map.61.held_ref), custom_call_target="tpu_custom_call" | custom-call | tf_op jit(solution)/shard_map/pallas_call | solution.py:228
  71.0 2.7 %collective-permute-start = (f32[128,128]{1,0:T(8,128)S(1)}, f32[128,128]{1,0:T(8,128)S(1)}, u32[]{:S(2)}, u32[]{:S(2)}) collective-permute-start(f32[128,128]{1,0:T(8,128)S(1)} %shard_map.62), channel_id=1, source_target_pairs={{0,4},{1,5},{2,6},{3,7},{4,0},{5,1},{6,2},{7,3},{8,12},{9,13},{10,... | collective-permute-start | bytes 196616 | tf_op jit(solution)/shard_map/ppermute | solution.py:239
  73.8 45.9 %collective-permute-done = f32[128,128]{1,0:T(8,128)S(1)} collective-permute-done((f32[128,128]{1,0:T(8,128)S(1)}, f32[128,128]{1,0:T(8,128)S(1)}, u32[]{:S(2)}, u32[]{:S(2)}) %collective-permute-start) | collective-permute-done | bytes 65568 | tf_op jit(solution)/shard_map/ppermute | solution.py:239
  119.7 0.1 collective-permute-start.1
  119.8 4.3 %collective-permute-done.1 = f32[128,128]{1,0:T(8,128)S(1)} collective-permute-done((f32[128,128]{1,0:T(8,128)S(1)}, f32[128,128]{1,0:T(8,128)S(1)}, u32[]{:S(2)}, u32[]{:S(2)}) %collective-permute-start.1) | collective-permute-done | bytes 65568 | tf_op jit(solution)/shard_map/ppermute | solution.py:239
  124.0 1.4 collective-permute-start.2
  125.4 3.0 %collective-permute-done.2 = f32[128,128]{1,0:T(8,128)S(1)} collective-permute-done((f32[128,128]{1,0:T(8,128)S(1)}, f32[128,128]{1,0:T(8,128)S(1)}, u32[]{:S(2)}, u32[]{:S(2)}) %collective-permute-start.2) | collective-permute-done | bytes 65568 | tf_op jit(solution)/shard_map/ppermute | solution.py:239
  128.4 1.5 collective-permute-start.3
  129.8 2.9 %collective-permute-done.3 = f32[128,128]{1,0:T(8,128)S(1)} collective-permute-done((f32[128,128]{1,0:T(8,128)S(1)}, f32[128,128]{1,0:T(8,128)S(1)}, u32[]{:S(2)}, u32[]{:S(2)}) %collective-permute-start.3) | collective-permute-done | bytes 65568 | tf_op jit(solution)/shard_map/ppermute | solution.py:239
  132.7 0.0 all-to-all-done.1
  132.7 1.3 gather_fusion
  134.1 4.0 %all-to-all-start.2 = ((f32[32,8,128]{2,1,0:T(8,128)}), f32[32,8,128]{2,1,0:T(8,128)S(1)}, u32[]{:S(2)}, u32[]{:S(2)}) async-start(f32[32,8,128]{2,1,0:T(8,128)} %bitcast.6), calls=%async_computation.2 | async-start | bytes 262144 | tf_op jit(solution)/shard_map/all_to_all | solution.py:274
  138.1 0.3 collective-permute-start.4
  138.4 1.3 shard_map.63
  139.8 0.6 add_multiply_fusion
  140.4 5.4 %all-to-all-done.2 = f32[32,8,128]{2,1,0:T(8,128)S(1)} async-done(((f32[32,8,128]{2,1,0:T(8,128)}), f32[32,8,128]{2,1,0:T(8,128)S(1)}, u32[]{:S(2)}, u32[]{:S(2)}) %all-to-all-start.2) | async-done | bytes 131104 | tf_op jit(solution)/shard_map/all_to_all | solution.py:274
  145.8 1.3 gather_fusion.1
  (12 shorter events, 0.1 us)
Async XLA Ops:
  0.6 1.6 %copy-start.1 = (f32[4096,128]{1,0:T(8,128)S(1)}, f32[4096,128]{1,0:T(8,128)}, u32[]{:S(2)}) copy-start(f32[4096,128]{1,0:T(8,128)} %panel_ref.1) | copy-start | bytes 6291460
  2.2 0.7 copy-start.3
  4.9 1.3 copy-start
  6.2 7.3 %copy-start.2 = (s32[8192]{0:T(1024)S(1)}, s32[8192]{0:T(1024)}, u32[]{:S(2)}) copy-start(s32[8192]{0:T(1024)} %param.5) | copy-start | bytes 98308
  6.2 56.2 %all-to-all-start = ((f32[32,128,128]{2,1,0:T(8,128)}), f32[32,128,128]{2,1,0:T(8,128)S(1)}, u32[]{:S(2)}, u32[]{:S(2)}) async-start(f32[32,128,128]{2,1,0:T(8,128)} %bitcast.10), calls=%async_computation | async-start | bytes 4194304 | tf_op jit(solution)/shard_map/all_to_all | solution.py:262
  63.9 68.8 %all-to-all-start.1 = ((f32[32,128,128]{2,1,0:T(8,128)}), f32[32,128,128]{2,1,0:T(8,128)S(1)}, u32[]{:S(2)}, u32[]{:S(2)}) async-start(f32[32,128,128]{2,1,0:T(8,128)} %shard_map.61.held_ref), calls=%async_computation.1 | async-start | bytes 4194304 | tf_op jit(solution)/shard_map/all_to_all | solution.py:265
  71.0 48.6 %collective-permute-start = (f32[128,128]{1,0:T(8,128)S(1)}, f32[128,128]{1,0:T(8,128)S(1)}, u32[]{:S(2)}, u32[]{:S(2)}) collective-permute-start(f32[128,128]{1,0:T(8,128)S(1)} %shard_map.62), channel_id=1, source_target_pairs={{0,4},{1,5},{2,6},{3,7},{4,0},{5,1},{6,2},{7,3},{8,12},{9,13},{10,... | collective-permute-start | bytes 196616 | tf_op jit(solution)/shard_map/ppermute | solution.py:239
  119.7 4.3 %collective-permute-start.1 = (f32[128,128]{1,0:T(8,128)S(1)}, f32[128,128]{1,0:T(8,128)S(1)}, u32[]{:S(2)}, u32[]{:S(2)}) collective-permute-start(f32[128,128]{1,0:T(8,128)S(1)} %add.32), channel_id=1, source_target_pairs={{0,2},{1,3},{2,0},{3,1},{4,6},{5,7},{6,4},{7,5},{8,10},{9,11},{10,... | collective-permute-start | bytes 196616 | tf_op jit(solution)/shard_map/ppermute | solution.py:239
  124.0 4.3 %collective-permute-start.2 = (f32[128,128]{1,0:T(8,128)S(1)}, f32[128,128]{1,0:T(8,128)S(1)}, u32[]{:S(2)}, u32[]{:S(2)}) collective-permute-start(f32[128,128]{1,0:T(8,128)S(1)} %add.33), channel_id=1, source_target_pairs={{0,1},{1,0},{2,3},{3,2},{4,5},{5,4},{6,7},{7,6},{8,9},{9,8},{10,11... | collective-permute-start | bytes 196616 | tf_op jit(solution)/shard_map/ppermute | solution.py:239
  128.4 4.3 %collective-permute-start.3 = (f32[128,128]{1,0:T(8,128)S(1)}, f32[128,128]{1,0:T(8,128)S(1)}, u32[]{:S(2)}, u32[]{:S(2)}) collective-permute-start(f32[128,128]{1,0:T(8,128)S(1)} %add.34), channel_id=1, source_target_pairs={{0,16},{8,24},{16,0},{24,8},{1,17},{9,25},{17,1},{25,9},{2,18},{10... | collective-permute-start | bytes 196616 | tf_op jit(solution)/shard_map/ppermute | solution.py:239
  134.1 11.8 %all-to-all-start.2 = ((f32[32,8,128]{2,1,0:T(8,128)}), f32[32,8,128]{2,1,0:T(8,128)S(1)}, u32[]{:S(2)}, u32[]{:S(2)}) async-start(f32[32,8,128]{2,1,0:T(8,128)} %bitcast.6), calls=%async_computation.2 | async-start | bytes 262144 | tf_op jit(solution)/shard_map/all_to_all | solution.py:274
  138.1 1.7 %collective-permute-start.4 = (f32[128,128]{1,0:T(8,128)S(1)}, f32[128,128]{1,0:T(8,128)S(1)}, u32[]{:S(2)}, u32[]{:S(2)}) collective-permute-start(f32[128,128]{1,0:T(8,128)S(1)} %add.35), channel_id=1, source_target_pairs={{0,8},{8,0},{16,24},{24,16},{1,9},{9,1},{17,25},{25,17},{2,10},{10... | collective-permute-start | bytes 196616 | tf_op jit(solution)/shard_map/ppermute | solution.py:239

commit v14 on v13

--- a/solution.py
+++ b/solution.py
@@ -21,17 +21,14 @@
     return (1 - 2 * parity).astype(jnp.float32)
 
 
-def local_kernel(scale, flips_ref, panel_ref, *refs):
-    *outs, held = refs
-    blocks = panel_ref.shape[0] // BLOCK
-    width = panel_ref.shape[1]
-    lanes = flips_ref.shape[1]
-    per = BLOCK // lanes
+def local_kernel(scale, flips_ref, panel_ref, out_ref, held, sent):
+    blocks, _, width = panel_ref.shape
+    per = BLOCK // flips_ref.shape[1]
     base = signs(BLOCK)
     for b in range(blocks):
         row = jnp.concatenate([flips_ref[b * per + i : b * per + i + 1, :] for i in range(per)], axis=1)
         mixer = (base * (1 - 2 * row).astype(jnp.float32)).astype(jnp.bfloat16)
-        values = panel_ref[b * BLOCK : (b + 1) * BLOCK, :]
+        values = panel_ref[b]
         high = values.astype(jnp.bfloat16)
         rest = values - high.astype(jnp.float32)
         middle = rest.astype(jnp.bfloat16)
@@ -40,7 +37,7 @@
         out = jnp.dot(mixer, parts, preferred_element_type=jnp.float32)
         held[b] = out[:, :width] + out[:, width : 2 * width] + out[:, 2 * width :]
     strip = 16
-    places = [(i, j) for i in range(len(outs)) for j in range(outs[i].shape[0] // BLOCK)]
+    quarter = BLOCK // 4
 
     def body(step, carry):
         at = pl.multiple_of(step * strip, strip)
@@ -53,24 +50,33 @@
             ]
             apart *= 2
         for b in range(blocks):
-            which, place = places[b]
-            spot = pl.multiple_of(place * BLOCK + at, strip)
-            outs[which][pl.ds(spot, strip), :] = items[b] * scale
+            held[b, pl.ds(at, strip), :] = items[b] * scale
         return carry
 
-    lax.fori_loop(0, BLOCK // strip, body, 0)
-
-
-def local_transform(panel, flips, scale, shares):
+    copies = []
+    for part in range(4):
+        first = part * quarter // strip
+        lax.fori_loop(first, first + quarter // strip, body, 0)
+        span = pl.ds(part * quarter, quarter)
+        copies.append(
+            pltpu.make_async_copy(held.at[:, span, :], out_ref.at[:, span, :], sent.at[part])
+        )
+        copies[-1].start()
+    for copy in copies:
+        copy.wait()
+
+
+def local_transform(panel, flips, scale):
     rows, width = panel.shape
+    shape = (rows // BLOCK, BLOCK, width)
     return pl.pallas_call(
         functools.partial(local_kernel, scale),
-        out_shape=[jax.ShapeDtypeStruct((share, width), jnp.float32) for share in shares],
+        out_shape=jax.ShapeDtypeStruct(shape, jnp.float32),
         in_specs=[pl.BlockSpec(memory_space=pltpu.VMEM)] * 2,
-        out_specs=[pl.BlockSpec(memory_space=pltpu.VMEM)] * len(shares),
-        scratch_shapes=[pltpu.VMEM((rows // BLOCK, BLOCK, width), jnp.float32)],
-        compiler_params=pltpu.CompilerParams(vmem_limit_bytes=32 * 2**20),
-    )(flips.reshape(rows // 128, 128), panel)
+        out_specs=pl.BlockSpec(memory_space=pl.ANY),
+        scratch_shapes=[pltpu.VMEM(shape, jnp.float32), pltpu.SemaphoreType.DMA((4,))],
+        compiler_params=pltpu.CompilerParams(vmem_limit_bytes=32 * 2**20),
+    )(flips.reshape(rows // 128, 128), panel.reshape(shape))
 
 
 def device_kernel(in_ref, out_ref, held, sent):
@@ -254,7 +260,7 @@
     per = picks.shape[0] // devices
     most = -(-per // devices)
 
-    local = local_transform(panel, flips, scale, [rows_here])[0]
+    local = local_transform(panel, flips, scale)
     local = local.reshape(devices, rows_here // devices, width)
     wanted = send_rows(picks, [me], rows_here, devices, most)
     spots = landing(lax.dynamic_slice(picks, (me * per,), (per,)), rows_here, most)
@@ -265,7 +271,7 @@
     mixed = lax.all_to_all(slices, TURNED, 0, 0, tiled=True)
     gram = gram_part(counts, slices)
     levels = [(axis, l) for axis in AXES for l in range(lax.axis_size(axis).bit_length() - 1)]
-    levels = levels[::-1]
+    levels = levels[1:] + levels[:1]
     for axis, level in levels[:-1]:
         gram = add_partner(gram, axis, level)
     mixed, gram = lax.optimization_barrier((mixed, gram))

time: 148 us -> 135 us (0.912)
  waiting for transfers between devices: 109 us -> 94.3 us
  starting transfers between devices: 21.3 us -> 22.8 us
    ppermute x5, waiting for transfers between devices: 56 us -> 41.5 us  [add_partner(): return value + lax.ppermute(value, axis, pairs)]
    ppermute x5, starting transfers between devices: 5.93 us -> 7.43 us  [add_partner(): return value + lax.ppermute(value, axis, pairs)]
where the time goes in v14:
time: 135 us; the launch traced here: 134 us
  waiting for transfers between devices  94.3 us (70%)
  starting transfers between devices  22.8 us (17%)
  Pallas kernels  8.96 us (7%)
  local copies, waits for them, and re-layouts  6.4 us (5%)
    all_to_all x1, waiting for transfers between devices, on_device(): slices = lax.all_to_all(local, TURNED, 0, 0, tiled=True)  47.4 us
    ppermute x5, waiting for transfers between devices, add_partner(): return value + lax.ppermute(value, axis, pairs)  41.5 us
    ppermute x5, starting transfers between devices, add_partner(): return value + lax.ppermute(value, axis, pairs)  7.43 us
    all_to_all x1, starting transfers between devices, on_device(): slices = lax.all_to_all(local, TURNED, 0, 0, tiled=True)  7.3 us
    all_to_all x1, waiting for transfers between devices, on_device(): lax.all_to_all(chosen.reshape(devices, most, width), AXES, 0, 0, tiled=True)  5.43 us
    all_to_all x1, starting transfers between devices, on_device(): mixed = lax.all_to_all(slices, TURNED, 0, 0, tiled=True)  4.02 us
    all_to_all x1, starting transfers between devices, on_device(): lax.all_to_all(chosen.reshape(devices, most, width), AXES, 0, 0, tiled=True)  4.02 us
    unnamed x8, local copies, waits for them, and re-layouts  3.62 us
  transfers between devices with their start and end apart: 8, of which 6 were waited for; matrix products, arithmetic and copies ran while one was open for 1% of the time, Pallas kernels for 4%

profile of v14, /device:TPU:0, one launch (start us, length us, event | category | flops | bytes accessed | tf_op | source)
XLA Modules:
  0.0 134.3 jit_solution(7732440864338382563)
XLA Ops:
  0.6 1.6 %copy-done.1 = f32[4096,128]{1,0:T(8,128)S(1)} copy-done((f32[4096,128]{1,0:T(8,128)S(1)}, f32[4096,128]{1,0:T(8,128)}, u32[]{:S(2)}) %copy-start.1) | copy-done | bytes 2097176
  2.2 0.7 copy-done.3
  2.9 2.1 %shard_map.58 = f32[16,256,128]{2,1,0:T(8,128)S(1)} custom-call(s32[32,128]{1,0:T(8,128)S(1)} %bitcast.14, f32[16,256,128]{2,1,0:T(8,128)S(1)} %bitcast.12), custom_call_target="tpu_custom_call" | custom-call | tf_op jit(solution)/shard_map/pallas_call | solution.py:72
  5.1 0.0 copy-start
  5.1 1.3 copy-done
  6.4 7.3 %all-to-all-start = ((f32[32,128,128]{2,1,0:T(8,128)}), f32[32,128,128]{2,1,0:T(8,128)S(1)}, u32[]{:S(2)}, u32[]{:S(2)}) async-start(f32[32,128,128]{2,1,0:T(8,128)} %bitcast.11), calls=%async_computation | async-start | bytes 4194304 | tf_op jit(solution)/shard_map/all_to_all | solution.py:268
  13.7 0.3 shard_map.59
  14.0 0.1 reshape.44
  14.1 0.7 shard_map.60.counts_ref
  14.8 0.1 and_select_fusion
  14.9 0.2 convert_reduce_fusion
  15.1 0.1 multiply_add_fusion
  15.2 47.4 %all-to-all-done.in_ref = f32[32,128,128]{2,1,0:T(8,128)S(1)} async-done(((f32[32,128,128]{2,1,0:T(8,128)}), f32[32,128,128]{2,1,0:T(8,128)S(1)}, u32[]{:S(2)}, u32[]{:S(2)}) %all-to-all-start) | async-done | bytes 2097184 | tf_op jit(solution)/shard_map/all_to_all | solution.py:268
  62.6 1.5 %shard_map.61.held_ref = f32[32,128,128]{2,1,0:T(8,128)} custom-call(f32[32,128,128]{2,1,0:T(8,128)S(1)} %all-to-all-done.in_ref), custom_call_target="tpu_custom_call" | custom-call | tf_op jit(solution)/shard_map/pallas_call | solution.py:115
  64.1 4.0 %all-to-all-start.1 = ((f32[32,128,128]{2,1,0:T(8,128)}), f32[32,128,128]{2,1,0:T(8,128)S(1)}, u32[]{:S(2)}, u32[]{:S(2)}) async-start(f32[32,128,128]{2,1,0:T(8,128)} %shard_map.61.held_ref), calls=%async_computation.1 | async-start | bytes 4194304 | tf_op jit(solution)/shard_map/all_to_all | solution.py:271
  68.1 3.1 %shard_map.62 = f32[128,128]{1,0:T(8,128)S(1)} custom-call(f32[128,32]{1,0:T(8,128)S(1)} %shard_map.60.counts_ref, f32[32,128,128]{2,1,0:T(8,128)} %shard_map.61.held_ref), custom_call_target="tpu_custom_call" | custom-call | tf_op jit(solution)/shard_map/pallas_call | solution.py:234
  71.2 1.8 %collective-permute-start = (f32[128,128]{1,0:T(8,128)S(1)}, f32[128,128]{1,0:T(8,128)S(1)}, u32[]{:S(2)}, u32[]{:S(2)}) collective-permute-start(f32[128,128]{1,0:T(8,128)S(1)} %shard_map.62), channel_id=1, source_target_pairs={{0,16},{8,24},{16,0},{24,8},{1,17},{9,25},{17,1},{25,9},{2,18},{10... | collective-permute-start | bytes 196616 | tf_op jit(solution)/shard_map/ppermute | solution.py:245
  73.0 12.3 %collective-permute-done = f32[128,128]{1,0:T(8,128)S(1)} collective-permute-done((f32[128,128]{1,0:T(8,128)S(1)}, f32[128,128]{1,0:T(8,128)S(1)}, u32[]{:S(2)}, u32[]{:S(2)}) %collective-permute-start) | collective-permute-done | bytes 65568 | tf_op jit(solution)/shard_map/ppermute | solution.py:245
  85.3 1.0 collective-permute-start.1
  86.4 4.3 %collective-permute-done.1 = f32[128,128]{1,0:T(8,128)S(1)} collective-permute-done((f32[128,128]{1,0:T(8,128)S(1)}, f32[128,128]{1,0:T(8,128)S(1)}, u32[]{:S(2)}, u32[]{:S(2)}) %collective-permute-start.1) | collective-permute-done | bytes 65568 | tf_op jit(solution)/shard_map/ppermute | solution.py:245
  90.7 0.1 collective-permute-start.2
  90.7 13.9 %collective-permute-done.2 = f32[128,128]{1,0:T(8,128)S(1)} collective-permute-done((f32[128,128]{1,0:T(8,128)S(1)}, f32[128,128]{1,0:T(8,128)S(1)}, u32[]{:S(2)}, u32[]{:S(2)}) %collective-permute-start.2) | collective-permute-done | bytes 65568 | tf_op jit(solution)/shard_map/ppermute | solution.py:245
  104.6 4.2 %collective-permute-start.3 = (f32[128,128]{1,0:T(8,128)S(1)}, f32[128,128]{1,0:T(8,128)S(1)}, u32[]{:S(2)}, u32[]{:S(2)}) collective-permute-start(f32[128,128]{1,0:T(8,128)S(1)} %add.34), channel_id=1, source_target_pairs={{0,4},{1,5},{2,6},{3,7},{4,0},{5,1},{6,2},{7,3},{8,12},{9,13},{10,... | collective-permute-start | bytes 196616 | tf_op jit(solution)/shard_map/ppermute | solution.py:245
  108.8 11.0 %collective-permute-done.3 = f32[128,128]{1,0:T(8,128)S(1)} collective-permute-done((f32[128,128]{1,0:T(8,128)S(1)}, f32[128,128]{1,0:T(8,128)S(1)}, u32[]{:S(2)}, u32[]{:S(2)}) %collective-permute-start.3) | collective-permute-done | bytes 65568 | tf_op jit(solution)/shard_map/ppermute | solution.py:245
  119.9 1.3 %gather_fusion = f32[256,128]{1,0:T(8,128)} fusion(f32[4096,128]{1,0:T(8,128)S(1)} %bitcast.9, s32[1024]{0:T(1024)S(1)} %pad_clamp_fusion.1), kind=kCustom, calls=%fused_computation | custom fusion | bytes 263168 | tf_op jit(solution)/shard_map/jit(_take)/gather | solution.py:279
  121.2 4.0 %all-to-all-start.2 = ((f32[32,8,128]{2,1,0:T(8,128)}), f32[32,8,128]{2,1,0:T(8,128)S(1)}, u32[]{:S(2)}, u32[]{:S(2)}) async-start(f32[32,8,128]{2,1,0:T(8,128)} %bitcast.7), calls=%async_computation.2 | async-start | bytes 262144 | tf_op jit(solution)/shard_map/all_to_all | solution.py:280
  125.2 0.3 collective-permute-start.4
  125.6 1.3 shard_map.63
  126.9 0.0 collective-permute-done.4
  126.9 0.6 add_multiply_fusion
  127.5 5.4 %all-to-all-done.2 = f32[32,8,128]{2,1,0:T(8,128)S(1)} async-done(((f32[32,8,128]{2,1,0:T(8,128)}), f32[32,8,128]{2,1,0:T(8,128)S(1)}, u32[]{:S(2)}, u32[]{:S(2)}) %all-to-all-start.2) | async-done | bytes 131104 | tf_op jit(solution)/shard_map/all_to_all | solution.py:280
  133.0 1.3 gather_fusion.1
  (12 shorter events, 0.1 us)
Async XLA Ops:
  0.6 1.6 %copy-start.1 = (f32[4096,128]{1,0:T(8,128)S(1)}, f32[4096,128]{1,0:T(8,128)}, u32[]{:S(2)}) copy-start(f32[4096,128]{1,0:T(8,128)} %param.3) | copy-start | bytes 6291460
  2.2 0.7 copy-start.3
  5.1 1.3 copy-start
  6.4 7.3 %copy-start.2 = (s32[8192]{0:T(1024)S(1)}, s32[8192]{0:T(1024)}, u32[]{:S(2)}) copy-start(s32[8192]{0:T(1024)} %param.5) | copy-start | bytes 98308
  6.4 56.2 %all-to-all-start = ((f32[32,128,128]{2,1,0:T(8,128)}), f32[32,128,128]{2,1,0:T(8,128)S(1)}, u32[]{:S(2)}, u32[]{:S(2)}) async-start(f32[32,128,128]{2,1,0:T(8,128)} %bitcast.11), calls=%async_computation | async-start | bytes 4194304 | tf_op jit(solution)/shard_map/all_to_all | solution.py:268
  64.1 55.7 %all-to-all-start.1 = ((f32[32,128,128]{2,1,0:T(8,128)}), f32[32,128,128]{2,1,0:T(8,128)S(1)}, u32[]{:S(2)}, u32[]{:S(2)}) async-start(f32[32,128,128]{2,1,0:T(8,128)} %shard_map.61.held_ref), calls=%async_computation.1 | async-start | bytes 4194304 | tf_op jit(solution)/shard_map/all_to_all | solution.py:271
  71.2 14.1 %collective-permute-start = (f32[128,128]{1,0:T(8,128)S(1)}, f32[128,128]{1,0:T(8,128)S(1)}, u32[]{:S(2)}, u32[]{:S(2)}) collective-permute-start(f32[128,128]{1,0:T(8,128)S(1)} %shard_map.62), channel_id=1, source_target_pairs={{0,16},{8,24},{16,0},{24,8},{1,17},{9,25},{17,1},{25,9},{2,18},{10... | collective-permute-start | bytes 196616 | tf_op jit(solution)/shard_map/ppermute | solution.py:245
  85.3 5.3 %collective-permute-start.1 = (f32[128,128]{1,0:T(8,128)S(1)}, f32[128,128]{1,0:T(8,128)S(1)}, u32[]{:S(2)}, u32[]{:S(2)}) collective-permute-start(f32[128,128]{1,0:T(8,128)S(1)} %add.32), channel_id=1, source_target_pairs={{0,1},{1,0},{2,3},{3,2},{4,5},{5,4},{6,7},{7,6},{8,9},{9,8},{10,11... | collective-permute-start | bytes 196616 | tf_op jit(solution)/shard_map/ppermute | solution.py:245
  90.7 14.0 %collective-permute-start.2 = (f32[128,128]{1,0:T(8,128)S(1)}, f32[128,128]{1,0:T(8,128)S(1)}, u32[]{:S(2)}, u32[]{:S(2)}) collective-permute-start(f32[128,128]{1,0:T(8,128)S(1)} %add.33), channel_id=1, source_target_pairs={{0,2},{1,3},{2,0},{3,1},{4,6},{5,7},{6,4},{7,5},{8,10},{9,11},{10,... | collective-permute-start | bytes 196616 | tf_op jit(solution)/shard_map/ppermute | solution.py:245
  104.6 15.2 %collective-permute-start.3 = (f32[128,128]{1,0:T(8,128)S(1)}, f32[128,128]{1,0:T(8,128)S(1)}, u32[]{:S(2)}, u32[]{:S(2)}) collective-permute-start(f32[128,128]{1,0:T(8,128)S(1)} %add.34), channel_id=1, source_target_pairs={{0,4},{1,5},{2,6},{3,7},{4,0},{5,1},{6,2},{7,3},{8,12},{9,13},{10,... | collective-permute-start | bytes 196616 | tf_op jit(solution)/shard_map/ppermute | solution.py:245
  121.2 11.8 %all-to-all-start.2 = ((f32[32,8,128]{2,1,0:T(8,128)}), f32[32,8,128]{2,1,0:T(8,128)S(1)}, u32[]{:S(2)}, u32[]{:S(2)}) async-start(f32[32,8,128]{2,1,0:T(8,128)} %bitcast.7), calls=%async_computation.2 | async-start | bytes 262144 | tf_op jit(solution)/shard_map/all_to_all | solution.py:280
  125.2 1.7 %collective-permute-start.4 = (f32[128,128]{1,0:T(8,128)S(1)}, f32[128,128]{1,0:T(8,128)S(1)}, u32[]{:S(2)}, u32[]{:S(2)}) collective-permute-start(f32[128,128]{1,0:T(8,128)S(1)} %add.35), channel_id=1, source_target_pairs={{0,8},{8,0},{16,24},{24,16},{1,9},{9,1},{17,25},{25,17},{2,10},{10... | collective-permute-start | bytes 196616 | tf_op jit(solution)/shard_map/ppermute | solution.py:245

commit v15 on v14

--- a/solution.py
+++ b/solution.py
@@ -21,14 +21,24 @@
     return (1 - 2 * parity).astype(jnp.float32)
 
 
-def local_kernel(scale, flips_ref, panel_ref, out_ref, held, sent):
+def local_kernel(scale, flips_ref, panel_ref, out_ref, flags, held, arrived, sent):
     blocks, _, width = panel_ref.shape
     per = BLOCK // flips_ref.shape[1]
+    share = blocks // 4
+    loads = [pltpu.make_async_copy(flips_ref, flags, arrived.at[4])]
+    for part in range(4):
+        span = pl.ds(part * share, share)
+        loads.append(pltpu.make_async_copy(panel_ref.at[span], held.at[span], arrived.at[part]))
+    for load in loads:
+        load.start()
     base = signs(BLOCK)
+    loads[0].wait()
     for b in range(blocks):
-        row = jnp.concatenate([flips_ref[b * per + i : b * per + i + 1, :] for i in range(per)], axis=1)
+        if b % share == 0:
+            loads[1 + b // share].wait()
+        row = jnp.concatenate([flags[b * per + i : b * per + i + 1, :] for i in range(per)], axis=1)
         mixer = (base * (1 - 2 * row).astype(jnp.float32)).astype(jnp.bfloat16)
-        values = panel_ref[b]
+        values = held[b]
         high = values.astype(jnp.bfloat16)
         rest = values - high.astype(jnp.float32)
         middle = rest.astype(jnp.bfloat16)
@@ -72,10 +82,15 @@
     return pl.pallas_call(
         functools.partial(local_kernel, scale),
         out_shape=jax.ShapeDtypeStruct(shape, jnp.float32),
-        in_specs=[pl.BlockSpec(memory_space=pltpu.VMEM)] * 2,
+        in_specs=[pl.BlockSpec(memory_space=pl.ANY)] * 2,
         out_specs=pl.BlockSpec(memory_space=pl.ANY),
-        scratch_shapes=[pltpu.VMEM(shape, jnp.float32), pltpu.SemaphoreType.DMA((4,))],
-        compiler_params=pltpu.CompilerParams(vmem_limit_bytes=32 * 2**20),
+        scratch_shapes=[
+            pltpu.VMEM((rows // 128, 128), jnp.int32),
+            pltpu.VMEM(shape, jnp.float32),
+            pltpu.SemaphoreType.DMA((5,)),
+            pltpu.SemaphoreType.DMA((4,)),
+        ],
+        compiler_params=pltpu.CompilerParams(vmem_limit_bytes=61 * 2**20),
     )(flips.reshape(rows // 128, 128), panel.reshape(shape))
 
 
@@ -271,7 +286,7 @@
     mixed = lax.all_to_all(slices, TURNED, 0, 0, tiled=True)
     gram = gram_part(counts, slices)
     levels = [(axis, l) for axis in AXES for l in range(lax.axis_size(axis).bit_length() - 1)]
-    levels = levels[1:] + levels[:1]
+    levels = levels[:1] + levels[2:] + levels[1:2]
     for axis, level in levels[:-1]:
         gram = add_partner(gram, axis, level)
     mixed, gram = lax.optimization_barrier((mixed, gram))

time: 135 us -> 133 us (0.985)
  local copies, waits for them, and re-layouts: 6.4 us -> 2.79 us
  starting transfers between devices: 22.8 us -> 26.1 us
  waiting for transfers between devices: 94.3 us -> 91.1 us
  Pallas kernels: 8.96 us -> 11.2 us
    unnamed x8 -> x2, local copies, waits for them, and re-layouts: 3.62 us -> 0.01 us
    all_to_all x1, waiting for transfers between devices: 5.43 us -> 2.04 us  [on_device(): lax.all_to_all(chosen.reshape(devices, most, width), AXES, 0, 0, tiled=True)]
    ppermute x5, starting transfers between devices: 7.43 us -> 10.7 us  [add_partner(): return value + lax.ppermute(value, axis, pairs)]
    pallas_call x1, Pallas kernels: 2.12 us -> 4.38 us  [local_transform(): pl.pallas_call(functools.partial(local_kernel, scale), out_shape=jax.Shap...]
  transfers between devices with their start and end apart: 8 -> 8, of which waited for: 6 -> 7; matrix products, arithmetic and copies ran while one was open for 1% -> 1% of each run, Pallas kernels for 4% -> 4%
where the time goes in v15:
time: 133 us
  waiting for transfers between devices  91.1 us (68%)
  starting transfers between devices  26.1 us (20%)
  Pallas kernels  11.2 us (8%)
  local copies, waits for them, and re-layouts  2.79 us (2%)
    all_to_all x1, waiting for transfers between devices, on_device(): slices = lax.all_to_all(local, TURNED, 0, 0, tiled=True)  47.4 us
    ppermute x5, waiting for transfers between devices, add_partner(): return value + lax.ppermute(value, axis, pairs)  41.6 us
    ppermute x5, starting transfers between devices, add_partner(): return value + lax.ppermute(value, axis, pairs)  10.7 us
    all_to_all x1, starting transfers between devices, on_device(): slices = lax.all_to_all(local, TURNED, 0, 0, tiled=True)  7.3 us
    pallas_call x1, Pallas kernels, local_transform(): pl.pallas_call(functools.partial(local_kernel, scale), out_shape=jax.Shap...  4.38 us
    all_to_all x1, starting transfers between devices, on_device(): mixed = lax.all_to_all(slices, TURNED, 0, 0, tiled=True)  4.02 us
    all_to_all x1, starting transfers between devices, on_device(): lax.all_to_all(chosen.reshape(devices, most, width), AXES, 0, 0, tiled=True)  4.01 us
    pallas_call x1, Pallas kernels, gram_part(): pl.pallas_call(part_kernel, out_shape=jax.ShapeDtypeStruct((width, width)...  3.05 us
  transfers between devices with their start and end apart: 8, of which 7 were waited for; matrix products, arithmetic and copies ran while one was open for 1% of the time, Pallas kernels for 4%

profile of v15, /device:TPU:0, one launch (start us, length us, event | category | flops | bytes accessed | tf_op | source)
XLA Modules:
  0.0 133.0 jit_solution(18145342747914187900)
XLA Ops:
  0.6 4.4 %shard_map.58 = f32[16,256,128]{2,1,0:T(8,128)} custom-call(s32[32,128]{1,0:T(8,128)} %bitcast.15, f32[16,256,128]{2,1,0:T(8,128)} %bitcast.14), custom_call_target="tpu_custom_call" | custom-call | tf_op jit(solution)/shard_map/pallas_call | solution.py:82
  5.0 0.0 copy-start
  5.0 7.3 %all-to-all-start = ((f32[32,128,128]{2,1,0:T(8,128)}), f32[32,128,128]{2,1,0:T(8,128)S(1)}, u32[]{:S(2)}, u32[]{:S(2)}) async-start(f32[32,128,128]{2,1,0:T(8,128)} %bitcast.13), calls=%async_computation | async-start | bytes 4194304 | tf_op jit(solution)/shard_map/all_to_all | solution.py:283
  12.3 0.0 copy-done
  12.4 0.3 shard_map.59
  12.7 0.1 reshape.44
  12.7 0.7 shard_map.60.counts_ref
  13.4 0.1 and_select_fusion
  13.5 0.2 convert_reduce_fusion
  13.7 0.1 multiply_add_fusion
  13.8 47.4 %all-to-all-done.in_ref = f32[32,128,128]{2,1,0:T(8,128)S(1)} async-done(((f32[32,128,128]{2,1,0:T(8,128)}), f32[32,128,128]{2,1,0:T(8,128)S(1)}, u32[]{:S(2)}, u32[]{:S(2)}) %all-to-all-start) | async-done | bytes 2097184 | tf_op jit(solution)/shard_map/all_to_all | solution.py:283
  61.2 1.5 %shard_map.61.held_ref = f32[32,128,128]{2,1,0:T(8,128)} custom-call(f32[32,128,128]{2,1,0:T(8,128)S(1)} %all-to-all-done.in_ref), custom_call_target="tpu_custom_call" | custom-call | tf_op jit(solution)/shard_map/pallas_call | solution.py:130
  62.8 4.0 %all-to-all-start.1 = ((f32[32,128,128]{2,1,0:T(8,128)}), f32[32,128,128]{2,1,0:T(8,128)S(1)}, u32[]{:S(2)}, u32[]{:S(2)}) async-start(f32[32,128,128]{2,1,0:T(8,128)} %shard_map.61.held_ref), calls=%async_computation.1 | async-start | bytes 4194304 | tf_op jit(solution)/shard_map/all_to_all | solution.py:286
  66.8 3.1 %shard_map.62 = f32[128,128]{1,0:T(8,128)S(1)} custom-call(f32[128,32]{1,0:T(8,128)S(1)} %shard_map.60.counts_ref, f32[32,128,128]{2,1,0:T(8,128)} %shard_map.61.held_ref), custom_call_target="tpu_custom_call" | custom-call | tf_op jit(solution)/shard_map/pallas_call | solution.py:249
  69.8 0.3 collective-permute-start
  70.2 1.0 collective-permute-done
  71.2 1.8 %collective-permute-start.1 = (f32[128,128]{1,0:T(8,128)S(1)}, f32[128,128]{1,0:T(8,128)S(1)}, u32[]{:S(2)}, u32[]{:S(2)}) collective-permute-start(f32[128,128]{1,0:T(8,128)S(1)} %add.32), channel_id=1, source_target_pairs={{0,1},{1,0},{2,3},{3,2},{4,5},{5,4},{6,7},{7,6},{8,9},{9,8},{10,11... | collective-permute-start | bytes 196616 | tf_op jit(solution)/shard_map/ppermute | solution.py:260
  73.0 5.7 %collective-permute-done.1 = f32[128,128]{1,0:T(8,128)S(1)} collective-permute-done((f32[128,128]{1,0:T(8,128)S(1)}, f32[128,128]{1,0:T(8,128)S(1)}, u32[]{:S(2)}, u32[]{:S(2)}) %collective-permute-start.1) | collective-permute-done | bytes 65568 | tf_op jit(solution)/shard_map/ppermute | solution.py:260
  78.7 2.5 %collective-permute-start.2 = (f32[128,128]{1,0:T(8,128)S(1)}, f32[128,128]{1,0:T(8,128)S(1)}, u32[]{:S(2)}, u32[]{:S(2)}) collective-permute-start(f32[128,128]{1,0:T(8,128)S(1)} %add.33), channel_id=1, source_target_pairs={{0,2},{1,3},{2,0},{3,1},{4,6},{5,7},{6,4},{7,5},{8,10},{9,11},{10,... | collective-permute-start | bytes 196616 | tf_op jit(solution)/shard_map/ppermute | solution.py:260
  81.2 22.0 %collective-permute-done.2 = f32[128,128]{1,0:T(8,128)S(1)} collective-permute-done((f32[128,128]{1,0:T(8,128)S(1)}, f32[128,128]{1,0:T(8,128)S(1)}, u32[]{:S(2)}, u32[]{:S(2)}) %collective-permute-start.2) | collective-permute-done | bytes 65568 | tf_op jit(solution)/shard_map/ppermute | solution.py:260
  103.3 4.2 %collective-permute-start.3 = (f32[128,128]{1,0:T(8,128)S(1)}, f32[128,128]{1,0:T(8,128)S(1)}, u32[]{:S(2)}, u32[]{:S(2)}) collective-permute-start(f32[128,128]{1,0:T(8,128)S(1)} %add.34), channel_id=1, source_target_pairs={{0,4},{1,5},{2,6},{3,7},{4,0},{5,1},{6,2},{7,3},{8,12},{9,13},{10,... | collective-permute-start | bytes 196616 | tf_op jit(solution)/shard_map/ppermute | solution.py:260
  107.5 11.0 %collective-permute-done.3 = f32[128,128]{1,0:T(8,128)S(1)} collective-permute-done((f32[128,128]{1,0:T(8,128)S(1)}, f32[128,128]{1,0:T(8,128)S(1)}, u32[]{:S(2)}, u32[]{:S(2)}) %collective-permute-start.3) | collective-permute-done | bytes 65568 | tf_op jit(solution)/shard_map/ppermute | solution.py:260
  118.5 0.0 all-to-all-done.1
  118.5 1.3 %gather_fusion = f32[256,128]{1,0:T(8,128)} fusion(f32[4096,128]{1,0:T(8,128)S(1)} %bitcast.9, s32[1024]{0:T(1024)S(1)} %pad_clamp_fusion.1), kind=kCustom, calls=%fused_computation | custom fusion | bytes 263168 | tf_op jit(solution)/shard_map/jit(_take)/gather | solution.py:294
  119.9 4.0 %all-to-all-start.2 = ((f32[32,8,128]{2,1,0:T(8,128)}), f32[32,8,128]{2,1,0:T(8,128)S(1)}, u32[]{:S(2)}, u32[]{:S(2)}) async-start(f32[32,8,128]{2,1,0:T(8,128)} %bitcast.7), calls=%async_computation.2 | async-start | bytes 262144 | tf_op jit(solution)/shard_map/all_to_all | solution.py:295
  123.9 1.8 %collective-permute-start.4 = (f32[128,128]{1,0:T(8,128)S(1)}, f32[128,128]{1,0:T(8,128)S(1)}, u32[]{:S(2)}, u32[]{:S(2)}) collective-permute-start(f32[128,128]{1,0:T(8,128)S(1)} %add.35), channel_id=1, source_target_pairs={{0,16},{8,24},{16,0},{24,8},{1,17},{9,25},{17,1},{25,9},{2,18},{10... | collective-permute-start | bytes 196616 | tf_op jit(solution)/shard_map/ppermute | solution.py:260
  125.7 1.3 shard_map.63
  127.0 1.9 %collective-permute-done.4 = f32[128,128]{1,0:T(8,128)S(1)} collective-permute-done((f32[128,128]{1,0:T(8,128)S(1)}, f32[128,128]{1,0:T(8,128)S(1)}, u32[]{:S(2)}, u32[]{:S(2)}) %collective-permute-start.4) | collective-permute-done | bytes 65568 | tf_op jit(solution)/shard_map/ppermute | solution.py:260
  128.9 0.6 add_multiply_fusion
  129.6 2.0 %all-to-all-done.2 = f32[32,8,128]{2,1,0:T(8,128)S(1)} async-done(((f32[32,8,128]{2,1,0:T(8,128)}), f32[32,8,128]{2,1,0:T(8,128)S(1)}, u32[]{:S(2)}, u32[]{:S(2)}) %all-to-all-start.2) | async-done | bytes 131104 | tf_op jit(solution)/shard_map/all_to_all | solution.py:295
  131.6 1.3 %gather_fusion.1 = f32[256,128]{1,0:T(8,128)} fusion(f32[256,128]{1,0:T(8,128)S(1)} %bitcast.12, s32[1024]{0:T(1024)S(1)} %pad_clamp_fusion), kind=kCustom, calls=%fused_computation.1 | custom fusion | bytes 263168 | tf_op jit(solution)/shard_map/jit(_take)/gather | solution.py:299
  (7 shorter events, 0.1 us)
Async XLA Ops:
  5.0 7.3 %copy-start = (s32[8192]{0:T(1024)S(1)}, s32[8192]{0:T(1024)}, u32[]{:S(2)}) copy-start(s32[8192]{0:T(1024)} %param.5) | copy-start | bytes 98308
  5.0 56.2 %all-to-all-start = ((f32[32,128,128]{2,1,0:T(8,128)}), f32[32,128,128]{2,1,0:T(8,128)S(1)}, u32[]{:S(2)}, u32[]{:S(2)}) async-start(f32[32,128,128]{2,1,0:T(8,128)} %bitcast.13), calls=%async_computation | async-start | bytes 4194304 | tf_op jit(solution)/shard_map/all_to_all | solution.py:283
  62.8 55.7 %all-to-all-start.1 = ((f32[32,128,128]{2,1,0:T(8,128)}), f32[32,128,128]{2,1,0:T(8,128)S(1)}, u32[]{:S(2)}, u32[]{:S(2)}) async-start(f32[32,128,128]{2,1,0:T(8,128)} %shard_map.61.held_ref), calls=%async_computation.1 | async-start | bytes 4194304 | tf_op jit(solution)/shard_map/all_to_all | solution.py:286
  69.8 1.3 collective-permute-start
  71.2 7.5 %collective-permute-start.1 = (f32[128,128]{1,0:T(8,128)S(1)}, f32[128,128]{1,0:T(8,128)S(1)}, u32[]{:S(2)}, u32[]{:S(2)}) collective-permute-start(f32[128,128]{1,0:T(8,128)S(1)} %add.32), channel_id=1, source_target_pairs={{0,1},{1,0},{2,3},{3,2},{4,5},{5,4},{6,7},{7,6},{8,9},{9,8},{10,11... | collective-permute-start | bytes 196616 | tf_op jit(solution)/shard_map/ppermute | solution.py:260
  78.7 24.6 %collective-permute-start.2 = (f32[128,128]{1,0:T(8,128)S(1)}, f32[128,128]{1,0:T(8,128)S(1)}, u32[]{:S(2)}, u32[]{:S(2)}) collective-permute-start(f32[128,128]{1,0:T(8,128)S(1)} %add.33), channel_id=1, source_target_pairs={{0,2},{1,3},{2,0},{3,1},{4,6},{5,7},{6,4},{7,5},{8,10},{9,11},{10,... | collective-permute-start | bytes 196616 | tf_op jit(solution)/shard_map/ppermute | solution.py:260
  103.3 15.2 %collective-permute-start.3 = (f32[128,128]{1,0:T(8,128)S(1)}, f32[128,128]{1,0:T(8,128)S(1)}, u32[]{:S(2)}, u32[]{:S(2)}) collective-permute-start(f32[128,128]{1,0:T(8,128)S(1)} %add.34), channel_id=1, source_target_pairs={{0,4},{1,5},{2,6},{3,7},{4,0},{5,1},{6,2},{7,3},{8,12},{9,13},{10,... | collective-permute-start | bytes 196616 | tf_op jit(solution)/shard_map/ppermute | solution.py:260
  119.9 11.8 %all-to-all-start.2 = ((f32[32,8,128]{2,1,0:T(8,128)}), f32[32,8,128]{2,1,0:T(8,128)S(1)}, u32[]{:S(2)}, u32[]{:S(2)}) async-start(f32[32,8,128]{2,1,0:T(8,128)} %bitcast.7), calls=%async_computation.2 | async-start | bytes 262144 | tf_op jit(solution)/shard_map/all_to_all | solution.py:295
  123.9 5.1 %collective-permute-start.4 = (f32[128,128]{1,0:T(8,128)S(1)}, f32[128,128]{1,0:T(8,128)S(1)}, u32[]{:S(2)}, u32[]{:S(2)}) collective-permute-start(f32[128,128]{1,0:T(8,128)S(1)} %add.35), channel_id=1, source_target_pairs={{0,16},{8,24},{16,0},{24,8},{1,17},{9,25},{17,1},{25,9},{2,18},{10... | collective-permute-start | bytes 196616 | tf_op jit(solution)/shard_map/ppermute | solution.py:260

commit v16 on v15

--- a/solution.py
+++ b/solution.py
@@ -255,9 +255,24 @@
     )(counts, held)
 
 
-def add_partner(value, axis, level):
-    pairs = [(source, source ^ 2**level) for source in range(lax.axis_size(axis))]
-    return value + lax.ppermute(value, axis, pairs)
+def swap(value, axis, apart):
+    pairs = [(source, source ^ apart) for source in range(lax.axis_size(axis))]
+    return lax.ppermute(value, axis, pairs)
+
+
+def scatter_sum(value, axis):
+    upper = lax.axis_index(axis) & 1
+    half = value.shape[0] // 2
+    keep = lax.dynamic_slice_in_dim(value, upper * half, half)
+    give = lax.dynamic_slice_in_dim(value, (1 - upper) * half, half)
+    return keep + swap(give, axis, 1)
+
+
+def join(value, axis):
+    upper = lax.axis_index(axis) & 1 == 1
+    other = swap(value, axis, 1)
+    first = jnp.where(upper, other, value)
+    return jnp.concatenate([first, jnp.where(upper, value, other)], axis=0)
 
 
 def landing(block, rows_here, most):
@@ -285,15 +300,20 @@
     slices = device_sums(slices)
     mixed = lax.all_to_all(slices, TURNED, 0, 0, tiled=True)
     gram = gram_part(counts, slices)
-    levels = [(axis, l) for axis in AXES for l in range(lax.axis_size(axis).bit_length() - 1)]
-    levels = levels[:1] + levels[2:] + levels[1:2]
-    for axis, level in levels[:-1]:
-        gram = add_partner(gram, axis, level)
+    gram = scatter_sum(scatter_sum(gram, "narrow"), "wide")
+    far = lax.axis_size("wide") // 4
+    near, one, two = [swap(gram, "wide", apart * far) for apart in (1, 2, 3)]
+    gram = (gram + near) + (one + two)
     mixed, gram = lax.optimization_barrier((mixed, gram))
     mixed = mixed.reshape(rows_here, width)
     chosen = jnp.take(mixed, wanted, axis=0, mode="clip")
+    chosen, gram = lax.optimization_barrier((chosen, gram))
     landed = lax.all_to_all(chosen.reshape(devices, most, width), AXES, 0, 0, tiled=True)
-    gram = add_partner(gram, *levels[-1]) / float(picks.shape[0])
+    for axis, low, high in (("narrow", 2, lax.axis_size("narrow")), ("wide", 2, far)):
+        while low < high:
+            gram = gram + swap(gram, axis, low)
+            low *= 2
+    gram = join(join(gram / float(picks.shape[0]), "wide"), "narrow")
     mixed = store(mixed)
     landed, mixed, gram = lax.optimization_barrier((landed, mixed, gram))
     sketch = jnp.take(landed.reshape(devices * most, width), spots, axis=0, mode="clip")

time: 133 us -> 141 us (1.060)
  waiting for transfers between devices: 91.1 us -> 96.8 us
    all_to_all x1, waiting for transfers between devices: 2.04 us -> 7.08 us  [on_device(): lax.all_to_all(chosen.reshape(devices, most, width), AXES, 0, 0, tiled=True)]
    ppermute x5 -> x8, starting transfers between devices: 10.7 us -> 12.2 us  [swap(): return lax.ppermute(value, axis, pairs)]
    ppermute x5 -> x8, waiting for transfers between devices: 41.6 us -> 42.3 us  [swap(): return lax.ppermute(value, axis, pairs)]
  transfers between devices with their start and end apart: 8 -> 11, of which waited for: 7 -> 7; matrix products, arithmetic and copies ran while one was open for 1% -> 1% of each run, Pallas kernels for 4% -> 4%
where the time goes in v16:
time: 141 us; the launch traced here: 140 us
  waiting for transfers between devices  96.8 us (69%)
  starting transfers between devices  27.5 us (20%)
  Pallas kernels  11.2 us (8%)
  local copies, waits for them, and re-layouts  2.81 us (2%)
    all_to_all x1, waiting for transfers between devices, on_device(): slices = lax.all_to_all(local, TURNED, 0, 0, tiled=True)  47.4 us
    ppermute x8, waiting for transfers between devices, swap(): return lax.ppermute(value, axis, pairs)  42.3 us
    ppermute x8, starting transfers between devices, swap(): return lax.ppermute(value, axis, pairs)  12.2 us
    all_to_all x1, starting transfers between devices, on_device(): slices = lax.all_to_all(local, TURNED, 0, 0, tiled=True)  7.3 us
    all_to_all x1, waiting for transfers between devices, on_device(): lax.all_to_all(chosen.reshape(devices, most, width), AXES, 0, 0, tiled=True)  7.08 us
    pallas_call x1, Pallas kernels, local_transform(): pl.pallas_call(functools.partial(local_kernel, scale), out_shape=jax.Shap...  4.38 us
    all_to_all x1, starting transfers between devices, on_device(): mixed = lax.all_to_all(slices, TURNED, 0, 0, tiled=True)  4.02 us
    all_to_all x1, starting transfers between devices, on_device(): lax.all_to_all(chosen.reshape(devices, most, width), AXES, 0, 0, tiled=True)  3.97 us
  transfers between devices with their start and end apart: 11, of which 7 were waited for; matrix products, arithmetic and copies ran while one was open for 1% of the time, Pallas kernels for 4%

profile of v16, /device:TPU:0, one launch (start us, length us, event | category | flops | bytes accessed | tf_op | source)
XLA Modules:
  0.0 140.3 jit_solution(8124451677113483767)
XLA Ops:
  0.6 4.4 %shard_map.58 = f32[16,256,128]{2,1,0:T(8,128)} custom-call(s32[32,128]{1,0:T(8,128)} %bitcast.15, f32[16,256,128]{2,1,0:T(8,128)} %bitcast.14), custom_call_target="tpu_custom_call" | custom-call | tf_op jit(solution)/shard_map/pallas_call | solution.py:82
  5.0 0.0 copy-start
  5.0 7.3 %all-to-all-start = ((f32[32,128,128]{2,1,0:T(8,128)}), f32[32,128,128]{2,1,0:T(8,128)S(1)}, u32[]{:S(2)}, u32[]{:S(2)}) async-start(f32[32,128,128]{2,1,0:T(8,128)} %bitcast.13), calls=%async_computation | async-start | bytes 4194304 | tf_op jit(solution)/shard_map/all_to_all | solution.py:298
  12.4 0.3 shard_map.59
  12.7 0.1 reshape.44
  12.7 0.7 shard_map.60.counts_ref
  13.4 0.1 and_select_fusion
  13.5 0.2 convert_reduce_fusion
  13.7 0.1 multiply_add_fusion
  13.8 47.4 %all-to-all-done.in_ref = f32[32,128,128]{2,1,0:T(8,128)S(1)} async-done(((f32[32,128,128]{2,1,0:T(8,128)}), f32[32,128,128]{2,1,0:T(8,128)S(1)}, u32[]{:S(2)}, u32[]{:S(2)}) %all-to-all-start) | async-done | bytes 2097184 | tf_op jit(solution)/shard_map/all_to_all | solution.py:298
  61.2 1.5 %shard_map.61.held_ref = f32[32,128,128]{2,1,0:T(8,128)} custom-call(f32[32,128,128]{2,1,0:T(8,128)S(1)} %all-to-all-done.in_ref), custom_call_target="tpu_custom_call" | custom-call | tf_op jit(solution)/shard_map/pallas_call | solution.py:130
  62.8 4.0 %all-to-all-start.1 = ((f32[32,128,128]{2,1,0:T(8,128)}), f32[32,128,128]{2,1,0:T(8,128)S(1)}, u32[]{:S(2)}, u32[]{:S(2)}) async-start(f32[32,128,128]{2,1,0:T(8,128)} %shard_map.61.held_ref), calls=%async_computation.1 | async-start | bytes 4194304 | tf_op jit(solution)/shard_map/all_to_all | solution.py:301
  66.8 3.1 %shard_map.62 = f32[128,128]{1,0:T(8,128)S(1)} custom-call(f32[128,32]{1,0:T(8,128)S(1)} %shard_map.60.counts_ref, f32[32,128,128]{2,1,0:T(8,128)} %shard_map.61.held_ref), custom_call_target="tpu_custom_call" | custom-call | tf_op jit(solution)/shard_map/pallas_call | solution.py:249
  69.9 0.3 collective-permute-start
  70.2 1.0 collective-permute-done
  71.2 1.8 %collective-permute-start.1 = (f32[32,128]{1,0:T(8,128)S(1)}, f32[32,128]{1,0:T(8,128)S(1)}, u32[]{:S(2)}, u32[]{:S(2)}) collective-permute-start(f32[32,128]{1,0:T(8,128)S(1)} %constant_dynamic-slice_fusion), channel_id=1, source_target_pairs={{0,1},{1,0},{2,3},{3,2},{4,5},{5,4},{6,7},{7,6},{8,9},{9,8},{10,11... | collective-permute-start | bytes 49160 | tf_op jit(solution)/shard_map/ppermute | solution.py:260
  73.0 4.0 %collective-permute-done.1 = f32[32,128]{1,0:T(8,128)S(1)} collective-permute-done((f32[32,128]{1,0:T(8,128)S(1)}, f32[32,128]{1,0:T(8,128)S(1)}, u32[]{:S(2)}, u32[]{:S(2)}) %collective-permute-start.1) | collective-permute-done | bytes 16416 | tf_op jit(solution)/shard_map/ppermute | solution.py:260
  77.0 2.7 %collective-permute-start.3 = (f32[32,128]{1,0:T(8,128)S(1)}, f32[32,128]{1,0:T(8,128)S(1)}, u32[]{:S(2)}, u32[]{:S(2)}) collective-permute-start(f32[32,128]{1,0:T(8,128)S(1)} %dynamic-slice_add_fusion.1), channel_id=1, source_target_pairs={{0,4},{1,5},{2,6},{3,7},{4,0},{5,1},{6,2},{7,3},{8,12},{9,13},{10,... | collective-permute-start | bytes 49160 | tf_op jit(solution)/shard_map/ppermute | solution.py:260
  79.7 4.1 %collective-permute-start.4 = (f32[32,128]{1,0:T(8,128)S(1)}, f32[32,128]{1,0:T(8,128)S(1)}, u32[]{:S(2)}, u32[]{:S(2)}) collective-permute-start(f32[32,128]{1,0:T(8,128)S(1)} %dynamic-slice_add_fusion.1), channel_id=1, source_target_pairs={{0,6},{1,7},{2,4},{3,5},{4,2},{5,3},{6,0},{7,1},{8,14},{9,15},{10,... | collective-permute-start | bytes 49160 | tf_op jit(solution)/shard_map/ppermute | solution.py:260
  83.8 0.6 collective-permute-start.2
  84.4 32.5 %collective-permute-done.3 = f32[32,128]{1,0:T(8,128)S(1)} collective-permute-done((f32[32,128]{1,0:T(8,128)S(1)}, f32[32,128]{1,0:T(8,128)S(1)}, u32[]{:S(2)}, u32[]{:S(2)}) %collective-permute-start.3) | collective-permute-done | bytes 16416 | tf_op jit(solution)/shard_map/ppermute | solution.py:260
  116.9 1.3 gather_fusion
  118.3 1.4 collective-permute-start.5
  119.7 2.4 %collective-permute-done.5 = f32[32,128]{1,0:T(8,128)S(1)} collective-permute-done((f32[32,128]{1,0:T(8,128)S(1)}, f32[32,128]{1,0:T(8,128)S(1)}, u32[]{:S(2)}, u32[]{:S(2)}) %collective-permute-start.5) | collective-permute-done | bytes 16416 | tf_op jit(solution)/shard_map/ppermute | solution.py:260
  122.0 1.3 collective-permute-start.6
  123.3 2.4 %collective-permute-done.6 = f32[32,128]{1,0:T(8,128)S(1)} collective-permute-done((f32[32,128]{1,0:T(8,128)S(1)}, f32[32,128]{1,0:T(8,128)S(1)}, u32[]{:S(2)}, u32[]{:S(2)}) %collective-permute-start.6) | collective-permute-done | bytes 16416 | tf_op jit(solution)/shard_map/ppermute | solution.py:260
  125.8 0.1 collective-permute-start.7
  125.9 1.3 shard_map.63
  127.2 4.0 %all-to-all-start.2 = ((f32[32,8,128]{2,1,0:T(8,128)}), f32[32,8,128]{2,1,0:T(8,128)S(1)}, u32[]{:S(2)}, u32[]{:S(2)}) async-start(f32[32,8,128]{2,1,0:T(8,128)} %bitcast.7), calls=%async_computation.2 | async-start | bytes 262144 | tf_op jit(solution)/shard_map/all_to_all | solution.py:311
  131.2 0.6 pad_maximum_fusion
  131.9 7.1 %all-to-all-done.2 = f32[32,8,128]{2,1,0:T(8,128)S(1)} async-done(((f32[32,8,128]{2,1,0:T(8,128)}), f32[32,8,128]{2,1,0:T(8,128)S(1)}, u32[]{:S(2)}, u32[]{:S(2)}) %all-to-all-start.2) | async-done | bytes 131104 | tf_op jit(solution)/shard_map/all_to_all | solution.py:311
  138.9 1.3 gather_fusion.1
  (17 shorter events, 0.1 us)
Async XLA Ops:
  5.0 7.3 %copy-start = (s32[8192]{0:T(1024)S(1)}, s32[8192]{0:T(1024)}, u32[]{:S(2)}) copy-start(s32[8192]{0:T(1024)} %param.5) | copy-start | bytes 98308
  5.0 56.2 %all-to-all-start = ((f32[32,128,128]{2,1,0:T(8,128)}), f32[32,128,128]{2,1,0:T(8,128)S(1)}, u32[]{:S(2)}, u32[]{:S(2)}) async-start(f32[32,128,128]{2,1,0:T(8,128)} %bitcast.13), calls=%async_computation | async-start | bytes 4194304 | tf_op jit(solution)/shard_map/all_to_all | solution.py:298
  62.8 54.2 %all-to-all-start.1 = ((f32[32,128,128]{2,1,0:T(8,128)}), f32[32,128,128]{2,1,0:T(8,128)S(1)}, u32[]{:S(2)}, u32[]{:S(2)}) async-start(f32[32,128,128]{2,1,0:T(8,128)} %shard_map.61.held_ref), calls=%async_computation.1 | async-start | bytes 4194304 | tf_op jit(solution)/shard_map/all_to_all | solution.py:301
  69.9 1.3 collective-permute-start
  71.2 5.9 %collective-permute-start.1 = (f32[32,128]{1,0:T(8,128)S(1)}, f32[32,128]{1,0:T(8,128)S(1)}, u32[]{:S(2)}, u32[]{:S(2)}) collective-permute-start(f32[32,128]{1,0:T(8,128)S(1)} %constant_dynamic-slice_fusion), channel_id=1, source_target_pairs={{0,1},{1,0},{2,3},{3,2},{4,5},{5,4},{6,7},{7,6},{8,9},{9,8},{10,11... | collective-permute-start | bytes 49160 | tf_op jit(solution)/shard_map/ppermute | solution.py:260
  77.0 39.9 %collective-permute-start.3 = (f32[32,128]{1,0:T(8,128)S(1)}, f32[32,128]{1,0:T(8,128)S(1)}, u32[]{:S(2)}, u32[]{:S(2)}) collective-permute-start(f32[32,128]{1,0:T(8,128)S(1)} %dynamic-slice_add_fusion.1), channel_id=1, source_target_pairs={{0,4},{1,5},{2,6},{3,7},{4,0},{5,1},{6,2},{7,3},{8,12},{9,13},{10,... | collective-permute-start | bytes 49160 | tf_op jit(solution)/shard_map/ppermute | solution.py:260
  79.7 37.2 %collective-permute-start.4 = (f32[32,128]{1,0:T(8,128)S(1)}, f32[32,128]{1,0:T(8,128)S(1)}, u32[]{:S(2)}, u32[]{:S(2)}) collective-permute-start(f32[32,128]{1,0:T(8,128)S(1)} %dynamic-slice_add_fusion.1), channel_id=1, source_target_pairs={{0,6},{1,7},{2,4},{3,5},{4,2},{5,3},{6,0},{7,1},{8,14},{9,15},{10,... | collective-permute-start | bytes 49160 | tf_op jit(solution)/shard_map/ppermute | solution.py:260
  83.8 33.1 %collective-permute-start.2 = (f32[32,128]{1,0:T(8,128)S(1)}, f32[32,128]{1,0:T(8,128)S(1)}, u32[]{:S(2)}, u32[]{:S(2)}) collective-permute-start(f32[32,128]{1,0:T(8,128)S(1)} %dynamic-slice_add_fusion.1), channel_id=1, source_target_pairs={{0,2},{1,3},{2,0},{3,1},{4,6},{5,7},{6,4},{7,5},{8,10},{9,11},{10,... | collective-permute-start | bytes 49160 | tf_op jit(solution)/shard_map/ppermute | solution.py:260
  118.3 3.7 %collective-permute-start.5 = (f32[32,128]{1,0:T(8,128)S(1)}, f32[32,128]{1,0:T(8,128)S(1)}, u32[]{:S(2)}, u32[]{:S(2)}) collective-permute-start(f32[32,128]{1,0:T(8,128)S(1)} %add_add_fusion), channel_id=1, source_target_pairs={{0,16},{8,24},{16,0},{24,8},{1,17},{9,25},{17,1},{25,9},{2,18},{10... | collective-permute-start | bytes 49160 | tf_op jit(solution)/shard_map/ppermute | solution.py:260
  122.0 3.7 %collective-permute-start.6 = (f32[32,128]{1,0:T(8,128)S(1)}, f32[32,128]{1,0:T(8,128)S(1)}, u32[]{:S(2)}, u32[]{:S(2)}) collective-permute-start(f32[32,128]{1,0:T(8,128)S(1)} %add_multiply_fusion), channel_id=1, source_target_pairs={{0,1},{1,0},{2,3},{3,2},{4,5},{5,4},{6,7},{7,6},{8,9},{9,8},{10,11... | collective-permute-start | bytes 49160 | tf_op jit(solution)/shard_map/ppermute | solution.py:260
  125.8 5.4 %collective-permute-start.7 = (f32[64,128]{1,0:T(8,128)S(1)}, f32[64,128]{1,0:T(8,128)S(1)}, u32[]{:S(2)}, u32[]{:S(2)}) collective-permute-start(f32[64,128]{1,0:T(8,128)S(1)} %pad_maximum_fusion.1), channel_id=1, source_target_pairs={{0,8},{8,0},{16,24},{24,16},{1,9},{9,1},{17,25},{25,17},{2,10},{10... | collective-permute-start | bytes 98312 | tf_op jit(solution)/shard_map/ppermute | solution.py:260
  127.2 11.7 %all-to-all-start.2 = ((f32[32,8,128]{2,1,0:T(8,128)}), f32[32,8,128]{2,1,0:T(8,128)S(1)}, u32[]{:S(2)}, u32[]{:S(2)}) async-start(f32[32,8,128]{2,1,0:T(8,128)} %bitcast.7), calls=%async_computation.2 | async-start | bytes 262144 | tf_op jit(solution)/shard_map/all_to_all | solution.py:311

commit v17 on v16

--- a/solution.py
+++ b/solution.py
@@ -300,8 +300,12 @@
     slices = device_sums(slices)
     mixed = lax.all_to_all(slices, TURNED, 0, 0, tiled=True)
     gram = gram_part(counts, slices)
-    gram = scatter_sum(scatter_sum(gram, "narrow"), "wide")
+    gram = scatter_sum(gram, "narrow")
     far = lax.axis_size("wide") // 4
+    for axis, low, high in (("wide", 1, far), ("narrow", 2, lax.axis_size("narrow"))):
+        while low < high:
+            gram = gram + swap(gram, axis, low)
+            low *= 2
     near, one, two = [swap(gram, "wide", apart * far) for apart in (1, 2, 3)]
     gram = (gram + near) + (one + two)
     mixed, gram = lax.optimization_barrier((mixed, gram))
@@ -309,11 +313,7 @@
     chosen = jnp.take(mixed, wanted, axis=0, mode="clip")
     chosen, gram = lax.optimization_barrier((chosen, gram))
     landed = lax.all_to_all(chosen.reshape(devices, most, width), AXES, 0, 0, tiled=True)
-    for axis, low, high in (("narrow", 2, lax.axis_size("narrow")), ("wide", 2, far)):
-        while low < high:
-            gram = gram + swap(gram, axis, low)
-            low *= 2
-    gram = join(join(gram / float(picks.shape[0]), "wide"), "narrow")
+    gram = join(gram / float(picks.shape[0]), "narrow")
     mixed = store(mixed)
     landed, mixed, gram = lax.optimization_barrier((landed, mixed, gram))
     sketch = jnp.take(landed.reshape(devices * most, width), spots, axis=0, mode="clip")

time: 141 us -> 134 us (0.950)
  waiting for transfers between devices: 96.8 us -> 89 us
    ppermute x8 -> x7, waiting for transfers between devices: 42.3 us -> 34.5 us  [swap(): return lax.ppermute(value, axis, pairs)]
    ppermute x8 -> x7, starting transfers between devices: 12.2 us -> 13.7 us  [swap(): return lax.ppermute(value, axis, pairs)]
  transfers between devices with their start and end apart: 11 -> 10, of which waited for: 7 -> 6; matrix products, arithmetic and copies ran while one was open for 1% -> 1% of each run, Pallas kernels for 4% -> 4%
where the time goes in v17:
time: 134 us
  waiting for transfers between devices  89 us (66%)
  starting transfers between devices  28.9 us (22%)
  Pallas kernels  11.2 us (8%)
  local copies, waits for them, and re-layouts  2.8 us (2%)
    all_to_all x1, waiting for transfers between devices, on_device(): slices = lax.all_to_all(local, TURNED, 0, 0, tiled=True)  47.4 us
    ppermute x7, waiting for transfers between devices, swap(): return lax.ppermute(value, axis, pairs)  34.5 us
    ppermute x7, starting transfers between devices, swap(): return lax.ppermute(value, axis, pairs)  13.7 us
    all_to_all x1, starting transfers between devices, on_device(): slices = lax.all_to_all(local, TURNED, 0, 0, tiled=True)  7.3 us
    all_to_all x1, waiting for transfers between devices, on_device(): lax.all_to_all(chosen.reshape(devices, most, width), AXES, 0, 0, tiled=True)  7.08 us
    pallas_call x1, Pallas kernels, local_transform(): pl.pallas_call(functools.partial(local_kernel, scale), out_shape=jax.Shap...  4.38 us
    all_to_all x1, starting transfers between devices, on_device(): mixed = lax.all_to_all(slices, TURNED, 0, 0, tiled=True)  4.02 us
    all_to_all x1, starting transfers between devices, on_device(): lax.all_to_all(chosen.reshape(devices, most, width), AXES, 0, 0, tiled=True)  3.81 us
  transfers between devices with their start and end apart: 10, of which 6 were waited for; matrix products, arithmetic and copies ran while one was open for 1% of the time, Pallas kernels for 4%

profile of v17, /device:TPU:0, one launch (start us, length us, event | category | flops | bytes accessed | tf_op | source)
XLA Modules:
  0.0 133.8 jit_solution(16254088944505074766)
XLA Ops:
  0.6 4.4 %shard_map.58 = f32[16,256,128]{2,1,0:T(8,128)} custom-call(s32[32,128]{1,0:T(8,128)} %bitcast.15, f32[16,256,128]{2,1,0:T(8,128)} %bitcast.14), custom_call_target="tpu_custom_call" | custom-call | tf_op jit(solution)/shard_map/pallas_call | solution.py:82
  5.0 0.0 copy-start
  5.0 7.3 %all-to-all-start = ((f32[32,128,128]{2,1,0:T(8,128)}), f32[32,128,128]{2,1,0:T(8,128)S(1)}, u32[]{:S(2)}, u32[]{:S(2)}) async-start(f32[32,128,128]{2,1,0:T(8,128)} %bitcast.13), calls=%async_computation | async-start | bytes 4194304 | tf_op jit(solution)/shard_map/all_to_all | solution.py:298
  12.4 0.3 shard_map.59
  12.7 0.1 reshape.44
  12.7 0.7 shard_map.60.counts_ref
  13.4 0.1 and_select_fusion
  13.5 0.2 convert_reduce_fusion
  13.7 0.1 multiply_add_fusion
  13.8 47.4 %all-to-all-done.in_ref = f32[32,128,128]{2,1,0:T(8,128)S(1)} async-done(((f32[32,128,128]{2,1,0:T(8,128)}), f32[32,128,128]{2,1,0:T(8,128)S(1)}, u32[]{:S(2)}, u32[]{:S(2)}) %all-to-all-start) | async-done | bytes 2097184 | tf_op jit(solution)/shard_map/all_to_all | solution.py:298
  61.2 1.5 %shard_map.61.held_ref = f32[32,128,128]{2,1,0:T(8,128)} custom-call(f32[32,128,128]{2,1,0:T(8,128)S(1)} %all-to-all-done.in_ref), custom_call_target="tpu_custom_call" | custom-call | tf_op jit(solution)/shard_map/pallas_call | solution.py:130
  62.8 4.0 %all-to-all-start.1 = ((f32[32,128,128]{2,1,0:T(8,128)}), f32[32,128,128]{2,1,0:T(8,128)S(1)}, u32[]{:S(2)}, u32[]{:S(2)}) async-start(f32[32,128,128]{2,1,0:T(8,128)} %shard_map.61.held_ref), calls=%async_computation.1 | async-start | bytes 4194304 | tf_op jit(solution)/shard_map/all_to_all | solution.py:301
  66.8 3.1 %shard_map.62 = f32[128,128]{1,0:T(8,128)S(1)} custom-call(f32[128,32]{1,0:T(8,128)S(1)} %shard_map.60.counts_ref, f32[32,128,128]{2,1,0:T(8,128)} %shard_map.61.held_ref), custom_call_target="tpu_custom_call" | custom-call | tf_op jit(solution)/shard_map/pallas_call | solution.py:249
  69.9 0.3 collective-permute-start
  70.2 1.0 collective-permute-done
  71.1 1.8 %collective-permute-start.1 = (f32[64,128]{1,0:T(8,128)S(1)}, f32[64,128]{1,0:T(8,128)S(1)}, u32[]{:S(2)}, u32[]{:S(2)}) collective-permute-start(f32[64,128]{1,0:T(8,128)S(1)} %dynamic-slice_add_fusion), channel_id=1, source_target_pairs={{0,1},{1,0},{2,3},{3,2},{4,5},{5,4},{6,7},{7,6},{8,9},{9,8},{10,11... | collective-permute-start | bytes 98312 | tf_op jit(solution)/shard_map/ppermute | solution.py:260
  72.9 4.4 %collective-permute-done.1 = f32[64,128]{1,0:T(8,128)S(1)} collective-permute-done((f32[64,128]{1,0:T(8,128)S(1)}, f32[64,128]{1,0:T(8,128)S(1)}, u32[]{:S(2)}, u32[]{:S(2)}) %collective-permute-start.1) | collective-permute-done | bytes 32800 | tf_op jit(solution)/shard_map/ppermute | solution.py:260
  77.4 6.8 %collective-permute-start.2 = (f32[64,128]{1,0:T(8,128)S(1)}, f32[64,128]{1,0:T(8,128)S(1)}, u32[]{:S(2)}, u32[]{:S(2)}) collective-permute-start(f32[64,128]{1,0:T(8,128)S(1)} %add.44), channel_id=1, source_target_pairs={{0,16},{8,24},{16,0},{24,8},{1,17},{9,25},{17,1},{25,9},{2,18},{10... | collective-permute-start | bytes 98312 | tf_op jit(solution)/shard_map/ppermute | solution.py:260
  84.2 1.9 %collective-permute-done.2 = f32[64,128]{1,0:T(8,128)S(1)} collective-permute-done((f32[64,128]{1,0:T(8,128)S(1)}, f32[64,128]{1,0:T(8,128)S(1)}, u32[]{:S(2)}, u32[]{:S(2)}) %collective-permute-start.2) | collective-permute-done | bytes 32800 | tf_op jit(solution)/shard_map/ppermute | solution.py:260
  86.1 1.0 collective-permute-start.4
  87.1 3.4 %collective-permute-start.5 = (f32[64,128]{1,0:T(8,128)S(1)}, f32[64,128]{1,0:T(8,128)S(1)}, u32[]{:S(2)}, u32[]{:S(2)}) collective-permute-start(f32[64,128]{1,0:T(8,128)S(1)} %add.45), channel_id=1, source_target_pairs={{0,6},{1,7},{2,4},{3,5},{4,2},{5,3},{6,0},{7,1},{8,14},{9,15},{10,... | collective-permute-start | bytes 98312 | tf_op jit(solution)/shard_map/ppermute | solution.py:260
  90.4 0.5 collective-permute-start.3
  90.9 27.2 %collective-permute-done.4 = f32[64,128]{1,0:T(8,128)S(1)} collective-permute-done((f32[64,128]{1,0:T(8,128)S(1)}, f32[64,128]{1,0:T(8,128)S(1)}, u32[]{:S(2)}, u32[]{:S(2)}) %collective-permute-start.4) | collective-permute-done | bytes 32800 | tf_op jit(solution)/shard_map/ppermute | solution.py:260
  118.1 0.0 collective-permute-done.5
  118.1 0.0 collective-permute-done.3
  118.2 1.3 %gather_fusion = f32[256,128]{1,0:T(8,128)} fusion(f32[4096,128]{1,0:T(8,128)S(1)} %bitcast.9, s32[1024]{0:T(1024)S(1)} %pad_clamp_fusion.1), kind=kCustom, calls=%fused_computation | custom fusion | bytes 263168 | tf_op jit(solution)/shard_map/jit(_take)/gather | solution.py:313
  119.5 0.0 collective-permute-start.6
  119.5 1.3 shard_map.63
  120.9 3.8 %all-to-all-start.2 = ((f32[32,8,128]{2,1,0:T(8,128)}), f32[32,8,128]{2,1,0:T(8,128)S(1)}, u32[]{:S(2)}, u32[]{:S(2)}) async-start(f32[32,8,128]{2,1,0:T(8,128)} %bitcast.7), calls=%async_computation.2 | async-start | bytes 262144 | tf_op jit(solution)/shard_map/all_to_all | solution.py:315
  124.7 0.6 pad_maximum_fusion
  125.3 7.1 %all-to-all-done.2 = f32[32,8,128]{2,1,0:T(8,128)S(1)} async-done(((f32[32,8,128]{2,1,0:T(8,128)}), f32[32,8,128]{2,1,0:T(8,128)S(1)}, u32[]{:S(2)}, u32[]{:S(2)}) %all-to-all-start.2) | async-done | bytes 131104 | tf_op jit(solution)/shard_map/all_to_all | solution.py:315
  132.4 1.3 %gather_fusion.1 = f32[256,128]{1,0:T(8,128)} fusion(f32[256,128]{1,0:T(8,128)S(1)} %bitcast.12, s32[1024]{0:T(1024)S(1)} %pad_clamp_fusion), kind=kCustom, calls=%fused_computation.1 | custom fusion | bytes 263168 | tf_op jit(solution)/shard_map/jit(_take)/gather | solution.py:319
  (13 shorter events, 0.1 us)
Async XLA Ops:
  5.0 7.3 %copy-start = (s32[8192]{0:T(1024)S(1)}, s32[8192]{0:T(1024)}, u32[]{:S(2)}) copy-start(s32[8192]{0:T(1024)} %param.5) | copy-start | bytes 98308
  5.0 56.2 %all-to-all-start = ((f32[32,128,128]{2,1,0:T(8,128)}), f32[32,128,128]{2,1,0:T(8,128)S(1)}, u32[]{:S(2)}, u32[]{:S(2)}) async-start(f32[32,128,128]{2,1,0:T(8,128)} %bitcast.13), calls=%async_computation | async-start | bytes 4194304 | tf_op jit(solution)/shard_map/all_to_all | solution.py:298
  62.8 55.4 %all-to-all-start.1 = ((f32[32,128,128]{2,1,0:T(8,128)}), f32[32,128,128]{2,1,0:T(8,128)S(1)}, u32[]{:S(2)}, u32[]{:S(2)}) async-start(f32[32,128,128]{2,1,0:T(8,128)} %shard_map.61.held_ref), calls=%async_computation.1 | async-start | bytes 4194304 | tf_op jit(solution)/shard_map/all_to_all | solution.py:301
  69.9 1.3 collective-permute-start
  71.1 6.2 %collective-permute-start.1 = (f32[64,128]{1,0:T(8,128)S(1)}, f32[64,128]{1,0:T(8,128)S(1)}, u32[]{:S(2)}, u32[]{:S(2)}) collective-permute-start(f32[64,128]{1,0:T(8,128)S(1)} %dynamic-slice_add_fusion), channel_id=1, source_target_pairs={{0,1},{1,0},{2,3},{3,2},{4,5},{5,4},{6,7},{7,6},{8,9},{9,8},{10,11... | collective-permute-start | bytes 98312 | tf_op jit(solution)/shard_map/ppermute | solution.py:260
  77.4 8.7 %collective-permute-start.2 = (f32[64,128]{1,0:T(8,128)S(1)}, f32[64,128]{1,0:T(8,128)S(1)}, u32[]{:S(2)}, u32[]{:S(2)}) collective-permute-start(f32[64,128]{1,0:T(8,128)S(1)} %add.44), channel_id=1, source_target_pairs={{0,16},{8,24},{16,0},{24,8},{1,17},{9,25},{17,1},{25,9},{2,18},{10... | collective-permute-start | bytes 98312 | tf_op jit(solution)/shard_map/ppermute | solution.py:260
  86.1 32.0 %collective-permute-start.4 = (f32[64,128]{1,0:T(8,128)S(1)}, f32[64,128]{1,0:T(8,128)S(1)}, u32[]{:S(2)}, u32[]{:S(2)}) collective-permute-start(f32[64,128]{1,0:T(8,128)S(1)} %add.45), channel_id=1, source_target_pairs={{0,4},{1,5},{2,6},{3,7},{4,0},{5,1},{6,2},{7,3},{8,12},{9,13},{10,... | collective-permute-start | bytes 98312 | tf_op jit(solution)/shard_map/ppermute | solution.py:260
  87.1 31.1 %collective-permute-start.5 = (f32[64,128]{1,0:T(8,128)S(1)}, f32[64,128]{1,0:T(8,128)S(1)}, u32[]{:S(2)}, u32[]{:S(2)}) collective-permute-start(f32[64,128]{1,0:T(8,128)S(1)} %add.45), channel_id=1, source_target_pairs={{0,6},{1,7},{2,4},{3,5},{4,2},{5,3},{6,0},{7,1},{8,14},{9,15},{10,... | collective-permute-start | bytes 98312 | tf_op jit(solution)/shard_map/ppermute | solution.py:260
  90.4 27.7 %collective-permute-start.3 = (f32[64,128]{1,0:T(8,128)S(1)}, f32[64,128]{1,0:T(8,128)S(1)}, u32[]{:S(2)}, u32[]{:S(2)}) collective-permute-start(f32[64,128]{1,0:T(8,128)S(1)} %add.45), channel_id=1, source_target_pairs={{0,2},{1,3},{2,0},{3,1},{4,6},{5,7},{6,4},{7,5},{8,10},{9,11},{10,... | collective-permute-start | bytes 98312 | tf_op jit(solution)/shard_map/ppermute | solution.py:260
  119.5 5.2 %collective-permute-start.6 = (f32[64,128]{1,0:T(8,128)S(1)}, f32[64,128]{1,0:T(8,128)S(1)}, u32[]{:S(2)}, u32[]{:S(2)}) collective-permute-start(f32[64,128]{1,0:T(8,128)S(1)} %broadcast_multiply_fusion), channel_id=1, source_target_pairs={{0,8},{8,0},{16,24},{24,16},{1,9},{9,1},{17,25},{25,17},{2,10},{10... | collective-permute-start | bytes 98312 | tf_op jit(solution)/shard_map/ppermute | solution.py:260
  120.9 11.6 %all-to-all-start.2 = ((f32[32,8,128]{2,1,0:T(8,128)}), f32[32,8,128]{2,1,0:T(8,128)S(1)}, u32[]{:S(2)}, u32[]{:S(2)}) async-start(f32[32,8,128]{2,1,0:T(8,128)} %bitcast.7), calls=%async_computation.2 | async-start | bytes 262144 | tf_op jit(solution)/shard_map/all_to_all | solution.py:315

commit v18 on v17

--- a/solution.py
+++ b/solution.py
@@ -268,11 +268,17 @@
     return keep + swap(give, axis, 1)
 
 
-def join(value, axis):
-    upper = lax.axis_index(axis) & 1 == 1
-    other = swap(value, axis, 1)
-    first = jnp.where(upper, other, value)
-    return jnp.concatenate([first, jnp.where(upper, value, other)], axis=0)
+def join(lower, upper, axis):
+    turned = lax.axis_index(axis) & 1 == 1
+    first = jnp.where(turned, upper, lower)
+    return jnp.concatenate([first, jnp.where(turned, lower, upper)], axis=0)
+
+
+def gather_quarters(value):
+    over_core, over_y = swap(value, "narrow", 1), swap(value, "wide", 1)
+    over_both = swap(value, AXES, lax.axis_size("wide") + 1)
+    mine = join(value, over_y, "wide")
+    return join(mine, join(over_core, over_both, "wide"), "narrow")
 
 
 def landing(block, rows_here, most):
@@ -300,9 +306,9 @@
     slices = device_sums(slices)
     mixed = lax.all_to_all(slices, TURNED, 0, 0, tiled=True)
     gram = gram_part(counts, slices)
-    gram = scatter_sum(gram, "narrow")
+    gram = scatter_sum(scatter_sum(gram, "narrow"), "wide")
     far = lax.axis_size("wide") // 4
-    for axis, low, high in (("wide", 1, far), ("narrow", 2, lax.axis_size("narrow"))):
+    for axis, low, high in (("narrow", 2, lax.axis_size("narrow")), ("wide", 2, far)):
         while low < high:
             gram = gram + swap(gram, axis, low)
             low *= 2
@@ -311,9 +317,8 @@
     mixed, gram = lax.optimization_barrier((mixed, gram))
     mixed = mixed.reshape(rows_here, width)
     chosen = jnp.take(mixed, wanted, axis=0, mode="clip")
-    chosen, gram = lax.optimization_barrier((chosen, gram))
     landed = lax.all_to_all(chosen.reshape(devices, most, width), AXES, 0, 0, tiled=True)
-    gram = join(gram / float(picks.shape[0]), "narrow")
+    gram = gather_quarters(gram) / float(picks.shape[0])
     mixed = store(mixed)
     landed, mixed, gram = lax.optimization_barrier((landed, mixed, gram))
     sketch = jnp.take(landed.reshape(devices * most, width), spots, axis=0, mode="clip")

time: 134 us -> 135 us (level)
  starting transfers between devices: 28.9 us -> 30.9 us
    ppermute x7 -> x9, starting transfers between devices: 13.7 us -> 15.7 us  [swap(): return lax.ppermute(value, axis, pairs)]
    ppermute x7 -> x9, waiting for transfers between devices: 34.5 us -> 33.5 us  [swap(): return lax.ppermute(value, axis, pairs)]
  transfers between devices with their start and end apart: 10 -> 12, of which waited for: 6 -> 6; matrix products, arithmetic and copies ran while one was open for 1% -> 2% of each run, Pallas kernels for 4% -> 4%
where the time goes in v18:
time: 135 us
  waiting for transfers between devices  88 us (65%)
  starting transfers between devices  30.9 us (23%)
  Pallas kernels  11.2 us (8%)
  local copies, waits for them, and re-layouts  2.81 us (2%)
    all_to_all x1, waiting for transfers between devices, on_device(): slices = lax.all_to_all(local, TURNED, 0, 0, tiled=True)  47.4 us
    ppermute x9, waiting for transfers between devices, swap(): return lax.ppermute(value, axis, pairs)  33.5 us
    ppermute x9, starting transfers between devices, swap(): return lax.ppermute(value, axis, pairs)  15.7 us
    all_to_all x1, starting transfers between devices, on_device(): slices = lax.all_to_all(local, TURNED, 0, 0, tiled=True)  7.3 us
    all_to_all x1, waiting for transfers between devices, on_device(): lax.all_to_all(chosen.reshape(devices, most, width), AXES, 0, 0, tiled=True)  7.02 us
    pallas_call x1, Pallas kernels, local_transform(): pl.pallas_call(functools.partial(local_kernel, scale), out_shape=jax.Shap...  4.38 us
    all_to_all x1, starting transfers between devices, on_device(): mixed = lax.all_to_all(slices, TURNED, 0, 0, tiled=True)  4.02 us
    all_to_all x1, starting transfers between devices, on_device(): lax.all_to_all(chosen.reshape(devices, most, width), AXES, 0, 0, tiled=True)  3.88 us
  transfers between devices with their start and end apart: 12, of which 6 were waited for; matrix products, arithmetic and copies ran while one was open for 2% of the time, Pallas kernels for 4%

profile of v18, /device:TPU:0, one launch (start us, length us, event | category | flops | bytes accessed | tf_op | source)
XLA Modules:
  0.0 134.8 jit_solution(791342331404079574)
XLA Ops:
  0.6 4.4 %shard_map.58 = f32[16,256,128]{2,1,0:T(8,128)} custom-call(s32[32,128]{1,0:T(8,128)} %bitcast.15, f32[16,256,128]{2,1,0:T(8,128)} %bitcast.14), custom_call_target="tpu_custom_call" | custom-call | tf_op jit(solution)/shard_map/pallas_call | solution.py:82
  5.0 0.0 copy-start
  5.0 7.3 %all-to-all-start = ((f32[32,128,128]{2,1,0:T(8,128)}), f32[32,128,128]{2,1,0:T(8,128)S(1)}, u32[]{:S(2)}, u32[]{:S(2)}) async-start(f32[32,128,128]{2,1,0:T(8,128)} %bitcast.13), calls=%async_computation | async-start | bytes 4194304 | tf_op jit(solution)/shard_map/all_to_all | solution.py:304
  12.4 0.3 shard_map.59
  12.7 0.1 reshape.44
  12.7 0.7 shard_map.60.counts_ref
  13.4 0.1 and_select_fusion
  13.5 0.2 convert_reduce_fusion
  13.7 0.1 multiply_add_fusion
  13.8 47.4 %all-to-all-done.in_ref = f32[32,128,128]{2,1,0:T(8,128)S(1)} async-done(((f32[32,128,128]{2,1,0:T(8,128)}), f32[32,128,128]{2,1,0:T(8,128)S(1)}, u32[]{:S(2)}, u32[]{:S(2)}) %all-to-all-start) | async-done | bytes 2097184 | tf_op jit(solution)/shard_map/all_to_all | solution.py:304
  61.2 1.5 %shard_map.61.held_ref = f32[32,128,128]{2,1,0:T(8,128)} custom-call(f32[32,128,128]{2,1,0:T(8,128)S(1)} %all-to-all-done.in_ref), custom_call_target="tpu_custom_call" | custom-call | tf_op jit(solution)/shard_map/pallas_call | solution.py:130
  62.8 4.0 %all-to-all-start.1 = ((f32[32,128,128]{2,1,0:T(8,128)}), f32[32,128,128]{2,1,0:T(8,128)S(1)}, u32[]{:S(2)}, u32[]{:S(2)}) async-start(f32[32,128,128]{2,1,0:T(8,128)} %shard_map.61.held_ref), calls=%async_computation.1 | async-start | bytes 4194304 | tf_op jit(solution)/shard_map/all_to_all | solution.py:307
  66.8 3.1 %shard_map.62 = f32[128,128]{1,0:T(8,128)S(1)} custom-call(f32[128,32]{1,0:T(8,128)S(1)} %shard_map.60.counts_ref, f32[32,128,128]{2,1,0:T(8,128)} %shard_map.61.held_ref), custom_call_target="tpu_custom_call" | custom-call | tf_op jit(solution)/shard_map/pallas_call | solution.py:249
  69.9 0.3 collective-permute-start
  70.2 1.0 collective-permute-done
  71.2 1.8 %collective-permute-start.1 = (f32[32,128]{1,0:T(8,128)S(1)}, f32[32,128]{1,0:T(8,128)S(1)}, u32[]{:S(2)}, u32[]{:S(2)}) collective-permute-start(f32[32,128]{1,0:T(8,128)S(1)} %constant_dynamic-slice_fusion), channel_id=1, source_target_pairs={{0,1},{1,0},{2,3},{3,2},{4,5},{5,4},{6,7},{7,6},{8,9},{9,8},{10,11... | collective-permute-start | bytes 49160 | tf_op jit(solution)/shard_map/ppermute | solution.py:260
  73.0 4.0 %collective-permute-done.1 = f32[32,128]{1,0:T(8,128)S(1)} collective-permute-done((f32[32,128]{1,0:T(8,128)S(1)}, f32[32,128]{1,0:T(8,128)S(1)}, u32[]{:S(2)}, u32[]{:S(2)}) %collective-permute-start.1) | collective-permute-done | bytes 16416 | tf_op jit(solution)/shard_map/ppermute | solution.py:260
  77.0 4.6 %collective-permute-start.2 = (f32[32,128]{1,0:T(8,128)S(1)}, f32[32,128]{1,0:T(8,128)S(1)}, u32[]{:S(2)}, u32[]{:S(2)}) collective-permute-start(f32[32,128]{1,0:T(8,128)S(1)} %dynamic-slice_add_fusion.1), channel_id=1, source_target_pairs={{0,16},{8,24},{16,0},{24,8},{1,17},{9,25},{17,1},{25,9},{2,18},{10... | collective-permute-start | bytes 49160 | tf_op jit(solution)/shard_map/ppermute | solution.py:260
  81.6 1.9 %collective-permute-done.2 = f32[32,128]{1,0:T(8,128)S(1)} collective-permute-done((f32[32,128]{1,0:T(8,128)S(1)}, f32[32,128]{1,0:T(8,128)S(1)}, u32[]{:S(2)}, u32[]{:S(2)}) %collective-permute-start.2) | collective-permute-done | bytes 16416 | tf_op jit(solution)/shard_map/ppermute | solution.py:260
  83.5 2.8 %collective-permute-start.4 = (f32[32,128]{1,0:T(8,128)S(1)}, f32[32,128]{1,0:T(8,128)S(1)}, u32[]{:S(2)}, u32[]{:S(2)}) collective-permute-start(f32[32,128]{1,0:T(8,128)S(1)} %add.53), channel_id=1, source_target_pairs={{0,4},{1,5},{2,6},{3,7},{4,0},{5,1},{6,2},{7,3},{8,12},{9,13},{10,... | collective-permute-start | bytes 49160 | tf_op jit(solution)/shard_map/ppermute | solution.py:260
  86.3 3.5 %collective-permute-start.5 = (f32[32,128]{1,0:T(8,128)S(1)}, f32[32,128]{1,0:T(8,128)S(1)}, u32[]{:S(2)}, u32[]{:S(2)}) collective-permute-start(f32[32,128]{1,0:T(8,128)S(1)} %add.53), channel_id=1, source_target_pairs={{0,6},{1,7},{2,4},{3,5},{4,2},{5,3},{6,0},{7,1},{8,14},{9,15},{10,... | collective-permute-start | bytes 49160 | tf_op jit(solution)/shard_map/ppermute | solution.py:260
  89.7 0.5 collective-permute-start.3
  90.2 26.7 %collective-permute-done.4 = f32[32,128]{1,0:T(8,128)S(1)} collective-permute-done((f32[32,128]{1,0:T(8,128)S(1)}, f32[32,128]{1,0:T(8,128)S(1)}, u32[]{:S(2)}, u32[]{:S(2)}) %collective-permute-start.4) | collective-permute-done | bytes 16416 | tf_op jit(solution)/shard_map/ppermute | solution.py:260
  116.9 1.4 %collective-permute-start.8 = (f32[32,128]{1,0:T(8,128)S(1)}, f32[32,128]{1,0:T(8,128)S(1)}, u32[]{:S(2)}, u32[]{:S(2)}) collective-permute-start(f32[32,128]{1,0:T(8,128)S(1)} %add_add_fusion), channel_id=1, source_target_pairs={{0,1},{1,0},{2,3},{3,2},{4,5},{5,4},{6,7},{7,6},{8,9},{9,8},{10,11... | collective-permute-start | bytes 49160 | tf_op jit(solution)/shard_map/ppermute | solution.py:260
  118.3 0.0 collective-permute-start.6
  118.3 0.8 collective-permute-start.7
  119.1 1.3 shard_map.63
  120.5 1.3 gather_fusion
  121.8 3.9 %all-to-all-start.2 = ((f32[32,8,128]{2,1,0:T(8,128)}), f32[32,8,128]{2,1,0:T(8,128)S(1)}, u32[]{:S(2)}, u32[]{:S(2)}) async-start(f32[32,8,128]{2,1,0:T(8,128)} %bitcast.7), calls=%async_computation.2 | async-start | bytes 262144 | tf_op jit(solution)/shard_map/all_to_all | solution.py:320
  125.8 0.6 maximum_multiply_fusion
  126.4 7.0 %all-to-all-done.2 = f32[32,8,128]{2,1,0:T(8,128)S(1)} async-done(((f32[32,8,128]{2,1,0:T(8,128)}), f32[32,8,128]{2,1,0:T(8,128)S(1)}, u32[]{:S(2)}, u32[]{:S(2)}) %all-to-all-start.2) | async-done | bytes 131104 | tf_op jit(solution)/shard_map/all_to_all | solution.py:320
  133.5 1.3 gather_fusion.1
  (19 shorter events, 0.1 us)
Async XLA Ops:
  5.0 7.3 %copy-start = (s32[8192]{0:T(1024)S(1)}, s32[8192]{0:T(1024)}, u32[]{:S(2)}) copy-start(s32[8192]{0:T(1024)} %param.5) | copy-start | bytes 98308
  5.0 56.2 %all-to-all-start = ((f32[32,128,128]{2,1,0:T(8,128)}), f32[32,128,128]{2,1,0:T(8,128)S(1)}, u32[]{:S(2)}, u32[]{:S(2)}) async-start(f32[32,128,128]{2,1,0:T(8,128)} %bitcast.13), calls=%async_computation | async-start | bytes 4194304 | tf_op jit(solution)/shard_map/all_to_all | solution.py:304
  62.8 54.2 %all-to-all-start.1 = ((f32[32,128,128]{2,1,0:T(8,128)}), f32[32,128,128]{2,1,0:T(8,128)S(1)}, u32[]{:S(2)}, u32[]{:S(2)}) async-start(f32[32,128,128]{2,1,0:T(8,128)} %shard_map.61.held_ref), calls=%async_computation.1 | async-start | bytes 4194304 | tf_op jit(solution)/shard_map/all_to_all | solution.py:307
  69.9 1.3 collective-permute-start
  71.2 5.9 %collective-permute-start.1 = (f32[32,128]{1,0:T(8,128)S(1)}, f32[32,128]{1,0:T(8,128)S(1)}, u32[]{:S(2)}, u32[]{:S(2)}) collective-permute-start(f32[32,128]{1,0:T(8,128)S(1)} %constant_dynamic-slice_fusion), channel_id=1, source_target_pairs={{0,1},{1,0},{2,3},{3,2},{4,5},{5,4},{6,7},{7,6},{8,9},{9,8},{10,11... | collective-permute-start | bytes 49160 | tf_op jit(solution)/shard_map/ppermute | solution.py:260
  77.0 6.4 %collective-permute-start.2 = (f32[32,128]{1,0:T(8,128)S(1)}, f32[32,128]{1,0:T(8,128)S(1)}, u32[]{:S(2)}, u32[]{:S(2)}) collective-permute-start(f32[32,128]{1,0:T(8,128)S(1)} %dynamic-slice_add_fusion.1), channel_id=1, source_target_pairs={{0,16},{8,24},{16,0},{24,8},{1,17},{9,25},{17,1},{25,9},{2,18},{10... | collective-permute-start | bytes 49160 | tf_op jit(solution)/shard_map/ppermute | solution.py:260
  83.5 33.4 %collective-permute-start.4 = (f32[32,128]{1,0:T(8,128)S(1)}, f32[32,128]{1,0:T(8,128)S(1)}, u32[]{:S(2)}, u32[]{:S(2)}) collective-permute-start(f32[32,128]{1,0:T(8,128)S(1)} %add.53), channel_id=1, source_target_pairs={{0,4},{1,5},{2,6},{3,7},{4,0},{5,1},{6,2},{7,3},{8,12},{9,13},{10,... | collective-permute-start | bytes 49160 | tf_op jit(solution)/shard_map/ppermute | solution.py:260
  86.3 30.6 %collective-permute-start.5 = (f32[32,128]{1,0:T(8,128)S(1)}, f32[32,128]{1,0:T(8,128)S(1)}, u32[]{:S(2)}, u32[]{:S(2)}) collective-permute-start(f32[32,128]{1,0:T(8,128)S(1)} %add.53), channel_id=1, source_target_pairs={{0,6},{1,7},{2,4},{3,5},{4,2},{5,3},{6,0},{7,1},{8,14},{9,15},{10,... | collective-permute-start | bytes 49160 | tf_op jit(solution)/shard_map/ppermute | solution.py:260
  89.7 27.2 %collective-permute-start.3 = (f32[32,128]{1,0:T(8,128)S(1)}, f32[32,128]{1,0:T(8,128)S(1)}, u32[]{:S(2)}, u32[]{:S(2)}) collective-permute-start(f32[32,128]{1,0:T(8,128)S(1)} %add.53), channel_id=1, source_target_pairs={{0,2},{1,3},{2,0},{3,1},{4,6},{5,7},{6,4},{7,5},{8,10},{9,11},{10,... | collective-permute-start | bytes 49160 | tf_op jit(solution)/shard_map/ppermute | solution.py:260
  116.9 8.8 %collective-permute-start.8 = (f32[32,128]{1,0:T(8,128)S(1)}, f32[32,128]{1,0:T(8,128)S(1)}, u32[]{:S(2)}, u32[]{:S(2)}) collective-permute-start(f32[32,128]{1,0:T(8,128)S(1)} %add_add_fusion), channel_id=1, source_target_pairs={{0,1},{1,0},{2,3},{3,2},{4,5},{5,4},{6,7},{7,6},{8,9},{9,8},{10,11... | collective-permute-start | bytes 49160 | tf_op jit(solution)/shard_map/ppermute | solution.py:260
  118.3 7.4 %collective-permute-start.6 = (f32[32,128]{1,0:T(8,128)S(1)}, f32[32,128]{1,0:T(8,128)S(1)}, u32[]{:S(2)}, u32[]{:S(2)}) collective-permute-start(f32[32,128]{1,0:T(8,128)S(1)} %add_add_fusion), channel_id=1, source_target_pairs={{0,9},{1,8},{2,11},{3,10},{4,13},{5,12},{6,15},{7,14},{8,1},{9,0},... | collective-permute-start | bytes 49160 | tf_op jit(solution)/shard_map/ppermute | solution.py:260
  118.3 7.5 %collective-permute-start.7 = (f32[32,128]{1,0:T(8,128)S(1)}, f32[32,128]{1,0:T(8,128)S(1)}, u32[]{:S(2)}, u32[]{:S(2)}) collective-permute-start(f32[32,128]{1,0:T(8,128)S(1)} %add_add_fusion), channel_id=1, source_target_pairs={{0,8},{8,0},{16,24},{24,16},{1,9},{9,1},{17,25},{25,17},{2,10},{10... | collective-permute-start | bytes 49160 | tf_op jit(solution)/shard_map/ppermute | solution.py:260
  121.8 11.6 %all-to-all-start.2 = ((f32[32,8,128]{2,1,0:T(8,128)}), f32[32,8,128]{2,1,0:T(8,128)S(1)}, u32[]{:S(2)}, u32[]{:S(2)}) async-start(f32[32,8,128]{2,1,0:T(8,128)} %bitcast.7), calls=%async_computation.2 | async-start | bytes 262144 | tf_op jit(solution)/shard_map/all_to_all | solution.py:320

commit v19 on v18

--- a/solution.py
+++ b/solution.py
@@ -268,17 +268,13 @@
     return keep + swap(give, axis, 1)
 
 
-def join(lower, upper, axis):
-    turned = lax.axis_index(axis) & 1 == 1
-    first = jnp.where(turned, upper, lower)
-    return jnp.concatenate([first, jnp.where(turned, lower, upper)], axis=0)
-
-
 def gather_quarters(value):
-    over_core, over_y = swap(value, "narrow", 1), swap(value, "wide", 1)
-    over_both = swap(value, AXES, lax.axis_size("wide") + 1)
-    mine = join(value, over_y, "wide")
-    return join(mine, join(over_core, over_both, "wide"), "narrow")
+    rows, width = value.shape
+    place = 2 * (lax.axis_index("narrow") & 1) + (lax.axis_index("wide") & 1)
+    blank = jnp.zeros((4 * rows, width), jnp.float32)
+    value = lax.dynamic_update_slice_in_dim(blank, value, place * rows, 0)
+    others = swap(value, "narrow", 1) + swap(value, AXES, lax.axis_size("wide") + 1)
+    return value + swap(value, "wide", 1) + others
 
 
 def landing(block, rows_here, most):

time: 135 us -> 135 us (level)
  no operation moved by 1% of the time
where the time goes in v19:
time: 135 us
  waiting for transfers between devices  88 us (65%)
  starting transfers between devices  30.9 us (23%)
  Pallas kernels  11.2 us (8%)
  local copies, waits for them, and re-layouts  2.82 us (2%)
    all_to_all x1, waiting for transfers between devices, on_device(): slices = lax.all_to_all(local, TURNED, 0, 0, tiled=True)  47.4 us
    ppermute x9, waiting for transfers between devices, swap(): return lax.ppermute(value, axis, pairs)  33.5 us
    ppermute x9, starting transfers between devices, swap(): return lax.ppermute(value, axis, pairs)  15.7 us
    all_to_all x1, starting transfers between devices, on_device(): slices = lax.all_to_all(local, TURNED, 0, 0, tiled=True)  7.3 us
    all_to_all x1, waiting for transfers between devices, on_device(): lax.all_to_all(chosen.reshape(devices, most, width), AXES, 0, 0, tiled=True)  7.04 us
    pallas_call x1, Pallas kernels, local_transform(): pl.pallas_call(functools.partial(local_kernel, scale), out_shape=jax.Shap...  4.38 us
    all_to_all x1, starting transfers between devices, on_device(): mixed = lax.all_to_all(slices, TURNED, 0, 0, tiled=True)  4.02 us
    all_to_all x1, starting transfers between devices, on_device(): lax.all_to_all(chosen.reshape(devices, most, width), AXES, 0, 0, tiled=True)  3.88 us
  transfers between devices with their start and end apart: 12, of which 6 were waited for; matrix products, arithmetic and copies ran while one was open for 2% of the time, Pallas kernels for 4%

profile of v19, /device:TPU:0, one launch (start us, length us, event | category | flops | bytes accessed | tf_op | source)
XLA Modules:
  0.0 134.8 jit_solution(335873175052660078)
XLA Ops:
  0.6 4.4 %shard_map.58 = f32[16,256,128]{2,1,0:T(8,128)} custom-call(s32[32,128]{1,0:T(8,128)} %bitcast.15, f32[16,256,128]{2,1,0:T(8,128)} %bitcast.14), custom_call_target="tpu_custom_call" | custom-call | tf_op jit(solution)/shard_map/pallas_call | solution.py:82
  5.0 0.0 copy-start
  5.0 7.3 %all-to-all-start = ((f32[32,128,128]{2,1,0:T(8,128)}), f32[32,128,128]{2,1,0:T(8,128)S(1)}, u32[]{:S(2)}, u32[]{:S(2)}) async-start(f32[32,128,128]{2,1,0:T(8,128)} %bitcast.13), calls=%async_computation | async-start | bytes 4194304 | tf_op jit(solution)/shard_map/all_to_all | solution.py:300
  12.4 0.3 shard_map.59
  12.7 0.1 reshape.44
  12.7 0.7 shard_map.60.counts_ref
  13.4 0.1 and_select_fusion
  13.5 0.2 convert_reduce_fusion
  13.7 0.1 multiply_add_fusion
  13.8 47.4 %all-to-all-done.in_ref = f32[32,128,128]{2,1,0:T(8,128)S(1)} async-done(((f32[32,128,128]{2,1,0:T(8,128)}), f32[32,128,128]{2,1,0:T(8,128)S(1)}, u32[]{:S(2)}, u32[]{:S(2)}) %all-to-all-start) | async-done | bytes 2097184 | tf_op jit(solution)/shard_map/all_to_all | solution.py:300
  61.2 1.5 %shard_map.61.held_ref = f32[32,128,128]{2,1,0:T(8,128)} custom-call(f32[32,128,128]{2,1,0:T(8,128)S(1)} %all-to-all-done.in_ref), custom_call_target="tpu_custom_call" | custom-call | tf_op jit(solution)/shard_map/pallas_call | solution.py:130
  62.8 4.0 %all-to-all-start.1 = ((f32[32,128,128]{2,1,0:T(8,128)}), f32[32,128,128]{2,1,0:T(8,128)S(1)}, u32[]{:S(2)}, u32[]{:S(2)}) async-start(f32[32,128,128]{2,1,0:T(8,128)} %shard_map.61.held_ref), calls=%async_computation.1 | async-start | bytes 4194304 | tf_op jit(solution)/shard_map/all_to_all | solution.py:303
  66.8 3.1 %shard_map.62 = f32[128,128]{1,0:T(8,128)S(1)} custom-call(f32[128,32]{1,0:T(8,128)S(1)} %shard_map.60.counts_ref, f32[32,128,128]{2,1,0:T(8,128)} %shard_map.61.held_ref), custom_call_target="tpu_custom_call" | custom-call | tf_op jit(solution)/shard_map/pallas_call | solution.py:249
  69.9 0.3 collective-permute-start
  70.2 1.0 collective-permute-done
  71.2 1.8 %collective-permute-start.1 = (f32[32,128]{1,0:T(8,128)S(1)}, f32[32,128]{1,0:T(8,128)S(1)}, u32[]{:S(2)}, u32[]{:S(2)}) collective-permute-start(f32[32,128]{1,0:T(8,128)S(1)} %constant_dynamic-slice_fusion), channel_id=1, source_target_pairs={{0,1},{1,0},{2,3},{3,2},{4,5},{5,4},{6,7},{7,6},{8,9},{9,8},{10,11... | collective-permute-start | bytes 49160 | tf_op jit(solution)/shard_map/ppermute | solution.py:260
  73.0 4.0 %collective-permute-done.1 = f32[32,128]{1,0:T(8,128)S(1)} collective-permute-done((f32[32,128]{1,0:T(8,128)S(1)}, f32[32,128]{1,0:T(8,128)S(1)}, u32[]{:S(2)}, u32[]{:S(2)}) %collective-permute-start.1) | collective-permute-done | bytes 16416 | tf_op jit(solution)/shard_map/ppermute | solution.py:260
  77.0 4.6 %collective-permute-start.2 = (f32[32,128]{1,0:T(8,128)S(1)}, f32[32,128]{1,0:T(8,128)S(1)}, u32[]{:S(2)}, u32[]{:S(2)}) collective-permute-start(f32[32,128]{1,0:T(8,128)S(1)} %dynamic-slice_add_fusion.1), channel_id=1, source_target_pairs={{0,16},{8,24},{16,0},{24,8},{1,17},{9,25},{17,1},{25,9},{2,18},{10... | collective-permute-start | bytes 49160 | tf_op jit(solution)/shard_map/ppermute | solution.py:260
  81.6 1.9 %collective-permute-done.2 = f32[32,128]{1,0:T(8,128)S(1)} collective-permute-done((f32[32,128]{1,0:T(8,128)S(1)}, f32[32,128]{1,0:T(8,128)S(1)}, u32[]{:S(2)}, u32[]{:S(2)}) %collective-permute-start.2) | collective-permute-done | bytes 16416 | tf_op jit(solution)/shard_map/ppermute | solution.py:260
  83.5 2.8 %collective-permute-start.4 = (f32[32,128]{1,0:T(8,128)S(1)}, f32[32,128]{1,0:T(8,128)S(1)}, u32[]{:S(2)}, u32[]{:S(2)}) collective-permute-start(f32[32,128]{1,0:T(8,128)S(1)} %add.69), channel_id=1, source_target_pairs={{0,4},{1,5},{2,6},{3,7},{4,0},{5,1},{6,2},{7,3},{8,12},{9,13},{10,... | collective-permute-start | bytes 49160 | tf_op jit(solution)/shard_map/ppermute | solution.py:260
  86.3 3.5 %collective-permute-start.5 = (f32[32,128]{1,0:T(8,128)S(1)}, f32[32,128]{1,0:T(8,128)S(1)}, u32[]{:S(2)}, u32[]{:S(2)}) collective-permute-start(f32[32,128]{1,0:T(8,128)S(1)} %add.69), channel_id=1, source_target_pairs={{0,6},{1,7},{2,4},{3,5},{4,2},{5,3},{6,0},{7,1},{8,14},{9,15},{10,... | collective-permute-start | bytes 49160 | tf_op jit(solution)/shard_map/ppermute | solution.py:260
  89.7 0.5 collective-permute-start.3
  90.2 26.7 %collective-permute-done.4 = f32[32,128]{1,0:T(8,128)S(1)} collective-permute-done((f32[32,128]{1,0:T(8,128)S(1)}, f32[32,128]{1,0:T(8,128)S(1)}, u32[]{:S(2)}, u32[]{:S(2)}) %collective-permute-start.4) | collective-permute-done | bytes 16416 | tf_op jit(solution)/shard_map/ppermute | solution.py:260
  117.0 1.4 %collective-permute-start.6 = (f32[128,128]{1,0:T(8,128)S(1)}, f32[128,128]{1,0:T(8,128)S(1)}, u32[]{:S(2)}, u32[]{:S(2)}) collective-permute-start(f32[128,128]{1,0:T(8,128)S(1)} %constant_dynamic-update-slice_fusion), channel_id=1, source_target_pairs={{0,1},{1,0},{2,3},{3,2},{4,5},{5,4},{6,7},{7,6},{8,9},{9,8},{10,11... | collective-permute-start | bytes 196616 | tf_op jit(solution)/shard_map/ppermute | solution.py:260
  118.3 0.0 collective-permute-start.7
  118.3 0.8 collective-permute-start.8
  119.2 1.3 shard_map.63
  120.5 1.3 gather_fusion
  121.9 3.9 %all-to-all-start.2 = ((f32[32,8,128]{2,1,0:T(8,128)}), f32[32,8,128]{2,1,0:T(8,128)S(1)}, u32[]{:S(2)}, u32[]{:S(2)}) async-start(f32[32,8,128]{2,1,0:T(8,128)} %bitcast.7), calls=%async_computation.2 | async-start | bytes 262144 | tf_op jit(solution)/shard_map/all_to_all | solution.py:316
  125.8 0.6 add_multiply_fusion
  126.4 7.0 %all-to-all-done.2 = f32[32,8,128]{2,1,0:T(8,128)S(1)} async-done(((f32[32,8,128]{2,1,0:T(8,128)}), f32[32,8,128]{2,1,0:T(8,128)S(1)}, u32[]{:S(2)}, u32[]{:S(2)}) %all-to-all-start.2) | async-done | bytes 131104 | tf_op jit(solution)/shard_map/all_to_all | solution.py:316
  133.5 1.3 gather_fusion.1
  (19 shorter events, 0.1 us)
Async XLA Ops:
  5.0 7.3 %copy-start = (s32[8192]{0:T(1024)S(1)}, s32[8192]{0:T(1024)}, u32[]{:S(2)}) copy-start(s32[8192]{0:T(1024)} %param.5) | copy-start | bytes 98308
  5.0 56.2 %all-to-all-start = ((f32[32,128,128]{2,1,0:T(8,128)}), f32[32,128,128]{2,1,0:T(8,128)S(1)}, u32[]{:S(2)}, u32[]{:S(2)}) async-start(f32[32,128,128]{2,1,0:T(8,128)} %bitcast.13), calls=%async_computation | async-start | bytes 4194304 | tf_op jit(solution)/shard_map/all_to_all | solution.py:300
  62.8 54.2 %all-to-all-start.1 = ((f32[32,128,128]{2,1,0:T(8,128)}), f32[32,128,128]{2,1,0:T(8,128)S(1)}, u32[]{:S(2)}, u32[]{:S(2)}) async-start(f32[32,128,128]{2,1,0:T(8,128)} %shard_map.61.held_ref), calls=%async_computation.1 | async-start | bytes 4194304 | tf_op jit(solution)/shard_map/all_to_all | solution.py:303
  69.9 1.3 collective-permute-start
  71.2 5.9 %collective-permute-start.1 = (f32[32,128]{1,0:T(8,128)S(1)}, f32[32,128]{1,0:T(8,128)S(1)}, u32[]{:S(2)}, u32[]{:S(2)}) collective-permute-start(f32[32,128]{1,0:T(8,128)S(1)} %constant_dynamic-slice_fusion), channel_id=1, source_target_pairs={{0,1},{1,0},{2,3},{3,2},{4,5},{5,4},{6,7},{7,6},{8,9},{9,8},{10,11... | collective-permute-start | bytes 49160 | tf_op jit(solution)/shard_map/ppermute | solution.py:260
  77.0 6.4 %collective-permute-start.2 = (f32[32,128]{1,0:T(8,128)S(1)}, f32[32,128]{1,0:T(8,128)S(1)}, u32[]{:S(2)}, u32[]{:S(2)}) collective-permute-start(f32[32,128]{1,0:T(8,128)S(1)} %dynamic-slice_add_fusion.1), channel_id=1, source_target_pairs={{0,16},{8,24},{16,0},{24,8},{1,17},{9,25},{17,1},{25,9},{2,18},{10... | collective-permute-start | bytes 49160 | tf_op jit(solution)/shard_map/ppermute | solution.py:260
  83.5 33.4 %collective-permute-start.4 = (f32[32,128]{1,0:T(8,128)S(1)}, f32[32,128]{1,0:T(8,128)S(1)}, u32[]{:S(2)}, u32[]{:S(2)}) collective-permute-start(f32[32,128]{1,0:T(8,128)S(1)} %add.69), channel_id=1, source_target_pairs={{0,4},{1,5},{2,6},{3,7},{4,0},{5,1},{6,2},{7,3},{8,12},{9,13},{10,... | collective-permute-start | bytes 49160 | tf_op jit(solution)/shard_map/ppermute | solution.py:260
  86.3 30.6 %collective-permute-start.5 = (f32[32,128]{1,0:T(8,128)S(1)}, f32[32,128]{1,0:T(8,128)S(1)}, u32[]{:S(2)}, u32[]{:S(2)}) collective-permute-start(f32[32,128]{1,0:T(8,128)S(1)} %add.69), channel_id=1, source_target_pairs={{0,6},{1,7},{2,4},{3,5},{4,2},{5,3},{6,0},{7,1},{8,14},{9,15},{10,... | collective-permute-start | bytes 49160 | tf_op jit(solution)/shard_map/ppermute | solution.py:260
  89.7 27.2 %collective-permute-start.3 = (f32[32,128]{1,0:T(8,128)S(1)}, f32[32,128]{1,0:T(8,128)S(1)}, u32[]{:S(2)}, u32[]{:S(2)}) collective-permute-start(f32[32,128]{1,0:T(8,128)S(1)} %add.69), channel_id=1, source_target_pairs={{0,2},{1,3},{2,0},{3,1},{4,6},{5,7},{6,4},{7,5},{8,10},{9,11},{10,... | collective-permute-start | bytes 49160 | tf_op jit(solution)/shard_map/ppermute | solution.py:260
  117.0 8.8 %collective-permute-start.6 = (f32[128,128]{1,0:T(8,128)S(1)}, f32[128,128]{1,0:T(8,128)S(1)}, u32[]{:S(2)}, u32[]{:S(2)}) collective-permute-start(f32[128,128]{1,0:T(8,128)S(1)} %constant_dynamic-update-slice_fusion), channel_id=1, source_target_pairs={{0,1},{1,0},{2,3},{3,2},{4,5},{5,4},{6,7},{7,6},{8,9},{9,8},{10,11... | collective-permute-start | bytes 196616 | tf_op jit(solution)/shard_map/ppermute | solution.py:260
  118.3 7.5 %collective-permute-start.7 = (f32[128,128]{1,0:T(8,128)S(1)}, f32[128,128]{1,0:T(8,128)S(1)}, u32[]{:S(2)}, u32[]{:S(2)}) collective-permute-start(f32[128,128]{1,0:T(8,128)S(1)} %constant_dynamic-update-slice_fusion), channel_id=1, source_target_pairs={{0,8},{8,0},{16,24},{24,16},{1,9},{9,1},{17,25},{25,17},{2,10},{10... | collective-permute-start | bytes 196616 | tf_op jit(solution)/shard_map/ppermute | solution.py:260
  118.3 7.5 %collective-permute-start.8 = (f32[128,128]{1,0:T(8,128)S(1)}, f32[128,128]{1,0:T(8,128)S(1)}, u32[]{:S(2)}, u32[]{:S(2)}) collective-permute-start(f32[128,128]{1,0:T(8,128)S(1)} %constant_dynamic-update-slice_fusion), channel_id=1, source_target_pairs={{0,9},{1,8},{2,11},{3,10},{4,13},{5,12},{6,15},{7,14},{8,1},{9,0},... | collective-permute-start | bytes 196616 | tf_op jit(solution)/shard_map/ppermute | solution.py:260
  121.9 11.6 %all-to-all-start.2 = ((f32[32,8,128]{2,1,0:T(8,128)}), f32[32,8,128]{2,1,0:T(8,128)S(1)}, u32[]{:S(2)}, u32[]{:S(2)}) async-start(f32[32,8,128]{2,1,0:T(8,128)} %bitcast.7), calls=%async_computation.2 | async-start | bytes 262144 | tf_op jit(solution)/shard_map/all_to_all | solution.py:316

commit v20 on v17

--- a/solution.py
+++ b/solution.py
@@ -268,11 +268,12 @@
     return keep + swap(give, axis, 1)
 
 
-def join(value, axis):
-    upper = lax.axis_index(axis) & 1 == 1
-    other = swap(value, axis, 1)
-    first = jnp.where(upper, other, value)
-    return jnp.concatenate([first, jnp.where(upper, value, other)], axis=0)
+def gather_halves(value, axis):
+    rows, width = value.shape
+    blank = jnp.zeros((2 * rows, width), jnp.float32)
+    at = (lax.axis_index(axis) & 1) * rows
+    value = lax.dynamic_update_slice_in_dim(blank, value, at, 0)
+    return value + swap(value, axis, 1)
 
 
 def landing(block, rows_here, most):
@@ -301,19 +302,15 @@
     mixed = lax.all_to_all(slices, TURNED, 0, 0, tiled=True)
     gram = gram_part(counts, slices)
     gram = scatter_sum(gram, "narrow")
-    far = lax.axis_size("wide") // 4
-    for axis, low, high in (("wide", 1, far), ("narrow", 2, lax.axis_size("narrow"))):
-        while low < high:
+    for axis, low in (("narrow", 2), ("wide", 1)):
+        while low < lax.axis_size(axis):
             gram = gram + swap(gram, axis, low)
             low *= 2
-    near, one, two = [swap(gram, "wide", apart * far) for apart in (1, 2, 3)]
-    gram = (gram + near) + (one + two)
     mixed, gram = lax.optimization_barrier((mixed, gram))
     mixed = mixed.reshape(rows_here, width)
     chosen = jnp.take(mixed, wanted, axis=0, mode="clip")
-    chosen, gram = lax.optimization_barrier((chosen, gram))
     landed = lax.all_to_all(chosen.reshape(devices, most, width), AXES, 0, 0, tiled=True)
-    gram = join(gram / float(picks.shape[0]), "narrow")
+    gram = gather_halves(gram, "narrow") / float(picks.shape[0])
     mixed = store(mixed)
     landed, mixed, gram = lax.optimization_barrier((landed, mixed, gram))
     sketch = jnp.take(landed.reshape(devices * most, width), spots, axis=0, mode="clip")

time: 134 us -> 133 us (level)
  starting transfers between devices: 28.9 us -> 22 us
  waiting for transfers between devices: 89 us -> 95.2 us
    ppermute x7 -> x6, starting transfers between devices: 13.7 us -> 6.59 us  [swap(): return lax.ppermute(value, axis, pairs)]
    ppermute x7 -> x6, waiting for transfers between devices: 34.5 us -> 40.6 us  [swap(): return lax.ppermute(value, axis, pairs)]
  transfers between devices with their start and end apart: 10 -> 9, of which waited for: 6 -> 7; matrix products, arithmetic and copies ran while one was open for 1% -> 2% of each run, Pallas kernels for 4% -> 4%
where the time goes in v20:
time: 133 us
  waiting for transfers between devices  95.2 us (72%)
  starting transfers between devices  22 us (17%)
  Pallas kernels  11.2 us (8%)
  local copies, waits for them, and re-layouts  2.82 us (2%)
    all_to_all x1, waiting for transfers between devices, on_device(): slices = lax.all_to_all(local, TURNED, 0, 0, tiled=True)  47.4 us
    ppermute x6, waiting for transfers between devices, swap(): return lax.ppermute(value, axis, pairs)  40.6 us
    all_to_all x1, starting transfers between devices, on_device(): slices = lax.all_to_all(local, TURNED, 0, 0, tiled=True)  7.3 us
    all_to_all x1, waiting for transfers between devices, on_device(): lax.all_to_all(chosen.reshape(devices, most, width), AXES, 0, 0, tiled=True)  7.07 us
    ppermute x6, starting transfers between devices, swap(): return lax.ppermute(value, axis, pairs)  6.59 us
    pallas_call x1, Pallas kernels, local_transform(): pl.pallas_call(functools.partial(local_kernel, scale), out_shape=jax.Shap...  4.38 us
    all_to_all x1, starting transfers between devices, on_device(): lax.all_to_all(chosen.reshape(devices, most, width), AXES, 0, 0, tiled=True)  4.11 us
    all_to_all x1, starting transfers between devices, on_device(): mixed = lax.all_to_all(slices, TURNED, 0, 0, tiled=True)  4.02 us
  transfers between devices with their start and end apart: 9, of which 7 were waited for; matrix products, arithmetic and copies ran while one was open for 2% of the time, Pallas kernels for 4%

profile of v20, /device:TPU:0, one launch (start us, length us, event | category | flops | bytes accessed | tf_op | source)
XLA Modules:
  0.0 133.1 jit_solution(10112841741969825434)
XLA Ops:
  0.6 4.4 %shard_map.58 = f32[16,256,128]{2,1,0:T(8,128)} custom-call(s32[32,128]{1,0:T(8,128)} %bitcast.15, f32[16,256,128]{2,1,0:T(8,128)} %bitcast.14), custom_call_target="tpu_custom_call" | custom-call | tf_op jit(solution)/shard_map/pallas_call | solution.py:82
  5.0 0.0 copy-start
  5.0 7.3 %all-to-all-start = ((f32[32,128,128]{2,1,0:T(8,128)}), f32[32,128,128]{2,1,0:T(8,128)S(1)}, u32[]{:S(2)}, u32[]{:S(2)}) async-start(f32[32,128,128]{2,1,0:T(8,128)} %bitcast.13), calls=%async_computation | async-start | bytes 4194304 | tf_op jit(solution)/shard_map/all_to_all | solution.py:299
  12.4 0.3 shard_map.59
  12.7 0.1 reshape.44
  12.8 0.7 shard_map.60.counts_ref
  13.4 0.1 and_select_fusion
  13.5 0.2 convert_reduce_fusion
  13.7 0.1 multiply_add_fusion
  13.8 47.4 %all-to-all-done.in_ref = f32[32,128,128]{2,1,0:T(8,128)S(1)} async-done(((f32[32,128,128]{2,1,0:T(8,128)}), f32[32,128,128]{2,1,0:T(8,128)S(1)}, u32[]{:S(2)}, u32[]{:S(2)}) %all-to-all-start) | async-done | bytes 2097184 | tf_op jit(solution)/shard_map/all_to_all | solution.py:299
  61.2 1.5 %shard_map.61.held_ref = f32[32,128,128]{2,1,0:T(8,128)} custom-call(f32[32,128,128]{2,1,0:T(8,128)S(1)} %all-to-all-done.in_ref), custom_call_target="tpu_custom_call" | custom-call | tf_op jit(solution)/shard_map/pallas_call | solution.py:130
  62.8 4.0 %all-to-all-start.1 = ((f32[32,128,128]{2,1,0:T(8,128)}), f32[32,128,128]{2,1,0:T(8,128)S(1)}, u32[]{:S(2)}, u32[]{:S(2)}) async-start(f32[32,128,128]{2,1,0:T(8,128)} %shard_map.61.held_ref), calls=%async_computation.1 | async-start | bytes 4194304 | tf_op jit(solution)/shard_map/all_to_all | solution.py:302
  66.8 3.1 %shard_map.62 = f32[128,128]{1,0:T(8,128)S(1)} custom-call(f32[128,32]{1,0:T(8,128)S(1)} %shard_map.60.counts_ref, f32[32,128,128]{2,1,0:T(8,128)} %shard_map.61.held_ref), custom_call_target="tpu_custom_call" | custom-call | tf_op jit(solution)/shard_map/pallas_call | solution.py:249
  69.9 0.3 collective-permute-start
  70.2 1.0 collective-permute-done
  71.2 1.8 %collective-permute-start.1 = (f32[64,128]{1,0:T(8,128)S(1)}, f32[64,128]{1,0:T(8,128)S(1)}, u32[]{:S(2)}, u32[]{:S(2)}) collective-permute-start(f32[64,128]{1,0:T(8,128)S(1)} %dynamic-slice_add_fusion), channel_id=1, source_target_pairs={{0,16},{8,24},{16,0},{24,8},{1,17},{9,25},{17,1},{25,9},{2,18},{10... | collective-permute-start | bytes 98312 | tf_op jit(solution)/shard_map/ppermute | solution.py:260
  72.9 10.0 %collective-permute-done.1 = f32[64,128]{1,0:T(8,128)S(1)} collective-permute-done((f32[64,128]{1,0:T(8,128)S(1)}, f32[64,128]{1,0:T(8,128)S(1)}, u32[]{:S(2)}, u32[]{:S(2)}) %collective-permute-start.1) | collective-permute-done | bytes 32800 | tf_op jit(solution)/shard_map/ppermute | solution.py:260
  82.9 0.3 collective-permute-start.2
  83.2 3.9 %collective-permute-done.2 = f32[64,128]{1,0:T(8,128)S(1)} collective-permute-done((f32[64,128]{1,0:T(8,128)S(1)}, f32[64,128]{1,0:T(8,128)S(1)}, u32[]{:S(2)}, u32[]{:S(2)}) %collective-permute-start.2) | collective-permute-done | bytes 32800 | tf_op jit(solution)/shard_map/ppermute | solution.py:260
  87.1 0.0 collective-permute-start.3
  87.2 15.4 %collective-permute-done.3 = f32[64,128]{1,0:T(8,128)S(1)} collective-permute-done((f32[64,128]{1,0:T(8,128)S(1)}, f32[64,128]{1,0:T(8,128)S(1)}, u32[]{:S(2)}, u32[]{:S(2)}) %collective-permute-start.3) | collective-permute-done | bytes 32800 | tf_op jit(solution)/shard_map/ppermute | solution.py:260
  102.6 4.1 %collective-permute-start.4 = (f32[64,128]{1,0:T(8,128)S(1)}, f32[64,128]{1,0:T(8,128)S(1)}, u32[]{:S(2)}, u32[]{:S(2)}) collective-permute-start(f32[64,128]{1,0:T(8,128)S(1)} %add.48), channel_id=1, source_target_pairs={{0,4},{1,5},{2,6},{3,7},{4,0},{5,1},{6,2},{7,3},{8,12},{9,13},{10,... | collective-permute-start | bytes 98312 | tf_op jit(solution)/shard_map/ppermute | solution.py:260
  106.7 10.4 %collective-permute-done.4 = f32[64,128]{1,0:T(8,128)S(1)} collective-permute-done((f32[64,128]{1,0:T(8,128)S(1)}, f32[64,128]{1,0:T(8,128)S(1)}, u32[]{:S(2)}, u32[]{:S(2)}) %collective-permute-start.4) | collective-permute-done | bytes 32800 | tf_op jit(solution)/shard_map/ppermute | solution.py:260
  117.1 0.0 all-to-all-done.1
  117.1 0.1 collective-permute-start.5
  117.2 1.3 shard_map.63
  118.6 1.3 %gather_fusion = f32[256,128]{1,0:T(8,128)} fusion(f32[4096,128]{1,0:T(8,128)S(1)} %bitcast.10, s32[1024]{0:T(1024)S(1)} %pad_clamp_fusion.1), kind=kCustom, calls=%fused_computation | custom fusion | bytes 263168 | tf_op jit(solution)/shard_map/jit(_take)/gather | solution.py:311
  119.9 4.1 %all-to-all-start.2 = ((f32[32,8,128]{2,1,0:T(8,128)}), f32[32,8,128]{2,1,0:T(8,128)S(1)}, u32[]{:S(2)}, u32[]{:S(2)}) async-start(f32[32,8,128]{2,1,0:T(8,128)} %bitcast.7), calls=%async_computation.2 | async-start | bytes 262144 | tf_op jit(solution)/shard_map/all_to_all | solution.py:312
  124.0 0.0 collective-permute-done.5
  124.0 0.6 broadcast_multiply_fusion
  124.7 7.1 %all-to-all-done.2 = f32[32,8,128]{2,1,0:T(8,128)S(1)} async-done(((f32[32,8,128]{2,1,0:T(8,128)}), f32[32,8,128]{2,1,0:T(8,128)S(1)}, u32[]{:S(2)}, u32[]{:S(2)}) %all-to-all-start.2) | async-done | bytes 131104 | tf_op jit(solution)/shard_map/all_to_all | solution.py:312
  131.8 1.3 %gather_fusion.1 = f32[256,128]{1,0:T(8,128)} fusion(f32[256,128]{1,0:T(8,128)S(1)} %bitcast.12, s32[1024]{0:T(1024)S(1)} %pad_clamp_fusion), kind=kCustom, calls=%fused_computation.1 | custom fusion | bytes 263168 | tf_op jit(solution)/shard_map/jit(_take)/gather | solution.py:316
  (13 shorter events, 0.1 us)
Async XLA Ops:
  5.0 7.3 %copy-start = (s32[8192]{0:T(1024)S(1)}, s32[8192]{0:T(1024)}, u32[]{:S(2)}) copy-start(s32[8192]{0:T(1024)} %param.5) | copy-start | bytes 98308
  5.0 56.2 %all-to-all-start = ((f32[32,128,128]{2,1,0:T(8,128)}), f32[32,128,128]{2,1,0:T(8,128)S(1)}, u32[]{:S(2)}, u32[]{:S(2)}) async-start(f32[32,128,128]{2,1,0:T(8,128)} %bitcast.13), calls=%async_computation | async-start | bytes 4194304 | tf_op jit(solution)/shard_map/all_to_all | solution.py:299
  62.8 54.3 %all-to-all-start.1 = ((f32[32,128,128]{2,1,0:T(8,128)}), f32[32,128,128]{2,1,0:T(8,128)S(1)}, u32[]{:S(2)}, u32[]{:S(2)}) async-start(f32[32,128,128]{2,1,0:T(8,128)} %shard_map.61.held_ref), calls=%async_computation.1 | async-start | bytes 4194304 | tf_op jit(solution)/shard_map/all_to_all | solution.py:302
  69.9 1.3 collective-permute-start
  71.2 11.8 %collective-permute-start.1 = (f32[64,128]{1,0:T(8,128)S(1)}, f32[64,128]{1,0:T(8,128)S(1)}, u32[]{:S(2)}, u32[]{:S(2)}) collective-permute-start(f32[64,128]{1,0:T(8,128)S(1)} %dynamic-slice_add_fusion), channel_id=1, source_target_pairs={{0,16},{8,24},{16,0},{24,8},{1,17},{9,25},{17,1},{25,9},{2,18},{10... | collective-permute-start | bytes 98312 | tf_op jit(solution)/shard_map/ppermute | solution.py:260
  82.9 4.2 %collective-permute-start.2 = (f32[64,128]{1,0:T(8,128)S(1)}, f32[64,128]{1,0:T(8,128)S(1)}, u32[]{:S(2)}, u32[]{:S(2)}) collective-permute-start(f32[64,128]{1,0:T(8,128)S(1)} %add.46), channel_id=1, source_target_pairs={{0,1},{1,0},{2,3},{3,2},{4,5},{5,4},{6,7},{7,6},{8,9},{9,8},{10,11... | collective-permute-start | bytes 98312 | tf_op jit(solution)/shard_map/ppermute | solution.py:260
  87.1 15.4 %collective-permute-start.3 = (f32[64,128]{1,0:T(8,128)S(1)}, f32[64,128]{1,0:T(8,128)S(1)}, u32[]{:S(2)}, u32[]{:S(2)}) collective-permute-start(f32[64,128]{1,0:T(8,128)S(1)} %add.47), channel_id=1, source_target_pairs={{0,2},{1,3},{2,0},{3,1},{4,6},{5,7},{6,4},{7,5},{8,10},{9,11},{10,... | collective-permute-start | bytes 98312 | tf_op jit(solution)/shard_map/ppermute | solution.py:260
  102.6 14.5 %collective-permute-start.4 = (f32[64,128]{1,0:T(8,128)S(1)}, f32[64,128]{1,0:T(8,128)S(1)}, u32[]{:S(2)}, u32[]{:S(2)}) collective-permute-start(f32[64,128]{1,0:T(8,128)S(1)} %add.48), channel_id=1, source_target_pairs={{0,4},{1,5},{2,6},{3,7},{4,0},{5,1},{6,2},{7,3},{8,12},{9,13},{10,... | collective-permute-start | bytes 98312 | tf_op jit(solution)/shard_map/ppermute | solution.py:260
  117.1 6.9 %collective-permute-start.5 = (f32[128,128]{1,0:T(8,128)S(1)}, f32[128,128]{1,0:T(8,128)S(1)}, u32[]{:S(2)}, u32[]{:S(2)}) collective-permute-start(f32[128,128]{1,0:T(8,128)S(1)} %constant_dynamic-update-slice_fusion), channel_id=1, source_target_pairs={{0,8},{8,0},{16,24},{24,16},{1,9},{9,1},{17,25},{25,17},{2,10},{10... | collective-permute-start | bytes 196616 | tf_op jit(solution)/shard_map/ppermute | solution.py:260
  119.9 11.9 %all-to-all-start.2 = ((f32[32,8,128]{2,1,0:T(8,128)}), f32[32,8,128]{2,1,0:T(8,128)S(1)}, u32[]{:S(2)}, u32[]{:S(2)}) async-start(f32[32,8,128]{2,1,0:T(8,128)} %bitcast.7), calls=%async_computation.2 | async-start | bytes 262144 | tf_op jit(solution)/shard_map/all_to_all | solution.py:312

commit v21 on v20

--- a/solution.py
+++ b/solution.py
@@ -273,7 +273,7 @@
     blank = jnp.zeros((2 * rows, width), jnp.float32)
     at = (lax.axis_index(axis) & 1) * rows
     value = lax.dynamic_update_slice_in_dim(blank, value, at, 0)
-    return value + swap(value, axis, 1)
+    return value, swap(value, axis, 1)
 
 
 def landing(block, rows_here, most):
@@ -310,8 +310,10 @@
     mixed = mixed.reshape(rows_here, width)
     chosen = jnp.take(mixed, wanted, axis=0, mode="clip")
     landed = lax.all_to_all(chosen.reshape(devices, most, width), AXES, 0, 0, tiled=True)
-    gram = gather_halves(gram, "narrow") / float(picks.shape[0])
+    gram, other = gather_halves(gram, "narrow")
+    mixed, other = lax.optimization_barrier((mixed, other))
     mixed = store(mixed)
+    gram = (gram + other) / float(picks.shape[0])
     landed, mixed, gram = lax.optimization_barrier((landed, mixed, gram))
     sketch = jnp.take(landed.reshape(devices * most, width), spots, axis=0, mode="clip")
     return (mixed, sketch, gram)

time: 133 us -> 132 us (level)
  waiting for transfers between devices: 95.2 us -> 93.8 us
    all_to_all x1, waiting for transfers between devices: 7.07 us -> 5.73 us  [on_device(): lax.all_to_all(chosen.reshape(devices, most, width), AXES, 0, 0, tiled=True)]
where the time goes in v21:
time: 132 us
  waiting for transfers between devices  93.8 us (71%)
  starting transfers between devices  22 us (17%)
  Pallas kernels  11.2 us (8%)
  local copies, waits for them, and re-layouts  2.82 us (2%)
    all_to_all x1, waiting for transfers between devices, on_device(): slices = lax.all_to_all(local, TURNED, 0, 0, tiled=True)  47.4 us
    ppermute x6, waiting for transfers between devices, swap(): return lax.ppermute(value, axis, pairs)  40.6 us
    all_to_all x1, starting transfers between devices, on_device(): slices = lax.all_to_all(local, TURNED, 0, 0, tiled=True)  7.3 us
    ppermute x6, starting transfers between devices, swap(): return lax.ppermute(value, axis, pairs)  6.59 us
    all_to_all x1, waiting for transfers between devices, on_device(): lax.all_to_all(chosen.reshape(devices, most, width), AXES, 0, 0, tiled=True)  5.73 us
    pallas_call x1, Pallas kernels, local_transform(): pl.pallas_call(functools.partial(local_kernel, scale), out_shape=jax.Shap...  4.38 us
    all_to_all x1, starting transfers between devices, on_device(): lax.all_to_all(chosen.reshape(devices, most, width), AXES, 0, 0, tiled=True)  4.11 us
    all_to_all x1, starting transfers between devices, on_device(): mixed = lax.all_to_all(slices, TURNED, 0, 0, tiled=True)  4.02 us
  transfers between devices with their start and end apart: 9, of which 7 were waited for; matrix products, arithmetic and copies ran while one was open for 2% of the time, Pallas kernels for 4%

profile of v21, /device:TPU:0, one launch (start us, length us, event | category | flops | bytes accessed | tf_op | source)
XLA Modules:
  0.0 131.8 jit_solution(13975159123968098271)
XLA Ops:
  0.6 4.4 %shard_map.58 = f32[16,256,128]{2,1,0:T(8,128)} custom-call(s32[32,128]{1,0:T(8,128)} %bitcast.15, f32[16,256,128]{2,1,0:T(8,128)} %bitcast.14), custom_call_target="tpu_custom_call" | custom-call | tf_op jit(solution)/shard_map/pallas_call | solution.py:82
  5.0 0.0 copy-start
  5.0 7.3 %all-to-all-start = ((f32[32,128,128]{2,1,0:T(8,128)}), f32[32,128,128]{2,1,0:T(8,128)S(1)}, u32[]{:S(2)}, u32[]{:S(2)}) async-start(f32[32,128,128]{2,1,0:T(8,128)} %bitcast.13), calls=%async_computation | async-start | bytes 4194304 | tf_op jit(solution)/shard_map/all_to_all | solution.py:299
  12.4 0.3 shard_map.59
  12.7 0.1 reshape.44
  12.7 0.7 shard_map.60.counts_ref
  13.4 0.1 and_select_fusion
  13.5 0.2 convert_reduce_fusion
  13.7 0.1 multiply_add_fusion
  13.8 47.4 %all-to-all-done.in_ref = f32[32,128,128]{2,1,0:T(8,128)S(1)} async-done(((f32[32,128,128]{2,1,0:T(8,128)}), f32[32,128,128]{2,1,0:T(8,128)S(1)}, u32[]{:S(2)}, u32[]{:S(2)}) %all-to-all-start) | async-done | bytes 2097184 | tf_op jit(solution)/shard_map/all_to_all | solution.py:299
  61.2 1.5 %shard_map.61.held_ref = f32[32,128,128]{2,1,0:T(8,128)} custom-call(f32[32,128,128]{2,1,0:T(8,128)S(1)} %all-to-all-done.in_ref), custom_call_target="tpu_custom_call" | custom-call | tf_op jit(solution)/shard_map/pallas_call | solution.py:130
  62.8 4.0 %all-to-all-start.1 = ((f32[32,128,128]{2,1,0:T(8,128)}), f32[32,128,128]{2,1,0:T(8,128)S(1)}, u32[]{:S(2)}, u32[]{:S(2)}) async-start(f32[32,128,128]{2,1,0:T(8,128)} %shard_map.61.held_ref), calls=%async_computation.1 | async-start | bytes 4194304 | tf_op jit(solution)/shard_map/all_to_all | solution.py:302
  66.8 3.1 %shard_map.62 = f32[128,128]{1,0:T(8,128)S(1)} custom-call(f32[128,32]{1,0:T(8,128)S(1)} %shard_map.60.counts_ref, f32[32,128,128]{2,1,0:T(8,128)} %shard_map.61.held_ref), custom_call_target="tpu_custom_call" | custom-call | tf_op jit(solution)/shard_map/pallas_call | solution.py:249
  69.9 0.3 collective-permute-start
  70.2 1.0 collective-permute-done
  71.2 1.8 %collective-permute-start.1 = (f32[64,128]{1,0:T(8,128)S(1)}, f32[64,128]{1,0:T(8,128)S(1)}, u32[]{:S(2)}, u32[]{:S(2)}) collective-permute-start(f32[64,128]{1,0:T(8,128)S(1)} %dynamic-slice_add_fusion), channel_id=1, source_target_pairs={{0,16},{8,24},{16,0},{24,8},{1,17},{9,25},{17,1},{25,9},{2,18},{10... | collective-permute-start | bytes 98312 | tf_op jit(solution)/shard_map/ppermute | solution.py:260
  72.9 10.0 %collective-permute-done.1 = f32[64,128]{1,0:T(8,128)S(1)} collective-permute-done((f32[64,128]{1,0:T(8,128)S(1)}, f32[64,128]{1,0:T(8,128)S(1)}, u32[]{:S(2)}, u32[]{:S(2)}) %collective-permute-start.1) | collective-permute-done | bytes 32800 | tf_op jit(solution)/shard_map/ppermute | solution.py:260
  82.9 0.3 collective-permute-start.2
  83.2 3.9 %collective-permute-done.2 = f32[64,128]{1,0:T(8,128)S(1)} collective-permute-done((f32[64,128]{1,0:T(8,128)S(1)}, f32[64,128]{1,0:T(8,128)S(1)}, u32[]{:S(2)}, u32[]{:S(2)}) %collective-permute-start.2) | collective-permute-done | bytes 32800 | tf_op jit(solution)/shard_map/ppermute | solution.py:260
  87.1 0.0 collective-permute-start.3
  87.2 15.4 %collective-permute-done.3 = f32[64,128]{1,0:T(8,128)S(1)} collective-permute-done((f32[64,128]{1,0:T(8,128)S(1)}, f32[64,128]{1,0:T(8,128)S(1)}, u32[]{:S(2)}, u32[]{:S(2)}) %collective-permute-start.3) | collective-permute-done | bytes 32800 | tf_op jit(solution)/shard_map/ppermute | solution.py:260
  102.6 4.1 %collective-permute-start.4 = (f32[64,128]{1,0:T(8,128)S(1)}, f32[64,128]{1,0:T(8,128)S(1)}, u32[]{:S(2)}, u32[]{:S(2)}) collective-permute-start(f32[64,128]{1,0:T(8,128)S(1)} %add.48), channel_id=1, source_target_pairs={{0,4},{1,5},{2,6},{3,7},{4,0},{5,1},{6,2},{7,3},{8,12},{9,13},{10,... | collective-permute-start | bytes 98312 | tf_op jit(solution)/shard_map/ppermute | solution.py:260
  106.7 10.4 %collective-permute-done.4 = f32[64,128]{1,0:T(8,128)S(1)} collective-permute-done((f32[64,128]{1,0:T(8,128)S(1)}, f32[64,128]{1,0:T(8,128)S(1)}, u32[]{:S(2)}, u32[]{:S(2)}) %collective-permute-start.4) | collective-permute-done | bytes 32800 | tf_op jit(solution)/shard_map/ppermute | solution.py:260
  117.1 0.0 all-to-all-done.1
  117.1 0.1 collective-permute-start.5
  117.2 1.3 %gather_fusion = f32[256,128]{1,0:T(8,128)} fusion(f32[4096,128]{1,0:T(8,128)S(1)} %bitcast.9, s32[1024]{0:T(1024)S(1)} %pad_clamp_fusion.1), kind=kCustom, calls=%fused_computation | custom fusion | bytes 263168 | tf_op jit(solution)/shard_map/jit(_take)/gather | solution.py:311
  118.6 4.1 %all-to-all-start.2 = ((f32[32,8,128]{2,1,0:T(8,128)}), f32[32,8,128]{2,1,0:T(8,128)S(1)}, u32[]{:S(2)}, u32[]{:S(2)}) async-start(f32[32,8,128]{2,1,0:T(8,128)} %bitcast.7), calls=%async_computation.2 | async-start | bytes 262144 | tf_op jit(solution)/shard_map/all_to_all | solution.py:312
  122.7 0.0 collective-permute-done.5
  122.7 1.3 %shard_map.63 = f32[4096,128]{1,0:T(8,128)} custom-call(f32[4096,128]{1,0:T(8,128)S(1)} %bitcast.10), custom_call_target="tpu_custom_call" | custom-call | tf_op jit(solution)/shard_map/pallas_call | solution.py:150
  124.0 0.6 broadcast_multiply_fusion
  124.7 5.7 %all-to-all-done.2 = f32[32,8,128]{2,1,0:T(8,128)S(1)} async-done(((f32[32,8,128]{2,1,0:T(8,128)}), f32[32,8,128]{2,1,0:T(8,128)S(1)}, u32[]{:S(2)}, u32[]{:S(2)}) %all-to-all-start.2) | async-done | bytes 131104 | tf_op jit(solution)/shard_map/all_to_all | solution.py:312
  130.4 1.3 %gather_fusion.1 = f32[256,128]{1,0:T(8,128)} fusion(f32[256,128]{1,0:T(8,128)S(1)} %bitcast.12, s32[1024]{0:T(1024)S(1)} %pad_clamp_fusion), kind=kCustom, calls=%fused_computation.1 | custom fusion | bytes 263168 | tf_op jit(solution)/shard_map/jit(_take)/gather | solution.py:318
  (13 shorter events, 0.1 us)
Async XLA Ops:
  5.0 7.3 %copy-start = (s32[8192]{0:T(1024)S(1)}, s32[8192]{0:T(1024)}, u32[]{:S(2)}) copy-start(s32[8192]{0:T(1024)} %param.5) | copy-start | bytes 98308
  5.0 56.2 %all-to-all-start = ((f32[32,128,128]{2,1,0:T(8,128)}), f32[32,128,128]{2,1,0:T(8,128)S(1)}, u32[]{:S(2)}, u32[]{:S(2)}) async-start(f32[32,128,128]{2,1,0:T(8,128)} %bitcast.13), calls=%async_computation | async-start | bytes 4194304 | tf_op jit(solution)/shard_map/all_to_all | solution.py:299
  62.8 54.3 %all-to-all-start.1 = ((f32[32,128,128]{2,1,0:T(8,128)}), f32[32,128,128]{2,1,0:T(8,128)S(1)}, u32[]{:S(2)}, u32[]{:S(2)}) async-start(f32[32,128,128]{2,1,0:T(8,128)} %shard_map.61.held_ref), calls=%async_computation.1 | async-start | bytes 4194304 | tf_op jit(solution)/shard_map/all_to_all | solution.py:302
  69.9 1.3 collective-permute-start
  71.2 11.8 %collective-permute-start.1 = (f32[64,128]{1,0:T(8,128)S(1)}, f32[64,128]{1,0:T(8,128)S(1)}, u32[]{:S(2)}, u32[]{:S(2)}) collective-permute-start(f32[64,128]{1,0:T(8,128)S(1)} %dynamic-slice_add_fusion), channel_id=1, source_target_pairs={{0,16},{8,24},{16,0},{24,8},{1,17},{9,25},{17,1},{25,9},{2,18},{10... | collective-permute-start | bytes 98312 | tf_op jit(solution)/shard_map/ppermute | solution.py:260
  82.9 4.2 %collective-permute-start.2 = (f32[64,128]{1,0:T(8,128)S(1)}, f32[64,128]{1,0:T(8,128)S(1)}, u32[]{:S(2)}, u32[]{:S(2)}) collective-permute-start(f32[64,128]{1,0:T(8,128)S(1)} %add.46), channel_id=1, source_target_pairs={{0,1},{1,0},{2,3},{3,2},{4,5},{5,4},{6,7},{7,6},{8,9},{9,8},{10,11... | collective-permute-start | bytes 98312 | tf_op jit(solution)/shard_map/ppermute | solution.py:260
  87.1 15.4 %collective-permute-start.3 = (f32[64,128]{1,0:T(8,128)S(1)}, f32[64,128]{1,0:T(8,128)S(1)}, u32[]{:S(2)}, u32[]{:S(2)}) collective-permute-start(f32[64,128]{1,0:T(8,128)S(1)} %add.47), channel_id=1, source_target_pairs={{0,2},{1,3},{2,0},{3,1},{4,6},{5,7},{6,4},{7,5},{8,10},{9,11},{10,... | collective-permute-start | bytes 98312 | tf_op jit(solution)/shard_map/ppermute | solution.py:260
  102.6 14.5 %collective-permute-start.4 = (f32[64,128]{1,0:T(8,128)S(1)}, f32[64,128]{1,0:T(8,128)S(1)}, u32[]{:S(2)}, u32[]{:S(2)}) collective-permute-start(f32[64,128]{1,0:T(8,128)S(1)} %add.48), channel_id=1, source_target_pairs={{0,4},{1,5},{2,6},{3,7},{4,0},{5,1},{6,2},{7,3},{8,12},{9,13},{10,... | collective-permute-start | bytes 98312 | tf_op jit(solution)/shard_map/ppermute | solution.py:260
  117.1 5.6 %collective-permute-start.5 = (f32[128,128]{1,0:T(8,128)S(1)}, f32[128,128]{1,0:T(8,128)S(1)}, u32[]{:S(2)}, u32[]{:S(2)}) collective-permute-start(f32[128,128]{1,0:T(8,128)S(1)} %constant_dynamic-update-slice_fusion), channel_id=1, source_target_pairs={{0,8},{8,0},{16,24},{24,16},{1,9},{9,1},{17,25},{25,17},{2,10},{10... | collective-permute-start | bytes 196616 | tf_op jit(solution)/shard_map/ppermute | solution.py:260
  118.6 11.9 %all-to-all-start.2 = ((f32[32,8,128]{2,1,0:T(8,128)}), f32[32,8,128]{2,1,0:T(8,128)S(1)}, u32[]{:S(2)}, u32[]{:S(2)}) async-start(f32[32,8,128]{2,1,0:T(8,128)} %bitcast.7), calls=%async_computation.2 | async-start | bytes 262144 | tf_op jit(solution)/shard_map/all_to_all | solution.py:312

commit v22 on v21

--- a/solution.py
+++ b/solution.py
@@ -24,9 +24,9 @@
 def local_kernel(scale, flips_ref, panel_ref, out_ref, flags, held, arrived, sent):
     blocks, _, width = panel_ref.shape
     per = BLOCK // flips_ref.shape[1]
-    share = blocks // 4
-    loads = [pltpu.make_async_copy(flips_ref, flags, arrived.at[4])]
-    for part in range(4):
+    share = blocks // 8
+    loads = [pltpu.make_async_copy(flips_ref, flags, arrived.at[8])]
+    for part in range(8):
         span = pl.ds(part * share, share)
         loads.append(pltpu.make_async_copy(panel_ref.at[span], held.at[span], arrived.at[part]))
     for load in loads:
@@ -47,7 +47,7 @@
         out = jnp.dot(mixer, parts, preferred_element_type=jnp.float32)
         held[b] = out[:, :width] + out[:, width : 2 * width] + out[:, 2 * width :]
     strip = 16
-    quarter = BLOCK // 4
+    piece = BLOCK // 8
 
     def body(step, carry):
         at = pl.multiple_of(step * strip, strip)
@@ -64,10 +64,10 @@
         return carry
 
     copies = []
-    for part in range(4):
-        first = part * quarter // strip
-        lax.fori_loop(first, first + quarter // strip, body, 0)
-        span = pl.ds(part * quarter, quarter)
+    for part in range(8):
+        first = part * piece // strip
+        lax.fori_loop(first, first + piece // strip, body, 0)
+        span = pl.ds(part * piece, piece)
         copies.append(
             pltpu.make_async_copy(held.at[:, span, :], out_ref.at[:, span, :], sent.at[part])
         )
@@ -87,8 +87,8 @@
         scratch_shapes=[
             pltpu.VMEM((rows // 128, 128), jnp.int32),
             pltpu.VMEM(shape, jnp.float32),
-            pltpu.SemaphoreType.DMA((5,)),
-            pltpu.SemaphoreType.DMA((4,)),
+            pltpu.SemaphoreType.DMA((9,)),
+            pltpu.SemaphoreType.DMA((8,)),
         ],
         compiler_params=pltpu.CompilerParams(vmem_limit_bytes=61 * 2**20),
     )(flips.reshape(rows // 128, 128), panel.reshape(shape))
@@ -97,7 +97,8 @@
 def device_kernel(in_ref, out_ref, held, sent):
     devices, rows, _ = in_ref.shape
     strip = 8
-    quarter = rows // 4
+    parts = sent.shape[0]
+    share = rows // parts
 
     def body(step, carry):
         at = pl.multiple_of(step * strip, strip)
@@ -114,10 +115,10 @@
         return carry
 
     copies = []
-    for part in range(4):
-        first = part * quarter // strip
-        lax.fori_loop(first, first + quarter // strip, body, 0)
-        span = pl.ds(part * quarter, quarter)
+    for part in range(parts):
+        first = part * share // strip
+        lax.fori_loop(first, first + share // strip, body, 0)
+        span = pl.ds(part * share, share)
         copies.append(
             pltpu.make_async_copy(held.at[:, span, :], out_ref.at[:, span, :], sent.at[part])
         )
@@ -134,7 +135,7 @@
         out_specs=pl.BlockSpec(memory_space=pl.ANY),
         scratch_shapes=[
             pltpu.VMEM(value.shape, jnp.float32),
-            pltpu.SemaphoreType.DMA((4,)),
+            pltpu.SemaphoreType.DMA((min(8, value.shape[1] // 8),)),
         ],
         compiler_params=pltpu.CompilerParams(vmem_limit_bytes=32 * 2**20),
     )(value)
@@ -295,9 +296,11 @@
     local = local.reshape(devices, rows_here // devices, width)
     wanted = send_rows(picks, [me], rows_here, devices, most)
     spots = landing(lax.dynamic_slice(picks, (me * per,), (per,)), rows_here, most)
+    slots = jnp.arange(devices * most, dtype=jnp.int32)
+    order = (spots[:, None] == slots[None, :]).astype(jnp.float32)
     counts = count_picks(picks, lax.axis_index(TURNED), rows_here, devices)
     slices = lax.all_to_all(local, TURNED, 0, 0, tiled=True)
-    slices, wanted, spots, counts = lax.optimization_barrier((slices, wanted, spots, counts))
+    slices, wanted, order, counts = lax.optimization_barrier((slices, wanted, order, counts))
     slices = device_sums(slices)
     mixed = lax.all_to_all(slices, TURNED, 0, 0, tiled=True)
     gram = gram_part(counts, slices)
@@ -315,7 +318,8 @@
     mixed = store(mixed)
     gram = (gram + other) / float(picks.shape[0])
     landed, mixed, gram = lax.optimization_barrier((landed, mixed, gram))
-    sketch = jnp.take(landed.reshape(devices * most, width), spots, axis=0, mode="clip")
+    landed = landed.reshape(devices * most, width)
+    sketch = jnp.dot(order, landed, precision=lax.Precision.HIGHEST)
     return (mixed, sketch, gram)
 
 

time: 132 us -> 132 us (level)
  local copies, waits for them, and re-layouts: 2.82 us -> 1.48 us
    gather x1 -> x0, local copies, waits for them, and re-layouts: 1.34 us -> none  [on_device(): jnp.take(landed.reshape(devices * most, width), spots, axis=0, mode='clip')]
where the time goes in v22:
time: 132 us
  waiting for transfers between devices  93.7 us (71%)
  starting transfers between devices  22 us (17%)
  Pallas kernels  11.8 us (9%)
  local copies, waits for them, and re-layouts  1.48 us (1%)
    all_to_all x1, waiting for transfers between devices, on_device(): slices = lax.all_to_all(local, TURNED, 0, 0, tiled=True)  47.3 us
    ppermute x6, waiting for transfers between devices, swap(): return lax.ppermute(value, axis, pairs)  40.7 us
    all_to_all x1, starting transfers between devices, on_device(): slices = lax.all_to_all(local, TURNED, 0, 0, tiled=True)  7.3 us
    ppermute x6, starting transfers between devices, swap(): return lax.ppermute(value, axis, pairs)  6.59 us
    all_to_all x1, waiting for transfers between devices, on_device(): lax.all_to_all(chosen.reshape(devices, most, width), AXES, 0, 0, tiled=True)  5.73 us
    pallas_call x1, Pallas kernels, local_transform(): pl.pallas_call(functools.partial(local_kernel, scale), out_shape=jax.Shap...  4.97 us
    all_to_all x1, starting transfers between devices, on_device(): lax.all_to_all(chosen.reshape(devices, most, width), AXES, 0, 0, tiled=True)  4.11 us
    all_to_all x1, starting transfers between devices, on_device(): mixed = lax.all_to_all(slices, TURNED, 0, 0, tiled=True)  4.02 us
  transfers between devices with their start and end apart: 9, of which 7 were waited for; matrix products, arithmetic and copies ran while one was open for 2% of the time, Pallas kernels for 4%

profile of v22, /device:TPU:0, one launch (start us, length us, event | category | flops | bytes accessed | tf_op | source)
XLA Modules:
  0.0 132.0 jit_solution(1718727400048286504)
XLA Ops:
  0.6 5.0 %shard_map.58 = f32[16,256,128]{2,1,0:T(8,128)} custom-call(s32[32,128]{1,0:T(8,128)} %bitcast.17, f32[16,256,128]{2,1,0:T(8,128)} %bitcast.16), custom_call_target="tpu_custom_call" | custom-call | tf_op jit(solution)/shard_map/pallas_call | solution.py:82
  5.6 0.0 copy-start
  5.6 7.3 %all-to-all-start = ((f32[32,128,128]{2,1,0:T(8,128)}), f32[32,128,128]{2,1,0:T(8,128)S(1)}, u32[]{:S(2)}, u32[]{:S(2)}) async-start(f32[32,128,128]{2,1,0:T(8,128)} %bitcast.15), calls=%async_computation | async-start | bytes 4194304 | tf_op jit(solution)/shard_map/all_to_all | solution.py:302
  13.0 0.3 shard_map.59
  13.2 0.1 reshape.45
  13.3 0.7 shard_map.60.counts_ref
  14.0 0.1 and_select_fusion
  14.1 0.2 convert_reduce_fusion
  14.3 0.1 multiply_add_fusion
  14.4 0.1 fusion.1
  14.5 47.3 %all-to-all-done.in_ref = f32[32,128,128]{2,1,0:T(8,128)S(1)} async-done(((f32[32,128,128]{2,1,0:T(8,128)}), f32[32,128,128]{2,1,0:T(8,128)S(1)}, u32[]{:S(2)}, u32[]{:S(2)}) %all-to-all-start) | async-done | bytes 2097184 | tf_op jit(solution)/shard_map/all_to_all | solution.py:302
  61.8 1.5 %shard_map.61.held_ref = f32[32,128,128]{2,1,0:T(8,128)} custom-call(f32[32,128,128]{2,1,0:T(8,128)S(1)} %all-to-all-done.in_ref), custom_call_target="tpu_custom_call" | custom-call | tf_op jit(solution)/shard_map/pallas_call | solution.py:131
  63.3 4.0 %all-to-all-start.1 = ((f32[32,128,128]{2,1,0:T(8,128)}), f32[32,128,128]{2,1,0:T(8,128)S(1)}, u32[]{:S(2)}, u32[]{:S(2)}) async-start(f32[32,128,128]{2,1,0:T(8,128)} %shard_map.61.held_ref), calls=%async_computation.1 | async-start | bytes 4194304 | tf_op jit(solution)/shard_map/all_to_all | solution.py:305
  67.3 3.1 %shard_map.62 = f32[128,128]{1,0:T(8,128)S(1)} custom-call(f32[128,32]{1,0:T(8,128)S(1)} %shard_map.60.counts_ref, f32[32,128,128]{2,1,0:T(8,128)} %shard_map.61.held_ref), custom_call_target="tpu_custom_call" | custom-call | tf_op jit(solution)/shard_map/pallas_call | solution.py:250
  70.4 0.3 collective-permute-start
  70.7 1.0 collective-permute-done
  71.7 1.8 %collective-permute-start.1 = (f32[64,128]{1,0:T(8,128)S(1)}, f32[64,128]{1,0:T(8,128)S(1)}, u32[]{:S(2)}, u32[]{:S(2)}) collective-permute-start(f32[64,128]{1,0:T(8,128)S(1)} %dynamic-slice_add_fusion), channel_id=1, source_target_pairs={{0,16},{8,24},{16,0},{24,8},{1,17},{9,25},{17,1},{25,9},{2,18},{10... | collective-permute-start | bytes 98312 | tf_op jit(solution)/shard_map/ppermute | solution.py:261
  73.5 10.0 %collective-permute-done.1 = f32[64,128]{1,0:T(8,128)S(1)} collective-permute-done((f32[64,128]{1,0:T(8,128)S(1)}, f32[64,128]{1,0:T(8,128)S(1)}, u32[]{:S(2)}, u32[]{:S(2)}) %collective-permute-start.1) | collective-permute-done | bytes 32800 | tf_op jit(solution)/shard_map/ppermute | solution.py:261
  83.5 0.3 collective-permute-start.2
  83.8 3.9 %collective-permute-done.2 = f32[64,128]{1,0:T(8,128)S(1)} collective-permute-done((f32[64,128]{1,0:T(8,128)S(1)}, f32[64,128]{1,0:T(8,128)S(1)}, u32[]{:S(2)}, u32[]{:S(2)}) %collective-permute-start.2) | collective-permute-done | bytes 32800 | tf_op jit(solution)/shard_map/ppermute | solution.py:261
  87.7 15.4 %collective-permute-done.3 = f32[64,128]{1,0:T(8,128)S(1)} collective-permute-done((f32[64,128]{1,0:T(8,128)S(1)}, f32[64,128]{1,0:T(8,128)S(1)}, u32[]{:S(2)}, u32[]{:S(2)}) %collective-permute-start.3) | collective-permute-done | bytes 32800 | tf_op jit(solution)/shard_map/ppermute | solution.py:261
  103.1 4.1 %collective-permute-start.4 = (f32[64,128]{1,0:T(8,128)S(1)}, f32[64,128]{1,0:T(8,128)S(1)}, u32[]{:S(2)}, u32[]{:S(2)}) collective-permute-start(f32[64,128]{1,0:T(8,128)S(1)} %add.48), channel_id=1, source_target_pairs={{0,4},{1,5},{2,6},{3,7},{4,0},{5,1},{6,2},{7,3},{8,12},{9,13},{10,... | collective-permute-start | bytes 98312 | tf_op jit(solution)/shard_map/ppermute | solution.py:261
  107.2 10.4 %collective-permute-done.4 = f32[64,128]{1,0:T(8,128)S(1)} collective-permute-done((f32[64,128]{1,0:T(8,128)S(1)}, f32[64,128]{1,0:T(8,128)S(1)}, u32[]{:S(2)}, u32[]{:S(2)}) %collective-permute-start.4) | collective-permute-done | bytes 32800 | tf_op jit(solution)/shard_map/ppermute | solution.py:261
  117.6 0.0 all-to-all-done.1
  117.7 0.1 collective-permute-start.5
  117.7 1.3 %gather_fusion = f32[256,128]{1,0:T(8,128)} fusion(f32[4096,128]{1,0:T(8,128)S(1)} %bitcast.12, s32[1024]{0:T(1024)S(1)} %pad_clamp_fusion), kind=kCustom, calls=%fused_computation | custom fusion | bytes 263168 | tf_op jit(solution)/shard_map/jit(_take)/gather | solution.py:314
  119.1 4.1 %all-to-all-start.2 = ((f32[32,8,128]{2,1,0:T(8,128)}), f32[32,8,128]{2,1,0:T(8,128)S(1)}, u32[]{:S(2)}, u32[]{:S(2)}) async-start(f32[32,8,128]{2,1,0:T(8,128)} %bitcast.7), calls=%async_computation.2 | async-start | bytes 262144 | tf_op jit(solution)/shard_map/all_to_all | solution.py:315
  123.2 0.0 collective-permute-done.5
  123.2 1.3 %shard_map.63 = f32[4096,128]{1,0:T(8,128)} custom-call(f32[4096,128]{1,0:T(8,128)S(1)} %bitcast.13), custom_call_target="tpu_custom_call" | custom-call | tf_op jit(solution)/shard_map/pallas_call | solution.py:151
  124.6 0.6 broadcast_multiply_fusion
  125.2 5.7 %all-to-all-done.2 = f32[32,8,128]{2,1,0:T(8,128)S(1)} async-done(((f32[32,8,128]{2,1,0:T(8,128)}), f32[32,8,128]{2,1,0:T(8,128)S(1)}, u32[]{:S(2)}, u32[]{:S(2)}) %all-to-all-start.2) | async-done | bytes 131104 | tf_op jit(solution)/shard_map/all_to_all | solution.py:315
  130.9 1.0 fusion.2
  (13 shorter events, 0.1 us)
Async XLA Ops:
  5.6 7.3 %copy-start = (s32[8192]{0:T(1024)S(1)}, s32[8192]{0:T(1024)}, u32[]{:S(2)}) copy-start(s32[8192]{0:T(1024)} %param.5) | copy-start | bytes 98308
  5.6 56.2 %all-to-all-start = ((f32[32,128,128]{2,1,0:T(8,128)}), f32[32,128,128]{2,1,0:T(8,128)S(1)}, u32[]{:S(2)}, u32[]{:S(2)}) async-start(f32[32,128,128]{2,1,0:T(8,128)} %bitcast.15), calls=%async_computation | async-start | bytes 4194304 | tf_op jit(solution)/shard_map/all_to_all | solution.py:302
  63.3 54.3 %all-to-all-start.1 = ((f32[32,128,128]{2,1,0:T(8,128)}), f32[32,128,128]{2,1,0:T(8,128)S(1)}, u32[]{:S(2)}, u32[]{:S(2)}) async-start(f32[32,128,128]{2,1,0:T(8,128)} %shard_map.61.held_ref), calls=%async_computation.1 | async-start | bytes 4194304 | tf_op jit(solution)/shard_map/all_to_all | solution.py:305
  70.4 1.3 collective-permute-start
  71.7 11.8 %collective-permute-start.1 = (f32[64,128]{1,0:T(8,128)S(1)}, f32[64,128]{1,0:T(8,128)S(1)}, u32[]{:S(2)}, u32[]{:S(2)}) collective-permute-start(f32[64,128]{1,0:T(8,128)S(1)} %dynamic-slice_add_fusion), channel_id=1, source_target_pairs={{0,16},{8,24},{16,0},{24,8},{1,17},{9,25},{17,1},{25,9},{2,18},{10... | collective-permute-start | bytes 98312 | tf_op jit(solution)/shard_map/ppermute | solution.py:261
  83.5 4.2 %collective-permute-start.2 = (f32[64,128]{1,0:T(8,128)S(1)}, f32[64,128]{1,0:T(8,128)S(1)}, u32[]{:S(2)}, u32[]{:S(2)}) collective-permute-start(f32[64,128]{1,0:T(8,128)S(1)} %add.46), channel_id=1, source_target_pairs={{0,1},{1,0},{2,3},{3,2},{4,5},{5,4},{6,7},{7,6},{8,9},{9,8},{10,11... | collective-permute-start | bytes 98312 | tf_op jit(solution)/shard_map/ppermute | solution.py:261
  87.7 15.4 %collective-permute-start.3 = (f32[64,128]{1,0:T(8,128)S(1)}, f32[64,128]{1,0:T(8,128)S(1)}, u32[]{:S(2)}, u32[]{:S(2)}) collective-permute-start(f32[64,128]{1,0:T(8,128)S(1)} %add.47), channel_id=1, source_target_pairs={{0,2},{1,3},{2,0},{3,1},{4,6},{5,7},{6,4},{7,5},{8,10},{9,11},{10,... | collective-permute-start | bytes 98312 | tf_op jit(solution)/shard_map/ppermute | solution.py:261
  103.1 14.5 %collective-permute-start.4 = (f32[64,128]{1,0:T(8,128)S(1)}, f32[64,128]{1,0:T(8,128)S(1)}, u32[]{:S(2)}, u32[]{:S(2)}) collective-permute-start(f32[64,128]{1,0:T(8,128)S(1)} %add.48), channel_id=1, source_target_pairs={{0,4},{1,5},{2,6},{3,7},{4,0},{5,1},{6,2},{7,3},{8,12},{9,13},{10,... | collective-permute-start | bytes 98312 | tf_op jit(solution)/shard_map/ppermute | solution.py:261
  117.7 5.6 %collective-permute-start.5 = (f32[128,128]{1,0:T(8,128)S(1)}, f32[128,128]{1,0:T(8,128)S(1)}, u32[]{:S(2)}, u32[]{:S(2)}) collective-permute-start(f32[128,128]{1,0:T(8,128)S(1)} %constant_dynamic-update-slice_fusion), channel_id=1, source_target_pairs={{0,8},{8,0},{16,24},{24,16},{1,9},{9,1},{17,25},{25,17},{2,10},{10... | collective-permute-start | bytes 196616 | tf_op jit(solution)/shard_map/ppermute | solution.py:261
  119.1 11.9 %all-to-all-start.2 = ((f32[32,8,128]{2,1,0:T(8,128)}), f32[32,8,128]{2,1,0:T(8,128)S(1)}, u32[]{:S(2)}, u32[]{:S(2)}) async-start(f32[32,8,128]{2,1,0:T(8,128)} %bitcast.7), calls=%async_computation.2 | async-start | bytes 262144 | tf_op jit(solution)/shard_map/all_to_all | solution.py:315

commit v23 on v22

--- a/solution.py
+++ b/solution.py
@@ -21,12 +21,17 @@
     return (1 - 2 * parity).astype(jnp.float32)
 
 
+def halves(value):
+    high = value.astype(jnp.bfloat16)
+    return high, (value - high.astype(jnp.float32)).astype(jnp.bfloat16)
+
+
 def local_kernel(scale, flips_ref, panel_ref, out_ref, flags, held, arrived, sent):
     blocks, _, width = panel_ref.shape
     per = BLOCK // flips_ref.shape[1]
-    share = blocks // 8
-    loads = [pltpu.make_async_copy(flips_ref, flags, arrived.at[8])]
-    for part in range(8):
+    share = blocks // 4
+    loads = [pltpu.make_async_copy(flips_ref, flags, arrived.at[4])]
+    for part in range(4):
         span = pl.ds(part * share, share)
         loads.append(pltpu.make_async_copy(panel_ref.at[span], held.at[span], arrived.at[part]))
     for load in loads:
@@ -38,16 +43,11 @@
             loads[1 + b // share].wait()
         row = jnp.concatenate([flags[b * per + i : b * per + i + 1, :] for i in range(per)], axis=1)
         mixer = (base * (1 - 2 * row).astype(jnp.float32)).astype(jnp.bfloat16)
-        values = held[b]
-        high = values.astype(jnp.bfloat16)
-        rest = values - high.astype(jnp.float32)
-        middle = rest.astype(jnp.bfloat16)
-        low = (rest - middle.astype(jnp.float32)).astype(jnp.bfloat16)
-        parts = jnp.concatenate([high, middle, low], axis=1)
+        parts = jnp.concatenate(halves(held[b]), axis=1)
         out = jnp.dot(mixer, parts, preferred_element_type=jnp.float32)
-        held[b] = out[:, :width] + out[:, width : 2 * width] + out[:, 2 * width :]
+        held[b] = out[:, :width] + out[:, width:]
     strip = 16
-    piece = BLOCK // 8
+    piece = BLOCK // 4
 
     def body(step, carry):
         at = pl.multiple_of(step * strip, strip)
@@ -64,7 +64,7 @@
         return carry
 
     copies = []
-    for part in range(8):
+    for part in range(4):
         first = part * piece // strip
         lax.fori_loop(first, first + piece // strip, body, 0)
         span = pl.ds(part * piece, piece)
@@ -87,8 +87,8 @@
         scratch_shapes=[
             pltpu.VMEM((rows // 128, 128), jnp.int32),
             pltpu.VMEM(shape, jnp.float32),
-            pltpu.SemaphoreType.DMA((9,)),
-            pltpu.SemaphoreType.DMA((8,)),
+            pltpu.SemaphoreType.DMA((5,)),
+            pltpu.SemaphoreType.DMA((4,)),
         ],
         compiler_params=pltpu.CompilerParams(vmem_limit_bytes=61 * 2**20),
     )(flips.reshape(rows // 128, 128), panel.reshape(shape))
@@ -223,11 +223,6 @@
         out_specs=pl.BlockSpec(memory_space=pltpu.VMEM),
         compiler_params=pltpu.CompilerParams(vmem_limit_bytes=32 * 2**20),
     )(me.reshape(1).astype(jnp.int32), picks.reshape(1, -1))
-
-
-def halves(value):
-    high = value.astype(jnp.bfloat16)
-    return high, (value - high.astype(jnp.float32)).astype(jnp.bfloat16)
 
 
 def part_kernel(counts_ref, held_ref, out_ref):

time: 132 us -> 131 us (level)
  no operation moved by 1% of the time
where the time goes in v23:
time: 131 us
  waiting for transfers between devices  93.7 us (72%)
  starting transfers between devices  22 us (17%)
  Pallas kernels  10.6 us (8%)
  local copies, waits for them, and re-layouts  1.48 us (1%)
    all_to_all x1, waiting for transfers between devices, on_device(): slices = lax.all_to_all(local, TURNED, 0, 0, tiled=True)  47.3 us
    ppermute x6, waiting for transfers between devices, swap(): return lax.ppermute(value, axis, pairs)  40.7 us
    all_to_all x1, starting transfers between devices, on_device(): slices = lax.all_to_all(local, TURNED, 0, 0, tiled=True)  7.3 us
    ppermute x6, starting transfers between devices, swap(): return lax.ppermute(value, axis, pairs)  6.59 us
    all_to_all x1, waiting for transfers between devices, on_device(): lax.all_to_all(chosen.reshape(devices, most, width), AXES, 0, 0, tiled=True)  5.73 us
    all_to_all x1, starting transfers between devices, on_device(): lax.all_to_all(chosen.reshape(devices, most, width), AXES, 0, 0, tiled=True)  4.11 us
    all_to_all x1, starting transfers between devices, on_device(): mixed = lax.all_to_all(slices, TURNED, 0, 0, tiled=True)  4.02 us
    pallas_call x1, Pallas kernels, local_transform(): pl.pallas_call(functools.partial(local_kernel, scale), out_shape=jax.Shap...  3.81 us
  transfers between devices with their start and end apart: 9, of which 7 were waited for; matrix products, arithmetic and copies ran while one was open for 2% of the time, Pallas kernels for 4%

profile of v23, /device:TPU:0, one launch (start us, length us, event | category | flops | bytes accessed | tf_op | source)
XLA Modules:
  0.0 130.8 jit_solution(2393162112479926543)
XLA Ops:
  0.6 3.8 %shard_map.58 = f32[16,256,128]{2,1,0:T(8,128)} custom-call(s32[32,128]{1,0:T(8,128)} %bitcast.17, f32[16,256,128]{2,1,0:T(8,128)} %bitcast.16), custom_call_target="tpu_custom_call" | custom-call | tf_op jit(solution)/shard_map/pallas_call | solution.py:82
  4.5 0.0 copy-start
  4.5 7.3 %all-to-all-start = ((f32[32,128,128]{2,1,0:T(8,128)}), f32[32,128,128]{2,1,0:T(8,128)S(1)}, u32[]{:S(2)}, u32[]{:S(2)}) async-start(f32[32,128,128]{2,1,0:T(8,128)} %bitcast.15), calls=%async_computation | async-start | bytes 4194304 | tf_op jit(solution)/shard_map/all_to_all | solution.py:297
  11.8 0.3 shard_map.59
  12.1 0.1 reshape.45
  12.2 0.7 shard_map.60.counts_ref
  12.9 0.1 and_select_fusion
  12.9 0.2 convert_reduce_fusion
  13.1 0.1 multiply_add_fusion
  13.2 0.1 fusion.1
  13.3 47.3 %all-to-all-done.in_ref = f32[32,128,128]{2,1,0:T(8,128)S(1)} async-done(((f32[32,128,128]{2,1,0:T(8,128)}), f32[32,128,128]{2,1,0:T(8,128)S(1)}, u32[]{:S(2)}, u32[]{:S(2)}) %all-to-all-start) | async-done | bytes 2097184 | tf_op jit(solution)/shard_map/all_to_all | solution.py:297
  60.7 1.5 %shard_map.61.held_ref = f32[32,128,128]{2,1,0:T(8,128)} custom-call(f32[32,128,128]{2,1,0:T(8,128)S(1)} %all-to-all-done.in_ref), custom_call_target="tpu_custom_call" | custom-call | tf_op jit(solution)/shard_map/pallas_call | solution.py:131
  62.1 4.0 %all-to-all-start.1 = ((f32[32,128,128]{2,1,0:T(8,128)}), f32[32,128,128]{2,1,0:T(8,128)S(1)}, u32[]{:S(2)}, u32[]{:S(2)}) async-start(f32[32,128,128]{2,1,0:T(8,128)} %shard_map.61.held_ref), calls=%async_computation.1 | async-start | bytes 4194304 | tf_op jit(solution)/shard_map/all_to_all | solution.py:300
  66.2 3.1 %shard_map.62 = f32[128,128]{1,0:T(8,128)S(1)} custom-call(f32[128,32]{1,0:T(8,128)S(1)} %shard_map.60.counts_ref, f32[32,128,128]{2,1,0:T(8,128)} %shard_map.61.held_ref), custom_call_target="tpu_custom_call" | custom-call | tf_op jit(solution)/shard_map/pallas_call | solution.py:245
  69.2 0.3 collective-permute-start
  69.6 1.0 collective-permute-done
  70.5 1.8 %collective-permute-start.1 = (f32[64,128]{1,0:T(8,128)S(1)}, f32[64,128]{1,0:T(8,128)S(1)}, u32[]{:S(2)}, u32[]{:S(2)}) collective-permute-start(f32[64,128]{1,0:T(8,128)S(1)} %dynamic-slice_add_fusion), channel_id=1, source_target_pairs={{0,16},{8,24},{16,0},{24,8},{1,17},{9,25},{17,1},{25,9},{2,18},{10... | collective-permute-start | bytes 98312 | tf_op jit(solution)/shard_map/ppermute | solution.py:256
  72.3 10.0 %collective-permute-done.1 = f32[64,128]{1,0:T(8,128)S(1)} collective-permute-done((f32[64,128]{1,0:T(8,128)S(1)}, f32[64,128]{1,0:T(8,128)S(1)}, u32[]{:S(2)}, u32[]{:S(2)}) %collective-permute-start.1) | collective-permute-done | bytes 32800 | tf_op jit(solution)/shard_map/ppermute | solution.py:256
  82.3 0.3 collective-permute-start.2
  82.6 3.9 %collective-permute-done.2 = f32[64,128]{1,0:T(8,128)S(1)} collective-permute-done((f32[64,128]{1,0:T(8,128)S(1)}, f32[64,128]{1,0:T(8,128)S(1)}, u32[]{:S(2)}, u32[]{:S(2)}) %collective-permute-start.2) | collective-permute-done | bytes 32800 | tf_op jit(solution)/shard_map/ppermute | solution.py:256
  86.5 0.0 collective-permute-start.3
  86.5 15.4 %collective-permute-done.3 = f32[64,128]{1,0:T(8,128)S(1)} collective-permute-done((f32[64,128]{1,0:T(8,128)S(1)}, f32[64,128]{1,0:T(8,128)S(1)}, u32[]{:S(2)}, u32[]{:S(2)}) %collective-permute-start.3) | collective-permute-done | bytes 32800 | tf_op jit(solution)/shard_map/ppermute | solution.py:256
  102.0 4.1 %collective-permute-start.4 = (f32[64,128]{1,0:T(8,128)S(1)}, f32[64,128]{1,0:T(8,128)S(1)}, u32[]{:S(2)}, u32[]{:S(2)}) collective-permute-start(f32[64,128]{1,0:T(8,128)S(1)} %add.48), channel_id=1, source_target_pairs={{0,4},{1,5},{2,6},{3,7},{4,0},{5,1},{6,2},{7,3},{8,12},{9,13},{10,... | collective-permute-start | bytes 98312 | tf_op jit(solution)/shard_map/ppermute | solution.py:256
  106.1 10.4 %collective-permute-done.4 = f32[64,128]{1,0:T(8,128)S(1)} collective-permute-done((f32[64,128]{1,0:T(8,128)S(1)}, f32[64,128]{1,0:T(8,128)S(1)}, u32[]{:S(2)}, u32[]{:S(2)}) %collective-permute-start.4) | collective-permute-done | bytes 32800 | tf_op jit(solution)/shard_map/ppermute | solution.py:256
  116.5 0.0 all-to-all-done.1
  116.5 0.1 collective-permute-start.5
  116.6 1.3 %gather_fusion = f32[256,128]{1,0:T(8,128)} fusion(f32[4096,128]{1,0:T(8,128)S(1)} %bitcast.12, s32[1024]{0:T(1024)S(1)} %pad_clamp_fusion), kind=kCustom, calls=%fused_computation | custom fusion | bytes 263168 | tf_op jit(solution)/shard_map/jit(_take)/gather | solution.py:309
  117.9 4.1 %all-to-all-start.2 = ((f32[32,8,128]{2,1,0:T(8,128)}), f32[32,8,128]{2,1,0:T(8,128)S(1)}, u32[]{:S(2)}, u32[]{:S(2)}) async-start(f32[32,8,128]{2,1,0:T(8,128)} %bitcast.7), calls=%async_computation.2 | async-start | bytes 262144 | tf_op jit(solution)/shard_map/all_to_all | solution.py:310
  122.1 1.3 %shard_map.63 = f32[4096,128]{1,0:T(8,128)} custom-call(f32[4096,128]{1,0:T(8,128)S(1)} %bitcast.13), custom_call_target="tpu_custom_call" | custom-call | tf_op jit(solution)/shard_map/pallas_call | solution.py:151
  123.4 0.6 broadcast_multiply_fusion
  124.0 5.7 %all-to-all-done.2 = f32[32,8,128]{2,1,0:T(8,128)S(1)} async-done(((f32[32,8,128]{2,1,0:T(8,128)}), f32[32,8,128]{2,1,0:T(8,128)S(1)}, u32[]{:S(2)}, u32[]{:S(2)}) %all-to-all-start.2) | async-done | bytes 131104 | tf_op jit(solution)/shard_map/all_to_all | solution.py:310
  129.8 1.0 fusion.2
  (13 shorter events, 0.1 us)
Async XLA Ops:
  4.5 7.3 %copy-start = (s32[8192]{0:T(1024)S(1)}, s32[8192]{0:T(1024)}, u32[]{:S(2)}) copy-start(s32[8192]{0:T(1024)} %param.5) | copy-start | bytes 98308
  4.5 56.2 %all-to-all-start = ((f32[32,128,128]{2,1,0:T(8,128)}), f32[32,128,128]{2,1,0:T(8,128)S(1)}, u32[]{:S(2)}, u32[]{:S(2)}) async-start(f32[32,128,128]{2,1,0:T(8,128)} %bitcast.15), calls=%async_computation | async-start | bytes 4194304 | tf_op jit(solution)/shard_map/all_to_all | solution.py:297
  62.1 54.3 %all-to-all-start.1 = ((f32[32,128,128]{2,1,0:T(8,128)}), f32[32,128,128]{2,1,0:T(8,128)S(1)}, u32[]{:S(2)}, u32[]{:S(2)}) async-start(f32[32,128,128]{2,1,0:T(8,128)} %shard_map.61.held_ref), calls=%async_computation.1 | async-start | bytes 4194304 | tf_op jit(solution)/shard_map/all_to_all | solution.py:300
  69.2 1.3 collective-permute-start
  70.5 11.8 %collective-permute-start.1 = (f32[64,128]{1,0:T(8,128)S(1)}, f32[64,128]{1,0:T(8,128)S(1)}, u32[]{:S(2)}, u32[]{:S(2)}) collective-permute-start(f32[64,128]{1,0:T(8,128)S(1)} %dynamic-slice_add_fusion), channel_id=1, source_target_pairs={{0,16},{8,24},{16,0},{24,8},{1,17},{9,25},{17,1},{25,9},{2,18},{10... | collective-permute-start | bytes 98312 | tf_op jit(solution)/shard_map/ppermute | solution.py:256
  82.3 4.2 %collective-permute-start.2 = (f32[64,128]{1,0:T(8,128)S(1)}, f32[64,128]{1,0:T(8,128)S(1)}, u32[]{:S(2)}, u32[]{:S(2)}) collective-permute-start(f32[64,128]{1,0:T(8,128)S(1)} %add.46), channel_id=1, source_target_pairs={{0,1},{1,0},{2,3},{3,2},{4,5},{5,4},{6,7},{7,6},{8,9},{9,8},{10,11... | collective-permute-start | bytes 98312 | tf_op jit(solution)/shard_map/ppermute | solution.py:256
  86.5 15.4 %collective-permute-start.3 = (f32[64,128]{1,0:T(8,128)S(1)}, f32[64,128]{1,0:T(8,128)S(1)}, u32[]{:S(2)}, u32[]{:S(2)}) collective-permute-start(f32[64,128]{1,0:T(8,128)S(1)} %add.47), channel_id=1, source_target_pairs={{0,2},{1,3},{2,0},{3,1},{4,6},{5,7},{6,4},{7,5},{8,10},{9,11},{10,... | collective-permute-start | bytes 98312 | tf_op jit(solution)/shard_map/ppermute | solution.py:256
  102.0 14.5 %collective-permute-start.4 = (f32[64,128]{1,0:T(8,128)S(1)}, f32[64,128]{1,0:T(8,128)S(1)}, u32[]{:S(2)}, u32[]{:S(2)}) collective-permute-start(f32[64,128]{1,0:T(8,128)S(1)} %add.48), channel_id=1, source_target_pairs={{0,4},{1,5},{2,6},{3,7},{4,0},{5,1},{6,2},{7,3},{8,12},{9,13},{10,... | collective-permute-start | bytes 98312 | tf_op jit(solution)/shard_map/ppermute | solution.py:256
  116.5 5.6 %collective-permute-start.5 = (f32[128,128]{1,0:T(8,128)S(1)}, f32[128,128]{1,0:T(8,128)S(1)}, u32[]{:S(2)}, u32[]{:S(2)}) collective-permute-start(f32[128,128]{1,0:T(8,128)S(1)} %constant_dynamic-update-slice_fusion), channel_id=1, source_target_pairs={{0,8},{8,0},{16,24},{24,16},{1,9},{9,1},{17,25},{25,17},{2,10},{10... | collective-permute-start | bytes 196616 | tf_op jit(solution)/shard_map/ppermute | solution.py:256
  117.9 11.9 %all-to-all-start.2 = ((f32[32,8,128]{2,1,0:T(8,128)}), f32[32,8,128]{2,1,0:T(8,128)S(1)}, u32[]{:S(2)}, u32[]{:S(2)}) async-start(f32[32,8,128]{2,1,0:T(8,128)} %bitcast.7), calls=%async_computation.2 | async-start | bytes 262144 | tf_op jit(solution)/shard_map/all_to_all | solution.py:310

commit v24 on v23

--- a/solution.py
+++ b/solution.py
@@ -9,7 +9,6 @@
 
 BLOCK = 256
 AXES = ("narrow", "wide")
-TURNED = ("wide", "narrow")
 
 
 def signs(order):
@@ -192,11 +191,10 @@
     return rows.reshape(len(owners) * devices * most)
 
 
-def count_kernel(rows_here, wide, me_ref, picks_ref, out_ref):
+def count_kernel(rows_here, me_ref, picks_ref, out_ref):
     picks = picks_ref[...]
     rows, devices = out_ref.shape
     owner = picks >> rows_here.bit_length() - 1
-    owner = (owner & wide - 1) * (devices // wide) + (owner >> wide.bit_length() - 1)
     local = picks & rows_here - 1
     held = local >> rows.bit_length() - 1 == me_ref[0]
     place = jnp.where(held, local & rows - 1, -1)
@@ -214,7 +212,7 @@
 
 def count_picks(picks, me, rows_here, devices):
     return pl.pallas_call(
-        functools.partial(count_kernel, rows_here, lax.axis_size("wide")),
+        functools.partial(count_kernel, rows_here),
         out_shape=jax.ShapeDtypeStruct((rows_here // devices, devices), jnp.float32),
         in_specs=[
             pl.BlockSpec(memory_space=pltpu.SMEM),
@@ -293,11 +291,11 @@
     spots = landing(lax.dynamic_slice(picks, (me * per,), (per,)), rows_here, most)
     slots = jnp.arange(devices * most, dtype=jnp.int32)
     order = (spots[:, None] == slots[None, :]).astype(jnp.float32)
-    counts = count_picks(picks, lax.axis_index(TURNED), rows_here, devices)
-    slices = lax.all_to_all(local, TURNED, 0, 0, tiled=True)
+    counts = count_picks(picks, me, rows_here, devices)
+    slices = lax.all_to_all(local, AXES, 0, 0, tiled=True)
     slices, wanted, order, counts = lax.optimization_barrier((slices, wanted, order, counts))
     slices = device_sums(slices)
-    mixed = lax.all_to_all(slices, TURNED, 0, 0, tiled=True)
+    mixed = lax.all_to_all(slices, AXES, 0, 0, tiled=True)
     gram = gram_part(counts, slices)
     gram = scatter_sum(gram, "narrow")
     for axis, low in (("narrow", 2), ("wide", 1)):

time: 131 us -> 131 us (level)
    ppermute x6, waiting for transfers between devices: 40.7 us -> 38.5 us  [swap(): return lax.ppermute(value, axis, pairs)]
    ppermute x6, starting transfers between devices: 6.59 us -> 8.57 us  [swap(): return lax.ppermute(value, axis, pairs)]
    all_to_all x2, waiting for transfers between devices: 47.3 us -> 49.2 us  [the longest x1 48.5 us: on_device(): slices = lax.all_to_all(local, AXES, 0, 0, tiled=True)]
  transfers between devices with their start and end apart: 9 -> 9, of which waited for: 7 -> 8; matrix products, arithmetic and copies ran while one was open for 2% -> 2% of each run, Pallas kernels for 4% -> 4%
where the time goes in v24:
time: 131 us; the launch traced here: 130 us
  waiting for transfers between devices  93.4 us (71%)
  starting transfers between devices  21.7 us (17%)
  Pallas kernels  10.6 us (8%)
  local copies, waits for them, and re-layouts  1.47 us (1%)
    all_to_all x1, waiting for transfers between devices, on_device(): slices = lax.all_to_all(local, AXES, 0, 0, tiled=True)  48.5 us
    ppermute x6, waiting for transfers between devices, swap(): return lax.ppermute(value, axis, pairs)  38.5 us
    ppermute x6, starting transfers between devices, swap(): return lax.ppermute(value, axis, pairs)  8.57 us
    all_to_all x1, starting transfers between devices, on_device(): slices = lax.all_to_all(local, AXES, 0, 0, tiled=True)  7.3 us
    all_to_all x1, waiting for transfers between devices, on_device(): lax.all_to_all(chosen.reshape(devices, most, width), AXES, 0, 0, tiled=True)  5.73 us
    pallas_call x1, Pallas kernels, local_transform(): pl.pallas_call(functools.partial(local_kernel, scale), out_shape=jax.Shap...  3.81 us
    all_to_all x1, starting transfers between devices, on_device(): lax.all_to_all(chosen.reshape(devices, most, width), AXES, 0, 0, tiled=True)  3.11 us
    pallas_call x1, Pallas kernels, gram_part(): pl.pallas_call(part_kernel, out_shape=jax.ShapeDtypeStruct((width, width)...  3.05 us
  transfers between devices with their start and end apart: 9, of which 8 were waited for; matrix products, arithmetic and copies ran while one was open for 2% of the time, Pallas kernels for 4%

profile of v24, /device:TPU:0, one launch (start us, length us, event | category | flops | bytes accessed | tf_op | source)
XLA Modules:
  0.0 130.2 jit_solution(3648346432147603628)
XLA Ops:
  0.6 3.8 %shard_map.58 = f32[16,256,128]{2,1,0:T(8,128)} custom-call(s32[32,128]{1,0:T(8,128)} %bitcast.16, f32[16,256,128]{2,1,0:T(8,128)} %bitcast.15), custom_call_target="tpu_custom_call" | custom-call | tf_op jit(solution)/shard_map/pallas_call | solution.py:81
  4.5 0.0 copy-start
  4.5 7.3 %all-to-all-start = ((f32[32,128,128]{2,1,0:T(8,128)}), f32[32,128,128]{2,1,0:T(8,128)S(1)}, u32[]{:S(2)}, u32[]{:S(2)}) async-start(f32[32,128,128]{2,1,0:T(8,128)} %bitcast.14), calls=%async_computation | async-start | bytes 4194304 | tf_op jit(solution)/shard_map/all_to_all | solution.py:295
  11.8 0.3 shard_map.59
  12.1 0.1 reshape.41
  12.2 0.7 shard_map.60.counts_ref
  12.9 0.1 and_select_fusion
  12.9 0.2 convert_reduce_fusion
  13.1 0.1 multiply_add_fusion
  13.2 0.1 fusion.1
  13.3 48.5 %all-to-all-done.in_ref = f32[32,128,128]{2,1,0:T(8,128)S(1)} async-done(((f32[32,128,128]{2,1,0:T(8,128)}), f32[32,128,128]{2,1,0:T(8,128)S(1)}, u32[]{:S(2)}, u32[]{:S(2)}) %all-to-all-start) | async-done | bytes 2097184 | tf_op jit(solution)/shard_map/all_to_all | solution.py:295
  61.9 1.5 %shard_map.61.held_ref = f32[32,128,128]{2,1,0:T(8,128)} custom-call(f32[32,128,128]{2,1,0:T(8,128)S(1)} %all-to-all-done.in_ref), custom_call_target="tpu_custom_call" | custom-call | tf_op jit(solution)/shard_map/pallas_call | solution.py:130
  63.3 2.7 %all-to-all-start.1 = ((f32[32,128,128]{2,1,0:T(8,128)}), f32[32,128,128]{2,1,0:T(8,128)S(1)}, u32[]{:S(2)}, u32[]{:S(2)}) async-start(f32[32,128,128]{2,1,0:T(8,128)} %shard_map.61.held_ref), calls=%async_computation.1 | async-start | bytes 4194304 | tf_op jit(solution)/shard_map/all_to_all | solution.py:298
  66.1 3.0 %shard_map.62 = f32[128,128]{1,0:T(8,128)S(1)} custom-call(f32[128,32]{1,0:T(8,128)S(1)} %shard_map.60.counts_ref, f32[32,128,128]{2,1,0:T(8,128)} %shard_map.61.held_ref), custom_call_target="tpu_custom_call" | custom-call | tf_op jit(solution)/shard_map/pallas_call | solution.py:243
  69.2 0.2 collective-permute-start
  69.3 1.1 collective-permute-done
  70.4 1.6 %collective-permute-start.1 = (f32[64,128]{1,0:T(8,128)S(1)}, f32[64,128]{1,0:T(8,128)S(1)}, u32[]{:S(2)}, u32[]{:S(2)}) collective-permute-start(f32[64,128]{1,0:T(8,128)S(1)} %dynamic-slice_add_fusion), channel_id=1, source_target_pairs={{0,16},{8,24},{16,0},{24,8},{1,17},{9,25},{17,1},{25,9},{2,18},{10... | collective-permute-start | bytes 98312 | tf_op jit(solution)/shard_map/ppermute | solution.py:254
  72.1 8.0 %collective-permute-done.1 = f32[64,128]{1,0:T(8,128)S(1)} collective-permute-done((f32[64,128]{1,0:T(8,128)S(1)}, f32[64,128]{1,0:T(8,128)S(1)}, u32[]{:S(2)}, u32[]{:S(2)}) %collective-permute-start.1) | collective-permute-done | bytes 32800 | tf_op jit(solution)/shard_map/ppermute | solution.py:254
  80.1 1.9 %collective-permute-start.2 = (f32[64,128]{1,0:T(8,128)S(1)}, f32[64,128]{1,0:T(8,128)S(1)}, u32[]{:S(2)}, u32[]{:S(2)}) collective-permute-start(f32[64,128]{1,0:T(8,128)S(1)} %add.42), channel_id=1, source_target_pairs={{0,1},{1,0},{2,3},{3,2},{4,5},{5,4},{6,7},{7,6},{8,9},{9,8},{10,11... | collective-permute-start | bytes 98312 | tf_op jit(solution)/shard_map/ppermute | solution.py:254
  82.0 9.7 %collective-permute-done.2 = f32[64,128]{1,0:T(8,128)S(1)} collective-permute-done((f32[64,128]{1,0:T(8,128)S(1)}, f32[64,128]{1,0:T(8,128)S(1)}, u32[]{:S(2)}, u32[]{:S(2)}) %collective-permute-start.2) | collective-permute-done | bytes 32800 | tf_op jit(solution)/shard_map/ppermute | solution.py:254
  91.7 0.0 collective-permute-start.3
  91.7 9.6 %collective-permute-done.3 = f32[64,128]{1,0:T(8,128)S(1)} collective-permute-done((f32[64,128]{1,0:T(8,128)S(1)}, f32[64,128]{1,0:T(8,128)S(1)}, u32[]{:S(2)}, u32[]{:S(2)}) %collective-permute-start.3) | collective-permute-done | bytes 32800 | tf_op jit(solution)/shard_map/ppermute | solution.py:254
  101.3 4.7 %collective-permute-start.4 = (f32[64,128]{1,0:T(8,128)S(1)}, f32[64,128]{1,0:T(8,128)S(1)}, u32[]{:S(2)}, u32[]{:S(2)}) collective-permute-start(f32[64,128]{1,0:T(8,128)S(1)} %add.44), channel_id=1, source_target_pairs={{0,4},{1,5},{2,6},{3,7},{4,0},{5,1},{6,2},{7,3},{8,12},{9,13},{10,... | collective-permute-start | bytes 98312 | tf_op jit(solution)/shard_map/ppermute | solution.py:254
  106.0 10.2 %collective-permute-done.4 = f32[64,128]{1,0:T(8,128)S(1)} collective-permute-done((f32[64,128]{1,0:T(8,128)S(1)}, f32[64,128]{1,0:T(8,128)S(1)}, u32[]{:S(2)}, u32[]{:S(2)}) %collective-permute-start.4) | collective-permute-done | bytes 32800 | tf_op jit(solution)/shard_map/ppermute | solution.py:254
  116.2 0.7 all-to-all-done.1
  116.9 0.1 collective-permute-start.5
  117.0 1.3 %gather_fusion = f32[256,128]{1,0:T(8,128)} fusion(f32[4096,128]{1,0:T(8,128)S(1)} %bitcast.11, s32[1024]{0:T(1024)S(1)} %pad_clamp_fusion), kind=kCustom, calls=%fused_computation | custom fusion | bytes 263168 | tf_op jit(solution)/shard_map/jit(_take)/gather | solution.py:307
  118.3 3.1 %all-to-all-start.2 = ((f32[32,8,128]{2,1,0:T(8,128)}), f32[32,8,128]{2,1,0:T(8,128)S(1)}, u32[]{:S(2)}, u32[]{:S(2)}) async-start(f32[32,8,128]{2,1,0:T(8,128)} %bitcast.6), calls=%async_computation.2 | async-start | bytes 262144 | tf_op jit(solution)/shard_map/all_to_all | solution.py:308
  121.5 1.3 %shard_map.63 = f32[4096,128]{1,0:T(8,128)} custom-call(f32[4096,128]{1,0:T(8,128)S(1)} %bitcast.12), custom_call_target="tpu_custom_call" | custom-call | tf_op jit(solution)/shard_map/pallas_call | solution.py:150
  122.8 0.6 broadcast_multiply_fusion
  123.4 5.7 %all-to-all-done.2 = f32[32,8,128]{2,1,0:T(8,128)S(1)} async-done(((f32[32,8,128]{2,1,0:T(8,128)}), f32[32,8,128]{2,1,0:T(8,128)S(1)}, u32[]{:S(2)}, u32[]{:S(2)}) %all-to-all-start.2) | async-done | bytes 131104 | tf_op jit(solution)/shard_map/all_to_all | solution.py:308
  129.2 1.0 fusion.2
  (13 shorter events, 0.1 us)
Async XLA Ops:
  4.5 7.3 %copy-start = (s32[8192]{0:T(1024)S(1)}, s32[8192]{0:T(1024)}, u32[]{:S(2)}) copy-start(s32[8192]{0:T(1024)} %param.5) | copy-start | bytes 98308
  4.5 57.4 %all-to-all-start = ((f32[32,128,128]{2,1,0:T(8,128)}), f32[32,128,128]{2,1,0:T(8,128)S(1)}, u32[]{:S(2)}, u32[]{:S(2)}) async-start(f32[32,128,128]{2,1,0:T(8,128)} %bitcast.14), calls=%async_computation | async-start | bytes 4194304 | tf_op jit(solution)/shard_map/all_to_all | solution.py:295
  63.3 53.5 %all-to-all-start.1 = ((f32[32,128,128]{2,1,0:T(8,128)}), f32[32,128,128]{2,1,0:T(8,128)S(1)}, u32[]{:S(2)}, u32[]{:S(2)}) async-start(f32[32,128,128]{2,1,0:T(8,128)} %shard_map.61.held_ref), calls=%async_computation.1 | async-start | bytes 4194304 | tf_op jit(solution)/shard_map/all_to_all | solution.py:298
  69.2 1.3 collective-permute-start
  70.4 9.6 %collective-permute-start.1 = (f32[64,128]{1,0:T(8,128)S(1)}, f32[64,128]{1,0:T(8,128)S(1)}, u32[]{:S(2)}, u32[]{:S(2)}) collective-permute-start(f32[64,128]{1,0:T(8,128)S(1)} %dynamic-slice_add_fusion), channel_id=1, source_target_pairs={{0,16},{8,24},{16,0},{24,8},{1,17},{9,25},{17,1},{25,9},{2,18},{10... | collective-permute-start | bytes 98312 | tf_op jit(solution)/shard_map/ppermute | solution.py:254
  80.1 11.6 %collective-permute-start.2 = (f32[64,128]{1,0:T(8,128)S(1)}, f32[64,128]{1,0:T(8,128)S(1)}, u32[]{:S(2)}, u32[]{:S(2)}) collective-permute-start(f32[64,128]{1,0:T(8,128)S(1)} %add.42), channel_id=1, source_target_pairs={{0,1},{1,0},{2,3},{3,2},{4,5},{5,4},{6,7},{7,6},{8,9},{9,8},{10,11... | collective-permute-start | bytes 98312 | tf_op jit(solution)/shard_map/ppermute | solution.py:254
  91.7 9.6 %collective-permute-start.3 = (f32[64,128]{1,0:T(8,128)S(1)}, f32[64,128]{1,0:T(8,128)S(1)}, u32[]{:S(2)}, u32[]{:S(2)}) collective-permute-start(f32[64,128]{1,0:T(8,128)S(1)} %add.43), channel_id=1, source_target_pairs={{0,2},{1,3},{2,0},{3,1},{4,6},{5,7},{6,4},{7,5},{8,10},{9,11},{10,... | collective-permute-start | bytes 98312 | tf_op jit(solution)/shard_map/ppermute | solution.py:254
  101.3 14.9 %collective-permute-start.4 = (f32[64,128]{1,0:T(8,128)S(1)}, f32[64,128]{1,0:T(8,128)S(1)}, u32[]{:S(2)}, u32[]{:S(2)}) collective-permute-start(f32[64,128]{1,0:T(8,128)S(1)} %add.44), channel_id=1, source_target_pairs={{0,4},{1,5},{2,6},{3,7},{4,0},{5,1},{6,2},{7,3},{8,12},{9,13},{10,... | collective-permute-start | bytes 98312 | tf_op jit(solution)/shard_map/ppermute | solution.py:254
  116.9 4.6 %collective-permute-start.5 = (f32[128,128]{1,0:T(8,128)S(1)}, f32[128,128]{1,0:T(8,128)S(1)}, u32[]{:S(2)}, u32[]{:S(2)}) collective-permute-start(f32[128,128]{1,0:T(8,128)S(1)} %constant_dynamic-update-slice_fusion), channel_id=1, source_target_pairs={{0,8},{8,0},{16,24},{24,16},{1,9},{9,1},{17,25},{25,17},{2,10},{10... | collective-permute-start | bytes 196616 | tf_op jit(solution)/shard_map/ppermute | solution.py:254
  118.3 10.9 %all-to-all-start.2 = ((f32[32,8,128]{2,1,0:T(8,128)}), f32[32,8,128]{2,1,0:T(8,128)S(1)}, u32[]{:S(2)}, u32[]{:S(2)}) async-start(f32[32,8,128]{2,1,0:T(8,128)} %bitcast.6), calls=%async_computation.2 | async-start | bytes 262144 | tf_op jit(solution)/shard_map/all_to_all | solution.py:308

commit v25 on v24

--- a/solution.py
+++ b/solution.py
@@ -35,13 +35,13 @@
         loads.append(pltpu.make_async_copy(panel_ref.at[span], held.at[span], arrived.at[part]))
     for load in loads:
         load.start()
-    base = signs(BLOCK)
+    base = signs(BLOCK).astype(jnp.bfloat16)
     loads[0].wait()
     for b in range(blocks):
         if b % share == 0:
             loads[1 + b // share].wait()
         row = jnp.concatenate([flags[b * per + i : b * per + i + 1, :] for i in range(per)], axis=1)
-        mixer = (base * (1 - 2 * row).astype(jnp.float32)).astype(jnp.bfloat16)
+        mixer = base * (1 - 2 * row).astype(jnp.float32).astype(jnp.bfloat16)
         parts = jnp.concatenate(halves(held[b]), axis=1)
         out = jnp.dot(mixer, parts, preferred_element_type=jnp.float32)
         held[b] = out[:, :width] + out[:, width:]
@@ -270,6 +270,26 @@
     return value, swap(value, axis, 1)
 
 
+def order_kernel(order_ref, rows_ref, out_ref):
+    width = rows_ref.shape[1]
+    rows = rows_ref[...]
+    high = rows.astype(jnp.bfloat16)
+    middle, low = halves(rows - high.astype(jnp.float32))
+    parts = jnp.concatenate([high, middle, low], axis=1)
+    out = jnp.dot(order_ref[...], parts, preferred_element_type=jnp.float32)
+    out_ref[...] = out[:, :width] + (out[:, width : 2 * width] + out[:, 2 * width :])
+
+
+def put_in_order(order, rows):
+    return pl.pallas_call(
+        order_kernel,
+        out_shape=jax.ShapeDtypeStruct((order.shape[0], rows.shape[1]), jnp.float32),
+        in_specs=[pl.BlockSpec(memory_space=pltpu.VMEM)] * 2,
+        out_specs=pl.BlockSpec(memory_space=pltpu.VMEM),
+        compiler_params=pltpu.CompilerParams(vmem_limit_bytes=8 * 2**20),
+    )(order, rows)
+
+
 def landing(block, rows_here, most):
     owners = block // rows_here
     order = jnp.arange(block.shape[0], dtype=jnp.int32)
@@ -290,7 +310,7 @@
     wanted = send_rows(picks, [me], rows_here, devices, most)
     spots = landing(lax.dynamic_slice(picks, (me * per,), (per,)), rows_here, most)
     slots = jnp.arange(devices * most, dtype=jnp.int32)
-    order = (spots[:, None] == slots[None, :]).astype(jnp.float32)
+    order = (spots[:, None] == slots[None, :]).astype(jnp.bfloat16)
     counts = count_picks(picks, me, rows_here, devices)
     slices = lax.all_to_all(local, AXES, 0, 0, tiled=True)
     slices, wanted, order, counts = lax.optimization_barrier((slices, wanted, order, counts))
@@ -312,7 +332,7 @@
     gram = (gram + other) / float(picks.shape[0])
     landed, mixed, gram = lax.optimization_barrier((landed, mixed, gram))
     landed = landed.reshape(devices * most, width)
-    sketch = jnp.dot(order, landed, precision=lax.Precision.HIGHEST)
+    sketch = put_in_order(order, landed)
     return (mixed, sketch, gram)
 
 

time: 131 us -> 130 us (level)
  no operation moved by 1% of the time
where the time goes in v25:
time: 130 us
  waiting for transfers between devices  93.4 us (72%)
  starting transfers between devices  21.7 us (17%)
  Pallas kernels  11.5 us (9%)
  local copies, waits for them, and re-layouts  1.47 us (1%)
    all_to_all x1, waiting for transfers between devices, on_device(): slices = lax.all_to_all(local, AXES, 0, 0, tiled=True)  48.5 us
    ppermute x6, waiting for transfers between devices, swap(): return lax.ppermute(value, axis, pairs)  38.5 us
    ppermute x6, starting transfers between devices, swap(): return lax.ppermute(value, axis, pairs)  8.57 us
    all_to_all x1, starting transfers between devices, on_device(): slices = lax.all_to_all(local, AXES, 0, 0, tiled=True)  7.3 us
    all_to_all x1, waiting for transfers between devices, on_device(): lax.all_to_all(chosen.reshape(devices, most, width), AXES, 0, 0, tiled=True)  5.73 us
    pallas_call x1, Pallas kernels, local_transform(): pl.pallas_call(functools.partial(local_kernel, scale), out_shape=jax.Shap...  3.8 us
    all_to_all x1, starting transfers between devices, on_device(): lax.all_to_all(chosen.reshape(devices, most, width), AXES, 0, 0, tiled=True)  3.11 us
    pallas_call x1, Pallas kernels, gram_part(): pl.pallas_call(part_kernel, out_shape=jax.ShapeDtypeStruct((width, width)...  3.04 us
  transfers between devices with their start and end apart: 9, of which 8 were waited for; matrix products, arithmetic and copies ran while one was open for 2% of the time, Pallas kernels for 4%

profile of v25, /device:TPU:0, one launch (start us, length us, event | category | flops | bytes accessed | tf_op | source)
XLA Modules:
  0.0 130.1 jit_solution(9699071112125908137)
XLA Ops:
  0.6 3.8 %shard_map.58 = f32[16,256,128]{2,1,0:T(8,128)} custom-call(s32[32,128]{1,0:T(8,128)} %bitcast.14, f32[16,256,128]{2,1,0:T(8,128)} %bitcast.13), custom_call_target="tpu_custom_call" | custom-call | tf_op jit(solution)/shard_map/pallas_call | solution.py:81
  4.4 0.0 copy-start
  4.5 7.3 %all-to-all-start = ((f32[32,128,128]{2,1,0:T(8,128)}), f32[32,128,128]{2,1,0:T(8,128)S(1)}, u32[]{:S(2)}, u32[]{:S(2)}) async-start(f32[32,128,128]{2,1,0:T(8,128)} %bitcast.12), calls=%async_computation | async-start | bytes 4194304 | tf_op jit(solution)/shard_map/all_to_all | solution.py:315
  11.8 0.3 shard_map.59
  12.1 0.1 reshape.41
  12.2 0.7 shard_map.60.counts_ref
  12.9 0.1 and_select_fusion
  12.9 0.2 convert_reduce_fusion
  13.1 0.1 multiply_add_fusion
  13.2 0.1 fusion.1.order_ref
  13.3 48.5 %all-to-all-done.in_ref = f32[32,128,128]{2,1,0:T(8,128)S(1)} async-done(((f32[32,128,128]{2,1,0:T(8,128)}), f32[32,128,128]{2,1,0:T(8,128)S(1)}, u32[]{:S(2)}, u32[]{:S(2)}) %all-to-all-start) | async-done | bytes 2097184 | tf_op jit(solution)/shard_map/all_to_all | solution.py:315
  61.9 1.5 %shard_map.61.held_ref = f32[32,128,128]{2,1,0:T(8,128)} custom-call(f32[32,128,128]{2,1,0:T(8,128)S(1)} %all-to-all-done.in_ref), custom_call_target="tpu_custom_call" | custom-call | tf_op jit(solution)/shard_map/pallas_call | solution.py:130
  63.3 2.7 %all-to-all-start.1 = ((f32[32,128,128]{2,1,0:T(8,128)}), f32[32,128,128]{2,1,0:T(8,128)S(1)}, u32[]{:S(2)}, u32[]{:S(2)}) async-start(f32[32,128,128]{2,1,0:T(8,128)} %shard_map.61.held_ref), calls=%async_computation.1 | async-start | bytes 4194304 | tf_op jit(solution)/shard_map/all_to_all | solution.py:318
  66.1 3.0 %shard_map.62 = f32[128,128]{1,0:T(8,128)S(1)} custom-call(f32[128,32]{1,0:T(8,128)S(1)} %shard_map.60.counts_ref, f32[32,128,128]{2,1,0:T(8,128)} %shard_map.61.held_ref), custom_call_target="tpu_custom_call" | custom-call | tf_op jit(solution)/shard_map/pallas_call | solution.py:243
  69.1 0.2 collective-permute-start
  69.3 1.1 collective-permute-done
  70.4 1.6 %collective-permute-start.1 = (f32[64,128]{1,0:T(8,128)S(1)}, f32[64,128]{1,0:T(8,128)S(1)}, u32[]{:S(2)}, u32[]{:S(2)}) collective-permute-start(f32[64,128]{1,0:T(8,128)S(1)} %dynamic-slice_add_fusion), channel_id=1, source_target_pairs={{0,16},{8,24},{16,0},{24,8},{1,17},{9,25},{17,1},{25,9},{2,18},{10... | collective-permute-start | bytes 98312 | tf_op jit(solution)/shard_map/ppermute | solution.py:254
  72.1 8.0 %collective-permute-done.1 = f32[64,128]{1,0:T(8,128)S(1)} collective-permute-done((f32[64,128]{1,0:T(8,128)S(1)}, f32[64,128]{1,0:T(8,128)S(1)}, u32[]{:S(2)}, u32[]{:S(2)}) %collective-permute-start.1) | collective-permute-done | bytes 32800 | tf_op jit(solution)/shard_map/ppermute | solution.py:254
  80.0 1.9 %collective-permute-start.2 = (f32[64,128]{1,0:T(8,128)S(1)}, f32[64,128]{1,0:T(8,128)S(1)}, u32[]{:S(2)}, u32[]{:S(2)}) collective-permute-start(f32[64,128]{1,0:T(8,128)S(1)} %add.42), channel_id=1, source_target_pairs={{0,1},{1,0},{2,3},{3,2},{4,5},{5,4},{6,7},{7,6},{8,9},{9,8},{10,11... | collective-permute-start | bytes 98312 | tf_op jit(solution)/shard_map/ppermute | solution.py:254
  82.0 9.7 %collective-permute-done.2 = f32[64,128]{1,0:T(8,128)S(1)} collective-permute-done((f32[64,128]{1,0:T(8,128)S(1)}, f32[64,128]{1,0:T(8,128)S(1)}, u32[]{:S(2)}, u32[]{:S(2)}) %collective-permute-start.2) | collective-permute-done | bytes 32800 | tf_op jit(solution)/shard_map/ppermute | solution.py:254
  91.7 0.0 collective-permute-start.3
  91.7 9.6 %collective-permute-done.3 = f32[64,128]{1,0:T(8,128)S(1)} collective-permute-done((f32[64,128]{1,0:T(8,128)S(1)}, f32[64,128]{1,0:T(8,128)S(1)}, u32[]{:S(2)}, u32[]{:S(2)}) %collective-permute-start.3) | collective-permute-done | bytes 32800 | tf_op jit(solution)/shard_map/ppermute | solution.py:254
  101.3 4.7 %collective-permute-start.4 = (f32[64,128]{1,0:T(8,128)S(1)}, f32[64,128]{1,0:T(8,128)S(1)}, u32[]{:S(2)}, u32[]{:S(2)}) collective-permute-start(f32[64,128]{1,0:T(8,128)S(1)} %add.44), channel_id=1, source_target_pairs={{0,4},{1,5},{2,6},{3,7},{4,0},{5,1},{6,2},{7,3},{8,12},{9,13},{10,... | collective-permute-start | bytes 98312 | tf_op jit(solution)/shard_map/ppermute | solution.py:254
  106.0 10.2 %collective-permute-done.4 = f32[64,128]{1,0:T(8,128)S(1)} collective-permute-done((f32[64,128]{1,0:T(8,128)S(1)}, f32[64,128]{1,0:T(8,128)S(1)}, u32[]{:S(2)}, u32[]{:S(2)}) %collective-permute-start.4) | collective-permute-done | bytes 32800 | tf_op jit(solution)/shard_map/ppermute | solution.py:254
  116.2 0.7 all-to-all-done.1
  116.9 0.1 collective-permute-start.5
  117.0 1.3 %gather_fusion = f32[256,128]{1,0:T(8,128)} fusion(f32[4096,128]{1,0:T(8,128)S(1)} %bitcast.8, s32[1024]{0:T(1024)S(1)} %pad_clamp_fusion), kind=kCustom, calls=%fused_computation | custom fusion | bytes 263168 | tf_op jit(solution)/shard_map/jit(_take)/gather | solution.py:327
  118.3 3.1 %all-to-all-start.2 = ((f32[32,8,128]{2,1,0:T(8,128)}), f32[32,8,128]{2,1,0:T(8,128)S(1)}, u32[]{:S(2)}, u32[]{:S(2)}) async-start(f32[32,8,128]{2,1,0:T(8,128)} %bitcast.6), calls=%async_computation.2 | async-start | bytes 262144 | tf_op jit(solution)/shard_map/all_to_all | solution.py:328
  121.5 1.3 %shard_map.63 = f32[4096,128]{1,0:T(8,128)} custom-call(f32[4096,128]{1,0:T(8,128)S(1)} %bitcast.9), custom_call_target="tpu_custom_call" | custom-call | tf_op jit(solution)/shard_map/pallas_call | solution.py:150
  122.8 0.6 broadcast_multiply_fusion
  123.4 5.7 %all-to-all-done.2 = f32[32,8,128]{2,1,0:T(8,128)S(1)} async-done(((f32[32,8,128]{2,1,0:T(8,128)}), f32[32,8,128]{2,1,0:T(8,128)S(1)}, u32[]{:S(2)}, u32[]{:S(2)}) %all-to-all-start.2) | async-done | bytes 131104 | tf_op jit(solution)/shard_map/all_to_all | solution.py:328
  129.2 0.9 shard_map.64
  (13 shorter events, 0.1 us)
Async XLA Ops:
  4.4 7.3 %copy-start = (s32[8192]{0:T(1024)S(1)}, s32[8192]{0:T(1024)}, u32[]{:S(2)}) copy-start(s32[8192]{0:T(1024)} %param.5) | copy-start | bytes 98308
  4.5 57.4 %all-to-all-start = ((f32[32,128,128]{2,1,0:T(8,128)}), f32[32,128,128]{2,1,0:T(8,128)S(1)}, u32[]{:S(2)}, u32[]{:S(2)}) async-start(f32[32,128,128]{2,1,0:T(8,128)} %bitcast.12), calls=%async_computation | async-start | bytes 4194304 | tf_op jit(solution)/shard_map/all_to_all | solution.py:315
  63.3 53.5 %all-to-all-start.1 = ((f32[32,128,128]{2,1,0:T(8,128)}), f32[32,128,128]{2,1,0:T(8,128)S(1)}, u32[]{:S(2)}, u32[]{:S(2)}) async-start(f32[32,128,128]{2,1,0:T(8,128)} %shard_map.61.held_ref), calls=%async_computation.1 | async-start | bytes 4194304 | tf_op jit(solution)/shard_map/all_to_all | solution.py:318
  69.1 1.3 collective-permute-start
  70.4 9.6 %collective-permute-start.1 = (f32[64,128]{1,0:T(8,128)S(1)}, f32[64,128]{1,0:T(8,128)S(1)}, u32[]{:S(2)}, u32[]{:S(2)}) collective-permute-start(f32[64,128]{1,0:T(8,128)S(1)} %dynamic-slice_add_fusion), channel_id=1, source_target_pairs={{0,16},{8,24},{16,0},{24,8},{1,17},{9,25},{17,1},{25,9},{2,18},{10... | collective-permute-start | bytes 98312 | tf_op jit(solution)/shard_map/ppermute | solution.py:254
  80.0 11.6 %collective-permute-start.2 = (f32[64,128]{1,0:T(8,128)S(1)}, f32[64,128]{1,0:T(8,128)S(1)}, u32[]{:S(2)}, u32[]{:S(2)}) collective-permute-start(f32[64,128]{1,0:T(8,128)S(1)} %add.42), channel_id=1, source_target_pairs={{0,1},{1,0},{2,3},{3,2},{4,5},{5,4},{6,7},{7,6},{8,9},{9,8},{10,11... | collective-permute-start | bytes 98312 | tf_op jit(solution)/shard_map/ppermute | solution.py:254
  91.7 9.6 %collective-permute-start.3 = (f32[64,128]{1,0:T(8,128)S(1)}, f32[64,128]{1,0:T(8,128)S(1)}, u32[]{:S(2)}, u32[]{:S(2)}) collective-permute-start(f32[64,128]{1,0:T(8,128)S(1)} %add.43), channel_id=1, source_target_pairs={{0,2},{1,3},{2,0},{3,1},{4,6},{5,7},{6,4},{7,5},{8,10},{9,11},{10,... | collective-permute-start | bytes 98312 | tf_op jit(solution)/shard_map/ppermute | solution.py:254
  101.3 14.9 %collective-permute-start.4 = (f32[64,128]{1,0:T(8,128)S(1)}, f32[64,128]{1,0:T(8,128)S(1)}, u32[]{:S(2)}, u32[]{:S(2)}) collective-permute-start(f32[64,128]{1,0:T(8,128)S(1)} %add.44), channel_id=1, source_target_pairs={{0,4},{1,5},{2,6},{3,7},{4,0},{5,1},{6,2},{7,3},{8,12},{9,13},{10,... | collective-permute-start | bytes 98312 | tf_op jit(solution)/shard_map/ppermute | solution.py:254
  116.9 4.6 %collective-permute-start.5 = (f32[128,128]{1,0:T(8,128)S(1)}, f32[128,128]{1,0:T(8,128)S(1)}, u32[]{:S(2)}, u32[]{:S(2)}) collective-permute-start(f32[128,128]{1,0:T(8,128)S(1)} %constant_dynamic-update-slice_fusion), channel_id=1, source_target_pairs={{0,8},{8,0},{16,24},{24,16},{1,9},{9,1},{17,25},{25,17},{2,10},{10... | collective-permute-start | bytes 196616 | tf_op jit(solution)/shard_map/ppermute | solution.py:254
  118.3 10.9 %all-to-all-start.2 = ((f32[32,8,128]{2,1,0:T(8,128)}), f32[32,8,128]{2,1,0:T(8,128)S(1)}, u32[]{:S(2)}, u32[]{:S(2)}) async-start(f32[32,8,128]{2,1,0:T(8,128)} %bitcast.6), calls=%async_computation.2 | async-start | bytes 262144 | tf_op jit(solution)/shard_map/all_to_all | solution.py:328

commit v26 on v25

--- a/solution.py
+++ b/solution.py
@@ -140,6 +140,30 @@
     )(value)
 
 
+def pick_kernel(wanted_ref, mixed_ref, out_ref):
+    def body(step, carry):
+        at = step * 8
+        for k in range(8):
+            row = mixed_ref[pl.ds(wanted_ref[at + k], 1), :]
+            out_ref[pl.ds(at + k, 1), :] = row
+        return carry
+
+    lax.fori_loop(0, out_ref.shape[0] // 8, body, 0)
+
+
+def pick_rows(wanted, mixed):
+    return pl.pallas_call(
+        pick_kernel,
+        out_shape=jax.ShapeDtypeStruct((wanted.shape[0], mixed.shape[1]), jnp.float32),
+        in_specs=[
+            pl.BlockSpec(memory_space=pltpu.SMEM),
+            pl.BlockSpec(memory_space=pltpu.VMEM),
+        ],
+        out_specs=pl.BlockSpec(memory_space=pltpu.VMEM),
+        compiler_params=pltpu.CompilerParams(vmem_limit_bytes=8 * 2**20),
+    )(wanted, mixed)
+
+
 def store_kernel(value_ref, out_ref, sent):
     copy = pltpu.make_async_copy(value_ref, out_ref, sent)
     copy.start()
@@ -308,6 +332,7 @@
     local = local_transform(panel, flips, scale)
     local = local.reshape(devices, rows_here // devices, width)
     wanted = send_rows(picks, [me], rows_here, devices, most)
+    wanted = jnp.maximum(wanted, 0)
     spots = landing(lax.dynamic_slice(picks, (me * per,), (per,)), rows_here, most)
     slots = jnp.arange(devices * most, dtype=jnp.int32)
     order = (spots[:, None] == slots[None, :]).astype(jnp.bfloat16)
@@ -324,7 +349,7 @@
             low *= 2
     mixed, gram = lax.optimization_barrier((mixed, gram))
     mixed = mixed.reshape(rows_here, width)
-    chosen = jnp.take(mixed, wanted, axis=0, mode="clip")
+    chosen = pick_rows(wanted, mixed)
     landed = lax.all_to_all(chosen.reshape(devices, most, width), AXES, 0, 0, tiled=True)
     gram, other = gather_halves(gram, "narrow")
     mixed, other = lax.optimization_barrier((mixed, other))

time: 130 us -> 132 us (1.015)
  local copies, waits for them, and re-layouts: 1.47 us -> 3.05 us
    unnamed x2 -> x6, local copies, waits for them, and re-layouts: 0.01 us -> 2.93 us
    pallas_call x1, Pallas kernels: 3.04 us -> 1.44 us  [gram_part(): pl.pallas_call(part_kernel, out_shape=jax.ShapeDtypeStruct((width, width)...]
    pallas_call x0 -> x1, Pallas kernels: none -> 1.56 us  [pick_rows(): pl.pallas_call(pick_kernel, out_shape=jax.ShapeDtypeStruct((wanted.shape[...]
    gather x1 -> x0, local copies, waits for them, and re-layouts: 1.34 us -> none  [on_device(): chosen = jnp.take(mixed, wanted, axis=0, mode='clip')]
  transfers between devices with their start and end apart: 9 -> 9, of which waited for: 8 -> 8; matrix products, arithmetic and copies ran while one was open for 2% -> 1% of each run, Pallas kernels for 4% -> 4%
where the time goes in v26:
time: 132 us; the launch traced here: 131 us
  waiting for transfers between devices  93.4 us (71%)
  starting transfers between devices  21.7 us (16%)
  Pallas kernels  11 us (8%)
  local copies, waits for them, and re-layouts  3.05 us (2%)
    all_to_all x1, waiting for transfers between devices, on_device(): slices = lax.all_to_all(local, AXES, 0, 0, tiled=True)  48.5 us
    ppermute x6, waiting for transfers between devices, swap(): return lax.ppermute(value, axis, pairs)  38.5 us
    ppermute x6, starting transfers between devices, swap(): return lax.ppermute(value, axis, pairs)  8.57 us
    all_to_all x1, starting transfers between devices, on_device(): slices = lax.all_to_all(local, AXES, 0, 0, tiled=True)  7.3 us
    all_to_all x1, waiting for transfers between devices, on_device(): lax.all_to_all(chosen.reshape(devices, most, width), AXES, 0, 0, tiled=True)  5.73 us
    pallas_call x1, Pallas kernels, local_transform(): pl.pallas_call(functools.partial(local_kernel, scale), out_shape=jax.Shap...  3.8 us
    all_to_all x1, starting transfers between devices, on_device(): lax.all_to_all(chosen.reshape(devices, most, width), AXES, 0, 0, tiled=True)  3.11 us
    unnamed x6, local copies, waits for them, and re-layouts  2.93 us
  transfers between devices with their start and end apart: 9, of which 8 were waited for; matrix products, arithmetic and copies ran while one was open for 1% of the time, Pallas kernels for 4%

profile of v26, /device:TPU:0, one launch (start us, length us, event | category | flops | bytes accessed | tf_op | source)
XLA Modules:
  0.0 131.1 jit_solution(14676538256815274302)
XLA Ops:
  0.6 3.8 %shard_map.58 = f32[16,256,128]{2,1,0:T(8,128)} custom-call(s32[32,128]{1,0:T(8,128)} %bitcast.14, f32[16,256,128]{2,1,0:T(8,128)} %bitcast.13), custom_call_target="tpu_custom_call" | custom-call | tf_op jit(solution)/shard_map/pallas_call | solution.py:81
  4.5 7.3 %all-to-all-start = ((f32[32,128,128]{2,1,0:T(8,128)}), f32[32,128,128]{2,1,0:T(8,128)S(1)}, u32[]{:S(2)}, u32[]{:S(2)}) async-start(f32[32,128,128]{2,1,0:T(8,128)} %bitcast.12), calls=%async_computation | async-start | bytes 4194304 | tf_op jit(solution)/shard_map/all_to_all | solution.py:340
  11.8 0.3 shard_map.59
  12.1 0.1 max.13.wanted_ref
  12.2 0.7 shard_map.60.counts_ref
  12.9 0.1 and_select_fusion
  13.0 0.2 convert_reduce_fusion
  13.1 0.1 multiply_add_fusion
  13.2 0.1 fusion.1.order_ref
  13.3 48.5 %all-to-all-done.in_ref = f32[32,128,128]{2,1,0:T(8,128)S(1)} async-done(((f32[32,128,128]{2,1,0:T(8,128)}), f32[32,128,128]{2,1,0:T(8,128)S(1)}, u32[]{:S(2)}, u32[]{:S(2)}) %all-to-all-start) | async-done | bytes 2097184 | tf_op jit(solution)/shard_map/all_to_all | solution.py:340
  61.9 1.0 shard_map.61.held_ref
  62.9 1.3 copy-done
  64.2 2.7 %all-to-all-start.1 = ((f32[32,128,128]{2,1,0:T(8,128)}), f32[32,128,128]{2,1,0:T(8,128)S(1)}, u32[]{:S(2)}, u32[]{:S(2)}) async-start(f32[32,128,128]{2,1,0:T(8,128)} %copy-done), calls=%async_computation.1 | async-start | bytes 4194304 | tf_op jit(solution)/shard_map/all_to_all | solution.py:343
  67.0 1.6 %copy-done.1 = f32[32,128,128]{2,1,0:T(8,128)S(1)} copy-done((f32[32,128,128]{2,1,0:T(8,128)S(1)}, f32[32,128,128]{2,1,0:T(8,128)}, u32[]{:S(2)}) %copy-start.1) | copy-done | bytes 2097176
  68.6 1.4 %shard_map.62 = f32[128,128]{1,0:T(8,128)S(1)} custom-call(f32[128,32]{1,0:T(8,128)S(1)} %shard_map.60.counts_ref, f32[32,128,128]{2,1,0:T(8,128)S(1)} %copy-done.1), custom_call_target="tpu_custom_call" | custom-call | tf_op jit(solution)/shard_map/pallas_call | solution.py:267
  70.0 0.2 collective-permute-start
  70.2 1.1 collective-permute-done
  71.3 1.6 %collective-permute-start.1 = (f32[64,128]{1,0:T(8,128)S(1)}, f32[64,128]{1,0:T(8,128)S(1)}, u32[]{:S(2)}, u32[]{:S(2)}) collective-permute-start(f32[64,128]{1,0:T(8,128)S(1)} %dynamic-slice_add_fusion), channel_id=1, source_target_pairs={{0,16},{8,24},{16,0},{24,8},{1,17},{9,25},{17,1},{25,9},{2,18},{10... | collective-permute-start | bytes 98312 | tf_op jit(solution)/shard_map/ppermute | solution.py:278
  73.0 8.0 %collective-permute-done.1 = f32[64,128]{1,0:T(8,128)S(1)} collective-permute-done((f32[64,128]{1,0:T(8,128)S(1)}, f32[64,128]{1,0:T(8,128)S(1)}, u32[]{:S(2)}, u32[]{:S(2)}) %collective-permute-start.1) | collective-permute-done | bytes 32800 | tf_op jit(solution)/shard_map/ppermute | solution.py:278
  80.9 1.9 %collective-permute-start.2 = (f32[64,128]{1,0:T(8,128)S(1)}, f32[64,128]{1,0:T(8,128)S(1)}, u32[]{:S(2)}, u32[]{:S(2)}) collective-permute-start(f32[64,128]{1,0:T(8,128)S(1)} %add.42), channel_id=1, source_target_pairs={{0,1},{1,0},{2,3},{3,2},{4,5},{5,4},{6,7},{7,6},{8,9},{9,8},{10,11... | collective-permute-start | bytes 98312 | tf_op jit(solution)/shard_map/ppermute | solution.py:278
  82.9 9.7 %collective-permute-done.2 = f32[64,128]{1,0:T(8,128)S(1)} collective-permute-done((f32[64,128]{1,0:T(8,128)S(1)}, f32[64,128]{1,0:T(8,128)S(1)}, u32[]{:S(2)}, u32[]{:S(2)}) %collective-permute-start.2) | collective-permute-done | bytes 32800 | tf_op jit(solution)/shard_map/ppermute | solution.py:278
  92.6 9.6 %collective-permute-done.3 = f32[64,128]{1,0:T(8,128)S(1)} collective-permute-done((f32[64,128]{1,0:T(8,128)S(1)}, f32[64,128]{1,0:T(8,128)S(1)}, u32[]{:S(2)}, u32[]{:S(2)}) %collective-permute-start.3) | collective-permute-done | bytes 32800 | tf_op jit(solution)/shard_map/ppermute | solution.py:278
  102.2 4.7 %collective-permute-start.4 = (f32[64,128]{1,0:T(8,128)S(1)}, f32[64,128]{1,0:T(8,128)S(1)}, u32[]{:S(2)}, u32[]{:S(2)}) collective-permute-start(f32[64,128]{1,0:T(8,128)S(1)} %add.44), channel_id=1, source_target_pairs={{0,4},{1,5},{2,6},{3,7},{4,0},{5,1},{6,2},{7,3},{8,12},{9,13},{10,... | collective-permute-start | bytes 98312 | tf_op jit(solution)/shard_map/ppermute | solution.py:278
  106.9 10.2 %collective-permute-done.4 = f32[64,128]{1,0:T(8,128)S(1)} collective-permute-done((f32[64,128]{1,0:T(8,128)S(1)}, f32[64,128]{1,0:T(8,128)S(1)}, u32[]{:S(2)}, u32[]{:S(2)}) %collective-permute-start.4) | collective-permute-done | bytes 32800 | tf_op jit(solution)/shard_map/ppermute | solution.py:278
  117.0 0.7 all-to-all-done.1
  117.8 0.1 collective-permute-start.5
  117.8 1.6 %shard_map.63 = f32[256,128]{1,0:T(8,128)} custom-call(s32[256]{0:T(256)S(1)} %max.13.wanted_ref, f32[4096,128]{1,0:T(8,128)S(1)} %bitcast.8), custom_call_target="tpu_custom_call" | custom-call | tf_op jit(solution)/shard_map/pallas_call | solution.py:155
  119.4 3.1 %all-to-all-start.2 = ((f32[32,8,128]{2,1,0:T(8,128)}), f32[32,8,128]{2,1,0:T(8,128)S(1)}, u32[]{:S(2)}, u32[]{:S(2)}) async-start(f32[32,8,128]{2,1,0:T(8,128)} %bitcast.6), calls=%async_computation.2 | async-start | bytes 262144 | tf_op jit(solution)/shard_map/all_to_all | solution.py:353
  122.5 1.3 %shard_map.64 = f32[4096,128]{1,0:T(8,128)} custom-call(f32[4096,128]{1,0:T(8,128)S(1)} %bitcast.9), custom_call_target="tpu_custom_call" | custom-call | tf_op jit(solution)/shard_map/pallas_call | solution.py:174
  123.9 0.6 broadcast_multiply_fusion
  124.5 5.7 %all-to-all-done.2 = f32[32,8,128]{2,1,0:T(8,128)S(1)} async-done(((f32[32,8,128]{2,1,0:T(8,128)}), f32[32,8,128]{2,1,0:T(8,128)S(1)}, u32[]{:S(2)}, u32[]{:S(2)}) %all-to-all-start.2) | async-done | bytes 131104 | tf_op jit(solution)/shard_map/all_to_all | solution.py:353
  130.3 0.9 shard_map.65
  (17 shorter events, 0.1 us)
Async XLA Ops:
  4.4 7.3 %copy-start.2 = (s32[8192]{0:T(1024)S(1)}, s32[8192]{0:T(1024)}, u32[]{:S(2)}) copy-start(s32[8192]{0:T(1024)} %param.5) | copy-start | bytes 98308
  4.5 57.4 %all-to-all-start = ((f32[32,128,128]{2,1,0:T(8,128)}), f32[32,128,128]{2,1,0:T(8,128)S(1)}, u32[]{:S(2)}, u32[]{:S(2)}) async-start(f32[32,128,128]{2,1,0:T(8,128)} %bitcast.12), calls=%async_computation | async-start | bytes 4194304 | tf_op jit(solution)/shard_map/all_to_all | solution.py:340
  62.9 1.3 %copy-start = (f32[32,128,128]{2,1,0:T(8,128)}, f32[32,128,128]{2,1,0:T(8,128)S(1)}, u32[]{:S(2)}) copy-start(f32[32,128,128]{2,1,0:T(8,128)S(1)} %shard_map.61.held_ref) | copy-start | bytes 6291460
  64.2 53.5 %all-to-all-start.1 = ((f32[32,128,128]{2,1,0:T(8,128)}), f32[32,128,128]{2,1,0:T(8,128)S(1)}, u32[]{:S(2)}, u32[]{:S(2)}) async-start(f32[32,128,128]{2,1,0:T(8,128)} %copy-done), calls=%async_computation.1 | async-start | bytes 4194304 | tf_op jit(solution)/shard_map/all_to_all | solution.py:343
  67.0 1.6 %copy-start.1 = (f32[32,128,128]{2,1,0:T(8,128)S(1)}, f32[32,128,128]{2,1,0:T(8,128)}, u32[]{:S(2)}) copy-start(f32[32,128,128]{2,1,0:T(8,128)} %copy-done) | copy-start | bytes 6291460
  70.0 1.3 collective-permute-start
  71.3 9.6 %collective-permute-start.1 = (f32[64,128]{1,0:T(8,128)S(1)}, f32[64,128]{1,0:T(8,128)S(1)}, u32[]{:S(2)}, u32[]{:S(2)}) collective-permute-start(f32[64,128]{1,0:T(8,128)S(1)} %dynamic-slice_add_fusion), channel_id=1, source_target_pairs={{0,16},{8,24},{16,0},{24,8},{1,17},{9,25},{17,1},{25,9},{2,18},{10... | collective-permute-start | bytes 98312 | tf_op jit(solution)/shard_map/ppermute | solution.py:278
  80.9 11.6 %collective-permute-start.2 = (f32[64,128]{1,0:T(8,128)S(1)}, f32[64,128]{1,0:T(8,128)S(1)}, u32[]{:S(2)}, u32[]{:S(2)}) collective-permute-start(f32[64,128]{1,0:T(8,128)S(1)} %add.42), channel_id=1, source_target_pairs={{0,1},{1,0},{2,3},{3,2},{4,5},{5,4},{6,7},{7,6},{8,9},{9,8},{10,11... | collective-permute-start | bytes 98312 | tf_op jit(solution)/shard_map/ppermute | solution.py:278
  92.6 9.6 %collective-permute-start.3 = (f32[64,128]{1,0:T(8,128)S(1)}, f32[64,128]{1,0:T(8,128)S(1)}, u32[]{:S(2)}, u32[]{:S(2)}) collective-permute-start(f32[64,128]{1,0:T(8,128)S(1)} %add.43), channel_id=1, source_target_pairs={{0,2},{1,3},{2,0},{3,1},{4,6},{5,7},{6,4},{7,5},{8,10},{9,11},{10,... | collective-permute-start | bytes 98312 | tf_op jit(solution)/shard_map/ppermute | solution.py:278
  102.2 14.9 %collective-permute-start.4 = (f32[64,128]{1,0:T(8,128)S(1)}, f32[64,128]{1,0:T(8,128)S(1)}, u32[]{:S(2)}, u32[]{:S(2)}) collective-permute-start(f32[64,128]{1,0:T(8,128)S(1)} %add.44), channel_id=1, source_target_pairs={{0,4},{1,5},{2,6},{3,7},{4,0},{5,1},{6,2},{7,3},{8,12},{9,13},{10,... | collective-permute-start | bytes 98312 | tf_op jit(solution)/shard_map/ppermute | solution.py:278
  117.8 4.8 %collective-permute-start.5 = (f32[128,128]{1,0:T(8,128)S(1)}, f32[128,128]{1,0:T(8,128)S(1)}, u32[]{:S(2)}, u32[]{:S(2)}) collective-permute-start(f32[128,128]{1,0:T(8,128)S(1)} %constant_dynamic-update-slice_fusion), channel_id=1, source_target_pairs={{0,8},{8,0},{16,24},{24,16},{1,9},{9,1},{17,25},{25,17},{2,10},{10... | collective-permute-start | bytes 196616 | tf_op jit(solution)/shard_map/ppermute | solution.py:278
  119.4 10.9 %all-to-all-start.2 = ((f32[32,8,128]{2,1,0:T(8,128)}), f32[32,8,128]{2,1,0:T(8,128)S(1)}, u32[]{:S(2)}, u32[]{:S(2)}) async-start(f32[32,8,128]{2,1,0:T(8,128)} %bitcast.6), calls=%async_computation.2 | async-start | bytes 262144 | tf_op jit(solution)/shard_map/all_to_all | solution.py:353

commit v27 on v25

--- a/solution.py
+++ b/solution.py
@@ -28,9 +28,9 @@
 def local_kernel(scale, flips_ref, panel_ref, out_ref, flags, held, arrived, sent):
     blocks, _, width = panel_ref.shape
     per = BLOCK // flips_ref.shape[1]
-    share = blocks // 4
-    loads = [pltpu.make_async_copy(flips_ref, flags, arrived.at[4])]
-    for part in range(4):
+    share = blocks // 2
+    loads = [pltpu.make_async_copy(flips_ref, flags, arrived.at[2])]
+    for part in range(2):
         span = pl.ds(part * share, share)
         loads.append(pltpu.make_async_copy(panel_ref.at[span], held.at[span], arrived.at[part]))
     for load in loads:
@@ -46,7 +46,7 @@
         out = jnp.dot(mixer, parts, preferred_element_type=jnp.float32)
         held[b] = out[:, :width] + out[:, width:]
     strip = 16
-    piece = BLOCK // 4
+    piece = BLOCK // 2
 
     def body(step, carry):
         at = pl.multiple_of(step * strip, strip)
@@ -63,7 +63,7 @@
         return carry
 
     copies = []
-    for part in range(4):
+    for part in range(2):
         first = part * piece // strip
         lax.fori_loop(first, first + piece // strip, body, 0)
         span = pl.ds(part * piece, piece)
@@ -86,8 +86,8 @@
         scratch_shapes=[
             pltpu.VMEM((rows // 128, 128), jnp.int32),
             pltpu.VMEM(shape, jnp.float32),
-            pltpu.SemaphoreType.DMA((5,)),
-            pltpu.SemaphoreType.DMA((4,)),
+            pltpu.SemaphoreType.DMA((3,)),
+            pltpu.SemaphoreType.DMA((2,)),
         ],
         compiler_params=pltpu.CompilerParams(vmem_limit_bytes=61 * 2**20),
     )(flips.reshape(rows // 128, 128), panel.reshape(shape))

time: 130 us -> 130 us (level)
  no operation moved by 1% of the time
where the time goes in v27:
time: 130 us
  waiting for transfers between devices  93.4 us (72%)
  starting transfers between devices  21.7 us (17%)
  Pallas kernels  11.4 us (9%)
  local copies, waits for them, and re-layouts  1.47 us (1%)
    all_to_all x1, waiting for transfers between devices, on_device(): slices = lax.all_to_all(local, AXES, 0, 0, tiled=True)  48.5 us
    ppermute x6, waiting for transfers between devices, swap(): return lax.ppermute(value, axis, pairs)  38.5 us
    ppermute x6, starting transfers between devices, swap(): return lax.ppermute(value, axis, pairs)  8.57 us
    all_to_all x1, starting transfers between devices, on_device(): slices = lax.all_to_all(local, AXES, 0, 0, tiled=True)  7.3 us
    all_to_all x1, waiting for transfers between devices, on_device(): lax.all_to_all(chosen.reshape(devices, most, width), AXES, 0, 0, tiled=True)  5.73 us
    pallas_call x1, Pallas kernels, local_transform(): pl.pallas_call(functools.partial(local_kernel, scale), out_shape=jax.Shap...  3.74 us
    all_to_all x1, starting transfers between devices, on_device(): lax.all_to_all(chosen.reshape(devices, most, width), AXES, 0, 0, tiled=True)  3.11 us
    pallas_call x1, Pallas kernels, gram_part(): pl.pallas_call(part_kernel, out_shape=jax.ShapeDtypeStruct((width, width)...  3.04 us
  transfers between devices with their start and end apart: 9, of which 8 were waited for; matrix products, arithmetic and copies ran while one was open for 2% of the time, Pallas kernels for 4%

profile of v27, /device:TPU:0, one launch (start us, length us, event | category | flops | bytes accessed | tf_op | source)
XLA Modules:
  0.0 130.0 jit_solution(5327021231724977030)
XLA Ops:
  0.6 3.7 %shard_map.58 = f32[16,256,128]{2,1,0:T(8,128)} custom-call(s32[32,128]{1,0:T(8,128)} %bitcast.14, f32[16,256,128]{2,1,0:T(8,128)} %bitcast.13), custom_call_target="tpu_custom_call" | custom-call | tf_op jit(solution)/shard_map/pallas_call | solution.py:81
  4.4 0.0 copy-start
  4.4 7.3 %all-to-all-start = ((f32[32,128,128]{2,1,0:T(8,128)}), f32[32,128,128]{2,1,0:T(8,128)S(1)}, u32[]{:S(2)}, u32[]{:S(2)}) async-start(f32[32,128,128]{2,1,0:T(8,128)} %bitcast.12), calls=%async_computation | async-start | bytes 4194304 | tf_op jit(solution)/shard_map/all_to_all | solution.py:315
  11.7 0.3 shard_map.59
  12.0 0.1 reshape.41
  12.1 0.7 shard_map.60.counts_ref
  12.8 0.1 and_select_fusion
  12.9 0.2 convert_reduce_fusion
  13.1 0.1 multiply_add_fusion
  13.1 0.1 fusion.1.order_ref
  13.3 48.5 %all-to-all-done.in_ref = f32[32,128,128]{2,1,0:T(8,128)S(1)} async-done(((f32[32,128,128]{2,1,0:T(8,128)}), f32[32,128,128]{2,1,0:T(8,128)S(1)}, u32[]{:S(2)}, u32[]{:S(2)}) %all-to-all-start) | async-done | bytes 2097184 | tf_op jit(solution)/shard_map/all_to_all | solution.py:315
  61.8 1.5 %shard_map.61.held_ref = f32[32,128,128]{2,1,0:T(8,128)} custom-call(f32[32,128,128]{2,1,0:T(8,128)S(1)} %all-to-all-done.in_ref), custom_call_target="tpu_custom_call" | custom-call | tf_op jit(solution)/shard_map/pallas_call | solution.py:130
  63.3 2.7 %all-to-all-start.1 = ((f32[32,128,128]{2,1,0:T(8,128)}), f32[32,128,128]{2,1,0:T(8,128)S(1)}, u32[]{:S(2)}, u32[]{:S(2)}) async-start(f32[32,128,128]{2,1,0:T(8,128)} %shard_map.61.held_ref), calls=%async_computation.1 | async-start | bytes 4194304 | tf_op jit(solution)/shard_map/all_to_all | solution.py:318
  66.0 3.0 %shard_map.62 = f32[128,128]{1,0:T(8,128)S(1)} custom-call(f32[128,32]{1,0:T(8,128)S(1)} %shard_map.60.counts_ref, f32[32,128,128]{2,1,0:T(8,128)} %shard_map.61.held_ref), custom_call_target="tpu_custom_call" | custom-call | tf_op jit(solution)/shard_map/pallas_call | solution.py:243
  69.1 0.2 collective-permute-start
  69.3 1.1 collective-permute-done
  70.4 1.6 %collective-permute-start.1 = (f32[64,128]{1,0:T(8,128)S(1)}, f32[64,128]{1,0:T(8,128)S(1)}, u32[]{:S(2)}, u32[]{:S(2)}) collective-permute-start(f32[64,128]{1,0:T(8,128)S(1)} %dynamic-slice_add_fusion), channel_id=1, source_target_pairs={{0,16},{8,24},{16,0},{24,8},{1,17},{9,25},{17,1},{25,9},{2,18},{10... | collective-permute-start | bytes 98312 | tf_op jit(solution)/shard_map/ppermute | solution.py:254
  72.0 8.0 %collective-permute-done.1 = f32[64,128]{1,0:T(8,128)S(1)} collective-permute-done((f32[64,128]{1,0:T(8,128)S(1)}, f32[64,128]{1,0:T(8,128)S(1)}, u32[]{:S(2)}, u32[]{:S(2)}) %collective-permute-start.1) | collective-permute-done | bytes 32800 | tf_op jit(solution)/shard_map/ppermute | solution.py:254
  80.0 1.9 %collective-permute-start.2 = (f32[64,128]{1,0:T(8,128)S(1)}, f32[64,128]{1,0:T(8,128)S(1)}, u32[]{:S(2)}, u32[]{:S(2)}) collective-permute-start(f32[64,128]{1,0:T(8,128)S(1)} %add.42), channel_id=1, source_target_pairs={{0,1},{1,0},{2,3},{3,2},{4,5},{5,4},{6,7},{7,6},{8,9},{9,8},{10,11... | collective-permute-start | bytes 98312 | tf_op jit(solution)/shard_map/ppermute | solution.py:254
  81.9 9.7 %collective-permute-done.2 = f32[64,128]{1,0:T(8,128)S(1)} collective-permute-done((f32[64,128]{1,0:T(8,128)S(1)}, f32[64,128]{1,0:T(8,128)S(1)}, u32[]{:S(2)}, u32[]{:S(2)}) %collective-permute-start.2) | collective-permute-done | bytes 32800 | tf_op jit(solution)/shard_map/ppermute | solution.py:254
  91.6 0.0 collective-permute-start.3
  91.6 9.6 %collective-permute-done.3 = f32[64,128]{1,0:T(8,128)S(1)} collective-permute-done((f32[64,128]{1,0:T(8,128)S(1)}, f32[64,128]{1,0:T(8,128)S(1)}, u32[]{:S(2)}, u32[]{:S(2)}) %collective-permute-start.3) | collective-permute-done | bytes 32800 | tf_op jit(solution)/shard_map/ppermute | solution.py:254
  101.2 4.7 %collective-permute-start.4 = (f32[64,128]{1,0:T(8,128)S(1)}, f32[64,128]{1,0:T(8,128)S(1)}, u32[]{:S(2)}, u32[]{:S(2)}) collective-permute-start(f32[64,128]{1,0:T(8,128)S(1)} %add.44), channel_id=1, source_target_pairs={{0,4},{1,5},{2,6},{3,7},{4,0},{5,1},{6,2},{7,3},{8,12},{9,13},{10,... | collective-permute-start | bytes 98312 | tf_op jit(solution)/shard_map/ppermute | solution.py:254
  105.9 10.2 %collective-permute-done.4 = f32[64,128]{1,0:T(8,128)S(1)} collective-permute-done((f32[64,128]{1,0:T(8,128)S(1)}, f32[64,128]{1,0:T(8,128)S(1)}, u32[]{:S(2)}, u32[]{:S(2)}) %collective-permute-start.4) | collective-permute-done | bytes 32800 | tf_op jit(solution)/shard_map/ppermute | solution.py:254
  116.1 0.7 all-to-all-done.1
  116.8 0.1 collective-permute-start.5
  116.9 1.3 %gather_fusion = f32[256,128]{1,0:T(8,128)} fusion(f32[4096,128]{1,0:T(8,128)S(1)} %bitcast.8, s32[1024]{0:T(1024)S(1)} %pad_clamp_fusion), kind=kCustom, calls=%fused_computation | custom fusion | bytes 263168 | tf_op jit(solution)/shard_map/jit(_take)/gather | solution.py:327
  118.2 3.1 %all-to-all-start.2 = ((f32[32,8,128]{2,1,0:T(8,128)}), f32[32,8,128]{2,1,0:T(8,128)S(1)}, u32[]{:S(2)}, u32[]{:S(2)}) async-start(f32[32,8,128]{2,1,0:T(8,128)} %bitcast.6), calls=%async_computation.2 | async-start | bytes 262144 | tf_op jit(solution)/shard_map/all_to_all | solution.py:328
  121.4 1.3 %shard_map.63 = f32[4096,128]{1,0:T(8,128)} custom-call(f32[4096,128]{1,0:T(8,128)S(1)} %bitcast.9), custom_call_target="tpu_custom_call" | custom-call | tf_op jit(solution)/shard_map/pallas_call | solution.py:150
  122.7 0.6 broadcast_multiply_fusion
  123.4 5.7 %all-to-all-done.2 = f32[32,8,128]{2,1,0:T(8,128)S(1)} async-done(((f32[32,8,128]{2,1,0:T(8,128)}), f32[32,8,128]{2,1,0:T(8,128)S(1)}, u32[]{:S(2)}, u32[]{:S(2)}) %all-to-all-start.2) | async-done | bytes 131104 | tf_op jit(solution)/shard_map/all_to_all | solution.py:328
  129.1 0.9 shard_map.64
  (13 shorter events, 0.1 us)
Async XLA Ops:
  4.4 7.3 %copy-start = (s32[8192]{0:T(1024)S(1)}, s32[8192]{0:T(1024)}, u32[]{:S(2)}) copy-start(s32[8192]{0:T(1024)} %param.5) | copy-start | bytes 98308
  4.4 57.4 %all-to-all-start = ((f32[32,128,128]{2,1,0:T(8,128)}), f32[32,128,128]{2,1,0:T(8,128)S(1)}, u32[]{:S(2)}, u32[]{:S(2)}) async-start(f32[32,128,128]{2,1,0:T(8,128)} %bitcast.12), calls=%async_computation | async-start | bytes 4194304 | tf_op jit(solution)/shard_map/all_to_all | solution.py:315
  63.3 53.5 %all-to-all-start.1 = ((f32[32,128,128]{2,1,0:T(8,128)}), f32[32,128,128]{2,1,0:T(8,128)S(1)}, u32[]{:S(2)}, u32[]{:S(2)}) async-start(f32[32,128,128]{2,1,0:T(8,128)} %shard_map.61.held_ref), calls=%async_computation.1 | async-start | bytes 4194304 | tf_op jit(solution)/shard_map/all_to_all | solution.py:318
  69.1 1.3 collective-permute-start
  70.4 9.6 %collective-permute-start.1 = (f32[64,128]{1,0:T(8,128)S(1)}, f32[64,128]{1,0:T(8,128)S(1)}, u32[]{:S(2)}, u32[]{:S(2)}) collective-permute-start(f32[64,128]{1,0:T(8,128)S(1)} %dynamic-slice_add_fusion), channel_id=1, source_target_pairs={{0,16},{8,24},{16,0},{24,8},{1,17},{9,25},{17,1},{25,9},{2,18},{10... | collective-permute-start | bytes 98312 | tf_op jit(solution)/shard_map/ppermute | solution.py:254
  80.0 11.6 %collective-permute-start.2 = (f32[64,128]{1,0:T(8,128)S(1)}, f32[64,128]{1,0:T(8,128)S(1)}, u32[]{:S(2)}, u32[]{:S(2)}) collective-permute-start(f32[64,128]{1,0:T(8,128)S(1)} %add.42), channel_id=1, source_target_pairs={{0,1},{1,0},{2,3},{3,2},{4,5},{5,4},{6,7},{7,6},{8,9},{9,8},{10,11... | collective-permute-start | bytes 98312 | tf_op jit(solution)/shard_map/ppermute | solution.py:254
  91.6 9.6 %collective-permute-start.3 = (f32[64,128]{1,0:T(8,128)S(1)}, f32[64,128]{1,0:T(8,128)S(1)}, u32[]{:S(2)}, u32[]{:S(2)}) collective-permute-start(f32[64,128]{1,0:T(8,128)S(1)} %add.43), channel_id=1, source_target_pairs={{0,2},{1,3},{2,0},{3,1},{4,6},{5,7},{6,4},{7,5},{8,10},{9,11},{10,... | collective-permute-start | bytes 98312 | tf_op jit(solution)/shard_map/ppermute | solution.py:254
  101.2 14.9 %collective-permute-start.4 = (f32[64,128]{1,0:T(8,128)S(1)}, f32[64,128]{1,0:T(8,128)S(1)}, u32[]{:S(2)}, u32[]{:S(2)}) collective-permute-start(f32[64,128]{1,0:T(8,128)S(1)} %add.44), channel_id=1, source_target_pairs={{0,4},{1,5},{2,6},{3,7},{4,0},{5,1},{6,2},{7,3},{8,12},{9,13},{10,... | collective-permute-start | bytes 98312 | tf_op jit(solution)/shard_map/ppermute | solution.py:254
  116.8 4.6 %collective-permute-start.5 = (f32[128,128]{1,0:T(8,128)S(1)}, f32[128,128]{1,0:T(8,128)S(1)}, u32[]{:S(2)}, u32[]{:S(2)}) collective-permute-start(f32[128,128]{1,0:T(8,128)S(1)} %constant_dynamic-update-slice_fusion), channel_id=1, source_target_pairs={{0,8},{8,0},{16,24},{24,16},{1,9},{9,1},{17,25},{25,17},{2,10},{10... | collective-permute-start | bytes 196616 | tf_op jit(solution)/shard_map/ppermute | solution.py:254
  118.2 10.9 %all-to-all-start.2 = ((f32[32,8,128]{2,1,0:T(8,128)}), f32[32,8,128]{2,1,0:T(8,128)S(1)}, u32[]{:S(2)}, u32[]{:S(2)}) async-start(f32[32,8,128]{2,1,0:T(8,128)} %bitcast.6), calls=%async_computation.2 | async-start | bytes 262144 | tf_op jit(solution)/shard_map/all_to_all | solution.py:328

commit v28 on v27

--- a/solution.py
+++ b/solution.py
@@ -45,7 +45,7 @@
         parts = jnp.concatenate(halves(held[b]), axis=1)
         out = jnp.dot(mixer, parts, preferred_element_type=jnp.float32)
         held[b] = out[:, :width] + out[:, width:]
-    strip = 16
+    strip = 8
     piece = BLOCK // 2
 
     def body(step, carry):

time: 130 us -> 130 us (level)
  no operation moved by 1% of the time
where the time goes in v28:
time: 130 us
  waiting for transfers between devices  93.5 us (72%)
  starting transfers between devices  21.7 us (17%)
  Pallas kernels  11.5 us (9%)
  local copies, waits for them, and re-layouts  1.47 us (1%)
    all_to_all x1, waiting for transfers between devices, on_device(): slices = lax.all_to_all(local, AXES, 0, 0, tiled=True)  48.5 us
    ppermute x6, waiting for transfers between devices, swap(): return lax.ppermute(value, axis, pairs)  38.5 us
    ppermute x6, starting transfers between devices, swap(): return lax.ppermute(value, axis, pairs)  8.55 us
    all_to_all x1, starting transfers between devices, on_device(): slices = lax.all_to_all(local, AXES, 0, 0, tiled=True)  7.3 us
    all_to_all x1, waiting for transfers between devices, on_device(): lax.all_to_all(chosen.reshape(devices, most, width), AXES, 0, 0, tiled=True)  5.73 us
    pallas_call x1, Pallas kernels, local_transform(): pl.pallas_call(functools.partial(local_kernel, scale), out_shape=jax.Shap...  3.84 us
    all_to_all x1, starting transfers between devices, on_device(): lax.all_to_all(chosen.reshape(devices, most, width), AXES, 0, 0, tiled=True)  3.11 us
    pallas_call x1, Pallas kernels, gram_part(): pl.pallas_call(part_kernel, out_shape=jax.ShapeDtypeStruct((width, width)...  3.05 us
  transfers between devices with their start and end apart: 9, of which 8 were waited for; matrix products, arithmetic and copies ran while one was open for 2% of the time, Pallas kernels for 4%

profile of v28, /device:TPU:0, one launch (start us, length us, event | category | flops | bytes accessed | tf_op | source)
XLA Modules:
  0.0 130.1 jit_solution(5665023762328651557)
XLA Ops:
  0.6 3.8 %shard_map.58 = f32[16,256,128]{2,1,0:T(8,128)} custom-call(s32[32,128]{1,0:T(8,128)} %bitcast.14, f32[16,256,128]{2,1,0:T(8,128)} %bitcast.13), custom_call_target="tpu_custom_call" | custom-call | tf_op jit(solution)/shard_map/pallas_call | solution.py:81
  4.5 0.0 copy-start
  4.5 7.3 %all-to-all-start = ((f32[32,128,128]{2,1,0:T(8,128)}), f32[32,128,128]{2,1,0:T(8,128)S(1)}, u32[]{:S(2)}, u32[]{:S(2)}) async-start(f32[32,128,128]{2,1,0:T(8,128)} %bitcast.12), calls=%async_computation | async-start | bytes 4194304 | tf_op jit(solution)/shard_map/all_to_all | solution.py:315
  11.8 0.3 shard_map.59
  12.1 0.1 reshape.41
  12.2 0.7 shard_map.60.counts_ref
  12.9 0.1 and_select_fusion
  13.0 0.2 convert_reduce_fusion
  13.2 0.1 multiply_add_fusion
  13.2 0.1 fusion.1.order_ref
  13.4 48.5 %all-to-all-done.in_ref = f32[32,128,128]{2,1,0:T(8,128)S(1)} async-done(((f32[32,128,128]{2,1,0:T(8,128)}), f32[32,128,128]{2,1,0:T(8,128)S(1)}, u32[]{:S(2)}, u32[]{:S(2)}) %all-to-all-start) | async-done | bytes 2097184 | tf_op jit(solution)/shard_map/all_to_all | solution.py:315
  61.9 1.5 %shard_map.61.held_ref = f32[32,128,128]{2,1,0:T(8,128)} custom-call(f32[32,128,128]{2,1,0:T(8,128)S(1)} %all-to-all-done.in_ref), custom_call_target="tpu_custom_call" | custom-call | tf_op jit(solution)/shard_map/pallas_call | solution.py:130
  63.4 2.7 %all-to-all-start.1 = ((f32[32,128,128]{2,1,0:T(8,128)}), f32[32,128,128]{2,1,0:T(8,128)S(1)}, u32[]{:S(2)}, u32[]{:S(2)}) async-start(f32[32,128,128]{2,1,0:T(8,128)} %shard_map.61.held_ref), calls=%async_computation.1 | async-start | bytes 4194304 | tf_op jit(solution)/shard_map/all_to_all | solution.py:318
  66.1 3.0 %shard_map.62 = f32[128,128]{1,0:T(8,128)S(1)} custom-call(f32[128,32]{1,0:T(8,128)S(1)} %shard_map.60.counts_ref, f32[32,128,128]{2,1,0:T(8,128)} %shard_map.61.held_ref), custom_call_target="tpu_custom_call" | custom-call | tf_op jit(solution)/shard_map/pallas_call | solution.py:243
  69.2 0.2 collective-permute-start
  69.4 1.1 collective-permute-done
  70.5 1.6 %collective-permute-start.1 = (f32[64,128]{1,0:T(8,128)S(1)}, f32[64,128]{1,0:T(8,128)S(1)}, u32[]{:S(2)}, u32[]{:S(2)}) collective-permute-start(f32[64,128]{1,0:T(8,128)S(1)} %dynamic-slice_add_fusion), channel_id=1, source_target_pairs={{0,16},{8,24},{16,0},{24,8},{1,17},{9,25},{17,1},{25,9},{2,18},{10... | collective-permute-start | bytes 98312 | tf_op jit(solution)/shard_map/ppermute | solution.py:254
  72.1 8.0 %collective-permute-done.1 = f32[64,128]{1,0:T(8,128)S(1)} collective-permute-done((f32[64,128]{1,0:T(8,128)S(1)}, f32[64,128]{1,0:T(8,128)S(1)}, u32[]{:S(2)}, u32[]{:S(2)}) %collective-permute-start.1) | collective-permute-done | bytes 32800 | tf_op jit(solution)/shard_map/ppermute | solution.py:254
  80.1 1.9 %collective-permute-start.2 = (f32[64,128]{1,0:T(8,128)S(1)}, f32[64,128]{1,0:T(8,128)S(1)}, u32[]{:S(2)}, u32[]{:S(2)}) collective-permute-start(f32[64,128]{1,0:T(8,128)S(1)} %add.42), channel_id=1, source_target_pairs={{0,1},{1,0},{2,3},{3,2},{4,5},{5,4},{6,7},{7,6},{8,9},{9,8},{10,11... | collective-permute-start | bytes 98312 | tf_op jit(solution)/shard_map/ppermute | solution.py:254
  82.0 9.7 %collective-permute-done.2 = f32[64,128]{1,0:T(8,128)S(1)} collective-permute-done((f32[64,128]{1,0:T(8,128)S(1)}, f32[64,128]{1,0:T(8,128)S(1)}, u32[]{:S(2)}, u32[]{:S(2)}) %collective-permute-start.2) | collective-permute-done | bytes 32800 | tf_op jit(solution)/shard_map/ppermute | solution.py:254
  91.7 0.0 collective-permute-start.3
  91.7 9.6 %collective-permute-done.3 = f32[64,128]{1,0:T(8,128)S(1)} collective-permute-done((f32[64,128]{1,0:T(8,128)S(1)}, f32[64,128]{1,0:T(8,128)S(1)}, u32[]{:S(2)}, u32[]{:S(2)}) %collective-permute-start.3) | collective-permute-done | bytes 32800 | tf_op jit(solution)/shard_map/ppermute | solution.py:254
  101.3 4.7 %collective-permute-start.4 = (f32[64,128]{1,0:T(8,128)S(1)}, f32[64,128]{1,0:T(8,128)S(1)}, u32[]{:S(2)}, u32[]{:S(2)}) collective-permute-start(f32[64,128]{1,0:T(8,128)S(1)} %add.44), channel_id=1, source_target_pairs={{0,4},{1,5},{2,6},{3,7},{4,0},{5,1},{6,2},{7,3},{8,12},{9,13},{10,... | collective-permute-start | bytes 98312 | tf_op jit(solution)/shard_map/ppermute | solution.py:254
  106.1 10.2 %collective-permute-done.4 = f32[64,128]{1,0:T(8,128)S(1)} collective-permute-done((f32[64,128]{1,0:T(8,128)S(1)}, f32[64,128]{1,0:T(8,128)S(1)}, u32[]{:S(2)}, u32[]{:S(2)}) %collective-permute-start.4) | collective-permute-done | bytes 32800 | tf_op jit(solution)/shard_map/ppermute | solution.py:254
  116.2 0.7 all-to-all-done.1
  116.9 0.1 collective-permute-start.5
  117.0 1.3 %gather_fusion = f32[256,128]{1,0:T(8,128)} fusion(f32[4096,128]{1,0:T(8,128)S(1)} %bitcast.8, s32[1024]{0:T(1024)S(1)} %pad_clamp_fusion), kind=kCustom, calls=%fused_computation | custom fusion | bytes 263168 | tf_op jit(solution)/shard_map/jit(_take)/gather | solution.py:327
  118.4 3.1 %all-to-all-start.2 = ((f32[32,8,128]{2,1,0:T(8,128)}), f32[32,8,128]{2,1,0:T(8,128)S(1)}, u32[]{:S(2)}, u32[]{:S(2)}) async-start(f32[32,8,128]{2,1,0:T(8,128)} %bitcast.6), calls=%async_computation.2 | async-start | bytes 262144 | tf_op jit(solution)/shard_map/all_to_all | solution.py:328
  121.5 1.3 %shard_map.63 = f32[4096,128]{1,0:T(8,128)} custom-call(f32[4096,128]{1,0:T(8,128)S(1)} %bitcast.9), custom_call_target="tpu_custom_call" | custom-call | tf_op jit(solution)/shard_map/pallas_call | solution.py:150
  122.8 0.6 broadcast_multiply_fusion
  123.5 5.7 %all-to-all-done.2 = f32[32,8,128]{2,1,0:T(8,128)S(1)} async-done(((f32[32,8,128]{2,1,0:T(8,128)}), f32[32,8,128]{2,1,0:T(8,128)S(1)}, u32[]{:S(2)}, u32[]{:S(2)}) %all-to-all-start.2) | async-done | bytes 131104 | tf_op jit(solution)/shard_map/all_to_all | solution.py:328
  129.2 0.9 shard_map.64
  (13 shorter events, 0.1 us)
Async XLA Ops:
  4.5 7.3 %copy-start = (s32[8192]{0:T(1024)S(1)}, s32[8192]{0:T(1024)}, u32[]{:S(2)}) copy-start(s32[8192]{0:T(1024)} %param.5) | copy-start | bytes 98308
  4.5 57.4 %all-to-all-start = ((f32[32,128,128]{2,1,0:T(8,128)}), f32[32,128,128]{2,1,0:T(8,128)S(1)}, u32[]{:S(2)}, u32[]{:S(2)}) async-start(f32[32,128,128]{2,1,0:T(8,128)} %bitcast.12), calls=%async_computation | async-start | bytes 4194304 | tf_op jit(solution)/shard_map/all_to_all | solution.py:315
  63.4 53.5 %all-to-all-start.1 = ((f32[32,128,128]{2,1,0:T(8,128)}), f32[32,128,128]{2,1,0:T(8,128)S(1)}, u32[]{:S(2)}, u32[]{:S(2)}) async-start(f32[32,128,128]{2,1,0:T(8,128)} %shard_map.61.held_ref), calls=%async_computation.1 | async-start | bytes 4194304 | tf_op jit(solution)/shard_map/all_to_all | solution.py:318
  69.2 1.3 collective-permute-start
  70.5 9.6 %collective-permute-start.1 = (f32[64,128]{1,0:T(8,128)S(1)}, f32[64,128]{1,0:T(8,128)S(1)}, u32[]{:S(2)}, u32[]{:S(2)}) collective-permute-start(f32[64,128]{1,0:T(8,128)S(1)} %dynamic-slice_add_fusion), channel_id=1, source_target_pairs={{0,16},{8,24},{16,0},{24,8},{1,17},{9,25},{17,1},{25,9},{2,18},{10... | collective-permute-start | bytes 98312 | tf_op jit(solution)/shard_map/ppermute | solution.py:254
  80.1 11.6 %collective-permute-start.2 = (f32[64,128]{1,0:T(8,128)S(1)}, f32[64,128]{1,0:T(8,128)S(1)}, u32[]{:S(2)}, u32[]{:S(2)}) collective-permute-start(f32[64,128]{1,0:T(8,128)S(1)} %add.42), channel_id=1, source_target_pairs={{0,1},{1,0},{2,3},{3,2},{4,5},{5,4},{6,7},{7,6},{8,9},{9,8},{10,11... | collective-permute-start | bytes 98312 | tf_op jit(solution)/shard_map/ppermute | solution.py:254
  91.7 9.6 %collective-permute-start.3 = (f32[64,128]{1,0:T(8,128)S(1)}, f32[64,128]{1,0:T(8,128)S(1)}, u32[]{:S(2)}, u32[]{:S(2)}) collective-permute-start(f32[64,128]{1,0:T(8,128)S(1)} %add.43), channel_id=1, source_target_pairs={{0,2},{1,3},{2,0},{3,1},{4,6},{5,7},{6,4},{7,5},{8,10},{9,11},{10,... | collective-permute-start | bytes 98312 | tf_op jit(solution)/shard_map/ppermute | solution.py:254
  101.3 14.9 %collective-permute-start.4 = (f32[64,128]{1,0:T(8,128)S(1)}, f32[64,128]{1,0:T(8,128)S(1)}, u32[]{:S(2)}, u32[]{:S(2)}) collective-permute-start(f32[64,128]{1,0:T(8,128)S(1)} %add.44), channel_id=1, source_target_pairs={{0,4},{1,5},{2,6},{3,7},{4,0},{5,1},{6,2},{7,3},{8,12},{9,13},{10,... | collective-permute-start | bytes 98312 | tf_op jit(solution)/shard_map/ppermute | solution.py:254
  116.9 4.6 %collective-permute-start.5 = (f32[128,128]{1,0:T(8,128)S(1)}, f32[128,128]{1,0:T(8,128)S(1)}, u32[]{:S(2)}, u32[]{:S(2)}) collective-permute-start(f32[128,128]{1,0:T(8,128)S(1)} %constant_dynamic-update-slice_fusion), channel_id=1, source_target_pairs={{0,8},{8,0},{16,24},{24,16},{1,9},{9,1},{17,25},{25,17},{2,10},{10... | collective-permute-start | bytes 196616 | tf_op jit(solution)/shard_map/ppermute | solution.py:254
  118.4 10.9 %all-to-all-start.2 = ((f32[32,8,128]{2,1,0:T(8,128)}), f32[32,8,128]{2,1,0:T(8,128)S(1)}, u32[]{:S(2)}, u32[]{:S(2)}) async-start(f32[32,8,128]{2,1,0:T(8,128)} %bitcast.6), calls=%async_computation.2 | async-start | bytes 262144 | tf_op jit(solution)/shard_map/all_to_all | solution.py:328

commit v29 on v25

--- a/solution.py
+++ b/solution.py
@@ -46,7 +46,7 @@
         out = jnp.dot(mixer, parts, preferred_element_type=jnp.float32)
         held[b] = out[:, :width] + out[:, width:]
     strip = 16
-    piece = BLOCK // 4
+    piece = BLOCK // 2
 
     def body(step, carry):
         at = pl.multiple_of(step * strip, strip)
@@ -63,7 +63,7 @@
         return carry
 
     copies = []
-    for part in range(4):
+    for part in range(2):
         first = part * piece // strip
         lax.fori_loop(first, first + piece // strip, body, 0)
         span = pl.ds(part * piece, piece)
@@ -87,7 +87,7 @@
             pltpu.VMEM((rows // 128, 128), jnp.int32),
             pltpu.VMEM(shape, jnp.float32),
             pltpu.SemaphoreType.DMA((5,)),
-            pltpu.SemaphoreType.DMA((4,)),
+            pltpu.SemaphoreType.DMA((2,)),
         ],
         compiler_params=pltpu.CompilerParams(vmem_limit_bytes=61 * 2**20),
     )(flips.reshape(rows // 128, 128), panel.reshape(shape))

time: 130 us -> 131 us (level)
  no operation moved by 1% of the time
where the time goes in v29:
time: 131 us; the launch traced here: 130 us
  waiting for transfers between devices  93.4 us (71%)
  starting transfers between devices  21.7 us (17%)
  Pallas kernels  11.6 us (9%)
  local copies, waits for them, and re-layouts  1.47 us (1%)
    all_to_all x1, waiting for transfers between devices, on_device(): slices = lax.all_to_all(local, AXES, 0, 0, tiled=True)  48.5 us
    ppermute x6, waiting for transfers between devices, swap(): return lax.ppermute(value, axis, pairs)  38.5 us
    ppermute x6, starting transfers between devices, swap(): return lax.ppermute(value, axis, pairs)  8.57 us
    all_to_all x1, starting transfers between devices, on_device(): slices = lax.all_to_all(local, AXES, 0, 0, tiled=True)  7.3 us
    all_to_all x1, waiting for transfers between devices, on_device(): lax.all_to_all(chosen.reshape(devices, most, width), AXES, 0, 0, tiled=True)  5.73 us
    pallas_call x1, Pallas kernels, local_transform(): pl.pallas_call(functools.partial(local_kernel, scale), out_shape=jax.Shap...  3.91 us
    all_to_all x1, starting transfers between devices, on_device(): lax.all_to_all(chosen.reshape(devices, most, width), AXES, 0, 0, tiled=True)  3.11 us
    pallas_call x1, Pallas kernels, gram_part(): pl.pallas_call(part_kernel, out_shape=jax.ShapeDtypeStruct((width, width)...  3.04 us
  transfers between devices with their start and end apart: 9, of which 8 were waited for; matrix products, arithmetic and copies ran while one was open for 2% of the time, Pallas kernels for 4%

profile of v29, /device:TPU:0, one launch (start us, length us, event | category | flops | bytes accessed | tf_op | source)
XLA Modules:
  0.0 130.2 jit_solution(3177625472673676473)
XLA Ops:
  0.6 3.9 %shard_map.58 = f32[16,256,128]{2,1,0:T(8,128)} custom-call(s32[32,128]{1,0:T(8,128)} %bitcast.14, f32[16,256,128]{2,1,0:T(8,128)} %bitcast.13), custom_call_target="tpu_custom_call" | custom-call | tf_op jit(solution)/shard_map/pallas_call | solution.py:81
  4.6 0.0 copy-start
  4.6 7.3 %all-to-all-start = ((f32[32,128,128]{2,1,0:T(8,128)}), f32[32,128,128]{2,1,0:T(8,128)S(1)}, u32[]{:S(2)}, u32[]{:S(2)}) async-start(f32[32,128,128]{2,1,0:T(8,128)} %bitcast.12), calls=%async_computation | async-start | bytes 4194304 | tf_op jit(solution)/shard_map/all_to_all | solution.py:315
  11.9 0.3 shard_map.59
  12.2 0.1 reshape.41
  12.3 0.7 shard_map.60.counts_ref
  13.0 0.1 and_select_fusion
  13.1 0.2 convert_reduce_fusion
  13.2 0.1 multiply_add_fusion
  13.3 0.1 fusion.1.order_ref
  13.4 48.5 %all-to-all-done.in_ref = f32[32,128,128]{2,1,0:T(8,128)S(1)} async-done(((f32[32,128,128]{2,1,0:T(8,128)}), f32[32,128,128]{2,1,0:T(8,128)S(1)}, u32[]{:S(2)}, u32[]{:S(2)}) %all-to-all-start) | async-done | bytes 2097184 | tf_op jit(solution)/shard_map/all_to_all | solution.py:315
  62.0 1.5 %shard_map.61.held_ref = f32[32,128,128]{2,1,0:T(8,128)} custom-call(f32[32,128,128]{2,1,0:T(8,128)S(1)} %all-to-all-done.in_ref), custom_call_target="tpu_custom_call" | custom-call | tf_op jit(solution)/shard_map/pallas_call | solution.py:130
  63.4 2.7 %all-to-all-start.1 = ((f32[32,128,128]{2,1,0:T(8,128)}), f32[32,128,128]{2,1,0:T(8,128)S(1)}, u32[]{:S(2)}, u32[]{:S(2)}) async-start(f32[32,128,128]{2,1,0:T(8,128)} %shard_map.61.held_ref), calls=%async_computation.1 | async-start | bytes 4194304 | tf_op jit(solution)/shard_map/all_to_all | solution.py:318
  66.2 3.0 %shard_map.62 = f32[128,128]{1,0:T(8,128)S(1)} custom-call(f32[128,32]{1,0:T(8,128)S(1)} %shard_map.60.counts_ref, f32[32,128,128]{2,1,0:T(8,128)} %shard_map.61.held_ref), custom_call_target="tpu_custom_call" | custom-call | tf_op jit(solution)/shard_map/pallas_call | solution.py:243
  69.3 0.2 collective-permute-start
  69.4 1.1 collective-permute-done
  70.5 1.6 %collective-permute-start.1 = (f32[64,128]{1,0:T(8,128)S(1)}, f32[64,128]{1,0:T(8,128)S(1)}, u32[]{:S(2)}, u32[]{:S(2)}) collective-permute-start(f32[64,128]{1,0:T(8,128)S(1)} %dynamic-slice_add_fusion), channel_id=1, source_target_pairs={{0,16},{8,24},{16,0},{24,8},{1,17},{9,25},{17,1},{25,9},{2,18},{10... | collective-permute-start | bytes 98312 | tf_op jit(solution)/shard_map/ppermute | solution.py:254
  72.2 8.0 %collective-permute-done.1 = f32[64,128]{1,0:T(8,128)S(1)} collective-permute-done((f32[64,128]{1,0:T(8,128)S(1)}, f32[64,128]{1,0:T(8,128)S(1)}, u32[]{:S(2)}, u32[]{:S(2)}) %collective-permute-start.1) | collective-permute-done | bytes 32800 | tf_op jit(solution)/shard_map/ppermute | solution.py:254
  80.2 1.9 %collective-permute-start.2 = (f32[64,128]{1,0:T(8,128)S(1)}, f32[64,128]{1,0:T(8,128)S(1)}, u32[]{:S(2)}, u32[]{:S(2)}) collective-permute-start(f32[64,128]{1,0:T(8,128)S(1)} %add.42), channel_id=1, source_target_pairs={{0,1},{1,0},{2,3},{3,2},{4,5},{5,4},{6,7},{7,6},{8,9},{9,8},{10,11... | collective-permute-start | bytes 98312 | tf_op jit(solution)/shard_map/ppermute | solution.py:254
  82.1 9.7 %collective-permute-done.2 = f32[64,128]{1,0:T(8,128)S(1)} collective-permute-done((f32[64,128]{1,0:T(8,128)S(1)}, f32[64,128]{1,0:T(8,128)S(1)}, u32[]{:S(2)}, u32[]{:S(2)}) %collective-permute-start.2) | collective-permute-done | bytes 32800 | tf_op jit(solution)/shard_map/ppermute | solution.py:254
  91.8 0.0 collective-permute-start.3
  91.8 9.6 %collective-permute-done.3 = f32[64,128]{1,0:T(8,128)S(1)} collective-permute-done((f32[64,128]{1,0:T(8,128)S(1)}, f32[64,128]{1,0:T(8,128)S(1)}, u32[]{:S(2)}, u32[]{:S(2)}) %collective-permute-start.3) | collective-permute-done | bytes 32800 | tf_op jit(solution)/shard_map/ppermute | solution.py:254
  101.4 4.7 %collective-permute-start.4 = (f32[64,128]{1,0:T(8,128)S(1)}, f32[64,128]{1,0:T(8,128)S(1)}, u32[]{:S(2)}, u32[]{:S(2)}) collective-permute-start(f32[64,128]{1,0:T(8,128)S(1)} %add.44), channel_id=1, source_target_pairs={{0,4},{1,5},{2,6},{3,7},{4,0},{5,1},{6,2},{7,3},{8,12},{9,13},{10,... | collective-permute-start | bytes 98312 | tf_op jit(solution)/shard_map/ppermute | solution.py:254
  106.1 10.2 %collective-permute-done.4 = f32[64,128]{1,0:T(8,128)S(1)} collective-permute-done((f32[64,128]{1,0:T(8,128)S(1)}, f32[64,128]{1,0:T(8,128)S(1)}, u32[]{:S(2)}, u32[]{:S(2)}) %collective-permute-start.4) | collective-permute-done | bytes 32800 | tf_op jit(solution)/shard_map/ppermute | solution.py:254
  116.3 0.7 all-to-all-done.1
  117.0 0.1 collective-permute-start.5
  117.1 1.3 %gather_fusion = f32[256,128]{1,0:T(8,128)} fusion(f32[4096,128]{1,0:T(8,128)S(1)} %bitcast.8, s32[1024]{0:T(1024)S(1)} %pad_clamp_fusion), kind=kCustom, calls=%fused_computation | custom fusion | bytes 263168 | tf_op jit(solution)/shard_map/jit(_take)/gather | solution.py:327
  118.4 3.1 %all-to-all-start.2 = ((f32[32,8,128]{2,1,0:T(8,128)}), f32[32,8,128]{2,1,0:T(8,128)S(1)}, u32[]{:S(2)}, u32[]{:S(2)}) async-start(f32[32,8,128]{2,1,0:T(8,128)} %bitcast.6), calls=%async_computation.2 | async-start | bytes 262144 | tf_op jit(solution)/shard_map/all_to_all | solution.py:328
  121.6 1.3 %shard_map.63 = f32[4096,128]{1,0:T(8,128)} custom-call(f32[4096,128]{1,0:T(8,128)S(1)} %bitcast.9), custom_call_target="tpu_custom_call" | custom-call | tf_op jit(solution)/shard_map/pallas_call | solution.py:150
  122.9 0.6 broadcast_multiply_fusion
  123.5 5.7 %all-to-all-done.2 = f32[32,8,128]{2,1,0:T(8,128)S(1)} async-done(((f32[32,8,128]{2,1,0:T(8,128)}), f32[32,8,128]{2,1,0:T(8,128)S(1)}, u32[]{:S(2)}, u32[]{:S(2)}) %all-to-all-start.2) | async-done | bytes 131104 | tf_op jit(solution)/shard_map/all_to_all | solution.py:328
  129.3 0.9 shard_map.64
  (13 shorter events, 0.1 us)
Async XLA Ops:
  4.6 7.3 %copy-start = (s32[8192]{0:T(1024)S(1)}, s32[8192]{0:T(1024)}, u32[]{:S(2)}) copy-start(s32[8192]{0:T(1024)} %param.5) | copy-start | bytes 98308
  4.6 57.4 %all-to-all-start = ((f32[32,128,128]{2,1,0:T(8,128)}), f32[32,128,128]{2,1,0:T(8,128)S(1)}, u32[]{:S(2)}, u32[]{:S(2)}) async-start(f32[32,128,128]{2,1,0:T(8,128)} %bitcast.12), calls=%async_computation | async-start | bytes 4194304 | tf_op jit(solution)/shard_map/all_to_all | solution.py:315
  63.4 53.5 %all-to-all-start.1 = ((f32[32,128,128]{2,1,0:T(8,128)}), f32[32,128,128]{2,1,0:T(8,128)S(1)}, u32[]{:S(2)}, u32[]{:S(2)}) async-start(f32[32,128,128]{2,1,0:T(8,128)} %shard_map.61.held_ref), calls=%async_computation.1 | async-start | bytes 4194304 | tf_op jit(solution)/shard_map/all_to_all | solution.py:318
  69.3 1.3 collective-permute-start
  70.5 9.6 %collective-permute-start.1 = (f32[64,128]{1,0:T(8,128)S(1)}, f32[64,128]{1,0:T(8,128)S(1)}, u32[]{:S(2)}, u32[]{:S(2)}) collective-permute-start(f32[64,128]{1,0:T(8,128)S(1)} %dynamic-slice_add_fusion), channel_id=1, source_target_pairs={{0,16},{8,24},{16,0},{24,8},{1,17},{9,25},{17,1},{25,9},{2,18},{10... | collective-permute-start | bytes 98312 | tf_op jit(solution)/shard_map/ppermute | solution.py:254
  80.2 11.6 %collective-permute-start.2 = (f32[64,128]{1,0:T(8,128)S(1)}, f32[64,128]{1,0:T(8,128)S(1)}, u32[]{:S(2)}, u32[]{:S(2)}) collective-permute-start(f32[64,128]{1,0:T(8,128)S(1)} %add.42), channel_id=1, source_target_pairs={{0,1},{1,0},{2,3},{3,2},{4,5},{5,4},{6,7},{7,6},{8,9},{9,8},{10,11... | collective-permute-start | bytes 98312 | tf_op jit(solution)/shard_map/ppermute | solution.py:254
  91.8 9.6 %collective-permute-start.3 = (f32[64,128]{1,0:T(8,128)S(1)}, f32[64,128]{1,0:T(8,128)S(1)}, u32[]{:S(2)}, u32[]{:S(2)}) collective-permute-start(f32[64,128]{1,0:T(8,128)S(1)} %add.43), channel_id=1, source_target_pairs={{0,2},{1,3},{2,0},{3,1},{4,6},{5,7},{6,4},{7,5},{8,10},{9,11},{10,... | collective-permute-start | bytes 98312 | tf_op jit(solution)/shard_map/ppermute | solution.py:254
  101.4 14.9 %collective-permute-start.4 = (f32[64,128]{1,0:T(8,128)S(1)}, f32[64,128]{1,0:T(8,128)S(1)}, u32[]{:S(2)}, u32[]{:S(2)}) collective-permute-start(f32[64,128]{1,0:T(8,128)S(1)} %add.44), channel_id=1, source_target_pairs={{0,4},{1,5},{2,6},{3,7},{4,0},{5,1},{6,2},{7,3},{8,12},{9,13},{10,... | collective-permute-start | bytes 98312 | tf_op jit(solution)/shard_map/ppermute | solution.py:254
  117.0 4.6 %collective-permute-start.5 = (f32[128,128]{1,0:T(8,128)S(1)}, f32[128,128]{1,0:T(8,128)S(1)}, u32[]{:S(2)}, u32[]{:S(2)}) collective-permute-start(f32[128,128]{1,0:T(8,128)S(1)} %constant_dynamic-update-slice_fusion), channel_id=1, source_target_pairs={{0,8},{8,0},{16,24},{24,16},{1,9},{9,1},{17,25},{25,17},{2,10},{10... | collective-permute-start | bytes 196616 | tf_op jit(solution)/shard_map/ppermute | solution.py:254
  118.4 10.9 %all-to-all-start.2 = ((f32[32,8,128]{2,1,0:T(8,128)}), f32[32,8,128]{2,1,0:T(8,128)S(1)}, u32[]{:S(2)}, u32[]{:S(2)}) async-start(f32[32,8,128]{2,1,0:T(8,128)} %bitcast.6), calls=%async_computation.2 | async-start | bytes 262144 | tf_op jit(solution)/shard_map/all_to_all | solution.py:328
